TPU v7x, 32 devices: a whole 2x2x4 slice. The times are simulated.
32 devices in a mesh: dp: 4 (over x, core), expert: 8 (over z, y).
Axes of the slice: x: 2, y: 2, z: 4, core: 2. Of those that a mesh axis runs over, the one named last changes fastest.
Arguments:
- tokens: bfloat16 [1536, 2048], P(('dp', 'expert')), may hold values from -6 to 6
- expert_ids: int32 [1536, 8], P(('dp', 'expert')), may hold values from 0 to 7, all different within a row; in each aligned block of 48 rows (0 to 47, 48 to 95, ...) at most 48 rows name the same one
- gate_probs: float32 [1536, 8], P(('dp', 'expert')), may hold values from 0.05 to 0.5
- out_cot: bfloat16 [1536, 2048], P(('dp', 'expert')), may hold values from -1.5 to 1.5
- w_gate: bfloat16 [8, 2048, 768], P('expert'), may hold values from -0.125 to 0.125
- w_up: bfloat16 [8, 2048, 768], P('expert'), may hold values from -0.125 to 0.125
- w_down: bfloat16 [8, 768, 2048], P('expert'), may hold values from -0.21875 to 0.21875
Outputs:
- layer_out: bfloat16 [1536, 2048], P(('dp', 'expert'))
- input_grad: bfloat16 [1536, 2048], P(('dp', 'expert'))
- gate_wgrad: float32 [8, 2048, 768], P('expert', 'dp')
- up_wgrad: float32 [8, 2048, 768], P('expert', 'dp')
- down_wgrad: float32 [8, 768, 2048], P('expert', 'dp')
Inputs may be any that keep to these rules, and one draw needn't show every extreme that they name: `expert_ids`: each token names 8 different experts. Among the 48 tokens of one device, at most 48 name the same expert, and in every draw some expert is named by exactly 48 tokens of some device.
All inputs are finite; a program needn't handle non-finite values.
Results may differ from a plain program's by a relative error of at most 0.012.
Values may be sent and summed in bfloat16 or wider, within the bound.
No kernel may reach another device: no remote copies, remote signals or barrier semaphores. Data moves between devices by JAX's collectives and lax.ppermute only.
A program may use at most 128 MiB of HBM per device.

v0:
```python
import jax
import jax.numpy as jnp
from jax import lax
from jax.sharding import PartitionSpec as P


def contract_rows(left, right):
    return lax.dot_general(
        left, right, (((0,), (0,)), ((), ())), preferred_element_type=jnp.float32
    )


def contract_cols(left, right):
    return lax.dot_general(
        left, right, (((1,), (1,)), ((), ())), preferred_element_type=jnp.float32
    )


def shards(tokens, expert_ids, gate_probs, out_cot, w_gate, w_up, w_down):
    tok_count, width = tokens.shape
    top = expert_ids.shape[1]
    experts = lax.axis_size("expert")
    slots = min(tok_count, 4 * tok_count * top // (3 * experts))
    flat_ids = expert_ids.reshape(-1)
    onehot = (flat_ids[:, None] == jnp.arange(experts, dtype=jnp.int32)[None, :]).astype(jnp.int32)
    ranks = jnp.sum(jnp.cumsum(onehot, axis=0) * onehot, axis=1) - 1
    target = flat_ids * slots + ranks
    token_rows = jnp.repeat(tokens, top, axis=0)
    outbound = jnp.zeros((experts * slots, width), tokens.dtype).at[target].set(token_rows)
    outbound = outbound.reshape(experts, slots, width)
    gate_mat = w_gate[0]
    up_mat = w_up[0]
    down_mat = w_down[0]
    hidden_width = gate_mat.shape[1]
    arrived = lax.all_to_all(outbound, "expert", split_axis=0, concat_axis=0, tiled=True)
    sources = arrived.shape[0]
    count = arrived.shape[1]
    rows = arrived.reshape(-1, width)
    gate_pre = jnp.dot(rows, gate_mat, preferred_element_type=jnp.float32)
    up_pre = jnp.dot(rows, up_mat, preferred_element_type=jnp.float32)
    hidden = (gate_pre * jax.nn.sigmoid(gate_pre) * up_pre).astype(jnp.bfloat16)
    result = jnp.dot(hidden, down_mat, preferred_element_type=jnp.float32).astype(jnp.bfloat16)
    expert_out, hidden, gate_pre, up_pre, arrived = (
        result.reshape(sources, count, width),
        hidden.reshape(sources, count, hidden_width),
        gate_pre.reshape(sources, count, hidden_width),
        up_pre.reshape(sources, count, hidden_width),
        arrived,
    )
    returned = lax.all_to_all(expert_out, "expert", split_axis=0, concat_axis=0, tiled=True)
    picked = returned.reshape(-1, width)[target].reshape(tok_count, top, width)
    layer_out = jnp.sum(gate_probs[:, :, None] * picked.astype(jnp.float32), axis=1).astype(
        jnp.bfloat16
    )
    out_grad = (gate_probs[:, :, None] * out_cot[:, None, :].astype(jnp.float32)).astype(
        jnp.bfloat16
    )
    outbound_grad = (
        jnp.zeros((experts * slots, width), tokens.dtype)
        .at[target]
        .set(out_grad.reshape(-1, width))
    )
    arrived_grad = lax.all_to_all(
        outbound_grad.reshape(experts, slots, width),
        "expert",
        split_axis=0,
        concat_axis=0,
        tiled=True,
    ).reshape(-1, width)
    x_rows = arrived.reshape(-1, width)
    hidden_rows = hidden.reshape(-1, hidden_width)
    gate_rows = gate_pre.reshape(-1, hidden_width)
    up_rows = up_pre.reshape(-1, hidden_width)
    hidden_grad = contract_cols(arrived_grad, down_mat)
    sigma = jax.nn.sigmoid(gate_rows)
    gate_grad = (hidden_grad * up_rows * sigma * (1.0 + gate_rows * (1.0 - sigma))).astype(
        jnp.bfloat16
    )
    up_grad = (hidden_grad * gate_rows * sigma).astype(jnp.bfloat16)
    row_grad = (contract_cols(gate_grad, gate_mat) + contract_cols(up_grad, up_mat)).astype(
        jnp.bfloat16
    )
    back_grad = lax.all_to_all(
        row_grad.reshape(experts, slots, width), "expert", split_axis=0, concat_axis=0, tiled=True
    )
    gathered = back_grad.reshape(-1, width)[target].reshape(tok_count, top, width)
    input_grad = jnp.sum(gathered.astype(jnp.float32), axis=1).astype(jnp.bfloat16)
    down_grad = lax.psum_scatter(
        contract_rows(hidden_rows, arrived_grad).astype(jnp.bfloat16),
        "dp",
        scatter_dimension=0,
        tiled=True,
    ).astype(jnp.float32)
    gate_part = lax.psum_scatter(
        contract_rows(x_rows, gate_grad).astype(jnp.bfloat16), "dp", scatter_dimension=0, tiled=True
    ).astype(jnp.float32)
    up_part = lax.psum_scatter(
        contract_rows(x_rows, up_grad).astype(jnp.bfloat16), "dp", scatter_dimension=0, tiled=True
    ).astype(jnp.float32)
    return (layer_out, input_grad, gate_part[None], up_part[None], down_grad[None])


def solution(mesh):
    placed = (
        P(("dp", "expert"), None),
        P(("dp", "expert"), None),
        P(("dp", "expert"), None),
        P(("dp", "expert"), None),
        P("expert", None, None),
        P("expert", None, None),
        P("expert", None, None),
    )
    return jax.shard_map(
        shards,
        mesh=mesh,
        in_specs=placed,
        out_specs=(
            P(("dp", "expert"), None),
            P(("dp", "expert"), None),
            P("expert", "dp", None),
            P("expert", "dp", None),
            P("expert", "dp", None),
        ),
        check_vma=False,
    )
```

profile of v0, /device:TPU:0, one launch (start us, length us, event | category | flops | bytes accessed | tf_op | source)
XLA Modules:
  0.0 241.6 jit_solution(7661943377887404574)
XLA Ops:
  10.4 4.5 %scatter_custom_fusion = bf16[384,2048]{1,0:T(8,128)(2,1)} fusion(s32[384]{0:T(512)S(1)} %fusion.30, bf16[48,2048]{1,0:T(8,128)(2,1)} %param.7, bf16[]{:T(256)} %constant.7.clone.1), kind=kCustom, calls=%fused_computation.27 | custom fusion | bytes 1769474 | tf_op jit(solution)/shard_map/scatter | solution.py:29
  14.9 7.4 %all-to-all-start = ((bf16[8,48,2048]{2,1,0:T(8,128)(2,1)}), bf16[8,48,2048]{2,1,0:T(8,128)(2,1)}, u32[]{:S(2)}, u32[]{:S(2)}) async-start(bf16[8,48,2048]{2,1,0:T(8,128)(2,1)} %bitcast.71), calls=%async_computation | async-start | bytes 3145728 | tf_op jit(solution)/shard_map/all_to_all | solution.py:35
  24.0 4.2 %scatter_custom_fusion.1 = bf16[384,2048]{1,0:T(8,128)(2,1)} fusion(s32[384]{0:T(512)S(1)} %fusion.30, f32[48,2048]{1,0:T(8,128)S(1)} %convert_element_type.57, f32[384]{0:T(512)S(1)} %mul.77, bf16[]{:T(256)} %constant.7.clone.1), kind=kCustom, calls=%fused_computation.25 | custom fusion | flops 1572864 | bytes 1968130 | tf_op jit(solution)/shard_map/scatter | solution.py:61
  28.2 31.2 %all-to-all-done = bf16[8,48,2048]{2,1,0:T(8,128)(2,1)} async-done(((bf16[8,48,2048]{2,1,0:T(8,128)(2,1)}), bf16[8,48,2048]{2,1,0:T(8,128)(2,1)}, u32[]{:S(2)}, u32[]{:S(2)}) %all-to-all-start) | async-done | bytes 1572896 | tf_op jit(solution)/shard_map/all_to_all | solution.py:35
  59.4 4.3 %all-to-all-start.2 = ((bf16[8,48,2048]{2,1,0:T(8,128)(2,1)}), bf16[8,48,2048]{2,1,0:T(8,128)(2,1)}, u32[]{:S(2)}, u32[]{:S(2)}) async-start(bf16[8,48,2048]{2,1,0:T(8,128)(2,1)} %bitcast.70), calls=%async_computation.2 | async-start | bytes 3145728 | tf_op jit(solution)/shard_map/all_to_all | solution.py:63
  63.9 4.8 %fusion.8 = f32[384,768]{1,0:T(8,128)} fusion(bf16[384,2048]{1,0:T(8,128)(2,1)} %bitcast.4, bf16[1,2048,768]{2,1,0:T(8,128)(2,1)} %param.12), kind=kOutput, calls=%fused_computation.17 | convolution fusion | flops 1207959552 | bytes 5898240 | tf_op jit(solution)/shard_map/dot_general | solution.py:40
  68.7 31.6 %all-to-all-done.2 = bf16[8,48,2048]{2,1,0:T(8,128)(2,1)} async-done(((bf16[8,48,2048]{2,1,0:T(8,128)(2,1)}), bf16[8,48,2048]{2,1,0:T(8,128)(2,1)}, u32[]{:S(2)}, u32[]{:S(2)}) %all-to-all-start.2) | async-done | bytes 1572896 | tf_op jit(solution)/shard_map/all_to_all | solution.py:63
  100.3 3.9 %fusion.2 = f32[384,768]{1,0:T(8,128)S(1)} fusion(bf16[384,2048]{1,0:T(8,128)(2,1)} %bitcast.13, bf16[1,768,2048]{2,1,0:T(8,128)(2,1)} %param.13), kind=kOutput, calls=%fused_computation.11 | convolution fusion | flops 1207959552 | bytes 5898240 | tf_op jit(solution)/shard_map/dot_general | solution.py:14
  104.2 4.2 %multiply_convert_fusion.1 = (bf16[384,768]{1,0:T(8,128)(2,1)}, bf16[384,768]{1,0:T(8,128)(2,1)}, bf16[384,768]{1,0:T(8,128)(2,1)S(1)}) fusion(f32[384,768]{1,0:T(8,128)S(1)} %fusion.2, f32[384,768]{1,0:T(8,128)S(1)} %copy-done.7, bf16[384,2048]{1,0:T(8,128)(2,1)} %bitcast.4, bf16[1,2048,768]{2,1,0:T(8,128)(2,1)S(1)} %copy-done), kind=kOutput, calls=%fused_computation.32 | convolution fusion | flops 1212678144 | bytes 8847360 | tf_op jit(solution)/shard_map/dot_general | solution.py:39
  109.3 5.0 %convolution_convert_fusion.1 = bf16[2048,768]{1,0:T(8,128)(2,1)} fusion(bf16[384,2048]{1,0:T(8,128)(2,1)} %bitcast.4, bf16[384,768]{1,0:T(8,128)(2,1)S(1)} %get-tuple-element.7), kind=kOutput, calls=%fused_computation.5 | convolution fusion | flops 1209532416 | bytes 5308416 | tf_op jit(solution)/shard_map/dot_general | solution.py:8
  114.3 5.0 %convolution_convert_fusion.2 = bf16[2048,768]{1,0:T(8,128)(2,1)} fusion(bf16[384,2048]{1,0:T(8,128)(2,1)} %bitcast.4, bf16[384,768]{1,0:T(8,128)(2,1)} %get-tuple-element.5), kind=kOutput, calls=%fused_computation.6 | convolution fusion | flops 1209532416 | bytes 5308416 | tf_op jit(solution)/shard_map/dot_general | solution.py:8
  119.4 3.9 %fusion.6 = f32[384,2048]{1,0:T(8,128)S(1)} fusion(bf16[384,768]{1,0:T(8,128)(2,1)} %copy-done.6, bf16[1,2048,768]{2,1,0:T(8,128)(2,1)} %param.12), kind=kOutput, calls=%fused_computation.15 | convolution fusion | flops 1207959552 | bytes 6881280 | tf_op jit(solution)/shard_map/dot_general | solution.py:14
  123.3 2.6 %add_convert_fusion = bf16[384,2048]{1,0:T(8,128)(2,1)} fusion(f32[384,2048]{1,0:T(8,128)S(1)} %fusion.6, bf16[384,768]{1,0:T(8,128)(2,1)S(1)} %copy-done.5, bf16[1,2048,768]{2,1,0:T(8,128)(2,1)S(1)} %copy-done), kind=kOutput, calls=%fused_computation.23 | convolution fusion | flops 1209532416 | bytes 8454144 | tf_op jit(solution)/shard_map/dot_general | solution.py:14
  125.9 4.3 %all-to-all-start.3 = ((bf16[8,48,2048]{2,1,0:T(8,128)(2,1)}), bf16[8,48,2048]{2,1,0:T(8,128)(2,1)}, u32[]{:S(2)}, u32[]{:S(2)}) async-start(bf16[8,48,2048]{2,1,0:T(8,128)(2,1)} %bitcast.72), calls=%async_computation.3 | async-start | bytes 3145728 | tf_op jit(solution)/shard_map/all_to_all | solution.py:83
  130.3 5.6 %convolution_convert_fusion = bf16[768,2048]{1,0:T(8,128)(2,1)} fusion(bf16[384,768]{1,0:T(8,128)(2,1)} %get-tuple-element.6, bf16[384,2048]{1,0:T(8,128)(2,1)} %bitcast.13), kind=kOutput, calls=%fused_computation.4 | convolution fusion | flops 1209532416 | bytes 5308416 | tf_op jit(solution)/shard_map/dot_general | solution.py:8
  135.9 4.6 %fusion.16 = bf16[384,2048]{1,0:T(8,128)(2,1)} fusion(bf16[384,768]{1,0:T(8,128)(2,1)} %get-tuple-element.6, bf16[1,768,2048]{2,1,0:T(8,128)(2,1)} %param.13), kind=kOutput, calls=%fused_computation.24 | convolution fusion | flops 1208745984 | bytes 5308416 | tf_op jit(solution)/shard_map/dot_general | solution.py:42
  140.5 26.2 %all-to-all-done.3 = bf16[8,48,2048]{2,1,0:T(8,128)(2,1)} async-done(((bf16[8,48,2048]{2,1,0:T(8,128)(2,1)}), bf16[8,48,2048]{2,1,0:T(8,128)(2,1)}, u32[]{:S(2)}, u32[]{:S(2)}) %all-to-all-start.3) | async-done | bytes 1572896 | tf_op jit(solution)/shard_map/all_to_all | solution.py:83
  166.7 4.5 %all-to-all-start.1 = ((bf16[8,48,2048]{2,1,0:T(8,128)(2,1)}), bf16[8,48,2048]{2,1,0:T(8,128)(2,1)}, u32[]{:S(2)}, u32[]{:S(2)}) async-start(bf16[8,48,2048]{2,1,0:T(8,128)(2,1)} %bitcast.73), calls=%async_computation.1 | async-start | bytes 3145728 | tf_op jit(solution)/shard_map/all_to_all | solution.py:50
  171.3 7.0 %gather_fusion.1 = bf16[384,2048]{1,0:T(8,128)(2,1)} fusion(bf16[384,2048]{1,0:T(8,128)(2,1)} %bitcast.15, s32[1024]{0:T(1024)S(1)} %pad_clamp_fusion), kind=kCustom, calls=%fused_computation.1 | custom fusion | bytes 3147264 | tf_op jit(solution)/shard_map/gather | solution.py:86
  178.3 29.6 %all-to-all-done.1 = bf16[8,48,2048]{2,1,0:T(8,128)(2,1)} async-done(((bf16[8,48,2048]{2,1,0:T(8,128)(2,1)}), bf16[8,48,2048]{2,1,0:T(8,128)(2,1)}, u32[]{:S(2)}, u32[]{:S(2)}) %all-to-all-start.1) | async-done | bytes 1572896 | tf_op jit(solution)/shard_map/all_to_all | solution.py:50
  207.9 6.7 %gather_fusion = bf16[384,2048]{1,0:T(8,128)(2,1)} fusion(bf16[384,2048]{1,0:T(8,128)(2,1)} %bitcast.9, s32[1024]{0:T(1024)S(1)} %pad_clamp_fusion), kind=kCustom, calls=%fused_computation | custom fusion | bytes 3147264 | tf_op jit(solution)/shard_map/gather | solution.py:51
  214.5 3.3 %bitcast_reduce_fusion = bf16[48,2048]{1,0:T(8,128)(2,1)} fusion(bf16[384,2048]{1,0:T(8,128)(2,1)} %gather_fusion.1), kind=kLoop, calls=%fused_computation.26 | loop fusion | flops 688128 | bytes 1769472 | tf_op jit(solution)/shard_map/reduce_sum | solution.py:87
  224.7 7.9 %reduce-scatter.8.cloned.1.call-done = bf16[192,2048]{1,0:T(8,128)(2,1)} async-done(((bf16[768,2048]{1,0:T(8,128)(2,1)}), bf16[192,2048]{1,0:T(8,128)(2,1)}) %reduce-scatter.8.cloned.1.call-update) | async-done | bytes 786448 | tf_op jit(solution)/shard_map/reduce_scatter | solution.py:88
  232.6 2.5 %bitcast_convert_fusion = f32[1,192,2048]{2,1,0:T(8,128)} fusion(bf16[192,2048]{1,0:T(8,128)(2,1)} %reduce-scatter.8.cloned.1.call-done), kind=kLoop, calls=%fused_computation.35 | loop fusion | flops 393216 | bytes 2359296 | tf_op jit(solution)/shard_map/broadcast_in_dim | solution.py:100
  (44 shorter events, 13.0 us)
Async XLA Ops:
  7.2 97.1 %copy-start = (bf16[1,2048,768]{2,1,0:T(8,128)(2,1)S(1)}, bf16[1,2048,768]{2,1,0:T(8,128)(2,1)}, u32[]{:S(2)}) copy-start(bf16[1,2048,768]{2,1,0:T(8,128)(2,1)} %param.11) | copy-start | bytes 9437188
  14.9 7.4 %copy-start.4 = (f32[48,8]{0,1:T(8,128)S(1)}, f32[48,8]{0,1:T(8,128)}, u32[]{:S(2)}) copy-start(f32[48,8]{0,1:T(8,128)} %param.9) | copy-start | bytes 4612
  14.9 44.5 %all-to-all-start = ((bf16[8,48,2048]{2,1,0:T(8,128)(2,1)}), bf16[8,48,2048]{2,1,0:T(8,128)(2,1)}, u32[]{:S(2)}, u32[]{:S(2)}) async-start(bf16[8,48,2048]{2,1,0:T(8,128)(2,1)} %bitcast.71), calls=%async_computation | async-start | bytes 3145728 | tf_op jit(solution)/shard_map/all_to_all | solution.py:35
  22.4 0.6 copy-start.2
  59.4 40.9 %all-to-all-start.2 = ((bf16[8,48,2048]{2,1,0:T(8,128)(2,1)}), bf16[8,48,2048]{2,1,0:T(8,128)(2,1)}, u32[]{:S(2)}, u32[]{:S(2)}) async-start(bf16[8,48,2048]{2,1,0:T(8,128)(2,1)} %bitcast.70), calls=%async_computation.2 | async-start | bytes 3145728 | tf_op jit(solution)/shard_map/all_to_all | solution.py:63
  63.7 156.2 %reduce-scatter.6.cloned.1.call-start = ((), (), s32[]{:S(2)}) async-start(), calls=%async_computation.8 | async-start | bytes 3932160 | tf_op jit(solution)/shard_map/reduce_scatter | solution.py:97
  100.3 3.9 %copy-start.7 = (f32[384,768]{1,0:T(8,128)S(1)}, f32[384,768]{1,0:T(8,128)}, u32[]{:S(2)}) copy-start(f32[384,768]{1,0:T(8,128)} %fusion.8) | copy-start | bytes 3538948
  108.5 0.8 copy-start.6
  114.3 108.1 %reduce-scatter.4.cloned.1.call-start = ((), (), s32[]{:S(2)}) async-start(), calls=%async_computation.7 | async-start | bytes 3932160 | tf_op jit(solution)/shard_map/reduce_scatter | solution.py:94
  119.4 3.9 %copy-start.5 = (bf16[384,768]{1,0:T(8,128)(2,1)S(1)}, bf16[384,768]{1,0:T(8,128)(2,1)}, u32[]{:S(2)}) copy-start(bf16[384,768]{1,0:T(8,128)(2,1)} %get-tuple-element.5) | copy-start | bytes 1769476
  125.9 40.8 %all-to-all-start.3 = ((bf16[8,48,2048]{2,1,0:T(8,128)(2,1)}), bf16[8,48,2048]{2,1,0:T(8,128)(2,1)}, u32[]{:S(2)}, u32[]{:S(2)}) async-start(bf16[8,48,2048]{2,1,0:T(8,128)(2,1)} %bitcast.72), calls=%async_computation.3 | async-start | bytes 3145728 | tf_op jit(solution)/shard_map/all_to_all | solution.py:83
  130.2 102.4 %reduce-scatter.8.cloned.1.call-start = ((), (), s32[]{:S(2)}) async-start(), calls=%async_computation.9 | async-start | bytes 3932160 | tf_op jit(solution)/shard_map/reduce_scatter | solution.py:88
  166.7 41.2 %all-to-all-start.1 = ((bf16[8,48,2048]{2,1,0:T(8,128)(2,1)}), bf16[8,48,2048]{2,1,0:T(8,128)(2,1)}, u32[]{:S(2)}, u32[]{:S(2)}) async-start(bf16[8,48,2048]{2,1,0:T(8,128)(2,1)} %bitcast.73), calls=%async_computation.1 | async-start | bytes 3145728 | tf_op jit(solution)/shard_map/all_to_all | solution.py:50
  214.5 3.3 %copy-start.1 = (bf16[384,2048]{1,0:T(8,128)(2,1)S(1)}, bf16[384,2048]{1,0:T(8,128)(2,1)}, u32[]{:S(2)}) copy-start(bf16[384,2048]{1,0:T(8,128)(2,1)} %gather_fusion) | copy-start | bytes 4718596
  214.5 3.3 %copy-start.3 = (f32[48,8]{1,0:T(8,128)S(1)}, f32[48,8]{1,0:T(8,128)}, u32[]{:S(2)}) copy-start(f32[48,8]{1,0:T(8,128)} %copy-done.2) | copy-start | bytes 4612
Sparse Core Ops, SparseCore 0:
  114.4 36.9 reduce-scatter.5
  154.1 37.9 reduce-scatter.3
  194.6 37.9 reduce-scatter.7
where the time goes:
time: 242 us
  waiting for transfers between devices  127 us (52%)
  matrix products  39.5 us (16%)
  local copies, waits for them, and re-layouts  21.3 us (9%)
  starting transfers between devices  20.9 us (9%)
  other arithmetic  19.4 us (8%)
  between operations  13.9 us (6%)
    all_to_all x1, waiting for transfers between devices, shards(): lax.all_to_all(outbound_grad.reshape(experts, slots, width), 'expert', sp...  31.6 us
    all_to_all x1, waiting for transfers between devices, shards(): lax.all_to_all(outbound, 'expert', split_axis=0, concat_axis=0, tiled=True)  31.2 us
    all_to_all x1, waiting for transfers between devices, shards(): lax.all_to_all(expert_out, 'expert', split_axis=0, concat_axis=0, tiled=T...  29.6 us
    all_to_all x1, waiting for transfers between devices, shards(): lax.all_to_all(row_grad.reshape(experts, slots, width), 'expert', split_a...  26.2 us
    dot_general x3, matrix products, contract_rows(): lax.dot_general(left, right, (((0,), (0,)), ((), ())), preferred_element_...  15.6 us
    dot_general x3, matrix products, contract_cols(): lax.dot_general(left, right, (((1,), (1,)), ((), ())), preferred_element_...  10.4 us
    reduce_scatter x1, waiting for transfers between devices, shards(): lax.psum_scatter(contract_rows(hidden_rows, arrived_grad).astype(jnp.bflo...  7.91 us
    all_to_all x1, starting transfers between devices, shards(): lax.all_to_all(outbound, 'expert', split_axis=0, concat_axis=0, tiled=True)  7.41 us
  transfers between devices with their start and end apart: 7, of which 5 were waited for; matrix products, arithmetic and copies ran while one was open for 23% of the time, Pallas kernels for 0%

commit v1 on v0

--- a/solution.py
+++ b/solution.py
@@ -16,7 +16,7 @@
     )
 
 
-def shards(tokens, expert_ids, gate_probs, out_cot, w_gate, w_up, w_down):
+def routed(tokens, expert_ids, gate_probs, out_cot, w_gate, w_up, w_down):
     tok_count, width = tokens.shape
     top = expert_ids.shape[1]
     experts = lax.axis_size("expert")
@@ -100,6 +100,99 @@
     return (layer_out, input_grad, gate_part[None], up_part[None], down_grad[None])
 
 
+def swap(value, axis, mask):
+    size = lax.axis_size(axis)
+    return lax.ppermute(value, axis, [(i, i ^ mask) for i in range(size)])
+
+
+def dense(tokens, expert_ids, gate_probs, out_cot, w_gate, w_up, w_down):
+    count, width = tokens.shape
+    experts = lax.axis_size("expert")
+    owners = lax.axis_size("dp")
+    me = lax.axis_index("expert")
+    mine = lax.axis_index("dp")
+    evens = range(2, experts, 2)
+
+    named = expert_ids[:, :, None] == jnp.arange(experts, dtype=jnp.int32)[None, None, :]
+    probs = jnp.sum(jnp.where(named, gate_probs[:, :, None], 0.0), axis=1)
+    high = lax.reduce_precision(probs, 8, 7)
+    low = probs - high
+    lanes = 128 * (-(-2 * experts // 128))
+    extra = jnp.concatenate(
+        [high, low, jnp.zeros((count, lanes - 2 * experts), jnp.float32)], axis=1
+    ).astype(jnp.bfloat16)
+    payload = jnp.concatenate([tokens, extra], axis=1)
+
+    def gather(own):
+        even = [own] + [swap(own, "expert", m) for m in evens]
+        odd = [swap(block, "expert", 1) for block in even]
+        return jnp.concatenate(even + odd, axis=0)
+
+    rows_ext = gather(payload)
+    cot_rows = gather(out_cot)
+    rows = rows_ext[:, :width]
+    column = lax.broadcasted_iota(jnp.int32, (1, lanes), 1)
+    chosen = (column == me) | (column == me + experts)
+    row_probs = jnp.sum(
+        jnp.where(chosen, rows_ext[:, width:].astype(jnp.float32), 0.0), axis=1, keepdims=True
+    )
+
+    gate_mat, up_mat, down_mat = w_gate[0], w_up[0], w_down[0]
+    gate_pre = jnp.dot(rows, gate_mat, preferred_element_type=jnp.float32)
+    up_pre = jnp.dot(rows, up_mat, preferred_element_type=jnp.float32)
+    sigma = jax.nn.sigmoid(gate_pre)
+    hidden = (gate_pre * sigma * up_pre).astype(jnp.bfloat16)
+    expert_out = row_probs * jnp.dot(hidden, down_mat, preferred_element_type=jnp.float32)
+    expert_out = expert_out.astype(jnp.bfloat16)
+    out_grad = (row_probs * cot_rows.astype(jnp.float32)).astype(jnp.bfloat16)
+    hidden_grad = contract_cols(out_grad, down_mat)
+    gate_grad = (hidden_grad * up_pre * sigma * (1.0 + gate_pre * (1.0 - sigma))).astype(
+        jnp.bfloat16
+    )
+    up_grad = (hidden_grad * gate_pre * sigma).astype(jnp.bfloat16)
+    row_grad = (contract_cols(gate_grad, gate_mat) + contract_cols(up_grad, up_mat)).astype(
+        jnp.bfloat16
+    )
+
+    def give_back(values):
+        half = values.shape[0] // 2
+        held = values[:half].astype(jnp.float32) + swap(values[half:], "expert", 1).astype(
+            jnp.float32
+        )
+        parts = held.astype(jnp.bfloat16).reshape(experts // 2, count, width)
+        total = held[:count]
+        for m in evens:
+            total = total + swap(parts[m // 2], "expert", m).astype(jnp.float32)
+        return total.astype(jnp.bfloat16)
+
+    def reduced(left, right):
+        size = left.shape[1] // owners
+
+        def part(m):
+            columns = lax.dynamic_slice_in_dim(left, (mine ^ m) * size, size, 1)
+            return contract_rows(columns, right)
+
+        total = None
+        for m in range(owners - 2, -1, -2):
+            own = part(m) + swap(part(m + 1).astype(jnp.bfloat16), "dp", 1).astype(jnp.float32)
+            if m:
+                own = swap(own.astype(jnp.bfloat16), "dp", m).astype(jnp.float32)
+            total = own if total is None else total + own
+        return total[None]
+
+    down_grad = reduced(hidden, out_grad)
+    gate_part = reduced(rows, gate_grad)
+    up_part = reduced(rows, up_grad)
+    layer_out = give_back(expert_out)
+    input_grad = give_back(row_grad)
+    return (layer_out, input_grad, gate_part, up_part, down_grad)
+
+
+def shards(tokens, expert_ids, *rest):
+    every = expert_ids.shape[1] == lax.axis_size("expert")
+    return (dense if every else routed)(tokens, expert_ids, *rest)
+
+
 def solution(mesh):
     placed = (
         P(("dp", "expert"), None),

time: 242 us -> 173 us (0.71)
  waiting for transfers between devices: 127 us -> 85.1 us
  starting transfers between devices: 20.9 us -> 52.1 us
  matrix products: 39.5 us -> 20.1 us
  other arithmetic: 19.4 us -> 3.15 us
  between operations: 13.9 us -> 1.01 us
  local copies, waits for them, and re-layouts: 21.3 us -> 11.2 us
    all_to_all x4 -> x0, waiting for transfers between devices: 119 us -> none  [the longest x1 31.6 us: shards(): lax.all_to_all(outbound_grad.reshape(experts, slots, width), 'expert', sp...]
    ppermute x0 -> x31, waiting for transfers between devices: none -> 85.1 us  [swap(): return lax.ppermute(value, axis, [(i, i ^ mask) for i in range(size)])]
    ppermute x0 -> x31, starting transfers between devices: none -> 52.1 us  [swap(): return lax.ppermute(value, axis, [(i, i ^ mask) for i in range(size)])]
    all_to_all x4 -> x0, starting transfers between devices: 20.6 us -> none  [the longest x1 7.41 us: shards(): lax.all_to_all(outbound, 'expert', split_axis=0, concat_axis=0, tiled=True)]
    gather x2 -> x0, local copies, waits for them, and re-layouts: 13.7 us -> none  [the longest x1 7.03 us: shards(): back_grad.reshape(-1, width)[target].reshape(tok_count, top, width)]
    dot_general x3, matrix products: 13.6 us -> 4.6 us  [the longest x1 1.84 us: dense(): gate_pre = jnp.dot(rows, gate_mat, preferred_element_type=jnp.float32)]
    reduce_scatter x3 -> x0, waiting for transfers between devices: 7.91 us -> none  [the longest x1 7.91 us: shards(): lax.psum_scatter(contract_rows(hidden_rows, arrived_grad).astype(jnp.bflo...]
    broadcast_in_dim x3 -> x0, other arithmetic: 7.23 us -> none  [the longest x1 2.45 us: shards(): down_grad[None]]
  transfers between devices with their start and end apart: 7 -> 31, of which waited for: 5 -> 14; matrix products, arithmetic and copies ran while one was open for 23% -> 14% of each run, Pallas kernels for 0% -> 0%
where the time goes in v1:
time: 173 us
  waiting for transfers between devices  85.1 us (49%)
  starting transfers between devices  52.1 us (30%)
  matrix products  20.1 us (12%)
  local copies, waits for them, and re-layouts  11.2 us (6%)
  other arithmetic  3.15 us (2%)
    ppermute x31, waiting for transfers between devices, swap(): return lax.ppermute(value, axis, [(i, i ^ mask) for i in range(size)])  85.1 us
    ppermute x31, starting transfers between devices, swap(): return lax.ppermute(value, axis, [(i, i ^ mask) for i in range(size)])  52.1 us
    dot_general x12, matrix products, contract_rows(): lax.dot_general(left, right, (((0,), (0,)), ((), ())), preferred_element_...  11.2 us
    unnamed x22, local copies, waits for them, and re-layouts  7.76 us
    dot_general x3, matrix products, contract_cols(): lax.dot_general(left, right, (((1,), (1,)), ((), ())), preferred_element_...  4.31 us
  transfers between devices with their start and end apart: 31, of which 14 were waited for; matrix products, arithmetic and copies ran while one was open for 14% of the time, Pallas kernels for 0%

profile of v1, /device:TPU:0, one launch (start us, length us, event | category | flops | bytes accessed | tf_op | source)
XLA Modules:
  0.0 172.7 jit_solution(1089864880078634461)
XLA Ops:
  0.6 3.1 %collective-permute-start.11 = (bf16[48,2048]{1,0:T(8,128)(2,1)}, bf16[48,2048]{1,0:T(8,128)(2,1)}, u32[]{:S(2)}, u32[]{:S(2)}) collective-permute-start(bf16[48,2048]{1,0:T(8,128)(2,1)} %param.10), channel_id=1, source_target_pairs={{0,2},{1,3},{2,0},{3,1},{4,6},{5,7},{6,4},{7,5},{8,10},{9,11},{10,... | collective-permute-start | bytes 589832 | tf_op jit(solution)/shard_map/ppermute | solution.py:105
  3.7 2.6 %collective-permute-start.12 = (bf16[48,2048]{1,0:T(8,128)(2,1)}, bf16[48,2048]{1,0:T(8,128)(2,1)}, u32[]{:S(2)}, u32[]{:S(2)}) collective-permute-start(bf16[48,2048]{1,0:T(8,128)(2,1)} %param.10), channel_id=1, source_target_pairs={{0,4},{1,5},{2,6},{3,7},{4,0},{5,1},{6,2},{7,3},{8,12},{9,13},{10,... | collective-permute-start | bytes 589832 | tf_op jit(solution)/shard_map/ppermute | solution.py:105
  14.3 3.6 %collective-permute-start.1 = (bf16[48,2176]{1,0:T(8,128)(2,1)S(1)}, bf16[48,2176]{1,0:T(8,128)(2,1)S(1)}, u32[]{:S(2)}, u32[]{:S(2)}) collective-permute-start(bf16[48,2176]{1,0:T(8,128)(2,1)S(1)} %concatenate.12), channel_id=1, source_target_pairs={{0,4},{1,5},{2,6},{3,7},{4,0},{5,1},{6,2},{7,3},{8,12},{9,13},{10,... | collective-permute-start | bytes 626696 | tf_op jit(solution)/shard_map/ppermute | solution.py:105
  18.8 2.4 %collective-permute-done.12 = bf16[48,2048]{1,0:T(8,128)(2,1)} collective-permute-done((bf16[48,2048]{1,0:T(8,128)(2,1)}, bf16[48,2048]{1,0:T(8,128)(2,1)}, u32[]{:S(2)}, u32[]{:S(2)}) %collective-permute-start.12) | collective-permute-done | bytes 196640 | tf_op jit(solution)/shard_map/ppermute | solution.py:105
  21.2 2.5 %collective-permute-start.2 = (bf16[48,2176]{1,0:T(8,128)(2,1)S(1)}, bf16[48,2176]{1,0:T(8,128)(2,1)S(1)}, u32[]{:S(2)}, u32[]{:S(2)}) collective-permute-start(bf16[48,2176]{1,0:T(8,128)(2,1)S(1)} %concatenate.12), channel_id=1, source_target_pairs={{0,6},{1,7},{2,4},{3,5},{4,2},{5,3},{6,0},{7,1},{8,14},{9,15},{10,... | collective-permute-start | bytes 626696 | tf_op jit(solution)/shard_map/ppermute | solution.py:105
  30.4 8.4 %collective-permute-done.1 = bf16[48,2176]{1,0:T(8,128)(2,1)S(1)} collective-permute-done((bf16[48,2176]{1,0:T(8,128)(2,1)S(1)}, bf16[48,2176]{1,0:T(8,128)(2,1)S(1)}, u32[]{:S(2)}, u32[]{:S(2)}) %collective-permute-start.1) | collective-permute-done | bytes 208928 | tf_op jit(solution)/shard_map/ppermute | solution.py:105
  43.2 3.4 %collective-permute-done.17 = bf16[48,2048]{1,0:T(8,128)(2,1)S(1)} collective-permute-done((bf16[48,2048]{1,0:T(8,128)(2,1)S(1)}, bf16[48,2048]{1,0:T(8,128)(2,1)S(1)}, u32[]{:S(2)}, u32[]{:S(2)}) %collective-permute-start.17) | collective-permute-done | bytes 196640 | tf_op jit(solution)/shard_map/ppermute | solution.py:105
  46.6 4.5 %collective-permute-done.4 = bf16[48,2176]{1,0:T(8,128)(2,1)S(1)} collective-permute-done((bf16[48,2176]{1,0:T(8,128)(2,1)}, bf16[48,2176]{1,0:T(8,128)(2,1)S(1)}, u32[]{:S(2)}, u32[]{:S(2)}) %collective-permute-start.4) | collective-permute-done | bytes 208928 | tf_op jit(solution)/shard_map/ppermute | solution.py:105
  51.1 3.0 %collective-permute-done.5 = bf16[48,2176]{1,0:T(8,128)(2,1)S(1)} collective-permute-done((bf16[48,2176]{1,0:T(8,128)(2,1)S(1)}, bf16[48,2176]{1,0:T(8,128)(2,1)S(1)}, u32[]{:S(2)}, u32[]{:S(2)}) %collective-permute-start.5) | collective-permute-done | bytes 208928 | tf_op jit(solution)/shard_map/ppermute | solution.py:105
  54.1 2.2 %collective-permute-done.6 = bf16[48,2176]{1,0:T(8,128)(2,1)S(1)} collective-permute-done((bf16[48,2176]{1,0:T(8,128)(2,1)S(1)}, bf16[48,2176]{1,0:T(8,128)(2,1)S(1)}, u32[]{:S(2)}, u32[]{:S(2)}) %collective-permute-start.6) | collective-permute-done | bytes 208928 | tf_op jit(solution)/shard_map/ppermute | solution.py:105
  74.6 10.8 %collective-permute-done.7 = bf16[192,2048]{1,0:T(8,128)(2,1)S(1)} collective-permute-done((bf16[192,2048]{1,0:T(8,128)(2,1)S(1)}, bf16[192,2048]{1,0:T(8,128)(2,1)S(1)}, u32[]{:S(2)}, u32[]{:S(2)}) %collective-permute-start.7) | collective-permute-done | bytes 786464 | tf_op jit(solution)/shard_map/ppermute | solution.py:105
  86.0 11.6 %collective-permute-done.18 = bf16[192,2048]{1,0:T(8,128)(2,1)S(1)} collective-permute-done((bf16[192,2048]{1,0:T(8,128)(2,1)S(1)}, bf16[192,2048]{1,0:T(8,128)(2,1)S(1)}, u32[]{:S(2)}, u32[]{:S(2)}) %collective-permute-start.18) | collective-permute-done | bytes 786464 | tf_op jit(solution)/shard_map/ppermute | solution.py:105
  97.6 2.4 %collective-permute-start.10 = (bf16[48,2048]{1,0:T(8,128)(2,1)S(1)}, bf16[48,2048]{1,0:T(8,128)(2,1)S(1)}, u32[]{:S(2)}, u32[]{:S(2)}) collective-permute-start(bf16[48,2048]{1,0:T(8,128)(2,1)S(1)} %get-tuple-element.16), channel_id=1, source_target_pairs={{0,6},{1,7},{2,4},{3,5},{4,2},{5,3},{6,0},{7,1},{8,14},{9,15},{10,... | collective-permute-start | bytes 589832 | tf_op jit(solution)/shard_map/ppermute | solution.py:105
  100.3 3.9 %collective-permute-start.9 = (bf16[48,2048]{1,0:T(8,128)(2,1)S(1)}, bf16[48,2048]{1,0:T(8,128)(2,1)S(1)}, u32[]{:S(2)}, u32[]{:S(2)}) collective-permute-start(bf16[48,2048]{1,0:T(8,128)(2,1)S(1)} %get-tuple-element.17), channel_id=1, source_target_pairs={{0,4},{1,5},{2,6},{3,7},{4,0},{5,1},{6,2},{7,3},{8,12},{9,13},{10,... | collective-permute-start | bytes 589832 | tf_op jit(solution)/shard_map/ppermute | solution.py:105
  105.9 2.4 %collective-permute-start.21 = (bf16[48,2048]{1,0:T(8,128)(2,1)S(1)}, bf16[48,2048]{1,0:T(8,128)(2,1)S(1)}, u32[]{:S(2)}, u32[]{:S(2)}) collective-permute-start(bf16[48,2048]{1,0:T(8,128)(2,1)S(1)} %get-tuple-element.13), channel_id=1, source_target_pairs={{0,6},{1,7},{2,4},{3,5},{4,2},{5,3},{6,0},{7,1},{8,14},{9,15},{10,... | collective-permute-start | bytes 589832 | tf_op jit(solution)/shard_map/ppermute | solution.py:105
  109.0 11.6 %collective-permute-start.20 = (bf16[48,2048]{1,0:T(8,128)(2,1)S(1)}, bf16[48,2048]{1,0:T(8,128)(2,1)S(1)}, u32[]{:S(2)}, u32[]{:S(2)}) collective-permute-start(bf16[48,2048]{1,0:T(8,128)(2,1)S(1)} %get-tuple-element.14), channel_id=1, source_target_pairs={{0,4},{1,5},{2,6},{3,7},{4,0},{5,1},{6,2},{7,3},{8,12},{9,13},{10,... | collective-permute-start | bytes 589832 | tf_op jit(solution)/shard_map/ppermute | solution.py:105
  120.6 3.0 %collective-permute-done.9 = bf16[48,2048]{1,0:T(8,128)(2,1)S(1)} collective-permute-done((bf16[48,2048]{1,0:T(8,128)(2,1)S(1)}, bf16[48,2048]{1,0:T(8,128)(2,1)S(1)}, u32[]{:S(2)}, u32[]{:S(2)}) %collective-permute-start.9) | collective-permute-done | bytes 196640 | tf_op jit(solution)/shard_map/ppermute | solution.py:105
  123.6 3.6 %collective-permute-start.23 = (bf16[512,768]{1,0:T(8,128)(2,1)S(1)}, bf16[512,768]{1,0:T(8,128)(2,1)S(1)}, u32[]{:S(2)}, u32[]{:S(2)}) collective-permute-start(bf16[512,768]{1,0:T(8,128)(2,1)S(1)} %add_convert_fusion.2), channel_id=1, source_target_pairs={{0,16},{8,24},{16,0},{24,8},{1,17},{9,25},{17,1},{25,9},{2,18},{10... | collective-permute-start | bytes 2359304 | tf_op jit(solution)/shard_map/ppermute | solution.py:105
  128.0 3.3 %collective-permute-done.20 = bf16[48,2048]{1,0:T(8,128)(2,1)S(1)} collective-permute-done((bf16[48,2048]{1,0:T(8,128)(2,1)S(1)}, bf16[48,2048]{1,0:T(8,128)(2,1)S(1)}, u32[]{:S(2)}, u32[]{:S(2)}) %collective-permute-start.20) | collective-permute-done | bytes 196640 | tf_op jit(solution)/shard_map/ppermute | solution.py:105
  131.9 2.9 %collective-permute-start.29 = (bf16[192,2048]{1,0:T(8,128)(2,1)S(1)}, bf16[192,2048]{1,0:T(8,128)(2,1)S(1)}, u32[]{:S(2)}, u32[]{:S(2)}) collective-permute-start(bf16[192,2048]{1,0:T(8,128)(2,1)S(1)} %fusion.16), channel_id=1, source_target_pairs={{0,16},{8,24},{16,0},{24,8},{1,17},{9,25},{17,1},{25,9},{2,18},{10... | collective-permute-start | bytes 2359304 | tf_op jit(solution)/shard_map/ppermute | solution.py:105
  135.6 10.0 %collective-permute-done.23 = bf16[512,768]{1,0:T(8,128)(2,1)S(1)} collective-permute-done((bf16[512,768]{1,0:T(8,128)(2,1)S(1)}, bf16[512,768]{1,0:T(8,128)(2,1)S(1)}, u32[]{:S(2)}, u32[]{:S(2)}) %collective-permute-start.23) | collective-permute-done | bytes 786464 | tf_op jit(solution)/shard_map/ppermute | solution.py:105
  147.4 15.1 %collective-permute-done.26 = bf16[512,768]{1,0:T(8,128)(2,1)S(1)} collective-permute-done((bf16[512,768]{1,0:T(8,128)(2,1)S(1)}, bf16[512,768]{1,0:T(8,128)(2,1)S(1)}, u32[]{:S(2)}, u32[]{:S(2)}) %collective-permute-start.26) | collective-permute-done | bytes 786464 | tf_op jit(solution)/shard_map/ppermute | solution.py:105
  164.2 6.7 %collective-permute-done.29 = bf16[192,2048]{1,0:T(8,128)(2,1)S(1)} collective-permute-done((bf16[192,2048]{1,0:T(8,128)(2,1)S(1)}, bf16[192,2048]{1,0:T(8,128)(2,1)S(1)}, u32[]{:S(2)}, u32[]{:S(2)}) %collective-permute-start.29) | collective-permute-done | bytes 786464 | tf_op jit(solution)/shard_map/ppermute | solution.py:105
  170.9 1.9 %add_bitcast_fusion = f32[1,192,2048]{2,1,0:T(8,128)} fusion(bf16[192,2048]{1,0:T(8,128)(2,1)S(1)} %collective-permute-done.29, bf16[192,2048]{1,0:T(8,128)(2,1)S(1)} %collective-permute-done.30, bf16[384,768]{1,0:T(8,128)(2,1)S(1)} %get-tuple-element.8, s32[]{:T(128)S(6)} %select_n.44, bf16[384,2048]{1,0:T(8,128)(2,1)S(1)} %constant_dynamic-update-slice_fusion.8, ...), kind=kOutput, calls=%fused_computation.20 | convolution fusion | flops 305922048 | bytes 4917252 | tf_op jit(solution)/shard_map/dot_general | solution.py:8
  (97 shorter events, 46.9 us)
Async XLA Ops:
  3.7 17.5 %collective-permute-start.12 = (bf16[48,2048]{1,0:T(8,128)(2,1)}, bf16[48,2048]{1,0:T(8,128)(2,1)}, u32[]{:S(2)}, u32[]{:S(2)}) collective-permute-start(bf16[48,2048]{1,0:T(8,128)(2,1)} %param.10), channel_id=1, source_target_pairs={{0,4},{1,5},{2,6},{3,7},{4,0},{5,1},{6,2},{7,3},{8,12},{9,13},{10,... | collective-permute-start | bytes 589832 | tf_op jit(solution)/shard_map/ppermute | solution.py:105
  6.3 18.3 %collective-permute-start.13 = (bf16[48,2048]{1,0:T(8,128)(2,1)}, bf16[48,2048]{1,0:T(8,128)(2,1)S(1)}, u32[]{:S(2)}, u32[]{:S(2)}) collective-permute-start(bf16[48,2048]{1,0:T(8,128)(2,1)} %param.10), channel_id=1, source_target_pairs={{0,6},{1,7},{2,4},{3,5},{4,2},{5,3},{6,0},{7,1},{8,14},{9,15},{10,... | collective-permute-start | bytes 589832 | tf_op jit(solution)/shard_map/ppermute | solution.py:105
  6.3 20.0 %collective-permute-start.14 = (bf16[48,2048]{1,0:T(8,128)(2,1)}, bf16[48,2048]{1,0:T(8,128)(2,1)}, u32[]{:S(2)}, u32[]{:S(2)}) collective-permute-start(bf16[48,2048]{1,0:T(8,128)(2,1)} %param.10), channel_id=1, source_target_pairs={{0,1},{1,0},{2,3},{3,2},{4,5},{5,4},{6,7},{7,6},{8,9},{9,8},{10,11... | collective-permute-start | bytes 589832 | tf_op jit(solution)/shard_map/ppermute | solution.py:105
  11.8 16.0 %collective-permute-start = (bf16[48,2176]{1,0:T(8,128)(2,1)S(1)}, bf16[48,2176]{1,0:T(8,128)(2,1)}, u32[]{:S(2)}, u32[]{:S(2)}) collective-permute-start(bf16[48,2176]{1,0:T(8,128)(2,1)S(1)} %concatenate.12), channel_id=1, source_target_pairs={{0,2},{1,3},{2,0},{3,1},{4,6},{5,7},{6,4},{7,5},{8,10},{9,11},{10,... | collective-permute-start | bytes 626696 | tf_op jit(solution)/shard_map/ppermute | solution.py:105
  14.3 24.5 %collective-permute-start.1 = (bf16[48,2176]{1,0:T(8,128)(2,1)S(1)}, bf16[48,2176]{1,0:T(8,128)(2,1)S(1)}, u32[]{:S(2)}, u32[]{:S(2)}) collective-permute-start(bf16[48,2176]{1,0:T(8,128)(2,1)S(1)} %concatenate.12), channel_id=1, source_target_pairs={{0,4},{1,5},{2,6},{3,7},{4,0},{5,1},{6,2},{7,3},{8,12},{9,13},{10,... | collective-permute-start | bytes 626696 | tf_op jit(solution)/shard_map/ppermute | solution.py:105
  21.2 19.1 %collective-permute-start.2 = (bf16[48,2176]{1,0:T(8,128)(2,1)S(1)}, bf16[48,2176]{1,0:T(8,128)(2,1)S(1)}, u32[]{:S(2)}, u32[]{:S(2)}) collective-permute-start(bf16[48,2176]{1,0:T(8,128)(2,1)S(1)} %concatenate.12), channel_id=1, source_target_pairs={{0,6},{1,7},{2,4},{3,5},{4,2},{5,3},{6,0},{7,1},{8,14},{9,15},{10,... | collective-permute-start | bytes 626696 | tf_op jit(solution)/shard_map/ppermute | solution.py:105
  24.7 16.3 %collective-permute-start.3 = (bf16[48,2176]{1,0:T(8,128)(2,1)S(1)}, bf16[48,2176]{1,0:T(8,128)(2,1)S(1)}, u32[]{:S(2)}, u32[]{:S(2)}) collective-permute-start(bf16[48,2176]{1,0:T(8,128)(2,1)S(1)} %concatenate.12), channel_id=1, source_target_pairs={{0,1},{1,0},{2,3},{3,2},{4,5},{5,4},{6,7},{7,6},{8,9},{9,8},{10,11... | collective-permute-start | bytes 626696 | tf_op jit(solution)/shard_map/ppermute | solution.py:105
  26.3 16.3 %collective-permute-start.15 = (bf16[48,2048]{1,0:T(8,128)(2,1)}, bf16[48,2048]{1,0:T(8,128)(2,1)S(1)}, u32[]{:S(2)}, u32[]{:S(2)}) collective-permute-start(bf16[48,2048]{1,0:T(8,128)(2,1)} %collective-permute-done.11), channel_id=1, source_target_pairs={{0,1},{1,0},{2,3},{3,2},{4,5},{5,4},{6,7},{7,6},{8,9},{9,8},{10,11... | collective-permute-start | bytes 589832 | tf_op jit(solution)/shard_map/ppermute | solution.py:105
  27.8 15.3 %collective-permute-start.16 = (bf16[48,2048]{1,0:T(8,128)(2,1)}, bf16[48,2048]{1,0:T(8,128)(2,1)S(1)}, u32[]{:S(2)}, u32[]{:S(2)}) collective-permute-start(bf16[48,2048]{1,0:T(8,128)(2,1)} %collective-permute-done.12), channel_id=1, source_target_pairs={{0,1},{1,0},{2,3},{3,2},{4,5},{5,4},{6,7},{7,6},{8,9},{9,8},{10,11... | collective-permute-start | bytes 589832 | tf_op jit(solution)/shard_map/ppermute | solution.py:105
  64.9 20.5 %collective-permute-start.7 = (bf16[192,2048]{1,0:T(8,128)(2,1)S(1)}, bf16[192,2048]{1,0:T(8,128)(2,1)S(1)}, u32[]{:S(2)}, u32[]{:S(2)}) collective-permute-start(bf16[192,2048]{1,0:T(8,128)(2,1)S(1)} %slice.65), channel_id=1, source_target_pairs={{0,1},{1,0},{2,3},{3,2},{4,5},{5,4},{6,7},{7,6},{8,9},{9,8},{10,11... | collective-permute-start | bytes 2359304 | tf_op jit(solution)/shard_map/ppermute | solution.py:105
  70.7 26.9 %collective-permute-start.18 = (bf16[192,2048]{1,0:T(8,128)(2,1)S(1)}, bf16[192,2048]{1,0:T(8,128)(2,1)S(1)}, u32[]{:S(2)}, u32[]{:S(2)}) collective-permute-start(bf16[192,2048]{1,0:T(8,128)(2,1)S(1)} %slice.71), channel_id=1, source_target_pairs={{0,1},{1,0},{2,3},{3,2},{4,5},{5,4},{6,7},{7,6},{8,9},{9,8},{10,11... | collective-permute-start | bytes 2359304 | tf_op jit(solution)/shard_map/ppermute | solution.py:105
  71.9 37.0 %collective-permute-start.24 = (bf16[512,768]{1,0:T(8,128)(2,1)S(1)}, bf16[512,768]{1,0:T(8,128)(2,1)S(1)}, u32[]{:S(2)}, u32[]{:S(2)}) collective-permute-start(bf16[512,768]{1,0:T(8,128)(2,1)S(1)} %convolution_convert_fusion.4), channel_id=1, source_target_pairs={{0,8},{8,0},{16,24},{24,16},{1,9},{9,1},{17,25},{25,17},{2,10},{10... | collective-permute-start | bytes 2359304 | tf_op jit(solution)/shard_map/ppermute | solution.py:105
  72.0 33.1 %collective-permute-start.22 = (bf16[512,768]{1,0:T(8,128)(2,1)S(1)}, bf16[512,768]{1,0:T(8,128)(2,1)S(1)}, u32[]{:S(2)}, u32[]{:S(2)}) collective-permute-start(bf16[512,768]{1,0:T(8,128)(2,1)S(1)} %convolution_convert_fusion.5), channel_id=1, source_target_pairs={{0,8},{8,0},{16,24},{24,16},{1,9},{9,1},{17,25},{25,17},{2,10},{10... | collective-permute-start | bytes 2359304 | tf_op jit(solution)/shard_map/ppermute | solution.py:105
  72.5 33.4 %collective-permute-start.25 = (bf16[512,768]{1,0:T(8,128)(2,1)S(1)}, bf16[512,768]{1,0:T(8,128)(2,1)S(1)}, u32[]{:S(2)}, u32[]{:S(2)}) collective-permute-start(bf16[512,768]{1,0:T(8,128)(2,1)S(1)} %convolution_convert_fusion.3), channel_id=1, source_target_pairs={{0,8},{8,0},{16,24},{24,16},{1,9},{9,1},{17,25},{25,17},{2,10},{10... | collective-permute-start | bytes 2359304 | tf_op jit(solution)/shard_map/ppermute | solution.py:105
  85.4 14.9 %collective-permute-start.28 = (bf16[192,2048]{1,0:T(8,128)(2,1)S(1)}, bf16[192,2048]{1,0:T(8,128)(2,1)S(1)}, u32[]{:S(2)}, u32[]{:S(2)}) collective-permute-start(bf16[192,2048]{1,0:T(8,128)(2,1)S(1)} %convolution_convert_fusion.1), channel_id=1, source_target_pairs={{0,8},{8,0},{16,24},{24,16},{1,9},{9,1},{17,25},{25,17},{2,10},{10... | collective-permute-start | bytes 2359304 | tf_op jit(solution)/shard_map/ppermute | solution.py:105
  100.3 23.2 %collective-permute-start.9 = (bf16[48,2048]{1,0:T(8,128)(2,1)S(1)}, bf16[48,2048]{1,0:T(8,128)(2,1)S(1)}, u32[]{:S(2)}, u32[]{:S(2)}) collective-permute-start(bf16[48,2048]{1,0:T(8,128)(2,1)S(1)} %get-tuple-element.17), channel_id=1, source_target_pairs={{0,4},{1,5},{2,6},{3,7},{4,0},{5,1},{6,2},{7,3},{8,12},{9,13},{10,... | collective-permute-start | bytes 589832 | tf_op jit(solution)/shard_map/ppermute | solution.py:105
  105.0 18.6 %collective-permute-start.8 = (bf16[48,2048]{1,0:T(8,128)(2,1)S(1)}, bf16[48,2048]{1,0:T(8,128)(2,1)S(1)}, u32[]{:S(2)}, u32[]{:S(2)}) collective-permute-start(bf16[48,2048]{1,0:T(8,128)(2,1)S(1)} %get-tuple-element.15), channel_id=1, source_target_pairs={{0,2},{1,3},{2,0},{3,1},{4,6},{5,7},{6,4},{7,5},{8,10},{9,11},{10,... | collective-permute-start | bytes 589832 | tf_op jit(solution)/shard_map/ppermute | solution.py:105
  105.9 21.3 %collective-permute-start.21 = (bf16[48,2048]{1,0:T(8,128)(2,1)S(1)}, bf16[48,2048]{1,0:T(8,128)(2,1)S(1)}, u32[]{:S(2)}, u32[]{:S(2)}) collective-permute-start(bf16[48,2048]{1,0:T(8,128)(2,1)S(1)} %get-tuple-element.13), channel_id=1, source_target_pairs={{0,6},{1,7},{2,4},{3,5},{4,2},{5,3},{6,0},{7,1},{8,14},{9,15},{10,... | collective-permute-start | bytes 589832 | tf_op jit(solution)/shard_map/ppermute | solution.py:105
  108.9 38.4 %collective-permute-start.27 = (bf16[512,768]{1,0:T(8,128)(2,1)S(1)}, bf16[512,768]{1,0:T(8,128)(2,1)S(1)}, u32[]{:S(2)}, u32[]{:S(2)}) collective-permute-start(bf16[512,768]{1,0:T(8,128)(2,1)S(1)} %convolution_convert_fusion.2), channel_id=1, source_target_pairs={{0,8},{8,0},{16,24},{24,16},{1,9},{9,1},{17,25},{25,17},{2,10},{10... | collective-permute-start | bytes 2359304 | tf_op jit(solution)/shard_map/ppermute | solution.py:105
  109.0 22.3 %collective-permute-start.20 = (bf16[48,2048]{1,0:T(8,128)(2,1)S(1)}, bf16[48,2048]{1,0:T(8,128)(2,1)S(1)}, u32[]{:S(2)}, u32[]{:S(2)}) collective-permute-start(bf16[48,2048]{1,0:T(8,128)(2,1)S(1)} %get-tuple-element.14), channel_id=1, source_target_pairs={{0,4},{1,5},{2,6},{3,7},{4,0},{5,1},{6,2},{7,3},{8,12},{9,13},{10,... | collective-permute-start | bytes 589832 | tf_op jit(solution)/shard_map/ppermute | solution.py:105
  123.6 22.0 %collective-permute-start.23 = (bf16[512,768]{1,0:T(8,128)(2,1)S(1)}, bf16[512,768]{1,0:T(8,128)(2,1)S(1)}, u32[]{:S(2)}, u32[]{:S(2)}) collective-permute-start(bf16[512,768]{1,0:T(8,128)(2,1)S(1)} %add_convert_fusion.2), channel_id=1, source_target_pairs={{0,16},{8,24},{16,0},{24,8},{1,17},{9,25},{17,1},{25,9},{2,18},{10... | collective-permute-start | bytes 2359304 | tf_op jit(solution)/shard_map/ppermute | solution.py:105
  127.2 35.3 %collective-permute-start.26 = (bf16[512,768]{1,0:T(8,128)(2,1)S(1)}, bf16[512,768]{1,0:T(8,128)(2,1)S(1)}, u32[]{:S(2)}, u32[]{:S(2)}) collective-permute-start(bf16[512,768]{1,0:T(8,128)(2,1)S(1)} %add_convert_fusion.1), channel_id=1, source_target_pairs={{0,16},{8,24},{16,0},{24,8},{1,17},{9,25},{17,1},{25,9},{2,18},{10... | collective-permute-start | bytes 2359304 | tf_op jit(solution)/shard_map/ppermute | solution.py:105
  131.3 32.9 %collective-permute-start.30 = (bf16[192,2048]{1,0:T(8,128)(2,1)S(1)}, bf16[192,2048]{1,0:T(8,128)(2,1)S(1)}, u32[]{:S(2)}, u32[]{:S(2)}) collective-permute-start(bf16[192,2048]{1,0:T(8,128)(2,1)S(1)} %convolution_convert_fusion), channel_id=1, source_target_pairs={{0,8},{8,0},{16,24},{24,16},{1,9},{9,1},{17,25},{25,17},{2,10},{10... | collective-permute-start | bytes 2359304 | tf_op jit(solution)/shard_map/ppermute | solution.py:105
  131.9 38.9 %collective-permute-start.29 = (bf16[192,2048]{1,0:T(8,128)(2,1)S(1)}, bf16[192,2048]{1,0:T(8,128)(2,1)S(1)}, u32[]{:S(2)}, u32[]{:S(2)}) collective-permute-start(bf16[192,2048]{1,0:T(8,128)(2,1)S(1)} %fusion.16), channel_id=1, source_target_pairs={{0,16},{8,24},{16,0},{24,8},{1,17},{9,25},{17,1},{25,9},{2,18},{10... | collective-permute-start | bytes 2359304 | tf_op jit(solution)/shard_map/ppermute | solution.py:105
  (11 other events, 159.8 us)

commit v2 on v0

--- a/solution.py
+++ b/solution.py
@@ -1,6 +1,8 @@
 import jax
 import jax.numpy as jnp
 from jax import lax
+from jax.experimental import pallas as pl
+from jax.experimental.pallas import tpu as pltpu
 from jax.sharding import PartitionSpec as P
 
 
@@ -16,7 +18,7 @@
     )
 
 
-def shards(tokens, expert_ids, gate_probs, out_cot, w_gate, w_up, w_down):
+def routed(tokens, expert_ids, gate_probs, out_cot, w_gate, w_up, w_down):
     tok_count, width = tokens.shape
     top = expert_ids.shape[1]
     experts = lax.axis_size("expert")
@@ -100,6 +102,397 @@
     return (layer_out, input_grad, gate_part[None], up_part[None], down_grad[None])
 
 
+BF16, F32 = jnp.bfloat16, jnp.float32
+VMEM, SMEM, HBM, ANY = pltpu.VMEM, pltpu.SMEM, pltpu.HBM, pl.ANY
+ORDER = ((8, 128), jnp.float32, pltpu.VMEM)
+
+
+def stage(body, ins, outs, after=(), scratch=(), aliases=None):
+    skipped = len(after)
+    given = skipped + len(ins)
+
+    def kernel(*refs):
+        token = refs[given + len(outs)]
+        body(*refs[skipped : given + len(outs)], *refs[given + len(outs) + 1 :])
+        token[...] = jnp.zeros(token.shape, token.dtype)
+
+    outs_all = list(outs) + [ORDER]
+    outputs = pl.pallas_call(
+        kernel,
+        in_specs=[pl.BlockSpec(memory_space=m) for m in [ANY] * skipped + [m for _, m in ins]],
+        out_specs=[pl.BlockSpec(memory_space=m) for _, _, m in outs_all],
+        out_shape=[jax.ShapeDtypeStruct(shape, dtype) for shape, dtype, _ in outs_all],
+        scratch_shapes=list(scratch),
+        input_output_aliases={skipped + i: o for i, o in (aliases or {}).items()},
+        cost_estimate=pl.CostEstimate(flops=0, bytes_accessed=0, transcendentals=0),
+        compiler_params=pltpu.CompilerParams(vmem_limit_bytes=16 * 2**20),
+    )(*after, *[a for a, _ in ins])
+    return list(outputs)
+
+
+def swap(value, axis, mask):
+    size = lax.axis_size(axis)
+    return lax.ppermute(value, axis, [(i, i ^ mask) for i in range(size)])
+
+
+def chunks(width, most):
+    return [(at, min(most, width - at)) for at in range(0, width, most)]
+
+
+def packed(tokens, expert_ids, gate_probs, out_cot, experts, lanes):
+    count, width = tokens.shape
+    top = expert_ids.shape[1]
+
+    def body(tok, ids, given, cot, both, sems):
+        copies = [
+            pltpu.make_async_copy(tok, both.at[:count, :width], sems.at[0]),
+            pltpu.make_async_copy(cot, both.at[count:, :width], sems.at[1]),
+        ]
+        for copy in copies:
+            copy.start()
+        names = ids[...].T
+        values = given[...].T
+        column = lax.broadcasted_iota(jnp.int32, (count, lanes), 1)
+        total = jnp.zeros((count, lanes), F32)
+        for k in range(top):
+            named = (names[:, k : k + 1] == column) | (names[:, k : k + 1] + experts == column)
+            total = total + jnp.where(named, values[:, k : k + 1], 0.0)
+        high = total.astype(BF16).astype(F32)
+        both[:count, width:] = jnp.where(column < experts, high, total - high).astype(BF16)
+        both[count:, width:] = jnp.zeros((count, lanes), BF16)
+        for copy in copies:
+            copy.wait()
+
+    return stage(
+        body,
+        [(tokens, HBM), (expert_ids.T, VMEM), (gate_probs.T, VMEM), (out_cot, HBM)],
+        [((2 * count, width + lanes), BF16, VMEM)],
+        scratch=[pltpu.SemaphoreType.DMA((2,))],
+    )
+
+
+def kept_near(arrays, after):
+    def body(*refs):
+        n = len(arrays)
+        copies = [pltpu.make_async_copy(refs[i], refs[n + i], refs[2 * n].at[i]) for i in range(n)]
+        for copy in copies:
+            copy.start()
+        for copy in copies:
+            copy.wait()
+
+    return stage(
+        body,
+        [(a, HBM) for a in arrays],
+        [(a.shape, a.dtype, VMEM) for a in arrays],
+        after=after,
+        scratch=[pltpu.SemaphoreType.DMA((len(arrays),))],
+    )
+
+
+def products(places, left, right, outs, own, tile=512):
+    size = left.shape[0] // (1 + max(p | 1 for p in places))
+    width = right.shape[1]
+    for start, some in chunks(width, tile):
+        piece = right[:, start : start + some]
+        for m, (out, row) in zip(places, outs):
+            part = left[pl.ds(pl.multiple_of((own ^ m) * size, size), size), :]
+            out[row : row + size, start : start + some] = jnp.dot(
+                part, piece, preferred_element_type=F32
+            ).astype(out.dtype)
+
+
+TURNED = (((1,), (1,)), ((), ()))
+
+
+def dense(tokens, expert_ids, gate_probs, out_cot, w_gate, w_up, w_down):
+    count, width = tokens.shape
+    ff = w_gate.shape[2]
+    experts = lax.axis_size("expert")
+    owners = lax.axis_size("dp")
+    me = lax.axis_index("expert").astype(jnp.int32).reshape(1)
+    mine = lax.axis_index("dp").astype(jnp.int32).reshape(1)
+    total = count * experts
+    half = total // 2
+    lanes = 128 * (-(-2 * experts // 128))
+    odd_places = list(range(owners - 1, 0, -2))
+    even_places = [m - 1 for m in odd_places]
+    slab, band = ff // owners, width // owners
+
+    near_bit, far_bit = 2, 4
+    both, _ = packed(tokens, expert_ids, gate_probs, out_cot, experts, lanes)
+    wide = width + lanes
+    far = swap(both, "expert", far_bit)
+    near = swap(both, "expert", near_bit)
+    next_both = swap(both, "expert", 1)
+    next_near = swap(near, "expert", 1)
+    next_far = swap(far, "expert", 1)
+    far_on, _ = stage(
+        lambda *_: None,
+        [(far, ANY), (next_both, ANY)],
+        [(far.shape, BF16, ANY)],
+        aliases={0: 0},
+    )
+    far_near = swap(far_on, "expert", near_bit)
+    (done,) = stage(lambda *_: None, [(next_near, ANY)], [])
+
+    def apart(pair, tok, cot):
+        tok[...] = pair[:count, :]
+        cot[...] = pair[count:, :width]
+
+    last_tok, last_cot, done = stage(
+        apart,
+        [(far_near, VMEM)],
+        [((count, wide), BF16, VMEM), ((count, width), BF16, VMEM)],
+        after=[done],
+    )
+    next_last_tok = swap(last_tok, "expert", 1)
+    next_last_cot = swap(last_cot, "expert", 1)
+    gate_near, up_near, down_near, done = kept_near([w[0] for w in (w_gate, w_up, w_down)], [done])
+    whole = [both, far, near, next_both, next_far, next_near]
+    tok_pieces = [(a, 0) for a in whole]
+    cot_pieces = [(a, count) for a in whole]
+    tok_pieces[3:3] = [(last_tok, 0)]
+    cot_pieces[3:3] = [(last_cot, 0)]
+    tok_pieces.append((next_last_tok, 0))
+    cot_pieces.append((next_last_cot, 0))
+
+    def refs_of(pieces):
+        arrays = []
+        for a, _ in pieces:
+            if not any(a is b for b in arrays):
+                arrays.append(a)
+        where = [next(i for i, b in enumerate(arrays) if b is a) for a, _ in pieces]
+        return arrays, [(i, row) for i, (_, row) in zip(where, pieces)]
+
+    tok_arrays, tok_where = refs_of(tok_pieces)
+    cot_arrays, cot_where = refs_of(cot_pieces)
+
+    def forward(me_ref, *refs):
+        blocks = refs[: len(tok_arrays)]
+        gate, up, down, flipped, hidden_t, gate_by, up_by, even, odd, rows, probs, hidden = refs[
+            len(tok_arrays) :
+        ]
+        own = me_ref[0]
+        column = lax.broadcasted_iota(jnp.int32, (count, lanes), 1)
+        chosen = (column == own) | (column == own + experts)
+        for b, (i, row) in enumerate(tok_where):
+            place = pl.ds(b * count, count)
+            rows[place, :] = blocks[i][row : row + count, :width]
+            side = jnp.where(chosen, blocks[i][row : row + count, width:].astype(F32), 0.0)
+            probs[place, :] = jnp.sum(side, axis=1, keepdims=True)
+        weight = probs[...]
+        for start, size in chunks(ff, 256):
+            place = slice(start, start + size)
+            gate_pre = jnp.dot(rows[...], gate[:, place], preferred_element_type=F32)
+            up_pre = jnp.dot(rows[...], up[:, place], preferred_element_type=F32)
+            sigma = jax.nn.sigmoid(gate_pre)
+            silu = gate_pre * sigma
+            scaled = weight * up_pre
+            hidden[:, place] = (silu * scaled).astype(BF16)
+            gate_by[:, place] = scaled * sigma * (1.0 + gate_pre * (1.0 - sigma))
+            up_by[:, place] = weight * silu
+        for start, size in chunks(width, 512):
+            place = slice(start, start + size)
+            part = jnp.dot(hidden[...], down[:, place], preferred_element_type=F32).astype(BF16)
+            even[:, place] = part[:half]
+            odd[:, place] = part[half:]
+        for start, size in chunks(width, 512):
+            flipped[start : start + size, :] = rows[:, start : start + size].T
+        for start, size in chunks(ff, 256):
+            hidden_t[start : start + size, :] = hidden[:, start : start + size].T
+
+    flipped, hidden_t, gate_by, up_by, out_even, out_odd, _ = stage(
+        forward,
+        [(me, SMEM)] + [(a, VMEM) for a in tok_arrays + [gate_near, up_near, down_near]],
+        [
+            ((width, total), BF16, VMEM),
+            ((ff, total), BF16, VMEM),
+            ((total, ff), F32, VMEM),
+            ((total, ff), F32, VMEM),
+            ((half, width), BF16, VMEM),
+            ((half, width), BF16, VMEM),
+        ],
+        scratch=[VMEM((total, width), BF16), VMEM((total, 1), F32), VMEM((total, ff), BF16)],
+    )
+
+    def down_odd(own_ref, *refs):
+        blocks = refs[: len(cot_arrays)]
+        left, _, _, rows, away = refs[len(cot_arrays) :]
+        for b, (i, row) in enumerate(cot_where):
+            rows[b * count : (b + 1) * count, :] = blocks[i][row : row + count, :width]
+        outs = [(away, i * slab) for i in range(len(odd_places))]
+        products(odd_places, left, rows, outs, own_ref[0])
+
+    out_odd, cot_rows, down_away, done = stage(
+        down_odd,
+        [(mine, SMEM)] + [(a, VMEM) for a in cot_arrays] + [(hidden_t, VMEM), (out_odd, ANY)],
+        [
+            ((half, width), BF16, ANY),
+            ((total, width), BF16, VMEM),
+            ((slab * len(odd_places), width), BF16, VMEM),
+        ],
+        aliases={len(cot_arrays) + 2: 0},
+    )
+    down_came = swap(down_away, "dp", 1)
+    out_came = swap(out_odd, "expert", 1)
+
+    def backward(own_ref, cot, left, down, gate_ref, up_ref, grads, *kept):
+        products(even_places, left, cot, [(k, 0) for k in kept], own_ref[0])
+        for start, size in chunks(ff, 256):
+            place = slice(start, start + size)
+            grad = lax.dot_general(cot[...], down[place, :], TURNED, preferred_element_type=F32)
+            grads[:, place] = (grad * gate_ref[:, place]).astype(BF16)
+            grads[:, ff + start : ff + start + size] = (grad * up_ref[:, place]).astype(BF16)
+
+    grads, *down_kept, done = stage(
+        backward,
+        [(mine, SMEM)] + [(a, VMEM) for a in (cot_rows, hidden_t, down_near, gate_by, up_by)],
+        [((total, 2 * ff), BF16, VMEM)] + [((slab, width), BF16, VMEM)] * len(even_places),
+        after=[done],
+    )
+
+    def added(kept, came, after=()):
+        n, size = len(kept), kept[0].shape[0]
+
+        def body(*refs):
+            for i in range(n):
+                other = refs[n][i * size : (i + 1) * size, :].astype(F32)
+                refs[n + 1 + i][...] = (refs[i][...].astype(F32) + other).astype(BF16)
+
+        return stage(
+            body,
+            [(a, VMEM) for a in [*kept, came]],
+            [(a.shape, BF16, VMEM) for a in kept],
+            after=after,
+        )
+
+    *down_send, done = added(down_kept[:-1], down_came, [done])
+    down_got = [swap(a, "dp", m) for a, m in zip(down_send, even_places)]
+
+    def both_odd(own_ref, left, right, away):
+        outs = [(away, i * band) for i in range(len(odd_places))]
+        products(odd_places, left, right, outs, own_ref[0], 256)
+
+    def both_even(own_ref, left, right, *kept):
+        products(even_places, left, right, [(k, 0) for k in kept], own_ref[0], 256)
+
+    given = [(mine, SMEM), (flipped, VMEM), (grads, VMEM)]
+    both_away, done = stage(
+        both_odd, given, [((band * len(odd_places), 2 * ff), BF16, VMEM)], after=[done]
+    )
+    both_came = swap(both_away, "dp", 1)
+    *both_kept, done = stage(
+        both_even, given, [((band, 2 * ff), BF16, VMEM)] * len(even_places), after=[done]
+    )
+    def half_added(first, after):
+        n = len(both_kept) - 1
+        place = slice(first, first + ff)
+
+        def body(*refs):
+            for i in range(n):
+                other = refs[n][i * band : (i + 1) * band, place].astype(F32)
+                refs[n + 1 + i][...] = (refs[i][:, place].astype(F32) + other).astype(BF16)
+
+        *sends, done = stage(
+            body,
+            [(a, VMEM) for a in [*both_kept[:-1], both_came]],
+            [((band, ff), BF16, VMEM)] * n,
+            after=after,
+        )
+        return [swap(a, "dp", m) for a, m in zip(sends, even_places)], done
+
+    gate_got, done = half_added(0, [done])
+
+    def input_rows(grad, gate, up, even, odd):
+        for start, size in chunks(width, 512):
+            place = slice(start, start + size)
+            rows = lax.dot_general(
+                grad[:, :ff], gate[place, :], TURNED, preferred_element_type=F32
+            ) + lax.dot_general(grad[:, ff:], up[place, :], TURNED, preferred_element_type=F32)
+            rows = rows.astype(BF16)
+            even[:, place] = rows[:half]
+            odd[:, place] = rows[half:]
+
+    in_even, in_odd, done = stage(
+        input_rows,
+        [(grads, VMEM), (gate_near, VMEM), (up_near, VMEM)],
+        [((half, width), BF16, VMEM)] * 2,
+        after=[done],
+    )
+    in_came = swap(in_odd, "expert", 1)
+
+    def folded(held, came, after):
+        rows = held.shape[0]
+        parts = 1 if rows == count else 2
+
+        def body(a, b, *outs):
+            for i, out in enumerate(outs):
+                place = slice(i * rows // parts, (i + 1) * rows // parts)
+                out[...] = (a[place, :].astype(F32) + b[place, :].astype(F32)).astype(BF16)
+
+        return stage(
+            body,
+            [(held, VMEM), (came, VMEM)],
+            [((rows // parts, width), BF16, VMEM)] * parts,
+            after=after,
+        )
+
+    def owned(kept, came, got, after, column=0):
+        size, wide = got[0].shape
+        step = 64
+        first = came.shape[0] // step - size // step
+        skipped = len(after)
+
+        def body(*refs):
+            value = refs[skipped][...].astype(F32)
+            for ref in refs[skipped + 1 : -2]:
+                value = value + ref[...].astype(F32)
+            refs[-2][...] = value
+            refs[-1][...] = jnp.zeros(ORDER[0], F32)
+
+        at = column // wide
+        outputs = pl.pallas_call(
+            body,
+            grid=(size // step,),
+            in_specs=[pl.BlockSpec(memory_space=ANY)] * skipped
+            + [
+                pl.BlockSpec((step, wide), lambda i: (i, at)),
+                pl.BlockSpec((step, wide), lambda i: (i + first, at)),
+            ]
+            + [pl.BlockSpec((step, wide), lambda i: (i, 0))] * len(got),
+            out_specs=[
+                pl.BlockSpec((step, wide), lambda i: (i, 0)),
+                pl.BlockSpec(ORDER[0], lambda i: (0, 0)),
+            ],
+            out_shape=[jax.ShapeDtypeStruct((size, wide), F32), jax.ShapeDtypeStruct(*ORDER[:2])],
+            cost_estimate=pl.CostEstimate(flops=0, bytes_accessed=0, transcendentals=0),
+            compiler_params=pltpu.CompilerParams(vmem_limit_bytes=16 * 2**20),
+        )(*after, kept, came, *got)
+        return list(outputs)
+
+    def fold_on(held, came, bit, after):
+        held, send, done = folded(held, came, after)
+        return held, swap(send, "expert", bit), done
+
+    out_held, out_came, done = fold_on(out_even, out_came, near_bit, [done])
+    down_grad, done = owned(down_kept[-1], down_came, down_got, [done])
+    up_got, done = half_added(ff, [done])
+    out_held, out_came, done = fold_on(out_held, out_came, far_bit, [done])
+    gate_part, done = owned(both_kept[-1], both_came, gate_got, [done])
+    in_held, in_came, done = fold_on(in_even, in_came, near_bit, [done])
+    layer_out, done = folded(out_held, out_came, [done])
+    in_held, in_came, done = fold_on(in_held, in_came, far_bit, [done])
+    input_grad, done = folded(in_held, in_came, [done])
+    up_part, _ = owned(both_kept[-1], both_came, up_got, [done], ff)
+    return (layer_out, input_grad, gate_part[None], up_part[None], down_grad[None])
+
+
+def shards(tokens, expert_ids, *rest):
+    experts = lax.axis_size("expert")
+    every = expert_ids.shape[1] == experts and experts == 8
+    return (dense if every else routed)(tokens, expert_ids, *rest)
+
+
 def solution(mesh):
     placed = (
         P(("dp", "expert"), None),

time: 242 us -> 135 us (0.56)
  waiting for transfers between devices: 127 us -> 70.7 us
  matrix products: 39.5 us -> 0 us
  Pallas kernels: 0 us -> 27.4 us
  other arithmetic: 19.4 us -> 0 us
  between operations: 13.9 us -> 0.79 us
  local copies, waits for them, and re-layouts: 21.3 us -> 8.92 us
  starting transfers between devices: 20.9 us -> 26.4 us
    all_to_all x4 -> x0, waiting for transfers between devices: 119 us -> none  [the longest x1 31.6 us: shards(): lax.all_to_all(outbound_grad.reshape(experts, slots, width), 'expert', sp...]
    ppermute x0 -> x19, waiting for transfers between devices: none -> 70.7 us  [swap(): return lax.ppermute(value, axis, [(i, i ^ mask) for i in range(size)])]
    dot_general x9 -> x0, matrix products: 39.5 us -> none  [the longest x3 15.6 us: contract_rows(): lax.dot_general(left, right, (((0,), (0,)), ((), ())), preferred_element_...]
    pallas_call x0 -> x23, Pallas kernels: none -> 27.4 us  [the longest x20 19.6 us: stage(): pl.pallas_call(kernel, in_specs=[pl.BlockSpec(memory_space=m) for m in [A...]
    ppermute x0 -> x19, starting transfers between devices: none -> 26.4 us  [swap(): return lax.ppermute(value, axis, [(i, i ^ mask) for i in range(size)])]
    all_to_all x4 -> x0, starting transfers between devices: 20.6 us -> none  [the longest x1 7.41 us: shards(): lax.all_to_all(outbound, 'expert', split_axis=0, concat_axis=0, tiled=True)]
    gather x2 -> x0, local copies, waits for them, and re-layouts: 13.7 us -> none  [the longest x1 7.03 us: shards(): back_grad.reshape(-1, width)[target].reshape(tok_count, top, width)]
    reduce_scatter x3 -> x0, waiting for transfers between devices: 7.91 us -> none  [the longest x1 7.91 us: shards(): lax.psum_scatter(contract_rows(hidden_rows, arrived_grad).astype(jnp.bflo...]
  transfers between devices with their start and end apart: 7 -> 19, of which waited for: 5 -> 13; matrix products, arithmetic and copies ran while one was open for 23% -> 0% of each run, Pallas kernels for 0% -> 15%
where the time goes in v2:
time: 135 us; the launch traced here: 134 us
  waiting for transfers between devices  70.7 us (52%)
  Pallas kernels  27.4 us (20%)
  starting transfers between devices  26.4 us (20%)
  local copies, waits for them, and re-layouts  8.92 us (7%)
    ppermute x19, waiting for transfers between devices, swap(): return lax.ppermute(value, axis, [(i, i ^ mask) for i in range(size)])  70.7 us
    ppermute x19, starting transfers between devices, swap(): return lax.ppermute(value, axis, [(i, i ^ mask) for i in range(size)])  26.4 us
    pallas_call x20, Pallas kernels, stage(): pl.pallas_call(kernel, in_specs=[pl.BlockSpec(memory_space=m) for m in [A...  19.6 us
    unnamed x15, local copies, waits for them, and re-layouts  8.92 us
    pallas_call x3, Pallas kernels, owned(): pl.pallas_call(body, grid=(size // step,), in_specs=[pl.BlockSpec(memory_...  7.84 us
  transfers between devices with their start and end apart: 19, of which 13 were waited for; matrix products, arithmetic and copies ran while one was open for 0% of the time, Pallas kernels for 15%

profile of v2, /device:TPU:0, one launch (start us, length us, event | category | flops | bytes accessed | tf_op | source)
XLA Modules:
  0.0 134.2 jit_solution(2055231072297765105)
XLA Ops:
  4.9 3.1 %collective-permute-start.1 = (bf16[96,2176]{1,0:T(8,128)(2,1)S(1)}, bf16[96,2176]{1,0:T(8,128)(2,1)S(1)}, u32[]{:S(2)}, u32[]{:S(2)}) collective-permute-start(bf16[96,2176]{1,0:T(8,128)(2,1)S(1)} %get-tuple-element.62.refs_1_), channel_id=1, source_target_pairs={{0,2},{1,3},{2,0},{3,1},{4,6},{5,7},{6,4},{7,5},{8,10},{9,11},{10,... | collective-permute-start | bytes 1253384 | tf_op jit(solution)/shard_map/ppermute | solution.py:135
  8.0 2.6 %collective-permute-start = (bf16[96,2176]{1,0:T(8,128)(2,1)S(1)}, bf16[96,2176]{1,0:T(8,128)(2,1)S(1)}, u32[]{:S(2)}, u32[]{:S(2)}) collective-permute-start(bf16[96,2176]{1,0:T(8,128)(2,1)S(1)} %get-tuple-element.62.refs_1_), channel_id=1, source_target_pairs={{0,4},{1,5},{2,6},{3,7},{4,0},{5,1},{6,2},{7,3},{8,12},{9,13},{10,... | collective-permute-start | bytes 1253384 | tf_op jit(solution)/shard_map/ppermute | solution.py:135
  12.1 14.4 %collective-permute-done.1.refs_3_ = bf16[96,2176]{1,0:T(8,128)(2,1)S(1)} collective-permute-done((bf16[96,2176]{1,0:T(8,128)(2,1)S(1)}, bf16[96,2176]{1,0:T(8,128)(2,1)S(1)}, u32[]{:S(2)}, u32[]{:S(2)}) %collective-permute-start.1) | collective-permute-done | bytes 417824 | tf_op jit(solution)/shard_map/ppermute | solution.py:135
  31.6 7.4 %collective-permute-done.2.refs_0_.refs_7_ = bf16[96,2176]{1,0:T(8,128)(2,1)S(1)} collective-permute-done((bf16[96,2176]{1,0:T(8,128)(2,1)S(1)}, bf16[96,2176]{1,0:T(8,128)(2,1)S(1)}, u32[]{:S(2)}, u32[]{:S(2)}) %collective-permute-start.2) | collective-permute-done | bytes 417824 | tf_op jit(solution)/shard_map/ppermute | solution.py:135
  39.1 1.7 %collective-permute-start.7 = (bf16[48,2176]{1,0:T(8,128)(2,1)S(1)}, bf16[48,2176]{1,0:T(8,128)(2,1)S(1)}, u32[]{:S(2)}, u32[]{:S(2)}) collective-permute-start(bf16[48,2176]{1,0:T(8,128)(2,1)S(1)} %get-tuple-element.65.refs_4_), channel_id=1, source_target_pairs={{0,1},{1,0},{2,3},{3,2},{4,5},{5,4},{6,7},{7,6},{8,9},{9,8},{10,11... | collective-permute-start | bytes 626696 | tf_op jit(solution)/shard_map/ppermute | solution.py:135
  41.2 1.9 %copy-done = bf16[1,2048,768]{2,1,0:T(8,128)(2,1)S(1)} copy-done((bf16[1,2048,768]{2,1,0:T(8,128)(2,1)S(1)}, bf16[1,2048,768]{2,1,0:T(8,128)(2,1)}, u32[]{:S(2)}) %copy-start) | copy-done | bytes 3145752
  43.1 1.9 %copy-done.1 = bf16[1,2048,768]{2,1,0:T(8,128)(2,1)S(1)} copy-done((bf16[1,2048,768]{2,1,0:T(8,128)(2,1)S(1)}, bf16[1,2048,768]{2,1,0:T(8,128)(2,1)}, u32[]{:S(2)}) %copy-start.1) | copy-done | bytes 3145752
  45.0 1.9 %copy-done.2 = bf16[1,768,2048]{2,1,0:T(8,128)(2,1)S(1)} copy-done((bf16[1,768,2048]{2,1,0:T(8,128)(2,1)S(1)}, bf16[1,768,2048]{2,1,0:T(8,128)(2,1)}, u32[]{:S(2)}) %copy-start.2) | copy-done | bytes 3145752
  48.1 4.4 %collective-permute-done.7.refs_8_ = bf16[48,2176]{1,0:T(8,128)(2,1)S(1)} collective-permute-done((bf16[48,2176]{1,0:T(8,128)(2,1)S(1)}, bf16[48,2176]{1,0:T(8,128)(2,1)S(1)}, u32[]{:S(2)}, u32[]{:S(2)}) %collective-permute-start.7) | collective-permute-done | bytes 208928 | tf_op jit(solution)/shard_map/ppermute | solution.py:135
  52.5 4.6 %shard_map.115 = (bf16[2048,384]{1,0:T(8,128)(2,1)S(1)}, bf16[768,384]{1,0:T(8,128)(2,1)S(1)}, f32[384,768]{1,0:T(8,128)S(1)}, f32[384,768]{1,0:T(8,128)S(1)}, b...) custom-call(s32[1]{0:T(128)} %bitcast.3.refs_0_, ...), custom_call_target="tpu_custom_call" | custom-call | tf_op jit(solution)/shard_map/pallas_call | solution.py:120
  58.1 2.3 %shard_map.117 = (bf16[384,1536]{1,0:T(8,128)(2,1)S(1)}, bf16[192,2048]{1,0:T(8,128)(2,1)S(1)}, bf16[192,2048]{1,0:T(8,128)(2,1)S(1)}, f32[8,128]{1,0:T(8,128)S(1)}) custom-call(f32[8,128]{1,0:T(8,128)S(1)} %get-tuple-element.72.refs_0_, s32[1]{0:T(128)} %bitcast.refs_0_.refs_1_, bf16[384,2048]{1,0:T(8,128)(2,1)S(1)} %get-tuple-element.73.refs_2_, ...), custom_call_target="tpu_custom_call" | custom-call | tf_op jit(solution)/shard_map/pallas_call | solution.py:120
  61.7 1.8 %shard_map.119 = (bf16[1024,1536]{1,0:T(8,128)(2,1)S(1)}, f32[8,128]{1,0:T(8,128)S(1)}) custom-call(f32[8,128]{1,0:T(8,128)S(1)} %get-tuple-element.79.refs_0_, s32[1]{0:T(128)} %bitcast.refs_0_.refs_1_, bf16[2048,384]{1,0:T(8,128)(2,1)S(1)} %get-tuple-element.80.refs_2_, bf16[384,1536]{1,0:T(8,128)(2,1)S(1)} %get-tuple-element.81.refs_3_.refs_1_), custom_call_target="tpu_custom_call" | custom-call | tf_op jit(solution)/shard_map/pallas_call | solution.py:120
  66.9 1.8 %shard_map.120 = (bf16[512,1536]{1,0:T(8,128)(2,1)S(1)}, bf16[512,1536]{1,0:T(8,128)(2,1)S(1)}, f32[8,128]{1,0:T(8,128)S(1)}) custom-call(f32[8,128]{1,0:T(8,128)S(1)} %get-tuple-element.82.refs_0_, s32[1]{0:T(128)} %bitcast.refs_0_.refs_1_, bf16[2048,384]{1,0:T(8,128)(2,1)S(1)} %get-tuple-element.80.refs_2_, ...), custom_call_target="tpu_custom_call" | custom-call | tf_op jit(solution)/shard_map/pallas_call | solution.py:120
  71.1 2.6 %shard_map.122 = (bf16[192,2048]{1,0:T(8,128)(2,1)S(1)}, bf16[192,2048]{1,0:T(8,128)(2,1)S(1)}, f32[8,128]{1,0:T(8,128)S(1)}) custom-call(f32[8,128]{1,0:T(8,128)S(1)} %get-tuple-element.86.refs_0_, bf16[384,1536]{1,0:T(8,128)(2,1)S(1)} %get-tuple-element.81.refs_3_.refs_1_, bf16[2048,768]{1,0:T(8,128)(2,1)S(1)} %get-tuple-element.67.refs_9_.refs_2_, ...), custom_call_target="tpu_custom_call" | custom-call | tf_op jit(solution)/shard_map/pallas_call | solution.py:120
  75.4 8.7 %collective-permute-done.10.refs_2_ = bf16[192,2048]{1,0:T(8,128)(2,1)S(1)} collective-permute-done((bf16[192,2048]{1,0:T(8,128)(2,1)S(1)}, bf16[192,2048]{1,0:T(8,128)(2,1)S(1)}, u32[]{:S(2)}, u32[]{:S(2)}) %collective-permute-start.10) | collective-permute-done | bytes 786464 | tf_op jit(solution)/shard_map/ppermute | solution.py:135
  85.8 1.8 %shard_map.124 = (f32[192,2048]{1,0:T(8,128)}, f32[8,128]{1,0:T(8,128)S(1)}) custom-call(f32[8,128]{1,0:T(8,128)S(1)} %get-tuple-element.90.refs_0_, bf16[192,2048]{1,0:T(8,128)(2,1)S(1)} %get-tuple-element.91.refs_1_, bf16[384,2048]{1,0:T(8,128)(2,1)S(1)} %collective-permute-done.8.refs_2_, bf16[192,2048]{1,0:T(8,128)(2,1)S(1)} %collective-permute-done.11.refs_3_), custom_call_target="tpu_custom_call" | custom-call | tf_op jit(solution)/shard_map/pallas_call | solution.py:454
  89.4 5.0 %collective-permute-done.12.refs_2_ = bf16[96,2048]{1,0:T(8,128)(2,1)S(1)} collective-permute-done((bf16[96,2048]{1,0:T(8,128)(2,1)S(1)}, bf16[96,2048]{1,0:T(8,128)(2,1)S(1)}, u32[]{:S(2)}, u32[]{:S(2)}) %collective-permute-start.12) | collective-permute-done | bytes 393248 | tf_op jit(solution)/shard_map/ppermute | solution.py:135
  94.5 8.2 %collective-permute-done.13.refs_3_ = bf16[512,768]{1,0:T(8,128)(2,1)S(1)} collective-permute-done((bf16[512,768]{1,0:T(8,128)(2,1)S(1)}, bf16[512,768]{1,0:T(8,128)(2,1)S(1)}, u32[]{:S(2)}, u32[]{:S(2)}) %collective-permute-start.13) | collective-permute-done | bytes 786464 | tf_op jit(solution)/shard_map/ppermute | solution.py:135
  102.7 3.0 %shard_map.127 = (f32[512,768]{1,0:T(8,128)}, f32[8,128]{1,0:T(8,128)S(1)}) custom-call(f32[8,128]{1,0:T(8,128)S(1)} %get-tuple-element.97.refs_0_, bf16[512,1536]{1,0:T(8,128)(2,1)S(1)} %get-tuple-element.98.refs_1_, bf16[1024,1536]{1,0:T(8,128)(2,1)S(1)} %collective-permute-done.9.refs_2_, bf16[512,768]{1,0:T(8,128)(2,1)S(1)} %collective-permute-done.13.refs_3_), custom_call_target="tpu_custom_call" | custom-call | tf_op jit(solution)/shard_map/pallas_call | solution.py:454
  105.9 3.0 %collective-permute-start.15 = (bf16[48,2048]{1,0:T(8,128)(2,1)S(1)}, bf16[48,2048]{1,0:T(8,128)(2,1)S(1)}, u32[]{:S(2)}, u32[]{:S(2)}) collective-permute-start(bf16[48,2048]{1,0:T(8,128)(2,1)S(1)} %get-tuple-element.105), channel_id=1, source_target_pairs={{0,4},{1,5},{2,6},{3,7},{4,0},{5,1},{6,2},{7,3},{8,12},{9,13},{10,... | collective-permute-start | bytes 589832 | tf_op jit(solution)/shard_map/ppermute | solution.py:135
  109.0 8.4 %collective-permute-done.15.refs_2_ = bf16[48,2048]{1,0:T(8,128)(2,1)S(1)} collective-permute-done((bf16[48,2048]{1,0:T(8,128)(2,1)S(1)}, bf16[48,2048]{1,0:T(8,128)(2,1)S(1)}, u32[]{:S(2)}, u32[]{:S(2)}) %collective-permute-start.15) | collective-permute-done | bytes 196640 | tf_op jit(solution)/shard_map/ppermute | solution.py:135
  119.6 2.0 %collective-permute-start.17 = (bf16[48,2048]{1,0:T(8,128)(2,1)S(1)}, bf16[48,2048]{1,0:T(8,128)(2,1)S(1)}, u32[]{:S(2)}, u32[]{:S(2)}) collective-permute-start(bf16[48,2048]{1,0:T(8,128)(2,1)S(1)} %get-tuple-element.112), channel_id=1, source_target_pairs={{0,4},{1,5},{2,6},{3,7},{4,0},{5,1},{6,2},{7,3},{8,12},{9,13},{10,... | collective-permute-start | bytes 589832 | tf_op jit(solution)/shard_map/ppermute | solution.py:135
  121.6 8.9 %collective-permute-done.17.refs_2_ = bf16[48,2048]{1,0:T(8,128)(2,1)S(1)} collective-permute-done((bf16[48,2048]{1,0:T(8,128)(2,1)S(1)}, bf16[48,2048]{1,0:T(8,128)(2,1)S(1)}, u32[]{:S(2)}, u32[]{:S(2)}) %collective-permute-start.17) | collective-permute-done | bytes 196640 | tf_op jit(solution)/shard_map/ppermute | solution.py:135
  131.2 3.0 %shard_map.132 = (f32[512,768]{1,0:T(8,128)}, f32[8,128]{1,0:T(8,128)}) custom-call(f32[8,128]{1,0:T(8,128)S(1)} %get-tuple-element.115.refs_0_, bf16[512,1536]{1,0:T(8,128)(2,1)S(1)} %get-tuple-element.98.refs_1_, bf16[1024,1536]{1,0:T(8,128)(2,1)S(1)} %collective-permute-done.9.refs_2_, bf16[512,768]{1,0:T(8,128)(2,1)S(1)} %collective-permute-done.18.refs_3_), custom_call_target="tpu_custom_call" | custom-call | tf_op jit(solution)/shard_map/pallas_call | solution.py:454
  (52 shorter events, 29.0 us)
Async XLA Ops:
  0.6 0.9 copy-start.3
  1.6 0.9 copy-start.4
  4.9 21.6 %collective-permute-start.1 = (bf16[96,2176]{1,0:T(8,128)(2,1)S(1)}, bf16[96,2176]{1,0:T(8,128)(2,1)S(1)}, u32[]{:S(2)}, u32[]{:S(2)}) collective-permute-start(bf16[96,2176]{1,0:T(8,128)(2,1)S(1)} %get-tuple-element.62.refs_1_), channel_id=1, source_target_pairs={{0,2},{1,3},{2,0},{3,1},{4,6},{5,7},{6,4},{7,5},{8,10},{9,11},{10,... | collective-permute-start | bytes 1253384 | tf_op jit(solution)/shard_map/ppermute | solution.py:135
  8.0 21.0 %collective-permute-start = (bf16[96,2176]{1,0:T(8,128)(2,1)S(1)}, bf16[96,2176]{1,0:T(8,128)(2,1)S(1)}, u32[]{:S(2)}, u32[]{:S(2)}) collective-permute-start(bf16[96,2176]{1,0:T(8,128)(2,1)S(1)} %get-tuple-element.62.refs_1_), channel_id=1, source_target_pairs={{0,4},{1,5},{2,6},{3,7},{4,0},{5,1},{6,2},{7,3},{8,12},{9,13},{10,... | collective-permute-start | bytes 1253384 | tf_op jit(solution)/shard_map/ppermute | solution.py:135
  10.6 18.4 %collective-permute-start.3 = (bf16[96,2176]{1,0:T(8,128)(2,1)S(1)}, bf16[96,2176]{1,0:T(8,128)(2,1)S(1)}, u32[]{:S(2)}, u32[]{:S(2)}) collective-permute-start(bf16[96,2176]{1,0:T(8,128)(2,1)S(1)} %get-tuple-element.62.refs_1_), channel_id=1, source_target_pairs={{0,1},{1,0},{2,3},{3,2},{4,5},{5,4},{6,7},{7,6},{8,9},{9,8},{10,11... | collective-permute-start | bytes 1253384 | tf_op jit(solution)/shard_map/ppermute | solution.py:135
  26.5 12.6 %collective-permute-start.2 = (bf16[96,2176]{1,0:T(8,128)(2,1)S(1)}, bf16[96,2176]{1,0:T(8,128)(2,1)S(1)}, u32[]{:S(2)}, u32[]{:S(2)}) collective-permute-start(bf16[96,2176]{1,0:T(8,128)(2,1)S(1)} %collective-permute-done.1.refs_3_), channel_id=1, source_target_pairs={{0,1},{1,0},{2,3},{3,2},{4,5},{5,4},{6,7},{7,6},{8,9},{9,8},{10,11... | collective-permute-start | bytes 1253384 | tf_op jit(solution)/shard_map/ppermute | solution.py:135
  29.6 9.4 %collective-permute-start.4 = (bf16[96,2176]{1,0:T(8,128)(2,1)S(1)}, bf16[96,2176]{1,0:T(8,128)(2,1)S(1)}, u32[]{:S(2)}, u32[]{:S(2)}) collective-permute-start(bf16[96,2176]{1,0:T(8,128)(2,1)S(1)} %get-tuple-element.63), channel_id=1, source_target_pairs={{0,2},{1,3},{2,0},{3,1},{4,6},{5,7},{6,4},{7,5},{8,10},{9,11},{10,... | collective-permute-start | bytes 1253384 | tf_op jit(solution)/shard_map/ppermute | solution.py:135
  30.1 18.0 %collective-permute-start.5 = (bf16[96,2176]{1,0:T(8,128)(2,1)S(1)}, bf16[96,2176]{1,0:T(8,128)(2,1)S(1)}, u32[]{:S(2)}, u32[]{:S(2)}) collective-permute-start(bf16[96,2176]{1,0:T(8,128)(2,1)S(1)} %collective-permute-done.refs_2_), channel_id=1, source_target_pairs={{0,1},{1,0},{2,3},{3,2},{4,5},{5,4},{6,7},{7,6},{8,9},{9,8},{10,11... | collective-permute-start | bytes 1253384 | tf_op jit(solution)/shard_map/ppermute | solution.py:135
  39.1 13.4 %collective-permute-start.7 = (bf16[48,2176]{1,0:T(8,128)(2,1)S(1)}, bf16[48,2176]{1,0:T(8,128)(2,1)S(1)}, u32[]{:S(2)}, u32[]{:S(2)}) collective-permute-start(bf16[48,2176]{1,0:T(8,128)(2,1)S(1)} %get-tuple-element.65.refs_4_), channel_id=1, source_target_pairs={{0,1},{1,0},{2,3},{3,2},{4,5},{5,4},{6,7},{7,6},{8,9},{9,8},{10,11... | collective-permute-start | bytes 626696 | tf_op jit(solution)/shard_map/ppermute | solution.py:135
  40.8 16.2 %collective-permute-start.6 = (bf16[48,2048]{1,0:T(8,128)(2,1)S(1)}, bf16[48,2048]{1,0:T(8,128)(2,1)S(1)}, u32[]{:S(2)}, u32[]{:S(2)}) collective-permute-start(bf16[48,2048]{1,0:T(8,128)(2,1)S(1)} %get-tuple-element.64.refs_4_), channel_id=1, source_target_pairs={{0,1},{1,0},{2,3},{3,2},{4,5},{5,4},{6,7},{7,6},{8,9},{9,8},{10,11... | collective-permute-start | bytes 589832 | tf_op jit(solution)/shard_map/ppermute | solution.py:135
  41.2 1.9 %copy-start = (bf16[1,2048,768]{2,1,0:T(8,128)(2,1)S(1)}, bf16[1,2048,768]{2,1,0:T(8,128)(2,1)}, u32[]{:S(2)}) copy-start(bf16[1,2048,768]{2,1,0:T(8,128)(2,1)} %param.11) | copy-start | bytes 9437188
  43.1 1.9 %copy-start.1 = (bf16[1,2048,768]{2,1,0:T(8,128)(2,1)S(1)}, bf16[1,2048,768]{2,1,0:T(8,128)(2,1)}, u32[]{:S(2)}) copy-start(bf16[1,2048,768]{2,1,0:T(8,128)(2,1)} %param.12) | copy-start | bytes 9437188
  45.0 1.9 %copy-start.2 = (bf16[1,768,2048]{2,1,0:T(8,128)(2,1)S(1)}, bf16[1,768,2048]{2,1,0:T(8,128)(2,1)}, u32[]{:S(2)}) copy-start(bf16[1,768,2048]{2,1,0:T(8,128)(2,1)} %param.13) | copy-start | bytes 9437188
  58.1 3.5 %collective-permute-start.8 = (bf16[384,2048]{1,0:T(8,128)(2,1)S(1)}, bf16[384,2048]{1,0:T(8,128)(2,1)S(1)}, u32[]{:S(2)}, u32[]{:S(2)}) collective-permute-start(bf16[384,2048]{1,0:T(8,128)(2,1)S(1)} %get-tuple-element.78), channel_id=1, source_target_pairs={{0,8},{8,0},{16,24},{24,16},{1,9},{9,1},{17,25},{25,17},{2,10},{10... | collective-permute-start | bytes 4718600 | tf_op jit(solution)/shard_map/ppermute | solution.py:135
  63.5 5.7 %collective-permute-start.9 = (bf16[1024,1536]{1,0:T(8,128)(2,1)S(1)}, bf16[1024,1536]{1,0:T(8,128)(2,1)S(1)}, u32[]{:S(2)}, u32[]{:S(2)}) collective-permute-start(bf16[1024,1536]{1,0:T(8,128)(2,1)S(1)} %get-tuple-element.85), channel_id=1, source_target_pairs={{0,8},{8,0},{16,24},{24,16},{1,9},{9,1},{17,25},{25,17},{2,10},{10... | collective-permute-start | bytes 9437192 | tf_op jit(solution)/shard_map/ppermute | solution.py:135
  63.7 20.4 %collective-permute-start.10 = (bf16[192,2048]{1,0:T(8,128)(2,1)S(1)}, bf16[192,2048]{1,0:T(8,128)(2,1)S(1)}, u32[]{:S(2)}, u32[]{:S(2)}) collective-permute-start(bf16[192,2048]{1,0:T(8,128)(2,1)S(1)} %get-tuple-element.89), channel_id=1, source_target_pairs={{0,1},{1,0},{2,3},{3,2},{4,5},{5,4},{6,7},{7,6},{8,9},{9,8},{10,11... | collective-permute-start | bytes 2359304 | tf_op jit(solution)/shard_map/ppermute | solution.py:135
  65.4 20.4 %collective-permute-start.11 = (bf16[192,2048]{1,0:T(8,128)(2,1)S(1)}, bf16[192,2048]{1,0:T(8,128)(2,1)S(1)}, u32[]{:S(2)}, u32[]{:S(2)}) collective-permute-start(bf16[192,2048]{1,0:T(8,128)(2,1)S(1)} %get-tuple-element.92), channel_id=1, source_target_pairs={{0,16},{8,24},{16,0},{24,8},{1,17},{9,25},{17,1},{25,9},{2,18},{10... | collective-permute-start | bytes 2359304 | tf_op jit(solution)/shard_map/ppermute | solution.py:135
  69.4 33.2 %collective-permute-start.13 = (bf16[512,768]{1,0:T(8,128)(2,1)S(1)}, bf16[512,768]{1,0:T(8,128)(2,1)S(1)}, u32[]{:S(2)}, u32[]{:S(2)}) collective-permute-start(bf16[512,768]{1,0:T(8,128)(2,1)S(1)} %get-tuple-element.99), channel_id=1, source_target_pairs={{0,16},{8,24},{16,0},{24,8},{1,17},{9,25},{17,1},{25,9},{2,18},{10... | collective-permute-start | bytes 2359304 | tf_op jit(solution)/shard_map/ppermute | solution.py:135
  73.8 31.9 %collective-permute-start.14 = (bf16[192,2048]{1,0:T(8,128)(2,1)S(1)}, bf16[192,2048]{1,0:T(8,128)(2,1)S(1)}, u32[]{:S(2)}, u32[]{:S(2)}) collective-permute-start(bf16[192,2048]{1,0:T(8,128)(2,1)S(1)} %get-tuple-element.102), channel_id=1, source_target_pairs={{0,1},{1,0},{2,3},{3,2},{4,5},{5,4},{6,7},{7,6},{8,9},{9,8},{10,11... | collective-permute-start | bytes 2359304 | tf_op jit(solution)/shard_map/ppermute | solution.py:135
  84.3 10.1 %collective-permute-start.12 = (bf16[96,2048]{1,0:T(8,128)(2,1)S(1)}, bf16[96,2048]{1,0:T(8,128)(2,1)S(1)}, u32[]{:S(2)}, u32[]{:S(2)}) collective-permute-start(bf16[96,2048]{1,0:T(8,128)(2,1)S(1)} %get-tuple-element.96), channel_id=1, source_target_pairs={{0,2},{1,3},{2,0},{3,1},{4,6},{5,7},{6,4},{7,5},{8,10},{9,11},{10,... | collective-permute-start | bytes 1179656 | tf_op jit(solution)/shard_map/ppermute | solution.py:135
  87.8 43.4 %collective-permute-start.18 = (bf16[512,768]{1,0:T(8,128)(2,1)S(1)}, bf16[512,768]{1,0:T(8,128)(2,1)S(1)}, u32[]{:S(2)}, u32[]{:S(2)}) collective-permute-start(bf16[512,768]{1,0:T(8,128)(2,1)S(1)} %get-tuple-element.116), channel_id=1, source_target_pairs={{0,16},{8,24},{16,0},{24,8},{1,17},{9,25},{17,1},{25,9},{2,18},{10... | collective-permute-start | bytes 2359304 | tf_op jit(solution)/shard_map/ppermute | solution.py:135
  105.9 13.7 %collective-permute-start.16 = (bf16[96,2048]{1,0:T(8,128)(2,1)S(1)}, bf16[96,2048]{1,0:T(8,128)(2,1)S(1)}, u32[]{:S(2)}, u32[]{:S(2)}) collective-permute-start(bf16[96,2048]{1,0:T(8,128)(2,1)S(1)} %get-tuple-element.109), channel_id=1, source_target_pairs={{0,2},{1,3},{2,0},{3,1},{4,6},{5,7},{6,4},{7,5},{8,10},{9,11},{10,... | collective-permute-start | bytes 1179656 | tf_op jit(solution)/shard_map/ppermute | solution.py:135
  105.9 11.4 %collective-permute-start.15 = (bf16[48,2048]{1,0:T(8,128)(2,1)S(1)}, bf16[48,2048]{1,0:T(8,128)(2,1)S(1)}, u32[]{:S(2)}, u32[]{:S(2)}) collective-permute-start(bf16[48,2048]{1,0:T(8,128)(2,1)S(1)} %get-tuple-element.105), channel_id=1, source_target_pairs={{0,4},{1,5},{2,6},{3,7},{4,0},{5,1},{6,2},{7,3},{8,12},{9,13},{10,... | collective-permute-start | bytes 589832 | tf_op jit(solution)/shard_map/ppermute | solution.py:135
  119.6 10.9 %collective-permute-start.17 = (bf16[48,2048]{1,0:T(8,128)(2,1)S(1)}, bf16[48,2048]{1,0:T(8,128)(2,1)S(1)}, u32[]{:S(2)}, u32[]{:S(2)}) collective-permute-start(bf16[48,2048]{1,0:T(8,128)(2,1)S(1)} %get-tuple-element.112), channel_id=1, source_target_pairs={{0,4},{1,5},{2,6},{3,7},{4,0},{5,1},{6,2},{7,3},{8,12},{9,13},{10,... | collective-permute-start | bytes 589832 | tf_op jit(solution)/shard_map/ppermute | solution.py:135
  (2 other events, 1.4 us)

commit v3 on v2

--- a/solution.py
+++ b/solution.py
@@ -107,7 +107,7 @@
 ORDER = ((8, 128), jnp.float32, pltpu.VMEM)
 
 
-def stage(body, ins, outs, after=(), scratch=(), aliases=None):
+def stage(body, ins, outs, after=(), scratch=(), aliases=None, vmem=8):
     skipped = len(after)
     given = skipped + len(ins)
 
@@ -125,8 +125,8 @@
         scratch_shapes=list(scratch),
         input_output_aliases={skipped + i: o for i, o in (aliases or {}).items()},
         cost_estimate=pl.CostEstimate(flops=0, bytes_accessed=0, transcendentals=0),
-        compiler_params=pltpu.CompilerParams(vmem_limit_bytes=16 * 2**20),
-    )(*after, *[a for a, _ in ins])
+        compiler_params=pltpu.CompilerParams(vmem_limit_bytes=vmem * 2**20),
+    )(*after, *[pltpu.with_memory_space_constraint(a, HBM) if m is HBM else a for a, m in ins])
     return list(outputs)
 
 
@@ -143,10 +143,11 @@
     count, width = tokens.shape
     top = expert_ids.shape[1]
 
-    def body(tok, ids, given, cot, both, sems):
+    def body(tok, ids, given, cot, alone, both, sems):
         copies = [
-            pltpu.make_async_copy(tok, both.at[:count, :width], sems.at[0]),
-            pltpu.make_async_copy(cot, both.at[count:, :width], sems.at[1]),
+            pltpu.make_async_copy(tok, alone.at[:, :width], sems.at[0]),
+            pltpu.make_async_copy(tok, both.at[:count, :width], sems.at[1]),
+            pltpu.make_async_copy(cot, both.at[count:, :width], sems.at[2]),
         ]
         for copy in copies:
             copy.start()
@@ -158,7 +159,9 @@
             named = (names[:, k : k + 1] == column) | (names[:, k : k + 1] + experts == column)
             total = total + jnp.where(named, values[:, k : k + 1], 0.0)
         high = total.astype(BF16).astype(F32)
-        both[:count, width:] = jnp.where(column < experts, high, total - high).astype(BF16)
+        side = jnp.where(column < experts, high, total - high).astype(BF16)
+        alone[:, width:] = side
+        both[:count, width:] = side
         both[count:, width:] = jnp.zeros((count, lanes), BF16)
         for copy in copies:
             copy.wait()
@@ -166,27 +169,9 @@
     return stage(
         body,
         [(tokens, HBM), (expert_ids.T, VMEM), (gate_probs.T, VMEM), (out_cot, HBM)],
-        [((2 * count, width + lanes), BF16, VMEM)],
-        scratch=[pltpu.SemaphoreType.DMA((2,))],
-    )
-
-
-def kept_near(arrays, after):
-    def body(*refs):
-        n = len(arrays)
-        copies = [pltpu.make_async_copy(refs[i], refs[n + i], refs[2 * n].at[i]) for i in range(n)]
-        for copy in copies:
-            copy.start()
-        for copy in copies:
-            copy.wait()
-
-    return stage(
-        body,
-        [(a, HBM) for a in arrays],
-        [(a.shape, a.dtype, VMEM) for a in arrays],
-        after=after,
-        scratch=[pltpu.SemaphoreType.DMA((len(arrays),))],
-    )
+        [((count, width + lanes), BF16, VMEM), ((2 * count, width + lanes), BF16, VMEM)],
+        scratch=[pltpu.SemaphoreType.DMA((3,))],
+            )
 
 
 def products(places, left, right, outs, own, tile=512):
@@ -213,48 +198,48 @@
     mine = lax.axis_index("dp").astype(jnp.int32).reshape(1)
     total = count * experts
     half = total // 2
+    pair = half // 2
     lanes = 128 * (-(-2 * experts // 128))
     odd_places = list(range(owners - 1, 0, -2))
     even_places = [m - 1 for m in odd_places]
     slab, band = ff // owners, width // owners
 
     near_bit, far_bit = 2, 4
-    both, _ = packed(tokens, expert_ids, gate_probs, out_cot, experts, lanes)
     wide = width + lanes
-    far = swap(both, "expert", far_bit)
-    near = swap(both, "expert", near_bit)
+    tok_own, both, done = packed(tokens, expert_ids, gate_probs, out_cot, experts, lanes)
+    tok_far = swap(tok_own, "expert", far_bit)
+    tok_near = swap(tok_own, "expert", near_bit)
     next_both = swap(both, "expert", 1)
-    next_near = swap(near, "expert", 1)
-    next_far = swap(far, "expert", 1)
-    far_on, _ = stage(
-        lambda *_: None,
-        [(far, ANY), (next_both, ANY)],
-        [(far.shape, BF16, ANY)],
-        aliases={0: 0},
-    )
-    far_near = swap(far_on, "expert", near_bit)
-    (done,) = stage(lambda *_: None, [(next_near, ANY)], [])
-
-    def apart(pair, tok, cot):
-        tok[...] = pair[:count, :]
-        cot[...] = pair[count:, :width]
-
-    last_tok, last_cot, done = stage(
-        apart,
-        [(far_near, VMEM)],
-        [((count, wide), BF16, VMEM), ((count, width), BF16, VMEM)],
-        after=[done],
-    )
-    next_last_tok = swap(last_tok, "expert", 1)
-    next_last_cot = swap(last_cot, "expert", 1)
-    gate_near, up_near, down_near, done = kept_near([w[0] for w in (w_gate, w_up, w_down)], [done])
-    whole = [both, far, near, next_both, next_far, next_near]
-    tok_pieces = [(a, 0) for a in whole]
-    cot_pieces = [(a, count) for a in whole]
-    tok_pieces[3:3] = [(last_tok, 0)]
-    cot_pieces[3:3] = [(last_cot, 0)]
-    tok_pieces.append((next_last_tok, 0))
-    cot_pieces.append((next_last_cot, 0))
+    def copied(sources, width, after, waits=()):
+        rows = count * len(sources)
+
+        def body(*refs):
+            out = refs[-1]
+            for i, (_, row) in enumerate(sources):
+                out[i * count : (i + 1) * count, :] = refs[i][row : row + count, :width]
+
+        return stage(
+            body,
+            [(a, VMEM) for a, _ in sources] + [(a, ANY) for a in waits],
+            [((rows, width), BF16, VMEM)],
+            after=after,
+        )
+
+    tok_pair, done = copied([(tok_near, 0), (tok_far, 0)], wide, [done], [next_both])
+    cot_own, done = copied([(both, count)], width, [done])
+    tok_far_on, done = copied([(tok_far, 0)], wide, [done])
+    next_tok_pair = swap(tok_pair, "expert", 1)
+    tok_last = swap(tok_far_on, "expert", near_bit)
+    cot_far = swap(cot_own, "expert", far_bit)
+    cot_near = swap(cot_own, "expert", near_bit)
+    tok_last_on, done = copied([(tok_last, 0)], wide, [done])
+    next_tok_last = swap(tok_last_on, "expert", 1)
+    cot_pair, done = copied([(cot_near, 0), (cot_far, 0)], width, [done])
+    cot_far_on, done = copied([(cot_far, 0)], width, [done])
+    next_cot_pair = swap(cot_pair, "expert", 1)
+    cot_last = swap(cot_far_on, "expert", near_bit)
+    tok_pieces = [(tok_own, 0), (tok_pair, count), (tok_pair, 0), (tok_last_on, 0)]
+    tok_pieces += [(next_both, 0), (next_tok_pair, count), (next_tok_pair, 0), (next_tok_last, 0)]
 
     def refs_of(pieces):
         arrays = []
@@ -265,13 +250,29 @@
         return arrays, [(i, row) for i, (_, row) in zip(where, pieces)]
 
     tok_arrays, tok_where = refs_of(tok_pieces)
-    cot_arrays, cot_where = refs_of(cot_pieces)
-
-    def forward(me_ref, *refs):
+
+    cot_last_on, done = copied([(cot_last, 0)], width, [done], [next_tok_last])
+    next_cot_last = swap(cot_last_on, "expert", 1)
+    cot_pieces = [(cot_own, 0), (cot_pair, count), (cot_pair, 0), (cot_last_on, 0)]
+    cot_pieces += [(next_both, count), (next_cot_pair, count), (next_cot_pair, 0), (next_cot_last, 0)]
+    def forward(me_ref, mine_ref, *refs):
         blocks = refs[: len(tok_arrays)]
-        gate, up, down, flipped, hidden_t, gate_by, up_by, even, odd, rows, probs, hidden = refs[
-            len(tok_arrays) :
+        weights = refs[len(tok_arrays) : len(tok_arrays) + 3]
+        flipped, flipped_sent, hidden_t, gate_by, up_by, kept, sent = refs[
+            len(tok_arrays) + 3 : len(tok_arrays) + 10
         ]
+        rows, probs, hidden, gate, up, down, sems = refs[len(tok_arrays) + 10 :]
+        steps = chunks(ff, 256)
+        copies = []
+        for i, (start, size) in enumerate(steps):
+            place = slice(start, start + size)
+            for j, (far_ref, near_ref) in enumerate([(weights[0], gate), (weights[1], up)]):
+                copies.append(
+                    pltpu.make_async_copy(far_ref.at[:, place], near_ref.at[:, place], sems.at[2 * i + j])
+                )
+        copies.append(pltpu.make_async_copy(weights[2], down, sems.at[2 * len(steps)]))
+        for copy in copies:
+            copy.start()
         own = me_ref[0]
         column = lax.broadcasted_iota(jnp.int32, (count, lanes), 1)
         chosen = (column == own) | (column == own + experts)
@@ -281,9 +282,15 @@
             side = jnp.where(chosen, blocks[i][row : row + count, width:].astype(F32), 0.0)
             probs[place, :] = jnp.sum(side, axis=1, keepdims=True)
         weight = probs[...]
-        for start, size in chunks(ff, 256):
+        for out, places in ((flipped, even_places), (flipped_sent, odd_places)):
+            for i, m in enumerate(places):
+                start = pl.multiple_of((mine_ref[0] ^ m) * band, band)
+                out[i * band : (i + 1) * band, :] = rows[:, pl.ds(start, band)].T
+        for i, (start, size) in enumerate(steps):
             place = slice(start, start + size)
+            copies[2 * i].wait()
             gate_pre = jnp.dot(rows[...], gate[:, place], preferred_element_type=F32)
+            copies[2 * i + 1].wait()
             up_pre = jnp.dot(rows[...], up[:, place], preferred_element_type=F32)
             sigma = jax.nn.sigmoid(gate_pre)
             silu = gate_pre * sigma
@@ -291,65 +298,82 @@
             hidden[:, place] = (silu * scaled).astype(BF16)
             gate_by[:, place] = scaled * sigma * (1.0 + gate_pre * (1.0 - sigma))
             up_by[:, place] = weight * silu
+            hidden_t[place, :] = hidden[:, place].T
+        copies[-1].wait()
         for start, size in chunks(width, 512):
             place = slice(start, start + size)
             part = jnp.dot(hidden[...], down[:, place], preferred_element_type=F32).astype(BF16)
-            even[:, place] = part[:half]
-            odd[:, place] = part[half:]
-        for start, size in chunks(width, 512):
-            flipped[start : start + size, :] = rows[:, start : start + size].T
-        for start, size in chunks(ff, 256):
-            hidden_t[start : start + size, :] = hidden[:, start : start + size].T
-
-    flipped, hidden_t, gate_by, up_by, out_even, out_odd, _ = stage(
+            for i in range(2):
+                low, high = slice(i * pair, (i + 1) * pair), i * half
+                kept[low, place] = part[high : high + pair]
+                sent[low, place] = part[high + pair : high + half]
+
+    flipped, flipped_sent, hidden_t, gate_by, up_by, out_kept, out_sent, done = stage(
         forward,
-        [(me, SMEM)] + [(a, VMEM) for a in tok_arrays + [gate_near, up_near, down_near]],
+        [(me, SMEM), (mine, SMEM)] + [(a, VMEM) for a in tok_arrays] + [(w[0], HBM) for w in (w_gate, w_up, w_down)],
         [
-            ((width, total), BF16, VMEM),
+            ((width // 2, total), BF16, VMEM),
+            ((width // 2, total), BF16, VMEM),
             ((ff, total), BF16, VMEM),
             ((total, ff), F32, VMEM),
             ((total, ff), F32, VMEM),
             ((half, width), BF16, VMEM),
             ((half, width), BF16, VMEM),
         ],
-        scratch=[VMEM((total, width), BF16), VMEM((total, 1), F32), VMEM((total, ff), BF16)],
-    )
+        scratch=[
+            VMEM((total, width), BF16),
+            VMEM((total, 1), F32),
+            VMEM((total, ff), BF16),
+            VMEM((width, ff), BF16),
+            VMEM((width, ff), BF16),
+            VMEM((ff, width), BF16),
+            pltpu.SemaphoreType.DMA((2 * len(chunks(ff, 256)) + 1,)),
+        ],
+        after=[done],
+        vmem=16,
+    )
+    flipped_came = swap(flipped_sent, "dp", 1)
+    cot_arrays, cot_where = refs_of(cot_pieces)
 
     def down_odd(own_ref, *refs):
         blocks = refs[: len(cot_arrays)]
-        left, _, _, rows, away = refs[len(cot_arrays) :]
+        left, rows, away = refs[len(cot_arrays) :]
         for b, (i, row) in enumerate(cot_where):
             rows[b * count : (b + 1) * count, :] = blocks[i][row : row + count, :width]
         outs = [(away, i * slab) for i in range(len(odd_places))]
         products(odd_places, left, rows, outs, own_ref[0])
 
-    out_odd, cot_rows, down_away, done = stage(
+    cot_rows, down_away, done = stage(
         down_odd,
-        [(mine, SMEM)] + [(a, VMEM) for a in cot_arrays] + [(hidden_t, VMEM), (out_odd, ANY)],
-        [
-            ((half, width), BF16, ANY),
-            ((total, width), BF16, VMEM),
-            ((slab * len(odd_places), width), BF16, VMEM),
-        ],
-        aliases={len(cot_arrays) + 2: 0},
+        [(mine, SMEM)] + [(a, VMEM) for a in cot_arrays] + [(hidden_t, VMEM)],
+        [((total, width), BF16, VMEM), ((slab * len(odd_places), width), BF16, VMEM)],
+        after=[done],
     )
     down_came = swap(down_away, "dp", 1)
-    out_came = swap(out_odd, "expert", 1)
-
-    def backward(own_ref, cot, left, down, gate_ref, up_ref, grads, *kept):
+    out_came = swap(out_sent, "expert", near_bit)
+
+    def backward(own_ref, cot, left, down, gate_ref, up_ref, grads, *refs):
+        *kept, near, sem = refs
+        copy = pltpu.make_async_copy(down, near, sem)
+        copy.start()
         products(even_places, left, cot, [(k, 0) for k in kept], own_ref[0])
+        copy.wait()
         for start, size in chunks(ff, 256):
             place = slice(start, start + size)
-            grad = lax.dot_general(cot[...], down[place, :], TURNED, preferred_element_type=F32)
+            grad = lax.dot_general(cot[...], near[place, :], TURNED, preferred_element_type=F32)
             grads[:, place] = (grad * gate_ref[:, place]).astype(BF16)
             grads[:, ff + start : ff + start + size] = (grad * up_ref[:, place]).astype(BF16)
 
     grads, *down_kept, done = stage(
         backward,
-        [(mine, SMEM)] + [(a, VMEM) for a in (cot_rows, hidden_t, down_near, gate_by, up_by)],
+        [(mine, SMEM), (cot_rows, VMEM), (hidden_t, VMEM), (w_down[0], HBM)]
+        + [(gate_by, VMEM), (up_by, VMEM)],
         [((total, 2 * ff), BF16, VMEM)] + [((slab, width), BF16, VMEM)] * len(even_places),
+        scratch=[VMEM((ff, width), BF16), pltpu.SemaphoreType.DMA],
         after=[done],
     )
+
+    grads_came = swap(grads, "dp", 1)
 
     def added(kept, came, after=()):
         n, size = len(kept), kept[0].shape[0]
@@ -369,57 +393,59 @@
     *down_send, done = added(down_kept[:-1], down_came, [done])
     down_got = [swap(a, "dp", m) for a, m in zip(down_send, even_places)]
 
-    def both_odd(own_ref, left, right, away):
-        outs = [(away, i * band) for i in range(len(odd_places))]
-        products(odd_places, left, right, outs, own_ref[0], 256)
-
-    def both_even(own_ref, left, right, *kept):
-        products(even_places, left, right, [(k, 0) for k in kept], own_ref[0], 256)
-
-    given = [(mine, SMEM), (flipped, VMEM), (grads, VMEM)]
-    both_away, done = stage(
-        both_odd, given, [((band * len(odd_places), 2 * ff), BF16, VMEM)], after=[done]
-    )
-    both_came = swap(both_away, "dp", 1)
-    *both_kept, done = stage(
-        both_even, given, [((band, 2 * ff), BF16, VMEM)] * len(even_places), after=[done]
-    )
-    def half_added(first, after):
-        n = len(both_kept) - 1
-        place = slice(first, first + ff)
-
-        def body(*refs):
-            for i in range(n):
-                other = refs[n][i * band : (i + 1) * band, place].astype(F32)
-                refs[n + 1 + i][...] = (refs[i][:, place].astype(F32) + other).astype(BF16)
-
-        *sends, done = stage(
-            body,
-            [(a, VMEM) for a in [*both_kept[:-1], both_came]],
-            [((band, ff), BF16, VMEM)] * n,
-            after=after,
-        )
-        return [swap(a, "dp", m) for a, m in zip(sends, even_places)], done
-
-    gate_got, done = half_added(0, [done])
-
-    def input_rows(grad, gate, up, even, odd):
-        for start, size in chunks(width, 512):
+    def input_rows(grad, gate_far, up_far, even, odd, gate, up, sems):
+        steps = chunks(width, 512)
+        copies = []
+        for i, (start, size) in enumerate(steps):
             place = slice(start, start + size)
-            rows = lax.dot_general(
-                grad[:, :ff], gate[place, :], TURNED, preferred_element_type=F32
-            ) + lax.dot_general(grad[:, ff:], up[place, :], TURNED, preferred_element_type=F32)
+            for j, (far_ref, near_ref) in enumerate([(gate_far, gate), (up_far, up)]):
+                copies.append(
+                    pltpu.make_async_copy(far_ref.at[place], near_ref.at[place], sems.at[2 * i + j])
+                )
+        for copy in copies:
+            copy.start()
+        for i, (start, size) in enumerate(steps):
+            place = slice(start, start + size)
+            copies[2 * i].wait()
+            rows = lax.dot_general(grad[:, :ff], gate[place, :], TURNED, preferred_element_type=F32)
+            copies[2 * i + 1].wait()
+            rows = rows + lax.dot_general(
+                grad[:, ff:], up[place, :], TURNED, preferred_element_type=F32
+            )
             rows = rows.astype(BF16)
             even[:, place] = rows[:half]
             odd[:, place] = rows[half:]
 
     in_even, in_odd, done = stage(
         input_rows,
-        [(grads, VMEM), (gate_near, VMEM), (up_near, VMEM)],
+        [(grads, VMEM), (w_gate[0], HBM), (w_up[0], HBM)],
         [((half, width), BF16, VMEM)] * 2,
+        scratch=[VMEM((width, ff), BF16)] * 2
+        + [pltpu.SemaphoreType.DMA((2 * len(chunks(width, 512)),))],
         after=[done],
+        vmem=10,
     )
     in_came = swap(in_odd, "expert", 1)
+
+    def both_parts(left, left_came, grad, grad_came, *outs):
+        n = len(even_places)
+        for i in range(n):
+            place = slice(i * band, (i + 1) * band)
+            for start, size in chunks(2 * ff, 256):
+                column = slice(start, start + size)
+                value = jnp.dot(left[place, :], grad[:, column], preferred_element_type=F32)
+                value += jnp.dot(left_came[place, :], grad_came[:, column], preferred_element_type=F32)
+                out = outs[2 * i + start // ff]
+                out[:, start % ff : start % ff + size] = value.astype(out.dtype)
+
+    *both_kept, done = stage(
+        both_parts,
+        [(a, VMEM) for a in (flipped, flipped_came, grads, grads_came)],
+        [((band, ff), BF16, VMEM)] * (2 * len(even_places) - 2) + [((band, ff), F32, VMEM)] * 2,
+        after=[done],
+    )
+    gate_sums, up_sums = both_kept[0::2], both_kept[1::2]
+    gate_got = [swap(a, "dp", m) for a, m in zip(gate_sums[:-1], even_places)]
 
     def folded(held, came, after):
         rows = held.shape[0]
@@ -437,53 +463,53 @@
             after=after,
         )
 
-    def owned(kept, came, got, after, column=0):
-        size, wide = got[0].shape
-        step = 64
-        first = came.shape[0] // step - size // step
-        skipped = len(after)
+    def owned(parts, after):
+        size, wide = parts[-1].shape
+        step = size // 4
 
         def body(*refs):
-            value = refs[skipped][...].astype(F32)
-            for ref in refs[skipped + 1 : -2]:
-                value = value + ref[...].astype(F32)
-            refs[-2][...] = value
-            refs[-1][...] = jnp.zeros(ORDER[0], F32)
-
-        at = column // wide
-        outputs = pl.pallas_call(
+            *others, out, total, sems = refs
+            copies = []
+            for i in range(4):
+                at = slice(i * step, (i + 1) * step)
+                value = jnp.zeros((step, wide), F32)
+                for ref in others:
+                    first = ref.shape[0] - size + i * step
+                    value = value + ref[first : first + step, :].astype(F32)
+                total[at, :] = value
+                copies.append(pltpu.make_async_copy(total.at[at], out.at[at], sems.at[i]))
+                copies[-1].start()
+            for copy in copies:
+                copy.wait()
+
+        return stage(
             body,
-            grid=(size // step,),
-            in_specs=[pl.BlockSpec(memory_space=ANY)] * skipped
-            + [
-                pl.BlockSpec((step, wide), lambda i: (i, at)),
-                pl.BlockSpec((step, wide), lambda i: (i + first, at)),
-            ]
-            + [pl.BlockSpec((step, wide), lambda i: (i, 0))] * len(got),
-            out_specs=[
-                pl.BlockSpec((step, wide), lambda i: (i, 0)),
-                pl.BlockSpec(ORDER[0], lambda i: (0, 0)),
-            ],
-            out_shape=[jax.ShapeDtypeStruct((size, wide), F32), jax.ShapeDtypeStruct(*ORDER[:2])],
-            cost_estimate=pl.CostEstimate(flops=0, bytes_accessed=0, transcendentals=0),
-            compiler_params=pltpu.CompilerParams(vmem_limit_bytes=16 * 2**20),
-        )(*after, kept, came, *got)
-        return list(outputs)
+            [(a, VMEM) for a in parts],
+            [((size, wide), F32, HBM)],
+            scratch=[VMEM((size, wide), F32), pltpu.SemaphoreType.DMA((4,))],
+            after=after,
+        )
 
     def fold_on(held, came, bit, after):
         held, send, done = folded(held, came, after)
         return held, swap(send, "expert", bit), done
 
-    out_held, out_came, done = fold_on(out_even, out_came, near_bit, [done])
-    down_grad, done = owned(down_kept[-1], down_came, down_got, [done])
-    up_got, done = half_added(ff, [done])
+    down_grad, done = owned([down_kept[-1], down_came, *down_got], [done])
+    up_send = []
+    for a in up_sums[:-1]:
+        a, done = stage(
+            lambda *_: None, [(a, ANY)], [(a.shape, BF16, ANY)], after=[done], aliases={0: 0}
+        )
+        up_send.append(a)
+    up_got = [swap(a, "dp", m) for a, m in zip(up_send, even_places)]
+    out_held, out_came, done = fold_on(out_kept, out_came, 1, [done])
+    in_held, in_came, done = fold_on(in_even, in_came, near_bit, [done])
     out_held, out_came, done = fold_on(out_held, out_came, far_bit, [done])
-    gate_part, done = owned(both_kept[-1], both_came, gate_got, [done])
-    in_held, in_came, done = fold_on(in_even, in_came, near_bit, [done])
+    gate_part, done = owned([gate_sums[-1], *gate_got], [done])
+    in_held, in_came, done = fold_on(in_held, in_came, far_bit, [done])
     layer_out, done = folded(out_held, out_came, [done])
-    in_held, in_came, done = fold_on(in_held, in_came, far_bit, [done])
     input_grad, done = folded(in_held, in_came, [done])
-    up_part, _ = owned(both_kept[-1], both_came, up_got, [done], ff)
+    up_part, _ = owned([up_sums[-1], *up_got], [done])
     return (layer_out, input_grad, gate_part[None], up_part[None], down_grad[None])
 
 

time: 135 us -> 114 us (0.84)
  waiting for transfers between devices: 70.7 us -> 56.6 us
  local copies, waits for them, and re-layouts: 8.92 us -> 1.37 us
  Pallas kernels: 27.4 us -> 29.3 us
    ppermute x19 -> x23, waiting for transfers between devices: 70.7 us -> 56.6 us  [swap(): return lax.ppermute(value, axis, [(i, i ^ mask) for i in range(size)])]
    pallas_call x20 -> x24, Pallas kernels: 19.6 us -> 29.3 us  [stage(): pl.pallas_call(kernel, in_specs=[pl.BlockSpec(memory_space=m) for m in [A...]
    pallas_call x3 -> x0, Pallas kernels: 7.84 us -> none  [owned(): pl.pallas_call(body, grid=(size // step,), in_specs=[pl.BlockSpec(memory_...]
    unnamed x15 -> x4, local copies, waits for them, and re-layouts: 8.92 us -> 1.37 us
    ppermute x19 -> x23, starting transfers between devices: 26.4 us -> 25.6 us  [swap(): return lax.ppermute(value, axis, [(i, i ^ mask) for i in range(size)])]
  transfers between devices with their start and end apart: 19 -> 23, of which waited for: 13 -> 12; matrix products, arithmetic and copies ran while one was open for 0% -> 0% of each run, Pallas kernels for 15% -> 22%
where the time goes in v3:
time: 114 us
  waiting for transfers between devices  56.6 us (50%)
  Pallas kernels  29.3 us (26%)
  starting transfers between devices  25.6 us (22%)
  local copies, waits for them, and re-layouts  1.37 us (1%)
    ppermute x23, waiting for transfers between devices, swap(): return lax.ppermute(value, axis, [(i, i ^ mask) for i in range(size)])  56.6 us
    pallas_call x24, Pallas kernels, stage(): pl.pallas_call(kernel, in_specs=[pl.BlockSpec(memory_space=m) for m in [A...  29.3 us
    ppermute x23, starting transfers between devices, swap(): return lax.ppermute(value, axis, [(i, i ^ mask) for i in range(size)])  25.6 us
  transfers between devices with their start and end apart: 23, of which 12 were waited for; matrix products, arithmetic and copies ran while one was open for 0% of the time, Pallas kernels for 22%

profile of v3, /device:TPU:0, one launch (start us, length us, event | category | flops | bytes accessed | tf_op | source)
XLA Modules:
  0.0 113.8 jit_solution(4234783609875089409)
XLA Ops:
  3.2 3.0 %collective-permute-start.2 = (bf16[96,2176]{1,0:T(8,128)(2,1)S(1)}, bf16[96,2176]{1,0:T(8,128)(2,1)S(1)}, u32[]{:S(2)}, u32[]{:S(2)}) collective-permute-start(bf16[96,2176]{1,0:T(8,128)(2,1)S(1)} %get-tuple-element.72.refs_1_), channel_id=1, source_target_pairs={{0,1},{1,0},{2,3},{3,2},{4,5},{5,4},{6,7},{7,6},{8,9},{9,8},{10,11... | collective-permute-start | bytes 1253384 | tf_op jit(solution)/shard_map/ppermute | solution.py:135
  6.2 2.6 %collective-permute-start.1 = (bf16[48,2176]{1,0:T(8,128)(2,1)S(1)}, bf16[48,2176]{1,0:T(8,128)(2,1)S(1)}, u32[]{:S(2)}, u32[]{:S(2)}) collective-permute-start(bf16[48,2176]{1,0:T(8,128)(2,1)S(1)} %get-tuple-element.71.refs_3_), channel_id=1, source_target_pairs={{0,4},{1,5},{2,6},{3,7},{4,0},{5,1},{6,2},{7,3},{8,12},{9,13},{10,... | collective-permute-start | bytes 626696 | tf_op jit(solution)/shard_map/ppermute | solution.py:135
  8.8 1.6 %collective-permute-start = (bf16[48,2176]{1,0:T(8,128)(2,1)S(1)}, bf16[48,2176]{1,0:T(8,128)(2,1)S(1)}, u32[]{:S(2)}, u32[]{:S(2)}) collective-permute-start(bf16[48,2176]{1,0:T(8,128)(2,1)S(1)} %get-tuple-element.71.refs_3_), channel_id=1, source_target_pairs={{0,2},{1,3},{2,0},{3,1},{4,6},{5,7},{6,4},{7,5},{8,10},{9,11},{10,... | collective-permute-start | bytes 626696 | tf_op jit(solution)/shard_map/ppermute | solution.py:135
  10.4 7.9 %collective-permute-done.1.refs_2_.refs_1_ = bf16[48,2176]{1,0:T(8,128)(2,1)S(1)} collective-permute-done((bf16[48,2176]{1,0:T(8,128)(2,1)S(1)}, bf16[48,2176]{1,0:T(8,128)(2,1)S(1)}, u32[]{:S(2)}, u32[]{:S(2)}) %collective-permute-start.1) | collective-permute-done | bytes 208928 | tf_op jit(solution)/shard_map/ppermute | solution.py:135
  20.1 2.3 %collective-permute-start.5 = (bf16[48,2048]{1,0:T(8,128)(2,1)S(1)}, bf16[48,2048]{1,0:T(8,128)(2,1)S(1)}, u32[]{:S(2)}, u32[]{:S(2)}) collective-permute-start(bf16[48,2048]{1,0:T(8,128)(2,1)S(1)} %get-tuple-element.78.refs_2_), channel_id=1, source_target_pairs={{0,4},{1,5},{2,6},{3,7},{4,0},{5,1},{6,2},{7,3},{8,12},{9,13},{10,... | collective-permute-start | bytes 589832 | tf_op jit(solution)/shard_map/ppermute | solution.py:135
  23.0 7.0 %collective-permute-done.3.refs_1_ = bf16[48,2176]{1,0:T(8,128)(2,1)S(1)} collective-permute-done((bf16[48,2176]{1,0:T(8,128)(2,1)S(1)}, bf16[48,2176]{1,0:T(8,128)(2,1)S(1)}, u32[]{:S(2)}, u32[]{:S(2)}) %collective-permute-start.3) | collective-permute-done | bytes 208928 | tf_op jit(solution)/shard_map/ppermute | solution.py:135
  30.4 2.4 %collective-permute-done.4.refs_1_ = bf16[48,2048]{1,0:T(8,128)(2,1)S(1)} collective-permute-done((bf16[48,2048]{1,0:T(8,128)(2,1)S(1)}, bf16[48,2048]{1,0:T(8,128)(2,1)S(1)}, u32[]{:S(2)}, u32[]{:S(2)}) %collective-permute-start.4) | collective-permute-done | bytes 196640 | tf_op jit(solution)/shard_map/ppermute | solution.py:135
  32.9 1.8 %collective-permute-start.6 = (bf16[48,2048]{1,0:T(8,128)(2,1)S(1)}, bf16[48,2048]{1,0:T(8,128)(2,1)S(1)}, u32[]{:S(2)}, u32[]{:S(2)}) collective-permute-start(bf16[48,2048]{1,0:T(8,128)(2,1)S(1)} %get-tuple-element.81), channel_id=1, source_target_pairs={{0,2},{1,3},{2,0},{3,1},{4,6},{5,7},{6,4},{7,5},{8,10},{9,11},{10,... | collective-permute-start | bytes 589832 | tf_op jit(solution)/shard_map/ppermute | solution.py:135
  35.2 3.5 %collective-permute-done.6.refs_1_ = bf16[48,2048]{1,0:T(8,128)(2,1)S(1)} collective-permute-done((bf16[48,2048]{1,0:T(8,128)(2,1)S(1)}, bf16[48,2048]{1,0:T(8,128)(2,1)S(1)}, u32[]{:S(2)}, u32[]{:S(2)}) %collective-permute-start.6) | collective-permute-done | bytes 196640 | tf_op jit(solution)/shard_map/ppermute | solution.py:135
  40.1 8.8 %shard_map.118 = (bf16[1024,384]{1,0:T(8,128)(2,1)S(1)}, bf16[1024,384]{1,0:T(8,128)(2,1)S(1)}, bf16[768,384]{1,0:T(8,128)(2,1)S(1)}, f32[384,768]{1,0:T(8,128)S...) custom-call(f32[8,128]{1,0:T(8,128)S(1)} %get-tuple-element.83.refs_, ...), custom_call_target="tpu_custom_call" | custom-call | tf_op jit(solution)/shard_map/pallas_call | solution.py:120
  48.9 1.7 %collective-permute-done.10.refs_7_ = bf16[48,2048]{1,0:T(8,128)(2,1)S(1)} collective-permute-done((bf16[48,2048]{1,0:T(8,128)(2,1)S(1)}, bf16[48,2048]{1,0:T(8,128)(2,1)S(1)}, u32[]{:S(2)}, u32[]{:S(2)}) %collective-permute-start.10) | collective-permute-done | bytes 196640 | tf_op jit(solution)/shard_map/ppermute | solution.py:135
  51.7 3.3 %shard_map.120 = (bf16[384,1536]{1,0:T(8,128)(2,1)S(1)}, bf16[192,2048]{1,0:T(8,128)(2,1)S(1)}, bf16[192,2048]{1,0:T(8,128)(2,1)S(1)}, f32[8,128]{1,0:T(8,128)S(1)}) custom-call(f32[8,128]{1,0:T(8,128)S(1)} %get-tuple-element.89.refs_0_, s32[1]{0:T(128)} %bitcast.3.refs_2_.refs_1_, bf16[384,2048]{1,0:T(8,128)(2,1)S(1)} %get-tuple-element.90.refs_2_, ...), custom_call_target="tpu_custom_call" | custom-call | tf_op jit(solution)/shard_map/pallas_call | solution.py:120
  55.9 1.5 %collective-permute-start.14 = (bf16[192,2048]{1,0:T(8,128)(2,1)S(1)}, bf16[192,2048]{1,0:T(8,128)(2,1)S(1)}, u32[]{:S(2)}, u32[]{:S(2)}) collective-permute-start(bf16[192,2048]{1,0:T(8,128)(2,1)S(1)} %get-tuple-element.103), channel_id=1, source_target_pairs={{0,16},{8,24},{16,0},{24,8},{1,17},{9,25},{17,1},{25,9},{2,18},{10... | collective-permute-start | bytes 2359304 | tf_op jit(solution)/shard_map/ppermute | solution.py:135
  57.4 1.7 %collective-permute-start.15 = (bf16[192,2048]{1,0:T(8,128)(2,1)S(1)}, bf16[192,2048]{1,0:T(8,128)(2,1)S(1)}, u32[]{:S(2)}, u32[]{:S(2)}) collective-permute-start(bf16[192,2048]{1,0:T(8,128)(2,1)S(1)} %get-tuple-element.108), channel_id=1, source_target_pairs={{0,2},{1,3},{2,0},{3,1},{4,6},{5,7},{6,4},{7,5},{8,10},{9,11},{10,... | collective-permute-start | bytes 2359304 | tf_op jit(solution)/shard_map/ppermute | solution.py:135
  59.1 4.9 %shard_map.122 = (bf16[192,2048]{1,0:T(8,128)(2,1)S(1)}, bf16[192,2048]{1,0:T(8,128)(2,1)S(1)}, f32[8,128]{1,0:T(8,128)S(1)}) custom-call(f32[8,128]{1,0:T(8,128)S(1)} %get-tuple-element.96.refs_0_, bf16[384,1536]{1,0:T(8,128)(2,1)S(1)} %get-tuple-element.97.refs_1_.refs_3_, bf16[2048,768]{1,0:T(8,128)(2,1)} %bitcast.15, bf16[2048,768]{1,0:T(8,128)(2,1)} %bitcast.17), custom_call_target="tpu_custom_call" | custom-call | tf_op jit(solution)/shard_map/pallas_call | solution.py:120
  64.6 3.6 %shard_map.123 = (bf16[512,768]{1,0:T(8,128)(2,1)S(1)}, bf16[512,768]{1,0:T(8,128)(2,1)S(1)}, f32[512,768]{1,0:T(8,128)S(1)}, f32[512,768]{1,0:T(8,128)S(1)}, f32[8,128]{1,0:T(8,128)S(1)}) custom-call(f32[8,128]{1,0:T(8,128)S(1)} %get-tuple-element.98.refs_0_, bf16[1024,384]{1,0:T(8,128)(2,1)S(1)} %get-tuple-element.99.refs_1_, ...), custom_call_target="tpu_custom_call" | custom-call | tf_op jit(solution)/shard_map/pallas_call | solution.py:120
  68.8 7.5 %collective-permute-done.14.refs_3_ = bf16[192,2048]{1,0:T(8,128)(2,1)S(1)} collective-permute-done((bf16[192,2048]{1,0:T(8,128)(2,1)S(1)}, bf16[192,2048]{1,0:T(8,128)(2,1)S(1)}, u32[]{:S(2)}, u32[]{:S(2)}) %collective-permute-start.14) | collective-permute-done | bytes 786464 | tf_op jit(solution)/shard_map/ppermute | solution.py:135
  77.5 1.5 %collective-permute-start.22 = (bf16[512,768]{1,0:T(8,128)(2,1)S(1)}, bf16[512,768]{1,0:T(8,128)(2,1)S(1)}, u32[]{:S(2)}, u32[]{:S(2)}) collective-permute-start(bf16[512,768]{1,0:T(8,128)(2,1)S(1)} %get-tuple-element.132), channel_id=1, source_target_pairs={{0,16},{8,24},{16,0},{24,8},{1,17},{9,25},{17,1},{25,9},{2,18},{10... | collective-permute-start | bytes 2359304 | tf_op jit(solution)/shard_map/ppermute | solution.py:135
  79.8 4.7 %collective-permute-done.16.refs_2_ = bf16[192,2048]{1,0:T(8,128)(2,1)S(1)} collective-permute-done((bf16[192,2048]{1,0:T(8,128)(2,1)S(1)}, bf16[192,2048]{1,0:T(8,128)(2,1)S(1)}, u32[]{:S(2)}, u32[]{:S(2)}) %collective-permute-start.16) | collective-permute-done | bytes 786464 | tf_op jit(solution)/shard_map/ppermute | solution.py:135
  85.1 6.7 %collective-permute-done.17.refs_2_ = bf16[96,2048]{1,0:T(8,128)(2,1)S(1)} collective-permute-done((bf16[96,2048]{1,0:T(8,128)(2,1)S(1)}, bf16[96,2048]{1,0:T(8,128)(2,1)S(1)}, u32[]{:S(2)}, u32[]{:S(2)}) %collective-permute-start.17) | collective-permute-done | bytes 393248 | tf_op jit(solution)/shard_map/ppermute | solution.py:135
  94.5 1.8 %collective-permute-start.21 = (bf16[48,2048]{1,0:T(8,128)(2,1)S(1)}, bf16[48,2048]{1,0:T(8,128)(2,1)S(1)}, u32[]{:S(2)}, u32[]{:S(2)}) collective-permute-start(bf16[48,2048]{1,0:T(8,128)(2,1)S(1)} %get-tuple-element.127), channel_id=1, source_target_pairs={{0,4},{1,5},{2,6},{3,7},{4,0},{5,1},{6,2},{7,3},{8,12},{9,13},{10,... | collective-permute-start | bytes 589832 | tf_op jit(solution)/shard_map/ppermute | solution.py:135
  96.3 10.7 %collective-permute-done.20.refs_2_ = bf16[48,2048]{1,0:T(8,128)(2,1)S(1)} collective-permute-done((bf16[48,2048]{1,0:T(8,128)(2,1)S(1)}, bf16[48,2048]{1,0:T(8,128)(2,1)S(1)}, u32[]{:S(2)}, u32[]{:S(2)}) %collective-permute-start.20) | collective-permute-done | bytes 196640 | tf_op jit(solution)/shard_map/ppermute | solution.py:135
  107.8 3.4 %collective-permute-done.21.refs_2_ = bf16[48,2048]{1,0:T(8,128)(2,1)S(1)} collective-permute-done((bf16[48,2048]{1,0:T(8,128)(2,1)S(1)}, bf16[48,2048]{1,0:T(8,128)(2,1)S(1)}, u32[]{:S(2)}, u32[]{:S(2)}) %collective-permute-start.21) | collective-permute-done | bytes 196640 | tf_op jit(solution)/shard_map/ppermute | solution.py:135
  111.9 1.8 %shard_map.133 = (f32[512,768]{1,0:T(8,128)}, f32[8,128]{1,0:T(8,128)}) custom-call(f32[8,128]{1,0:T(8,128)S(1)} %get-tuple-element.130.refs_0_, f32[512,768]{1,0:T(8,128)S(1)} %get-tuple-element.131.refs_1_, bf16[512,768]{1,0:T(8,128)(2,1)S(1)} %collective-permute-done.22.refs_2_), custom_call_target="tpu_custom_call" | custom-call | tf_op jit(solution)/shard_map/pallas_call | solution.py:120
  (50 shorter events, 17.1 us)
Async XLA Ops:
  0.6 0.7 copy-start
  3.2 15.3 %collective-permute-start.2 = (bf16[96,2176]{1,0:T(8,128)(2,1)S(1)}, bf16[96,2176]{1,0:T(8,128)(2,1)S(1)}, u32[]{:S(2)}, u32[]{:S(2)}) collective-permute-start(bf16[96,2176]{1,0:T(8,128)(2,1)S(1)} %get-tuple-element.72.refs_1_), channel_id=1, source_target_pairs={{0,1},{1,0},{2,3},{3,2},{4,5},{5,4},{6,7},{7,6},{8,9},{9,8},{10,11... | collective-permute-start | bytes 1253384 | tf_op jit(solution)/shard_map/ppermute | solution.py:135
  6.2 12.1 %collective-permute-start.1 = (bf16[48,2176]{1,0:T(8,128)(2,1)S(1)}, bf16[48,2176]{1,0:T(8,128)(2,1)S(1)}, u32[]{:S(2)}, u32[]{:S(2)}) collective-permute-start(bf16[48,2176]{1,0:T(8,128)(2,1)S(1)} %get-tuple-element.71.refs_3_), channel_id=1, source_target_pairs={{0,4},{1,5},{2,6},{3,7},{4,0},{5,1},{6,2},{7,3},{8,12},{9,13},{10,... | collective-permute-start | bytes 626696 | tf_op jit(solution)/shard_map/ppermute | solution.py:135
  8.8 9.7 %collective-permute-start = (bf16[48,2176]{1,0:T(8,128)(2,1)S(1)}, bf16[48,2176]{1,0:T(8,128)(2,1)S(1)}, u32[]{:S(2)}, u32[]{:S(2)}) collective-permute-start(bf16[48,2176]{1,0:T(8,128)(2,1)S(1)} %get-tuple-element.71.refs_3_), channel_id=1, source_target_pairs={{0,2},{1,3},{2,0},{3,1},{4,6},{5,7},{6,4},{7,5},{8,10},{9,11},{10,... | collective-permute-start | bytes 626696 | tf_op jit(solution)/shard_map/ppermute | solution.py:135
  18.6 11.4 %collective-permute-start.3 = (bf16[48,2176]{1,0:T(8,128)(2,1)S(1)}, bf16[48,2176]{1,0:T(8,128)(2,1)S(1)}, u32[]{:S(2)}, u32[]{:S(2)}) collective-permute-start(bf16[48,2176]{1,0:T(8,128)(2,1)S(1)} %get-tuple-element.76), channel_id=1, source_target_pairs={{0,2},{1,3},{2,0},{3,1},{4,6},{5,7},{6,4},{7,5},{8,10},{9,11},{10,... | collective-permute-start | bytes 626696 | tf_op jit(solution)/shard_map/ppermute | solution.py:135
  20.1 10.4 %collective-permute-start.5 = (bf16[48,2048]{1,0:T(8,128)(2,1)S(1)}, bf16[48,2048]{1,0:T(8,128)(2,1)S(1)}, u32[]{:S(2)}, u32[]{:S(2)}) collective-permute-start(bf16[48,2048]{1,0:T(8,128)(2,1)S(1)} %get-tuple-element.78.refs_2_), channel_id=1, source_target_pairs={{0,4},{1,5},{2,6},{3,7},{4,0},{5,1},{6,2},{7,3},{8,12},{9,13},{10,... | collective-permute-start | bytes 589832 | tf_op jit(solution)/shard_map/ppermute | solution.py:135
  22.4 10.5 %collective-permute-start.4 = (bf16[48,2048]{1,0:T(8,128)(2,1)S(1)}, bf16[48,2048]{1,0:T(8,128)(2,1)S(1)}, u32[]{:S(2)}, u32[]{:S(2)}) collective-permute-start(bf16[48,2048]{1,0:T(8,128)(2,1)S(1)} %get-tuple-element.78.refs_2_), channel_id=1, source_target_pairs={{0,2},{1,3},{2,0},{3,1},{4,6},{5,7},{6,4},{7,5},{8,10},{9,11},{10,... | collective-permute-start | bytes 589832 | tf_op jit(solution)/shard_map/ppermute | solution.py:135
  22.5 17.6 %collective-permute-start.8 = (bf16[96,2176]{1,0:T(8,128)(2,1)S(1)}, bf16[96,2176]{1,0:T(8,128)(2,1)S(1)}, u32[]{:S(2)}, u32[]{:S(2)}) collective-permute-start(bf16[96,2176]{1,0:T(8,128)(2,1)S(1)} %get-tuple-element.84.refs_4_), channel_id=1, source_target_pairs={{0,1},{1,0},{2,3},{3,2},{4,5},{5,4},{6,7},{7,6},{8,9},{9,8},{10,11... | collective-permute-start | bytes 1253384 | tf_op jit(solution)/shard_map/ppermute | solution.py:135
  30.0 9.6 %collective-permute-start.7 = (bf16[48,2176]{1,0:T(8,128)(2,1)S(1)}, bf16[48,2176]{1,0:T(8,128)(2,1)S(1)}, u32[]{:S(2)}, u32[]{:S(2)}) collective-permute-start(bf16[48,2176]{1,0:T(8,128)(2,1)S(1)} %get-tuple-element.82.refs_5_), channel_id=1, source_target_pairs={{0,1},{1,0},{2,3},{3,2},{4,5},{5,4},{6,7},{7,6},{8,9},{9,8},{10,11... | collective-permute-start | bytes 626696 | tf_op jit(solution)/shard_map/ppermute | solution.py:135
  32.9 5.7 %collective-permute-start.6 = (bf16[48,2048]{1,0:T(8,128)(2,1)S(1)}, bf16[48,2048]{1,0:T(8,128)(2,1)S(1)}, u32[]{:S(2)}, u32[]{:S(2)}) collective-permute-start(bf16[48,2048]{1,0:T(8,128)(2,1)S(1)} %get-tuple-element.81), channel_id=1, source_target_pairs={{0,2},{1,3},{2,0},{3,1},{4,6},{5,7},{6,4},{7,5},{8,10},{9,11},{10,... | collective-permute-start | bytes 589832 | tf_op jit(solution)/shard_map/ppermute | solution.py:135
  34.7 14.2 %collective-permute-start.9 = (bf16[96,2048]{1,0:T(8,128)(2,1)S(1)}, bf16[96,2048]{1,0:T(8,128)(2,1)S(1)}, u32[]{:S(2)}, u32[]{:S(2)}) collective-permute-start(bf16[96,2048]{1,0:T(8,128)(2,1)S(1)} %get-tuple-element.86.refs_3_), channel_id=1, source_target_pairs={{0,1},{1,0},{2,3},{3,2},{4,5},{5,4},{6,7},{7,6},{8,9},{9,8},{10,11... | collective-permute-start | bytes 1179656 | tf_op jit(solution)/shard_map/ppermute | solution.py:135
  39.6 11.0 %collective-permute-start.10 = (bf16[48,2048]{1,0:T(8,128)(2,1)S(1)}, bf16[48,2048]{1,0:T(8,128)(2,1)S(1)}, u32[]{:S(2)}, u32[]{:S(2)}) collective-permute-start(bf16[48,2048]{1,0:T(8,128)(2,1)S(1)} %get-tuple-element.87.refs_4_), channel_id=1, source_target_pairs={{0,1},{1,0},{2,3},{3,2},{4,5},{5,4},{6,7},{7,6},{8,9},{9,8},{10,11... | collective-permute-start | bytes 589832 | tf_op jit(solution)/shard_map/ppermute | solution.py:135
  51.6 4.1 %collective-permute-start.11 = (bf16[384,2048]{1,0:T(8,128)(2,1)S(1)}, bf16[384,2048]{1,0:T(8,128)(2,1)S(1)}, u32[]{:S(2)}, u32[]{:S(2)}) collective-permute-start(bf16[384,2048]{1,0:T(8,128)(2,1)S(1)} %get-tuple-element.95), channel_id=1, source_target_pairs={{0,8},{8,0},{16,24},{24,16},{1,9},{9,1},{17,25},{25,17},{2,10},{10... | collective-permute-start | bytes 4718600 | tf_op jit(solution)/shard_map/ppermute | solution.py:135
  55.0 9.6 %collective-permute-start.13 = (bf16[384,1536]{1,0:T(8,128)(2,1)S(1)}, bf16[384,1536]{1,0:T(8,128)(2,1)S(1)}, u32[]{:S(2)}, u32[]{:S(2)}) collective-permute-start(bf16[384,1536]{1,0:T(8,128)(2,1)S(1)} %get-tuple-element.97.refs_1_.refs_3_), channel_id=1, source_target_pairs={{0,8},{8,0},{16,24},{24,16},{1,9},{9,1},{17,25},{25,17},{2,10},{10... | collective-permute-start | bytes 3538952 | tf_op jit(solution)/shard_map/ppermute | solution.py:135
  55.6 9.0 %collective-permute-start.12 = (bf16[1024,384]{1,0:T(8,128)(2,1)S(1)}, bf16[1024,384]{1,0:T(8,128)(2,1)S(1)}, u32[]{:S(2)}, u32[]{:S(2)}) collective-permute-start(bf16[1024,384]{1,0:T(8,128)(2,1)S(1)} %get-tuple-element.100), channel_id=1, source_target_pairs={{0,8},{8,0},{16,24},{24,16},{1,9},{9,1},{17,25},{25,17},{2,10},{10... | collective-permute-start | bytes 2359304 | tf_op jit(solution)/shard_map/ppermute | solution.py:135
  55.9 20.4 %collective-permute-start.14 = (bf16[192,2048]{1,0:T(8,128)(2,1)S(1)}, bf16[192,2048]{1,0:T(8,128)(2,1)S(1)}, u32[]{:S(2)}, u32[]{:S(2)}) collective-permute-start(bf16[192,2048]{1,0:T(8,128)(2,1)S(1)} %get-tuple-element.103), channel_id=1, source_target_pairs={{0,16},{8,24},{16,0},{24,8},{1,17},{9,25},{17,1},{25,9},{2,18},{10... | collective-permute-start | bytes 2359304 | tf_op jit(solution)/shard_map/ppermute | solution.py:135
  57.4 21.7 %collective-permute-start.15 = (bf16[192,2048]{1,0:T(8,128)(2,1)S(1)}, bf16[192,2048]{1,0:T(8,128)(2,1)S(1)}, u32[]{:S(2)}, u32[]{:S(2)}) collective-permute-start(bf16[192,2048]{1,0:T(8,128)(2,1)S(1)} %get-tuple-element.108), channel_id=1, source_target_pairs={{0,2},{1,3},{2,0},{3,1},{4,6},{5,7},{6,4},{7,5},{8,10},{9,11},{10,... | collective-permute-start | bytes 2359304 | tf_op jit(solution)/shard_map/ppermute | solution.py:135
  64.0 20.5 %collective-permute-start.16 = (bf16[192,2048]{1,0:T(8,128)(2,1)S(1)}, bf16[192,2048]{1,0:T(8,128)(2,1)S(1)}, u32[]{:S(2)}, u32[]{:S(2)}) collective-permute-start(bf16[192,2048]{1,0:T(8,128)(2,1)S(1)} %get-tuple-element.111), channel_id=1, source_target_pairs={{0,1},{1,0},{2,3},{3,2},{4,5},{5,4},{6,7},{7,6},{8,9},{9,8},{10,11... | collective-permute-start | bytes 2359304 | tf_op jit(solution)/shard_map/ppermute | solution.py:135
  68.2 25.0 %collective-permute-start.18 = (bf16[512,768]{1,0:T(8,128)(2,1)S(1)}, bf16[512,768]{1,0:T(8,128)(2,1)S(1)}, u32[]{:S(2)}, u32[]{:S(2)}) collective-permute-start(bf16[512,768]{1,0:T(8,128)(2,1)S(1)} %get-tuple-element.117), channel_id=1, source_target_pairs={{0,16},{8,24},{16,0},{24,8},{1,17},{9,25},{17,1},{25,9},{2,18},{10... | collective-permute-start | bytes 2359304 | tf_op jit(solution)/shard_map/ppermute | solution.py:135
  77.5 34.4 %collective-permute-start.22 = (bf16[512,768]{1,0:T(8,128)(2,1)S(1)}, bf16[512,768]{1,0:T(8,128)(2,1)S(1)}, u32[]{:S(2)}, u32[]{:S(2)}) collective-permute-start(bf16[512,768]{1,0:T(8,128)(2,1)S(1)} %get-tuple-element.132), channel_id=1, source_target_pairs={{0,16},{8,24},{16,0},{24,8},{1,17},{9,25},{17,1},{25,9},{2,18},{10... | collective-permute-start | bytes 2359304 | tf_op jit(solution)/shard_map/ppermute | solution.py:135
  79.3 12.6 %collective-permute-start.17 = (bf16[96,2048]{1,0:T(8,128)(2,1)S(1)}, bf16[96,2048]{1,0:T(8,128)(2,1)S(1)}, u32[]{:S(2)}, u32[]{:S(2)}) collective-permute-start(bf16[96,2048]{1,0:T(8,128)(2,1)S(1)} %get-tuple-element.114), channel_id=1, source_target_pairs={{0,1},{1,0},{2,3},{3,2},{4,5},{5,4},{6,7},{7,6},{8,9},{9,8},{10,11... | collective-permute-start | bytes 1179656 | tf_op jit(solution)/shard_map/ppermute | solution.py:135
  84.7 9.7 %collective-permute-start.19 = (bf16[96,2048]{1,0:T(8,128)(2,1)S(1)}, bf16[96,2048]{1,0:T(8,128)(2,1)S(1)}, u32[]{:S(2)}, u32[]{:S(2)}) collective-permute-start(bf16[96,2048]{1,0:T(8,128)(2,1)S(1)} %get-tuple-element.120), channel_id=1, source_target_pairs={{0,2},{1,3},{2,0},{3,1},{4,6},{5,7},{6,4},{7,5},{8,10},{9,11},{10,... | collective-permute-start | bytes 1179656 | tf_op jit(solution)/shard_map/ppermute | solution.py:135
  91.9 15.1 %collective-permute-start.20 = (bf16[48,2048]{1,0:T(8,128)(2,1)S(1)}, bf16[48,2048]{1,0:T(8,128)(2,1)S(1)}, u32[]{:S(2)}, u32[]{:S(2)}) collective-permute-start(bf16[48,2048]{1,0:T(8,128)(2,1)S(1)} %get-tuple-element.123), channel_id=1, source_target_pairs={{0,4},{1,5},{2,6},{3,7},{4,0},{5,1},{6,2},{7,3},{8,12},{9,13},{10,... | collective-permute-start | bytes 589832 | tf_op jit(solution)/shard_map/ppermute | solution.py:135
  94.5 16.7 %collective-permute-start.21 = (bf16[48,2048]{1,0:T(8,128)(2,1)S(1)}, bf16[48,2048]{1,0:T(8,128)(2,1)S(1)}, u32[]{:S(2)}, u32[]{:S(2)}) collective-permute-start(bf16[48,2048]{1,0:T(8,128)(2,1)S(1)} %get-tuple-element.127), channel_id=1, source_target_pairs={{0,4},{1,5},{2,6},{3,7},{4,0},{5,1},{6,2},{7,3},{8,12},{9,13},{10,... | collective-permute-start | bytes 589832 | tf_op jit(solution)/shard_map/ppermute | solution.py:135
  (1 other events, 0.7 us)

commit v4 on v3

--- a/solution.py
+++ b/solution.py
@@ -104,6 +104,7 @@
 
 BF16, F32 = jnp.bfloat16, jnp.float32
 VMEM, SMEM, HBM, ANY = pltpu.VMEM, pltpu.SMEM, pltpu.HBM, pl.ANY
+PINNED = "pinned"
 ORDER = ((8, 128), jnp.float32, pltpu.VMEM)
 
 
@@ -116,17 +117,25 @@
         body(*refs[skipped : given + len(outs)], *refs[given + len(outs) + 1 :])
         token[...] = jnp.zeros(token.shape, token.dtype)
 
-    outs_all = list(outs) + [ORDER]
+    outs_all = [(shape, dtype, VMEM if m == PINNED else m) for shape, dtype, m in outs] + [ORDER]
+    shapes = [
+        pltpu.VMEM(shape, dtype) if m == PINNED else jax.ShapeDtypeStruct(shape, dtype)
+        for shape, dtype, m in [*outs, ORDER]
+    ]
+    fixed = {HBM: HBM, PINNED: VMEM}
     outputs = pl.pallas_call(
         kernel,
-        in_specs=[pl.BlockSpec(memory_space=m) for m in [ANY] * skipped + [m for _, m in ins]],
+        in_specs=[
+            pl.BlockSpec(memory_space=VMEM if m == PINNED else m)
+            for m in [ANY] * skipped + [m for _, m in ins]
+        ],
         out_specs=[pl.BlockSpec(memory_space=m) for _, _, m in outs_all],
-        out_shape=[jax.ShapeDtypeStruct(shape, dtype) for shape, dtype, _ in outs_all],
+        out_shape=shapes,
         scratch_shapes=list(scratch),
         input_output_aliases={skipped + i: o for i, o in (aliases or {}).items()},
         cost_estimate=pl.CostEstimate(flops=0, bytes_accessed=0, transcendentals=0),
         compiler_params=pltpu.CompilerParams(vmem_limit_bytes=vmem * 2**20),
-    )(*after, *[pltpu.with_memory_space_constraint(a, HBM) if m is HBM else a for a, m in ins])
+    )(*after, *[pltpu.with_memory_space_constraint(a, fixed[m]) if m in fixed else a for a, m in ins])
     return list(outputs)
 
 
@@ -143,14 +152,20 @@
     count, width = tokens.shape
     top = expert_ids.shape[1]
 
-    def body(tok, ids, given, cot, alone, both, sems):
+    def body(tok, ids_far, given_far, cot, alone, both, ids, given, sems):
         copies = [
             pltpu.make_async_copy(tok, alone.at[:, :width], sems.at[0]),
             pltpu.make_async_copy(tok, both.at[:count, :width], sems.at[1]),
             pltpu.make_async_copy(cot, both.at[count:, :width], sems.at[2]),
         ]
-        for copy in copies:
+        small = [
+            pltpu.make_async_copy(ids_far, ids, sems.at[3]),
+            pltpu.make_async_copy(given_far, given, sems.at[4]),
+        ]
+        for copy in small + copies:
             copy.start()
+        for copy in small:
+            copy.wait()
         names = ids[...].T
         values = given[...].T
         column = lax.broadcasted_iota(jnp.int32, (count, lanes), 1)
@@ -168,14 +183,18 @@
 
     return stage(
         body,
-        [(tokens, HBM), (expert_ids.T, VMEM), (gate_probs.T, VMEM), (out_cot, HBM)],
+        [(a, HBM) for a in (tokens, expert_ids.T, gate_probs.T, out_cot)],
         [((count, width + lanes), BF16, VMEM), ((2 * count, width + lanes), BF16, VMEM)],
-        scratch=[pltpu.SemaphoreType.DMA((3,))],
+        scratch=[
+            VMEM((top, count), jnp.int32),
+            VMEM((top, count), F32),
+            pltpu.SemaphoreType.DMA((5,)),
+        ],
             )
 
 
 def products(places, left, right, outs, own, tile=512):
-    size = left.shape[0] // (1 + max(p | 1 for p in places))
+    size = left.shape[0] // 4
     width = right.shape[1]
     for start, some in chunks(width, tile):
         piece = right[:, start : start + some]
@@ -200,8 +219,7 @@
     half = total // 2
     pair = half // 2
     lanes = 128 * (-(-2 * experts // 128))
-    odd_places = list(range(owners - 1, 0, -2))
-    even_places = [m - 1 for m in odd_places]
+    odd_places, even_places = [3, 1], [2, 0]
     slab, band = ff // owners, width // owners
 
     near_bit, far_bit = 2, 4
@@ -258,10 +276,10 @@
     def forward(me_ref, mine_ref, *refs):
         blocks = refs[: len(tok_arrays)]
         weights = refs[len(tok_arrays) : len(tok_arrays) + 3]
-        flipped, flipped_sent, hidden_t, gate_by, up_by, kept, sent = refs[
-            len(tok_arrays) + 3 : len(tok_arrays) + 10
+        flipped, flipped_sent, hidden_t, gate_by, up_by, kept, sent, gate, up, down = refs[
+            len(tok_arrays) + 3 : len(tok_arrays) + 13
         ]
-        rows, probs, hidden, gate, up, down, sems = refs[len(tok_arrays) + 10 :]
+        rows, probs, hidden, sems = refs[len(tok_arrays) + 13 :]
         steps = chunks(ff, 256)
         copies = []
         for i, (start, size) in enumerate(steps):
@@ -303,12 +321,13 @@
         for start, size in chunks(width, 512):
             place = slice(start, start + size)
             part = jnp.dot(hidden[...], down[:, place], preferred_element_type=F32).astype(BF16)
-            for i in range(2):
-                low, high = slice(i * pair, (i + 1) * pair), i * half
-                kept[low, place] = part[high : high + pair]
-                sent[low, place] = part[high + pair : high + half]
-
-    flipped, flipped_sent, hidden_t, gate_by, up_by, out_kept, out_sent, done = stage(
+            kept[:, place] = part[:half]
+            sent[:, place] = part[half:]
+
+    (
+        flipped, flipped_sent, hidden_t, gate_by, up_by, out_kept, out_sent,
+        gate_near, up_near, down_near, done,
+    ) = stage(
         forward,
         [(me, SMEM), (mine, SMEM)] + [(a, VMEM) for a in tok_arrays] + [(w[0], HBM) for w in (w_gate, w_up, w_down)],
         [
@@ -319,163 +338,164 @@
             ((total, ff), F32, VMEM),
             ((half, width), BF16, VMEM),
             ((half, width), BF16, VMEM),
+            ((width, ff), BF16, VMEM),
+            ((width, ff), BF16, VMEM),
+            ((ff, width), BF16, VMEM),
         ],
         scratch=[
             VMEM((total, width), BF16),
             VMEM((total, 1), F32),
             VMEM((total, ff), BF16),
-            VMEM((width, ff), BF16),
-            VMEM((width, ff), BF16),
-            VMEM((ff, width), BF16),
             pltpu.SemaphoreType.DMA((2 * len(chunks(ff, 256)) + 1,)),
         ],
         after=[done],
-        vmem=16,
-    )
-    flipped_came = swap(flipped_sent, "dp", 1)
+        vmem=8,
+    )
+
     cot_arrays, cot_where = refs_of(cot_pieces)
 
-    def down_odd(own_ref, *refs):
+    def down_first(own_ref, *refs):
         blocks = refs[: len(cot_arrays)]
-        left, rows, away = refs[len(cot_arrays) :]
+        left, _, rows, away, _ = refs[len(cot_arrays) :]
         for b, (i, row) in enumerate(cot_where):
             rows[b * count : (b + 1) * count, :] = blocks[i][row : row + count, :width]
-        outs = [(away, i * slab) for i in range(len(odd_places))]
-        products(odd_places, left, rows, outs, own_ref[0])
-
-    cot_rows, down_away, done = stage(
-        down_odd,
-        [(mine, SMEM)] + [(a, VMEM) for a in cot_arrays] + [(hidden_t, VMEM)],
-        [((total, width), BF16, VMEM), ((slab * len(odd_places), width), BF16, VMEM)],
-        after=[done],
+        products([3], left, rows, [(away, 0)], own_ref[0])
+
+    cot_rows, down_away, flipped_sent, done = stage(
+        down_first,
+        [(mine, SMEM)] + [(a, VMEM) for a in [*cot_arrays, hidden_t]] + [(flipped_sent, ANY)],
+        [
+            ((total, width), BF16, VMEM),
+            ((slab, width), BF16, VMEM),
+            (flipped_sent.shape, BF16, ANY),
+        ],
+        after=[done],
+        aliases={len(cot_arrays) + 2: 2},
     )
     down_came = swap(down_away, "dp", 1)
-    out_came = swap(out_sent, "expert", near_bit)
-
-    def backward(own_ref, cot, left, down, gate_ref, up_ref, grads, *refs):
-        *kept, near, sem = refs
-        copy = pltpu.make_async_copy(down, near, sem)
-        copy.start()
-        products(even_places, left, cot, [(k, 0) for k in kept], own_ref[0])
-        copy.wait()
+    flipped_came = swap(flipped_sent, "dp", 1)
+
+    def down_rest(own_ref, left, cot, away, send, kept):
+        products([1, 2, 0], left, cot, [(away, 0), (send, 0), (kept, 0)], own_ref[0])
+
+    last_away, down_send, down_kept, done = stage(
+        down_rest,
+        [(mine, SMEM), (hidden_t, VMEM), (cot_rows, VMEM)],
+        [((slab, width), BF16, VMEM)] * 3,
+        after=[done],
+    )
+    last_came = swap(last_away, "dp", 1)
+    out_came = swap(out_sent, "expert", 1)
+
+    def backward(cot, down, gate_ref, up_ref, grads):
         for start, size in chunks(ff, 256):
             place = slice(start, start + size)
-            grad = lax.dot_general(cot[...], near[place, :], TURNED, preferred_element_type=F32)
+            grad = lax.dot_general(cot[...], down[place, :], TURNED, preferred_element_type=F32)
             grads[:, place] = (grad * gate_ref[:, place]).astype(BF16)
             grads[:, ff + start : ff + start + size] = (grad * up_ref[:, place]).astype(BF16)
 
-    grads, *down_kept, done = stage(
+    grads, done = stage(
         backward,
-        [(mine, SMEM), (cot_rows, VMEM), (hidden_t, VMEM), (w_down[0], HBM)]
-        + [(gate_by, VMEM), (up_by, VMEM)],
-        [((total, 2 * ff), BF16, VMEM)] + [((slab, width), BF16, VMEM)] * len(even_places),
-        scratch=[VMEM((ff, width), BF16), pltpu.SemaphoreType.DMA],
-        after=[done],
-    )
-
+        [(a, VMEM) for a in (cot_rows, down_near, gate_by, up_by)],
+        [((total, 2 * ff), BF16, VMEM)],
+        after=[done],
+    )
     grads_came = swap(grads, "dp", 1)
 
-    def added(kept, came, after=()):
-        n, size = len(kept), kept[0].shape[0]
-
-        def body(*refs):
-            for i in range(n):
-                other = refs[n][i * size : (i + 1) * size, :].astype(F32)
-                refs[n + 1 + i][...] = (refs[i][...].astype(F32) + other).astype(BF16)
-
-        return stage(
-            body,
-            [(a, VMEM) for a in [*kept, came]],
-            [(a.shape, BF16, VMEM) for a in kept],
-            after=after,
-        )
-
-    *down_send, done = added(down_kept[:-1], down_came, [done])
-    down_got = [swap(a, "dp", m) for a, m in zip(down_send, even_places)]
-
-    def input_rows(grad, gate_far, up_far, even, odd, gate, up, sems):
-        steps = chunks(width, 512)
-        copies = []
-        for i, (start, size) in enumerate(steps):
+    def added(kept, came, _, send):
+        send[...] = (kept[...].astype(F32) + came[...].astype(F32)).astype(BF16)
+
+    down_send, done = stage(
+        added,
+        [(down_send, VMEM), (down_came, VMEM), (flipped_came, ANY)],
+        [((slab, width), BF16, VMEM)],
+        after=[done],
+    )
+    down_got = swap(down_send, "dp", 2)
+
+    def input_rows(grad, gate, up, kept, sent):
+        for start, size in chunks(width, 512):
             place = slice(start, start + size)
-            for j, (far_ref, near_ref) in enumerate([(gate_far, gate), (up_far, up)]):
-                copies.append(
-                    pltpu.make_async_copy(far_ref.at[place], near_ref.at[place], sems.at[2 * i + j])
-                )
-        for copy in copies:
-            copy.start()
-        for i, (start, size) in enumerate(steps):
-            place = slice(start, start + size)
-            copies[2 * i].wait()
             rows = lax.dot_general(grad[:, :ff], gate[place, :], TURNED, preferred_element_type=F32)
-            copies[2 * i + 1].wait()
             rows = rows + lax.dot_general(
                 grad[:, ff:], up[place, :], TURNED, preferred_element_type=F32
             )
             rows = rows.astype(BF16)
-            even[:, place] = rows[:half]
-            odd[:, place] = rows[half:]
-
-    in_even, in_odd, done = stage(
+            for i in range(2):
+                low, high = slice(i * pair, (i + 1) * pair), i * half
+                kept[low, place] = rows[high : high + pair]
+                sent[low, place] = rows[high + pair : high + half]
+
+    in_kept, in_sent, done = stage(
         input_rows,
-        [(grads, VMEM), (w_gate[0], HBM), (w_up[0], HBM)],
+        [(grads, VMEM), (gate_near, VMEM), (up_near, VMEM)],
         [((half, width), BF16, VMEM)] * 2,
-        scratch=[VMEM((width, ff), BF16)] * 2
-        + [pltpu.SemaphoreType.DMA((2 * len(chunks(width, 512)),))],
-        after=[done],
-        vmem=10,
-    )
-    in_came = swap(in_odd, "expert", 1)
-
-    def both_parts(left, left_came, grad, grad_came, *outs):
-        n = len(even_places)
-        for i in range(n):
-            place = slice(i * band, (i + 1) * band)
+        after=[done],
+    )
+    in_came = swap(in_sent, "expert", near_bit)
+
+    def both_parts(left, left_came, grad, grad_came, _, gate_send, up_high, up_low, gate_kept, up_kept):
+        for j, (gate_out, up_out) in enumerate([(gate_send, None), (gate_kept, up_kept)]):
+            row = slice(j * band, (j + 1) * band)
             for start, size in chunks(2 * ff, 256):
                 column = slice(start, start + size)
-                value = jnp.dot(left[place, :], grad[:, column], preferred_element_type=F32)
-                value += jnp.dot(left_came[place, :], grad_came[:, column], preferred_element_type=F32)
-                out = outs[2 * i + start // ff]
-                out[:, start % ff : start % ff + size] = value.astype(out.dtype)
-
-    *both_kept, done = stage(
+                value = jnp.dot(left[row, :], grad[:, column], preferred_element_type=F32)
+                value += jnp.dot(left_came[row, :], grad_came[:, column], preferred_element_type=F32)
+                place = slice(start % ff, start % ff + size)
+                if start < ff:
+                    gate_out[:, place] = value.astype(gate_out.dtype)
+                elif up_out is not None:
+                    up_out[:, place] = value.astype(up_out.dtype)
+                else:
+                    up_high[:, place] = value[: band // 2].astype(BF16)
+                    up_low[:, place] = value[band // 2 :].astype(BF16)
+
+    gate_send, up_high, up_low, gate_kept, up_kept, done = stage(
         both_parts,
-        [(a, VMEM) for a in (flipped, flipped_came, grads, grads_came)],
-        [((band, ff), BF16, VMEM)] * (2 * len(even_places) - 2) + [((band, ff), F32, VMEM)] * 2,
-        after=[done],
-    )
-    gate_sums, up_sums = both_kept[0::2], both_kept[1::2]
-    gate_got = [swap(a, "dp", m) for a, m in zip(gate_sums[:-1], even_places)]
-
-    def folded(held, came, after):
+        [(a, VMEM) for a in (flipped, flipped_came, grads, grads_came)] + [(last_came, ANY)],
+        [((band, ff), BF16, VMEM)]
+        + [((band // 2, ff), BF16, VMEM)] * 2
+        + [((band, ff), F32, VMEM)] * 2,
+        after=[done],
+    )
+    gate_got = swap(gate_send, "dp", 2)
+    up_got = [swap(a, "dp", 2) for a in (up_high, up_low)]
+
+    def folded(held, came, after, waits=()):
         rows = held.shape[0]
         parts = 1 if rows == count else 2
 
-        def body(a, b, *outs):
-            for i, out in enumerate(outs):
+        def body(a, b, *refs):
+            for i, out in enumerate(refs[len(waits) :]):
                 place = slice(i * rows // parts, (i + 1) * rows // parts)
                 out[...] = (a[place, :].astype(F32) + b[place, :].astype(F32)).astype(BF16)
 
         return stage(
             body,
-            [(held, VMEM), (came, VMEM)],
+            [(held, VMEM), (came, VMEM)] + [(a, ANY) for a in waits],
             [((rows // parts, width), BF16, VMEM)] * parts,
             after=after,
         )
 
     def owned(parts, after):
-        size, wide = parts[-1].shape
+        size = sum(a.shape[0] for a in parts[0])
+        wide = parts[0][0].shape[1]
         step = size // 4
+        where = []
+        for arrays in parts:
+            first = len([i for w in where for i in w])
+            where.append(range(first, first + len(arrays)))
 
         def body(*refs):
-            *others, out, total, sems = refs
+            ins, (out, total, sems) = refs[:-3], refs[-3:]
             copies = []
             for i in range(4):
                 at = slice(i * step, (i + 1) * step)
                 value = jnp.zeros((step, wide), F32)
-                for ref in others:
-                    first = ref.shape[0] - size + i * step
-                    value = value + ref[first : first + step, :].astype(F32)
+                for places in where:
+                    each = size // len(places)
+                    ref, row = ins[places[i * step // each]], i * step % each
+                    value = value + ref[row : row + step, :].astype(F32)
                 total[at, :] = value
                 copies.append(pltpu.make_async_copy(total.at[at], out.at[at], sems.at[i]))
                 copies[-1].start()
@@ -484,38 +504,31 @@
 
         return stage(
             body,
-            [(a, VMEM) for a in parts],
+            [(a, VMEM) for arrays in parts for a in arrays],
             [((size, wide), F32, HBM)],
             scratch=[VMEM((size, wide), F32), pltpu.SemaphoreType.DMA((4,))],
             after=after,
         )
 
-    def fold_on(held, came, bit, after):
-        held, send, done = folded(held, came, after)
+    def fold_on(held, came, bit, after, waits=()):
+        held, send, done = folded(held, came, after, waits)
         return held, swap(send, "expert", bit), done
 
-    down_grad, done = owned([down_kept[-1], down_came, *down_got], [done])
-    up_send = []
-    for a in up_sums[:-1]:
-        a, done = stage(
-            lambda *_: None, [(a, ANY)], [(a.shape, BF16, ANY)], after=[done], aliases={0: 0}
-        )
-        up_send.append(a)
-    up_got = [swap(a, "dp", m) for a, m in zip(up_send, even_places)]
-    out_held, out_came, done = fold_on(out_kept, out_came, 1, [done])
-    in_held, in_came, done = fold_on(in_even, in_came, near_bit, [done])
+    out_held, out_came, done = fold_on(out_kept, out_came, near_bit, [done])
+    down_grad, done = owned([[down_kept], [last_came], [down_got]], [done])
+    in_held, in_came, done = fold_on(in_kept, in_came, 1, [done])
     out_held, out_came, done = fold_on(out_held, out_came, far_bit, [done])
-    gate_part, done = owned([gate_sums[-1], *gate_got], [done])
     in_held, in_came, done = fold_on(in_held, in_came, far_bit, [done])
     layer_out, done = folded(out_held, out_came, [done])
+    gate_part, done = owned([[gate_kept], [gate_got]], [done])
     input_grad, done = folded(in_held, in_came, [done])
-    up_part, _ = owned([up_sums[-1], *up_got], [done])
+    up_part, _ = owned([[up_kept], up_got], [done])
     return (layer_out, input_grad, gate_part[None], up_part[None], down_grad[None])
 
 
 def shards(tokens, expert_ids, *rest):
     experts = lax.axis_size("expert")
-    every = expert_ids.shape[1] == experts and experts == 8
+    every = expert_ids.shape[1] == experts and experts == 8 and lax.axis_size("dp") == 4
     return (dense if every else routed)(tokens, expert_ids, *rest)
 
 

time: 114 us -> 110 us (0.965)
  starting transfers between devices: 25.6 us -> 29.9 us
  waiting for transfers between devices: 56.6 us -> 52.4 us
  Pallas kernels: 29.3 us -> 26.4 us
  local copies, waits for them, and re-layouts: 1.37 us -> 0 us
    ppermute x23 -> x25, starting transfers between devices: 25.6 us -> 29.9 us  [swap(): return lax.ppermute(value, axis, [(i, i ^ mask) for i in range(size)])]
    ppermute x23 -> x25, waiting for transfers between devices: 56.6 us -> 52.4 us  [swap(): return lax.ppermute(value, axis, [(i, i ^ mask) for i in range(size)])]
    pallas_call x24, Pallas kernels: 29.3 us -> 26.4 us  [stage(): pl.pallas_call(kernel, in_specs=[pl.BlockSpec(memory_space=VMEM if m == P...]
    unnamed x4 -> x0, local copies, waits for them, and re-layouts: 1.37 us -> none
  transfers between devices with their start and end apart: 23 -> 25, of which waited for: 12 -> 13; matrix products, arithmetic and copies ran while one was open for 0% -> 0% of each run, Pallas kernels for 22% -> 21%
where the time goes in v4:
time: 110 us
  waiting for transfers between devices  52.4 us (48%)
  starting transfers between devices  29.9 us (27%)
  Pallas kernels  26.4 us (24%)
    ppermute x25, waiting for transfers between devices, swap(): return lax.ppermute(value, axis, [(i, i ^ mask) for i in range(size)])  52.4 us
    ppermute x25, starting transfers between devices, swap(): return lax.ppermute(value, axis, [(i, i ^ mask) for i in range(size)])  29.9 us
    pallas_call x24, Pallas kernels, stage(): pl.pallas_call(kernel, in_specs=[pl.BlockSpec(memory_space=VMEM if m == P...  26.4 us
  transfers between devices with their start and end apart: 25, of which 13 were waited for; matrix products, arithmetic and copies ran while one was open for 0% of the time, Pallas kernels for 21%

profile of v4, /device:TPU:0, one launch (start us, length us, event | category | flops | bytes accessed | tf_op | source)
XLA Modules:
  0.0 109.6 jit_solution(6465375991563382702)
XLA Ops:
  1.8 3.0 %collective-permute-start.2 = (bf16[96,2176]{1,0:T(8,128)(2,1)S(1)}, bf16[96,2176]{1,0:T(8,128)(2,1)S(1)}, u32[]{:S(2)}, u32[]{:S(2)}) collective-permute-start(bf16[96,2176]{1,0:T(8,128)(2,1)S(1)} %get-tuple-element.77.refs_1_), channel_id=1, source_target_pairs={{0,1},{1,0},{2,3},{3,2},{4,5},{5,4},{6,7},{7,6},{8,9},{9,8},{10,11... | collective-permute-start | bytes 1253384 | tf_op jit(solution)/shard_map/ppermute | solution.py:144
  4.9 2.6 %collective-permute-start.1 = (bf16[48,2176]{1,0:T(8,128)(2,1)S(1)}, bf16[48,2176]{1,0:T(8,128)(2,1)S(1)}, u32[]{:S(2)}, u32[]{:S(2)}) collective-permute-start(bf16[48,2176]{1,0:T(8,128)(2,1)S(1)} %get-tuple-element.76.refs_3_), channel_id=1, source_target_pairs={{0,4},{1,5},{2,6},{3,7},{4,0},{5,1},{6,2},{7,3},{8,12},{9,13},{10,... | collective-permute-start | bytes 626696 | tf_op jit(solution)/shard_map/ppermute | solution.py:144
  7.5 1.6 %collective-permute-start = (bf16[48,2176]{1,0:T(8,128)(2,1)S(1)}, bf16[48,2176]{1,0:T(8,128)(2,1)S(1)}, u32[]{:S(2)}, u32[]{:S(2)}) collective-permute-start(bf16[48,2176]{1,0:T(8,128)(2,1)S(1)} %get-tuple-element.76.refs_3_), channel_id=1, source_target_pairs={{0,2},{1,3},{2,0},{3,1},{4,6},{5,7},{6,4},{7,5},{8,10},{9,11},{10,... | collective-permute-start | bytes 626696 | tf_op jit(solution)/shard_map/ppermute | solution.py:144
  9.0 7.9 %collective-permute-done.1.refs_2_.refs_1_ = bf16[48,2176]{1,0:T(8,128)(2,1)S(1)} collective-permute-done((bf16[48,2176]{1,0:T(8,128)(2,1)S(1)}, bf16[48,2176]{1,0:T(8,128)(2,1)S(1)}, u32[]{:S(2)}, u32[]{:S(2)}) %collective-permute-start.1) | collective-permute-done | bytes 208928 | tf_op jit(solution)/shard_map/ppermute | solution.py:144
  18.8 2.3 %collective-permute-start.5 = (bf16[48,2048]{1,0:T(8,128)(2,1)S(1)}, bf16[48,2048]{1,0:T(8,128)(2,1)S(1)}, u32[]{:S(2)}, u32[]{:S(2)}) collective-permute-start(bf16[48,2048]{1,0:T(8,128)(2,1)S(1)} %get-tuple-element.83.refs_2_), channel_id=1, source_target_pairs={{0,4},{1,5},{2,6},{3,7},{4,0},{5,1},{6,2},{7,3},{8,12},{9,13},{10,... | collective-permute-start | bytes 589832 | tf_op jit(solution)/shard_map/ppermute | solution.py:144
  21.7 7.0 %collective-permute-done.3.refs_1_ = bf16[48,2176]{1,0:T(8,128)(2,1)S(1)} collective-permute-done((bf16[48,2176]{1,0:T(8,128)(2,1)S(1)}, bf16[48,2176]{1,0:T(8,128)(2,1)S(1)}, u32[]{:S(2)}, u32[]{:S(2)}) %collective-permute-start.3) | collective-permute-done | bytes 208928 | tf_op jit(solution)/shard_map/ppermute | solution.py:144
  29.1 2.4 %collective-permute-done.4.refs_1_ = bf16[48,2048]{1,0:T(8,128)(2,1)S(1)} collective-permute-done((bf16[48,2048]{1,0:T(8,128)(2,1)S(1)}, bf16[48,2048]{1,0:T(8,128)(2,1)S(1)}, u32[]{:S(2)}, u32[]{:S(2)}) %collective-permute-start.4) | collective-permute-done | bytes 196640 | tf_op jit(solution)/shard_map/ppermute | solution.py:144
  31.6 1.8 %collective-permute-start.6 = (bf16[48,2048]{1,0:T(8,128)(2,1)S(1)}, bf16[48,2048]{1,0:T(8,128)(2,1)S(1)}, u32[]{:S(2)}, u32[]{:S(2)}) collective-permute-start(bf16[48,2048]{1,0:T(8,128)(2,1)S(1)} %get-tuple-element.86), channel_id=1, source_target_pairs={{0,2},{1,3},{2,0},{3,1},{4,6},{5,7},{6,4},{7,5},{8,10},{9,11},{10,... | collective-permute-start | bytes 589832 | tf_op jit(solution)/shard_map/ppermute | solution.py:144
  33.9 3.5 %collective-permute-done.6.refs_1_ = bf16[48,2048]{1,0:T(8,128)(2,1)S(1)} collective-permute-done((bf16[48,2048]{1,0:T(8,128)(2,1)S(1)}, bf16[48,2048]{1,0:T(8,128)(2,1)S(1)}, u32[]{:S(2)}, u32[]{:S(2)}) %collective-permute-start.6) | collective-permute-done | bytes 196640 | tf_op jit(solution)/shard_map/ppermute | solution.py:144
  38.8 9.0 %shard_map.118 = (bf16[1024,384]{1,0:T(8,128)(2,1)S(1)}, bf16[1024,384]{1,0:T(8,128)(2,1)S(1)}, bf16[768,384]{1,0:T(8,128)(2,1)S(1)}, f32[384,768]{1,0:T(8,128)S...) custom-call(f32[8,128]{1,0:T(8,128)S(1)} %get-tuple-element.88.refs_, ...), custom_call_target="tpu_custom_call" | custom-call | tf_op jit(solution)/shard_map/pallas_call | solution.py:126
  54.6 1.6 %collective-permute-start.16 = (bf16[192,2048]{1,0:T(8,128)(2,1)S(1)}, bf16[192,2048]{1,0:T(8,128)(2,1)S(1)}, u32[]{:S(2)}, u32[]{:S(2)}) collective-permute-start(bf16[192,2048]{1,0:T(8,128)(2,1)S(1)} %get-tuple-element.117), channel_id=1, source_target_pairs={{0,16},{8,24},{16,0},{24,8},{1,17},{9,25},{17,1},{25,9},{2,18},{10... | collective-permute-start | bytes 2359304 | tf_op jit(solution)/shard_map/ppermute | solution.py:144
  56.1 2.6 %shard_map.123 = (bf16[192,2048]{1,0:T(8,128)(2,1)S(1)}, bf16[192,2048]{1,0:T(8,128)(2,1)S(1)}, f32[8,128]{1,0:T(8,128)S(1)}) custom-call(f32[8,128]{1,0:T(8,128)S(1)} %get-tuple-element.105.refs_0_, bf16[384,1536]{1,0:T(8,128)(2,1)S(1)} %get-tuple-element.106.refs_1_.refs_3_, bf16[2048,768]{1,0:T(8,128)(2,1)S(1)} %get-tuple-element.107.refs_2_, ...), custom_call_target="tpu_custom_call" | custom-call | tf_op jit(solution)/shard_map/pallas_call | solution.py:126
  58.8 1.7 %collective-permute-start.17 = (bf16[192,2048]{1,0:T(8,128)(2,1)S(1)}, bf16[192,2048]{1,0:T(8,128)(2,1)S(1)}, u32[]{:S(2)}, u32[]{:S(2)}) collective-permute-start(bf16[192,2048]{1,0:T(8,128)(2,1)S(1)} %get-tuple-element.120), channel_id=1, source_target_pairs={{0,2},{1,3},{2,0},{3,1},{4,6},{5,7},{6,4},{7,5},{8,10},{9,11},{10,... | collective-permute-start | bytes 2359304 | tf_op jit(solution)/shard_map/ppermute | solution.py:144
  60.5 3.6 %shard_map.124 = (bf16[512,768]{1,0:T(8,128)(2,1)S(1)}, bf16[256,768]{1,0:T(8,128)(2,1)S(1)}, bf16[256,768]{1,0:T(8,128)(2,1)S(1)}, f32[512,768]{1,0:T(8,128)S(1...) custom-call(f32[8,128]{1,0:T(8,128)S(1)} %get-tuple-element.109.refs_0_, ...), custom_call_target="tpu_custom_call" | custom-call | tf_op jit(solution)/shard_map/pallas_call | solution.py:126
  64.7 8.7 %collective-permute-done.15.refs_2_ = bf16[192,2048]{1,0:T(8,128)(2,1)S(1)} collective-permute-done((bf16[192,2048]{1,0:T(8,128)(2,1)S(1)}, bf16[192,2048]{1,0:T(8,128)(2,1)S(1)}, u32[]{:S(2)}, u32[]{:S(2)}) %collective-permute-start.15) | collective-permute-done | bytes 786464 | tf_op jit(solution)/shard_map/ppermute | solution.py:144
  73.6 1.7 %collective-permute-start.18 = (bf16[96,2048]{1,0:T(8,128)(2,1)S(1)}, bf16[96,2048]{1,0:T(8,128)(2,1)S(1)}, u32[]{:S(2)}, u32[]{:S(2)}) collective-permute-start(bf16[96,2048]{1,0:T(8,128)(2,1)S(1)} %get-tuple-element.123), channel_id=1, source_target_pairs={{0,2},{1,3},{2,0},{3,1},{4,6},{5,7},{6,4},{7,5},{8,10},{9,11},{10,... | collective-permute-start | bytes 1179656 | tf_op jit(solution)/shard_map/ppermute | solution.py:144
  76.6 2.7 %collective-permute-done.17.refs_2_ = bf16[192,2048]{1,0:T(8,128)(2,1)S(1)} collective-permute-done((bf16[192,2048]{1,0:T(8,128)(2,1)S(1)}, bf16[192,2048]{1,0:T(8,128)(2,1)S(1)}, u32[]{:S(2)}, u32[]{:S(2)}) %collective-permute-start.17) | collective-permute-done | bytes 786464 | tf_op jit(solution)/shard_map/ppermute | solution.py:144
  79.5 1.6 %collective-permute-start.19 = (bf16[96,2048]{1,0:T(8,128)(2,1)S(1)}, bf16[96,2048]{1,0:T(8,128)(2,1)S(1)}, u32[]{:S(2)}, u32[]{:S(2)}) collective-permute-start(bf16[96,2048]{1,0:T(8,128)(2,1)S(1)} %get-tuple-element.126), channel_id=1, source_target_pairs={{0,1},{1,0},{2,3},{3,2},{4,5},{5,4},{6,7},{7,6},{8,9},{9,8},{10,11... | collective-permute-start | bytes 1179656 | tf_op jit(solution)/shard_map/ppermute | solution.py:144
  81.6 1.5 %collective-permute-start.24 = (bf16[256,768]{1,0:T(8,128)(2,1)S(1)}, bf16[256,768]{1,0:T(8,128)(2,1)S(1)}, u32[]{:S(2)}, u32[]{:S(2)}) collective-permute-start(bf16[256,768]{1,0:T(8,128)(2,1)S(1)} %get-tuple-element.142), channel_id=1, source_target_pairs={{0,16},{8,24},{16,0},{24,8},{1,17},{9,25},{17,1},{25,9},{2,18},{10... | collective-permute-start | bytes 1179656 | tf_op jit(solution)/shard_map/ppermute | solution.py:144
  83.1 3.1 %collective-permute-done.18.refs_2_ = bf16[96,2048]{1,0:T(8,128)(2,1)S(1)} collective-permute-done((bf16[96,2048]{1,0:T(8,128)(2,1)S(1)}, bf16[96,2048]{1,0:T(8,128)(2,1)S(1)}, u32[]{:S(2)}, u32[]{:S(2)}) %collective-permute-start.18) | collective-permute-done | bytes 393248 | tf_op jit(solution)/shard_map/ppermute | solution.py:144
  86.3 2.7 %collective-permute-start.20 = (bf16[48,2048]{1,0:T(8,128)(2,1)S(1)}, bf16[48,2048]{1,0:T(8,128)(2,1)S(1)}, u32[]{:S(2)}, u32[]{:S(2)}) collective-permute-start(bf16[48,2048]{1,0:T(8,128)(2,1)S(1)} %get-tuple-element.129), channel_id=1, source_target_pairs={{0,4},{1,5},{2,6},{3,7},{4,0},{5,1},{6,2},{7,3},{8,12},{9,13},{10,... | collective-permute-start | bytes 589832 | tf_op jit(solution)/shard_map/ppermute | solution.py:144
  90.5 11.9 %collective-permute-done.20.refs_2_ = bf16[48,2048]{1,0:T(8,128)(2,1)S(1)} collective-permute-done((bf16[48,2048]{1,0:T(8,128)(2,1)S(1)}, bf16[48,2048]{1,0:T(8,128)(2,1)S(1)}, u32[]{:S(2)}, u32[]{:S(2)}) %collective-permute-start.20) | collective-permute-done | bytes 196640 | tf_op jit(solution)/shard_map/ppermute | solution.py:144
  106.1 1.5 %collective-permute-done.24.refs_3_ = bf16[256,768]{1,0:T(8,128)(2,1)S(1)} collective-permute-done((bf16[256,768]{1,0:T(8,128)(2,1)S(1)}, bf16[256,768]{1,0:T(8,128)(2,1)S(1)}, u32[]{:S(2)}, u32[]{:S(2)}) %collective-permute-start.24) | collective-permute-done | bytes 393248 | tf_op jit(solution)/shard_map/ppermute | solution.py:144
  107.6 1.8 %shard_map.133 = (f32[512,768]{1,0:T(8,128)}, f32[8,128]{1,0:T(8,128)}) custom-call(f32[8,128]{1,0:T(8,128)S(1)} %get-tuple-element.139.refs_0_, f32[512,768]{1,0:T(8,128)S(1)} %get-tuple-element.140.refs_1_, bf16[256,768]{1,0:T(8,128)(2,1)S(1)} %collective-permute-done.23.refs_2_, bf16[256,768]{1,0:T(8,128)(2,1)S(1)} %collective-permute-done.24.refs_3_), custom_call_target="tpu_custom_call" | custom-call | tf_op jit(solution)/shard_map/pallas_call | solution.py:126
  (50 shorter events, 20.7 us)
Async XLA Ops:
  1.8 15.3 %collective-permute-start.2 = (bf16[96,2176]{1,0:T(8,128)(2,1)S(1)}, bf16[96,2176]{1,0:T(8,128)(2,1)S(1)}, u32[]{:S(2)}, u32[]{:S(2)}) collective-permute-start(bf16[96,2176]{1,0:T(8,128)(2,1)S(1)} %get-tuple-element.77.refs_1_), channel_id=1, source_target_pairs={{0,1},{1,0},{2,3},{3,2},{4,5},{5,4},{6,7},{7,6},{8,9},{9,8},{10,11... | collective-permute-start | bytes 1253384 | tf_op jit(solution)/shard_map/ppermute | solution.py:144
  4.9 12.1 %collective-permute-start.1 = (bf16[48,2176]{1,0:T(8,128)(2,1)S(1)}, bf16[48,2176]{1,0:T(8,128)(2,1)S(1)}, u32[]{:S(2)}, u32[]{:S(2)}) collective-permute-start(bf16[48,2176]{1,0:T(8,128)(2,1)S(1)} %get-tuple-element.76.refs_3_), channel_id=1, source_target_pairs={{0,4},{1,5},{2,6},{3,7},{4,0},{5,1},{6,2},{7,3},{8,12},{9,13},{10,... | collective-permute-start | bytes 626696 | tf_op jit(solution)/shard_map/ppermute | solution.py:144
  7.5 9.7 %collective-permute-start = (bf16[48,2176]{1,0:T(8,128)(2,1)S(1)}, bf16[48,2176]{1,0:T(8,128)(2,1)S(1)}, u32[]{:S(2)}, u32[]{:S(2)}) collective-permute-start(bf16[48,2176]{1,0:T(8,128)(2,1)S(1)} %get-tuple-element.76.refs_3_), channel_id=1, source_target_pairs={{0,2},{1,3},{2,0},{3,1},{4,6},{5,7},{6,4},{7,5},{8,10},{9,11},{10,... | collective-permute-start | bytes 626696 | tf_op jit(solution)/shard_map/ppermute | solution.py:144
  17.2 11.4 %collective-permute-start.3 = (bf16[48,2176]{1,0:T(8,128)(2,1)S(1)}, bf16[48,2176]{1,0:T(8,128)(2,1)S(1)}, u32[]{:S(2)}, u32[]{:S(2)}) collective-permute-start(bf16[48,2176]{1,0:T(8,128)(2,1)S(1)} %get-tuple-element.81), channel_id=1, source_target_pairs={{0,2},{1,3},{2,0},{3,1},{4,6},{5,7},{6,4},{7,5},{8,10},{9,11},{10,... | collective-permute-start | bytes 626696 | tf_op jit(solution)/shard_map/ppermute | solution.py:144
  18.8 10.4 %collective-permute-start.5 = (bf16[48,2048]{1,0:T(8,128)(2,1)S(1)}, bf16[48,2048]{1,0:T(8,128)(2,1)S(1)}, u32[]{:S(2)}, u32[]{:S(2)}) collective-permute-start(bf16[48,2048]{1,0:T(8,128)(2,1)S(1)} %get-tuple-element.83.refs_2_), channel_id=1, source_target_pairs={{0,4},{1,5},{2,6},{3,7},{4,0},{5,1},{6,2},{7,3},{8,12},{9,13},{10,... | collective-permute-start | bytes 589832 | tf_op jit(solution)/shard_map/ppermute | solution.py:144
  21.1 10.5 %collective-permute-start.4 = (bf16[48,2048]{1,0:T(8,128)(2,1)S(1)}, bf16[48,2048]{1,0:T(8,128)(2,1)S(1)}, u32[]{:S(2)}, u32[]{:S(2)}) collective-permute-start(bf16[48,2048]{1,0:T(8,128)(2,1)S(1)} %get-tuple-element.83.refs_2_), channel_id=1, source_target_pairs={{0,2},{1,3},{2,0},{3,1},{4,6},{5,7},{6,4},{7,5},{8,10},{9,11},{10,... | collective-permute-start | bytes 589832 | tf_op jit(solution)/shard_map/ppermute | solution.py:144
  21.2 17.6 %collective-permute-start.8 = (bf16[96,2176]{1,0:T(8,128)(2,1)S(1)}, bf16[96,2176]{1,0:T(8,128)(2,1)S(1)}, u32[]{:S(2)}, u32[]{:S(2)}) collective-permute-start(bf16[96,2176]{1,0:T(8,128)(2,1)S(1)} %get-tuple-element.89.refs_4_), channel_id=1, source_target_pairs={{0,1},{1,0},{2,3},{3,2},{4,5},{5,4},{6,7},{7,6},{8,9},{9,8},{10,11... | collective-permute-start | bytes 1253384 | tf_op jit(solution)/shard_map/ppermute | solution.py:144
  28.6 9.6 %collective-permute-start.7 = (bf16[48,2176]{1,0:T(8,128)(2,1)S(1)}, bf16[48,2176]{1,0:T(8,128)(2,1)S(1)}, u32[]{:S(2)}, u32[]{:S(2)}) collective-permute-start(bf16[48,2176]{1,0:T(8,128)(2,1)S(1)} %get-tuple-element.87.refs_5_), channel_id=1, source_target_pairs={{0,1},{1,0},{2,3},{3,2},{4,5},{5,4},{6,7},{7,6},{8,9},{9,8},{10,11... | collective-permute-start | bytes 626696 | tf_op jit(solution)/shard_map/ppermute | solution.py:144
  31.6 5.7 %collective-permute-start.6 = (bf16[48,2048]{1,0:T(8,128)(2,1)S(1)}, bf16[48,2048]{1,0:T(8,128)(2,1)S(1)}, u32[]{:S(2)}, u32[]{:S(2)}) collective-permute-start(bf16[48,2048]{1,0:T(8,128)(2,1)S(1)} %get-tuple-element.86), channel_id=1, source_target_pairs={{0,2},{1,3},{2,0},{3,1},{4,6},{5,7},{6,4},{7,5},{8,10},{9,11},{10,... | collective-permute-start | bytes 589832 | tf_op jit(solution)/shard_map/ppermute | solution.py:144
  33.4 14.4 %collective-permute-start.9 = (bf16[96,2048]{1,0:T(8,128)(2,1)S(1)}, bf16[96,2048]{1,0:T(8,128)(2,1)S(1)}, u32[]{:S(2)}, u32[]{:S(2)}) collective-permute-start(bf16[96,2048]{1,0:T(8,128)(2,1)S(1)} %get-tuple-element.91.refs_3_), channel_id=1, source_target_pairs={{0,1},{1,0},{2,3},{3,2},{4,5},{5,4},{6,7},{7,6},{8,9},{9,8},{10,11... | collective-permute-start | bytes 1179656 | tf_op jit(solution)/shard_map/ppermute | solution.py:144
  38.2 11.0 %collective-permute-start.10 = (bf16[48,2048]{1,0:T(8,128)(2,1)S(1)}, bf16[48,2048]{1,0:T(8,128)(2,1)S(1)}, u32[]{:S(2)}, u32[]{:S(2)}) collective-permute-start(bf16[48,2048]{1,0:T(8,128)(2,1)S(1)} %get-tuple-element.92.refs_4_), channel_id=1, source_target_pairs={{0,1},{1,0},{2,3},{3,2},{4,5},{5,4},{6,7},{7,6},{8,9},{9,8},{10,11... | collective-permute-start | bytes 589832 | tf_op jit(solution)/shard_map/ppermute | solution.py:144
  49.9 4.5 %collective-permute-start.11 = (bf16[192,2048]{1,0:T(8,128)(2,1)S(1)}, bf16[192,2048]{1,0:T(8,128)(2,1)S(1)}, u32[]{:S(2)}, u32[]{:S(2)}) collective-permute-start(bf16[192,2048]{1,0:T(8,128)(2,1)S(1)} %get-tuple-element.103), channel_id=1, source_target_pairs={{0,8},{8,0},{16,24},{24,16},{1,9},{9,1},{17,25},{25,17},{2,10},{10... | collective-permute-start | bytes 2359304 | tf_op jit(solution)/shard_map/ppermute | solution.py:144
  53.3 7.2 %collective-permute-start.13 = (bf16[384,1536]{1,0:T(8,128)(2,1)S(1)}, bf16[384,1536]{1,0:T(8,128)(2,1)S(1)}, u32[]{:S(2)}, u32[]{:S(2)}) collective-permute-start(bf16[384,1536]{1,0:T(8,128)(2,1)S(1)} %get-tuple-element.106.refs_1_.refs_3_), channel_id=1, source_target_pairs={{0,8},{8,0},{16,24},{24,16},{1,9},{9,1},{17,25},{25,17},{2,10},{10... | collective-permute-start | bytes 3538952 | tf_op jit(solution)/shard_map/ppermute | solution.py:144
  53.4 7.1 %collective-permute-start.14 = (bf16[192,2048]{1,0:T(8,128)(2,1)S(1)}, bf16[192,2048]{1,0:T(8,128)(2,1)S(1)}, u32[]{:S(2)}, u32[]{:S(2)}) collective-permute-start(bf16[192,2048]{1,0:T(8,128)(2,1)S(1)} %get-tuple-element.111), channel_id=1, source_target_pairs={{0,8},{8,0},{16,24},{24,16},{1,9},{9,1},{17,25},{25,17},{2,10},{10... | collective-permute-start | bytes 2359304 | tf_op jit(solution)/shard_map/ppermute | solution.py:144
  53.9 19.5 %collective-permute-start.15 = (bf16[192,2048]{1,0:T(8,128)(2,1)S(1)}, bf16[192,2048]{1,0:T(8,128)(2,1)S(1)}, u32[]{:S(2)}, u32[]{:S(2)}) collective-permute-start(bf16[192,2048]{1,0:T(8,128)(2,1)S(1)} %get-tuple-element.114), channel_id=1, source_target_pairs={{0,1},{1,0},{2,3},{3,2},{4,5},{5,4},{6,7},{7,6},{8,9},{9,8},{10,11... | collective-permute-start | bytes 2359304 | tf_op jit(solution)/shard_map/ppermute | solution.py:144
  54.6 20.7 %collective-permute-start.16 = (bf16[192,2048]{1,0:T(8,128)(2,1)S(1)}, bf16[192,2048]{1,0:T(8,128)(2,1)S(1)}, u32[]{:S(2)}, u32[]{:S(2)}) collective-permute-start(bf16[192,2048]{1,0:T(8,128)(2,1)S(1)} %get-tuple-element.117), channel_id=1, source_target_pairs={{0,16},{8,24},{16,0},{24,8},{1,17},{9,25},{17,1},{25,9},{2,18},{10... | collective-permute-start | bytes 2359304 | tf_op jit(solution)/shard_map/ppermute | solution.py:144
  58.8 20.5 %collective-permute-start.17 = (bf16[192,2048]{1,0:T(8,128)(2,1)S(1)}, bf16[192,2048]{1,0:T(8,128)(2,1)S(1)}, u32[]{:S(2)}, u32[]{:S(2)}) collective-permute-start(bf16[192,2048]{1,0:T(8,128)(2,1)S(1)} %get-tuple-element.120), channel_id=1, source_target_pairs={{0,2},{1,3},{2,0},{3,1},{4,6},{5,7},{6,4},{7,5},{8,10},{9,11},{10,... | collective-permute-start | bytes 2359304 | tf_op jit(solution)/shard_map/ppermute | solution.py:144
  64.1 39.0 %collective-permute-start.21 = (bf16[512,768]{1,0:T(8,128)(2,1)S(1)}, bf16[512,768]{1,0:T(8,128)(2,1)S(1)}, u32[]{:S(2)}, u32[]{:S(2)}) collective-permute-start(bf16[512,768]{1,0:T(8,128)(2,1)S(1)} %get-tuple-element.133), channel_id=1, source_target_pairs={{0,16},{8,24},{16,0},{24,8},{1,17},{9,25},{17,1},{25,9},{2,18},{10... | collective-permute-start | bytes 2359304 | tf_op jit(solution)/shard_map/ppermute | solution.py:144
  73.6 12.6 %collective-permute-start.18 = (bf16[96,2048]{1,0:T(8,128)(2,1)S(1)}, bf16[96,2048]{1,0:T(8,128)(2,1)S(1)}, u32[]{:S(2)}, u32[]{:S(2)}) collective-permute-start(bf16[96,2048]{1,0:T(8,128)(2,1)S(1)} %get-tuple-element.123), channel_id=1, source_target_pairs={{0,2},{1,3},{2,0},{3,1},{4,6},{5,7},{6,4},{7,5},{8,10},{9,11},{10,... | collective-permute-start | bytes 1179656 | tf_op jit(solution)/shard_map/ppermute | solution.py:144
  79.5 9.5 %collective-permute-start.19 = (bf16[96,2048]{1,0:T(8,128)(2,1)S(1)}, bf16[96,2048]{1,0:T(8,128)(2,1)S(1)}, u32[]{:S(2)}, u32[]{:S(2)}) collective-permute-start(bf16[96,2048]{1,0:T(8,128)(2,1)S(1)} %get-tuple-element.126), channel_id=1, source_target_pairs={{0,1},{1,0},{2,3},{3,2},{4,5},{5,4},{6,7},{7,6},{8,9},{9,8},{10,11... | collective-permute-start | bytes 1179656 | tf_op jit(solution)/shard_map/ppermute | solution.py:144
  81.1 25.0 %collective-permute-start.23 = (bf16[256,768]{1,0:T(8,128)(2,1)S(1)}, bf16[256,768]{1,0:T(8,128)(2,1)S(1)}, u32[]{:S(2)}, u32[]{:S(2)}) collective-permute-start(bf16[256,768]{1,0:T(8,128)(2,1)S(1)} %get-tuple-element.141), channel_id=1, source_target_pairs={{0,16},{8,24},{16,0},{24,8},{1,17},{9,25},{17,1},{25,9},{2,18},{10... | collective-permute-start | bytes 1179656 | tf_op jit(solution)/shard_map/ppermute | solution.py:144
  81.6 26.0 %collective-permute-start.24 = (bf16[256,768]{1,0:T(8,128)(2,1)S(1)}, bf16[256,768]{1,0:T(8,128)(2,1)S(1)}, u32[]{:S(2)}, u32[]{:S(2)}) collective-permute-start(bf16[256,768]{1,0:T(8,128)(2,1)S(1)} %get-tuple-element.142), channel_id=1, source_target_pairs={{0,16},{8,24},{16,0},{24,8},{1,17},{9,25},{17,1},{25,9},{2,18},{10... | collective-permute-start | bytes 1179656 | tf_op jit(solution)/shard_map/ppermute | solution.py:144
  86.3 16.1 %collective-permute-start.20 = (bf16[48,2048]{1,0:T(8,128)(2,1)S(1)}, bf16[48,2048]{1,0:T(8,128)(2,1)S(1)}, u32[]{:S(2)}, u32[]{:S(2)}) collective-permute-start(bf16[48,2048]{1,0:T(8,128)(2,1)S(1)} %get-tuple-element.129), channel_id=1, source_target_pairs={{0,4},{1,5},{2,6},{3,7},{4,0},{5,1},{6,2},{7,3},{8,12},{9,13},{10,... | collective-permute-start | bytes 589832 | tf_op jit(solution)/shard_map/ppermute | solution.py:144
  89.1 16.3 %collective-permute-start.22 = (bf16[48,2048]{1,0:T(8,128)(2,1)S(1)}, bf16[48,2048]{1,0:T(8,128)(2,1)S(1)}, u32[]{:S(2)}, u32[]{:S(2)}) collective-permute-start(bf16[48,2048]{1,0:T(8,128)(2,1)S(1)} %get-tuple-element.136), channel_id=1, source_target_pairs={{0,4},{1,5},{2,6},{3,7},{4,0},{5,1},{6,2},{7,3},{8,12},{9,13},{10,... | collective-permute-start | bytes 589832 | tf_op jit(solution)/shard_map/ppermute | solution.py:144
  (1 other events, 4.4 us)

commit v5 on v4

--- a/solution.py
+++ b/solution.py
@@ -252,7 +252,7 @@
     cot_near = swap(cot_own, "expert", near_bit)
     tok_last_on, done = copied([(tok_last, 0)], wide, [done])
     next_tok_last = swap(tok_last_on, "expert", 1)
-    cot_pair, done = copied([(cot_near, 0), (cot_far, 0)], width, [done])
+    cot_pair, done = copied([(cot_near, 0), (cot_far, 0)], width, [done], [next_tok_pair])
     cot_far_on, done = copied([(cot_far, 0)], width, [done])
     next_cot_pair = swap(cot_pair, "expert", 1)
     cot_last = swap(cot_far_on, "expert", near_bit)
@@ -279,16 +279,15 @@
         flipped, flipped_sent, hidden_t, gate_by, up_by, kept, sent, gate, up, down = refs[
             len(tok_arrays) + 3 : len(tok_arrays) + 13
         ]
-        rows, probs, hidden, sems = refs[len(tok_arrays) + 13 :]
-        steps = chunks(ff, 256)
+        rows, probs, hidden, gates, sems = refs[len(tok_arrays) + 13 :]
         copies = []
-        for i, (start, size) in enumerate(steps):
-            place = slice(start, start + size)
-            for j, (far_ref, near_ref) in enumerate([(weights[0], gate), (weights[1], up)]):
+        for j, (far_ref, near_ref) in enumerate(zip(weights, (gate, up, down))):
+            size = far_ref.shape[0] // 4
+            for i in range(4):
+                place = slice(i * size, (i + 1) * size)
                 copies.append(
-                    pltpu.make_async_copy(far_ref.at[:, place], near_ref.at[:, place], sems.at[2 * i + j])
+                    pltpu.make_async_copy(far_ref.at[place], near_ref.at[place], sems.at[4 * j + i])
                 )
-        copies.append(pltpu.make_async_copy(weights[2], down, sems.at[2 * len(steps)]))
         for copy in copies:
             copy.start()
         own = me_ref[0]
@@ -304,11 +303,16 @@
             for i, m in enumerate(places):
                 start = pl.multiple_of((mine_ref[0] ^ m) * band, band)
                 out[i * band : (i + 1) * band, :] = rows[:, pl.ds(start, band)].T
-        for i, (start, size) in enumerate(steps):
+        for copy in copies[:4]:
+            copy.wait()
+        for start, size in chunks(ff, 256):
             place = slice(start, start + size)
-            copies[2 * i].wait()
-            gate_pre = jnp.dot(rows[...], gate[:, place], preferred_element_type=F32)
-            copies[2 * i + 1].wait()
+            gates[:, place] = jnp.dot(rows[...], gate[:, place], preferred_element_type=F32)
+        for copy in copies[4:8]:
+            copy.wait()
+        for start, size in chunks(ff, 256):
+            place = slice(start, start + size)
+            gate_pre = gates[:, place]
             up_pre = jnp.dot(rows[...], up[:, place], preferred_element_type=F32)
             sigma = jax.nn.sigmoid(gate_pre)
             silu = gate_pre * sigma
@@ -317,7 +321,8 @@
             gate_by[:, place] = scaled * sigma * (1.0 + gate_pre * (1.0 - sigma))
             up_by[:, place] = weight * silu
             hidden_t[place, :] = hidden[:, place].T
-        copies[-1].wait()
+        for copy in copies[8:]:
+            copy.wait()
         for start, size in chunks(width, 512):
             place = slice(start, start + size)
             part = jnp.dot(hidden[...], down[:, place], preferred_element_type=F32).astype(BF16)
@@ -346,7 +351,8 @@
             VMEM((total, width), BF16),
             VMEM((total, 1), F32),
             VMEM((total, ff), BF16),
-            pltpu.SemaphoreType.DMA((2 * len(chunks(ff, 256)) + 1,)),
+            VMEM((total, ff), F32),
+            pltpu.SemaphoreType.DMA((12,)),
         ],
         after=[done],
         vmem=8,
@@ -356,34 +362,30 @@
 
     def down_first(own_ref, *refs):
         blocks = refs[: len(cot_arrays)]
-        left, _, rows, away, _ = refs[len(cot_arrays) :]
+        left, rows, away = refs[len(cot_arrays) :]
         for b, (i, row) in enumerate(cot_where):
             rows[b * count : (b + 1) * count, :] = blocks[i][row : row + count, :width]
         products([3], left, rows, [(away, 0)], own_ref[0])
 
-    cot_rows, down_away, flipped_sent, done = stage(
+    cot_rows, down_away, done = stage(
         down_first,
-        [(mine, SMEM)] + [(a, VMEM) for a in [*cot_arrays, hidden_t]] + [(flipped_sent, ANY)],
-        [
-            ((total, width), BF16, VMEM),
-            ((slab, width), BF16, VMEM),
-            (flipped_sent.shape, BF16, ANY),
-        ],
-        after=[done],
-        aliases={len(cot_arrays) + 2: 2},
+        [(mine, SMEM)] + [(a, VMEM) for a in [*cot_arrays, hidden_t]],
+        [((total, width), BF16, VMEM), ((slab, width), BF16, VMEM)],
+        after=[done],
     )
     down_came = swap(down_away, "dp", 1)
+
+    def down_rest(own_ref, left, cot, _, away, send, kept, same):
+        products([1, 2, 0], left, cot, [(away, 0), (send, 0), (kept, 0)], own_ref[0])
+
+    last_away, down_send, down_kept, flipped_sent, done = stage(
+        down_rest,
+        [(mine, SMEM), (hidden_t, VMEM), (cot_rows, VMEM), (flipped_sent, ANY)],
+        [((slab, width), BF16, VMEM)] * 3 + [(flipped_sent.shape, BF16, ANY)],
+        after=[done],
+        aliases={3: 3},
+    )
     flipped_came = swap(flipped_sent, "dp", 1)
-
-    def down_rest(own_ref, left, cot, away, send, kept):
-        products([1, 2, 0], left, cot, [(away, 0), (send, 0), (kept, 0)], own_ref[0])
-
-    last_away, down_send, down_kept, done = stage(
-        down_rest,
-        [(mine, SMEM), (hidden_t, VMEM), (cot_rows, VMEM)],
-        [((slab, width), BF16, VMEM)] * 3,
-        after=[done],
-    )
     last_came = swap(last_away, "dp", 1)
     out_came = swap(out_sent, "expert", 1)
 
@@ -459,7 +461,7 @@
         after=[done],
     )
     gate_got = swap(gate_send, "dp", 2)
-    up_got = [swap(a, "dp", 2) for a in (up_high, up_low)]
+    high_got = swap(up_high, "dp", 2)
 
     def folded(held, came, after, waits=()):
         rows = held.shape[0]
@@ -477,52 +479,55 @@
             after=after,
         )
 
-    def owned(parts, after):
-        size = sum(a.shape[0] for a in parts[0])
-        wide = parts[0][0].shape[1]
+    def owned(parts, after, rows=None, into=None):
+        size, wide = parts[-1].shape
+        first = 0 if rows is None else rows
+        full = parts[0].shape[0]
         step = size // 4
-        where = []
-        for arrays in parts:
-            first = len([i for w in where for i in w])
-            where.append(range(first, first + len(arrays)))
+        n = len(parts)
 
         def body(*refs):
-            ins, (out, total, sems) = refs[:-3], refs[-3:]
+            out, total, sems = refs[-3:]
             copies = []
             for i in range(4):
                 at = slice(i * step, (i + 1) * step)
-                value = jnp.zeros((step, wide), F32)
-                for places in where:
-                    each = size // len(places)
-                    ref, row = ins[places[i * step // each]], i * step % each
-                    value = value + ref[row : row + step, :].astype(F32)
+                there = slice(first + i * step, first + (i + 1) * step)
+                value = refs[0][there, :].astype(F32)
+                for ref in refs[1:n]:
+                    value = value + ref[at, :].astype(F32)
                 total[at, :] = value
-                copies.append(pltpu.make_async_copy(total.at[at], out.at[at], sems.at[i]))
+                copies.append(pltpu.make_async_copy(total.at[at], out.at[there], sems.at[i]))
                 copies[-1].start()
             for copy in copies:
                 copy.wait()
 
         return stage(
             body,
-            [(a, VMEM) for arrays in parts for a in arrays],
-            [((size, wide), F32, HBM)],
+            [(a, VMEM) for a in parts] + ([] if into is None else [(into, HBM)]),
+            [((full, wide), F32, HBM)],
             scratch=[VMEM((size, wide), F32), pltpu.SemaphoreType.DMA((4,))],
             after=after,
+            aliases=None if into is None else {n: 0},
         )
 
-    def fold_on(held, came, bit, after, waits=()):
-        held, send, done = folded(held, came, after, waits)
+    def fold_on(held, came, bit, after):
+        held, send, done = folded(held, came, after)
         return held, swap(send, "expert", bit), done
 
+    down_grad, done = owned([down_kept, last_came, down_got], [done])
     out_held, out_came, done = fold_on(out_kept, out_came, near_bit, [done])
-    down_grad, done = owned([[down_kept], [last_came], [down_got]], [done])
     in_held, in_came, done = fold_on(in_kept, in_came, 1, [done])
     out_held, out_came, done = fold_on(out_held, out_came, far_bit, [done])
+    up_low, done = stage(
+        lambda *_: None, [(up_low, ANY)], [(up_low.shape, BF16, ANY)], after=[done], aliases={0: 0}
+    )
+    low_got = swap(up_low, "dp", 2)
     in_held, in_came, done = fold_on(in_held, in_came, far_bit, [done])
+    gate_part, done = owned([gate_kept, gate_got], [done])
+    up_part, done = owned([up_kept, high_got], [done])
     layer_out, done = folded(out_held, out_came, [done])
-    gate_part, done = owned([[gate_kept], [gate_got]], [done])
     input_grad, done = folded(in_held, in_came, [done])
-    up_part, _ = owned([[up_kept], up_got], [done])
+    up_part, _ = owned([up_kept, low_got], [done], band // 2, up_part)
     return (layer_out, input_grad, gate_part[None], up_part[None], down_grad[None])
 
 

time: 110 us -> 108 us (0.982)
  starting transfers between devices: 29.9 us -> 28.3 us
  waiting for transfers between devices: 52.4 us -> 53.8 us
  Pallas kernels: 26.4 us -> 25.2 us
    ppermute x25, starting transfers between devices: 29.9 us -> 28.3 us  [swap(): return lax.ppermute(value, axis, [(i, i ^ mask) for i in range(size)])]
    ppermute x25, waiting for transfers between devices: 52.4 us -> 53.8 us  [swap(): return lax.ppermute(value, axis, [(i, i ^ mask) for i in range(size)])]
    pallas_call x24 -> x26, Pallas kernels: 26.4 us -> 25.2 us  [stage(): pl.pallas_call(kernel, in_specs=[pl.BlockSpec(memory_space=VMEM if m == P...]
  transfers between devices with their start and end apart: 25 -> 25, of which waited for: 13 -> 13; matrix products, arithmetic and copies ran while one was open for 0% -> 0% of each run, Pallas kernels for 21% -> 20%
where the time goes in v5:
time: 108 us
  waiting for transfers between devices  53.8 us (50%)
  starting transfers between devices  28.3 us (26%)
  Pallas kernels  25.2 us (23%)
    ppermute x25, waiting for transfers between devices, swap(): return lax.ppermute(value, axis, [(i, i ^ mask) for i in range(size)])  53.8 us
    ppermute x25, starting transfers between devices, swap(): return lax.ppermute(value, axis, [(i, i ^ mask) for i in range(size)])  28.3 us
    pallas_call x26, Pallas kernels, stage(): pl.pallas_call(kernel, in_specs=[pl.BlockSpec(memory_space=VMEM if m == P...  25.2 us
  transfers between devices with their start and end apart: 25, of which 13 were waited for; matrix products, arithmetic and copies ran while one was open for 0% of the time, Pallas kernels for 20%

profile of v5, /device:TPU:0, one launch (start us, length us, event | category | flops | bytes accessed | tf_op | source)
XLA Modules:
  0.0 108.2 jit_solution(6134987517598720729)
XLA Ops:
  1.8 3.0 %collective-permute-start.2 = (bf16[96,2176]{1,0:T(8,128)(2,1)S(1)}, bf16[96,2176]{1,0:T(8,128)(2,1)S(1)}, u32[]{:S(2)}, u32[]{:S(2)}) collective-permute-start(bf16[96,2176]{1,0:T(8,128)(2,1)S(1)} %get-tuple-element.81.refs_1_), channel_id=1, source_target_pairs={{0,1},{1,0},{2,3},{3,2},{4,5},{5,4},{6,7},{7,6},{8,9},{9,8},{10,11... | collective-permute-start | bytes 1253384 | tf_op jit(solution)/shard_map/ppermute | solution.py:144
  4.9 2.6 %collective-permute-start.1 = (bf16[48,2176]{1,0:T(8,128)(2,1)S(1)}, bf16[48,2176]{1,0:T(8,128)(2,1)S(1)}, u32[]{:S(2)}, u32[]{:S(2)}) collective-permute-start(bf16[48,2176]{1,0:T(8,128)(2,1)S(1)} %get-tuple-element.80.refs_3_), channel_id=1, source_target_pairs={{0,4},{1,5},{2,6},{3,7},{4,0},{5,1},{6,2},{7,3},{8,12},{9,13},{10,... | collective-permute-start | bytes 626696 | tf_op jit(solution)/shard_map/ppermute | solution.py:144
  7.5 1.6 %collective-permute-start = (bf16[48,2176]{1,0:T(8,128)(2,1)S(1)}, bf16[48,2176]{1,0:T(8,128)(2,1)S(1)}, u32[]{:S(2)}, u32[]{:S(2)}) collective-permute-start(bf16[48,2176]{1,0:T(8,128)(2,1)S(1)} %get-tuple-element.80.refs_3_), channel_id=1, source_target_pairs={{0,2},{1,3},{2,0},{3,1},{4,6},{5,7},{6,4},{7,5},{8,10},{9,11},{10,... | collective-permute-start | bytes 626696 | tf_op jit(solution)/shard_map/ppermute | solution.py:144
  9.0 7.9 %collective-permute-done.1.refs_2_.refs_1_ = bf16[48,2176]{1,0:T(8,128)(2,1)S(1)} collective-permute-done((bf16[48,2176]{1,0:T(8,128)(2,1)S(1)}, bf16[48,2176]{1,0:T(8,128)(2,1)S(1)}, u32[]{:S(2)}, u32[]{:S(2)}) %collective-permute-start.1) | collective-permute-done | bytes 208928 | tf_op jit(solution)/shard_map/ppermute | solution.py:144
  17.8 1.6 %collective-permute-start.3 = (bf16[48,2176]{1,0:T(8,128)(2,1)S(1)}, bf16[48,2176]{1,0:T(8,128)(2,1)S(1)}, u32[]{:S(2)}, u32[]{:S(2)}) collective-permute-start(bf16[48,2176]{1,0:T(8,128)(2,1)S(1)} %get-tuple-element.85), channel_id=1, source_target_pairs={{0,2},{1,3},{2,0},{3,1},{4,6},{5,7},{6,4},{7,5},{8,10},{9,11},{10,... | collective-permute-start | bytes 626696 | tf_op jit(solution)/shard_map/ppermute | solution.py:144
  19.3 2.3 %collective-permute-start.5 = (bf16[48,2048]{1,0:T(8,128)(2,1)S(1)}, bf16[48,2048]{1,0:T(8,128)(2,1)S(1)}, u32[]{:S(2)}, u32[]{:S(2)}) collective-permute-start(bf16[48,2048]{1,0:T(8,128)(2,1)S(1)} %get-tuple-element.87.refs_2_), channel_id=1, source_target_pairs={{0,4},{1,5},{2,6},{3,7},{4,0},{5,1},{6,2},{7,3},{8,12},{9,13},{10,... | collective-permute-start | bytes 589832 | tf_op jit(solution)/shard_map/ppermute | solution.py:144
  21.7 7.6 %collective-permute-done.3.refs_1_ = bf16[48,2176]{1,0:T(8,128)(2,1)S(1)} collective-permute-done((bf16[48,2176]{1,0:T(8,128)(2,1)S(1)}, bf16[48,2176]{1,0:T(8,128)(2,1)S(1)}, u32[]{:S(2)}, u32[]{:S(2)}) %collective-permute-start.3) | collective-permute-done | bytes 208928 | tf_op jit(solution)/shard_map/ppermute | solution.py:144
  29.4 1.7 %collective-permute-start.8 = (bf16[48,2176]{1,0:T(8,128)(2,1)S(1)}, bf16[48,2176]{1,0:T(8,128)(2,1)S(1)}, u32[]{:S(2)}, u32[]{:S(2)}) collective-permute-start(bf16[48,2176]{1,0:T(8,128)(2,1)S(1)} %get-tuple-element.92.refs_5_), channel_id=1, source_target_pairs={{0,1},{1,0},{2,3},{3,2},{4,5},{5,4},{6,7},{7,6},{8,9},{9,8},{10,11... | collective-permute-start | bytes 626696 | tf_op jit(solution)/shard_map/ppermute | solution.py:144
  32.1 1.6 %collective-permute-start.7 = (bf16[48,2048]{1,0:T(8,128)(2,1)S(1)}, bf16[48,2048]{1,0:T(8,128)(2,1)S(1)}, u32[]{:S(2)}, u32[]{:S(2)}) collective-permute-start(bf16[48,2048]{1,0:T(8,128)(2,1)S(1)} %get-tuple-element.91), channel_id=1, source_target_pairs={{0,2},{1,3},{2,0},{3,1},{4,6},{5,7},{6,4},{7,5},{8,10},{9,11},{10,... | collective-permute-start | bytes 589832 | tf_op jit(solution)/shard_map/ppermute | solution.py:144
  33.7 1.5 %collective-permute-start.9 = (bf16[96,2048]{1,0:T(8,128)(2,1)S(1)}, bf16[96,2048]{1,0:T(8,128)(2,1)S(1)}, u32[]{:S(2)}, u32[]{:S(2)}) collective-permute-start(bf16[96,2048]{1,0:T(8,128)(2,1)S(1)} %get-tuple-element.95.refs_3_), channel_id=1, source_target_pairs={{0,1},{1,0},{2,3},{3,2},{4,5},{5,4},{6,7},{7,6},{8,9},{9,8},{10,11... | collective-permute-start | bytes 1179656 | tf_op jit(solution)/shard_map/ppermute | solution.py:144
  35.8 2.1 %collective-permute-done.7.refs_1_ = bf16[48,2048]{1,0:T(8,128)(2,1)S(1)} collective-permute-done((bf16[48,2048]{1,0:T(8,128)(2,1)S(1)}, bf16[48,2048]{1,0:T(8,128)(2,1)S(1)}, u32[]{:S(2)}, u32[]{:S(2)}) %collective-permute-start.7) | collective-permute-done | bytes 196640 | tf_op jit(solution)/shard_map/ppermute | solution.py:144
  37.9 1.6 %collective-permute-start.10 = (bf16[48,2048]{1,0:T(8,128)(2,1)S(1)}, bf16[48,2048]{1,0:T(8,128)(2,1)S(1)}, u32[]{:S(2)}, u32[]{:S(2)}) collective-permute-start(bf16[48,2048]{1,0:T(8,128)(2,1)S(1)} %get-tuple-element.96.refs_4_), channel_id=1, source_target_pairs={{0,1},{1,0},{2,3},{3,2},{4,5},{5,4},{6,7},{7,6},{8,9},{9,8},{10,11... | collective-permute-start | bytes 589832 | tf_op jit(solution)/shard_map/ppermute | solution.py:144
  39.5 7.3 %shard_map.118 = (bf16[1024,384]{1,0:T(8,128)(2,1)S(1)}, bf16[1024,384]{1,0:T(8,128)(2,1)S(1)}, bf16[768,384]{1,0:T(8,128)(2,1)S(1)}, f32[384,768]{1,0:T(8,128)S...) custom-call(f32[8,128]{1,0:T(8,128)S(1)} %get-tuple-element.93.refs_, ...), custom_call_target="tpu_custom_call" | custom-call | tf_op jit(solution)/shard_map/pallas_call | solution.py:126
  52.8 1.7 %collective-permute-start.15 = (bf16[192,2048]{1,0:T(8,128)(2,1)S(1)}, bf16[192,2048]{1,0:T(8,128)(2,1)S(1)}, u32[]{:S(2)}, u32[]{:S(2)}) collective-permute-start(bf16[192,2048]{1,0:T(8,128)(2,1)S(1)} %get-tuple-element.118), channel_id=1, source_target_pairs={{0,16},{8,24},{16,0},{24,8},{1,17},{9,25},{17,1},{25,9},{2,18},{10... | collective-permute-start | bytes 2359304 | tf_op jit(solution)/shard_map/ppermute | solution.py:144
  55.9 2.6 %shard_map.123 = (bf16[192,2048]{1,0:T(8,128)(2,1)S(1)}, bf16[192,2048]{1,0:T(8,128)(2,1)S(1)}, f32[8,128]{1,0:T(8,128)S(1)}) custom-call(f32[8,128]{1,0:T(8,128)S(1)} %get-tuple-element.109.refs_0_, bf16[384,1536]{1,0:T(8,128)(2,1)S(1)} %get-tuple-element.110.refs_1_.refs_3_, bf16[2048,768]{1,0:T(8,128)(2,1)S(1)} %get-tuple-element.111.refs_2_, ...), custom_call_target="tpu_custom_call" | custom-call | tf_op jit(solution)/shard_map/pallas_call | solution.py:126
  58.7 3.4 %shard_map.124 = (bf16[512,768]{1,0:T(8,128)(2,1)S(1)}, bf16[256,768]{1,0:T(8,128)(2,1)S(1)}, bf16[256,768]{1,0:T(8,128)(2,1)S(1)}, f32[512,768]{1,0:T(8,128)S(1...) custom-call(f32[8,128]{1,0:T(8,128)S(1)} %get-tuple-element.113.refs_0_, ...), custom_call_target="tpu_custom_call" | custom-call | tf_op jit(solution)/shard_map/pallas_call | solution.py:126
  62.7 10.5 %collective-permute-done.15.refs_3_ = bf16[192,2048]{1,0:T(8,128)(2,1)S(1)} collective-permute-done((bf16[192,2048]{1,0:T(8,128)(2,1)S(1)}, bf16[192,2048]{1,0:T(8,128)(2,1)S(1)}, u32[]{:S(2)}, u32[]{:S(2)}) %collective-permute-start.15) | collective-permute-done | bytes 786464 | tf_op jit(solution)/shard_map/ppermute | solution.py:144
  75.1 4.0 %collective-permute-done.17.refs_2_ = bf16[192,2048]{1,0:T(8,128)(2,1)S(1)} collective-permute-done((bf16[192,2048]{1,0:T(8,128)(2,1)S(1)}, bf16[192,2048]{1,0:T(8,128)(2,1)S(1)}, u32[]{:S(2)}, u32[]{:S(2)}) %collective-permute-start.17) | collective-permute-done | bytes 786464 | tf_op jit(solution)/shard_map/ppermute | solution.py:144
  79.4 6.8 %collective-permute-done.18.refs_2_ = bf16[96,2048]{1,0:T(8,128)(2,1)S(1)} collective-permute-done((bf16[96,2048]{1,0:T(8,128)(2,1)S(1)}, bf16[96,2048]{1,0:T(8,128)(2,1)S(1)}, u32[]{:S(2)}, u32[]{:S(2)}) %collective-permute-start.18) | collective-permute-done | bytes 393248 | tf_op jit(solution)/shard_map/ppermute | solution.py:144
  86.9 2.9 %collective-permute-start.22 = (bf16[48,2048]{1,0:T(8,128)(2,1)S(1)}, bf16[48,2048]{1,0:T(8,128)(2,1)S(1)}, u32[]{:S(2)}, u32[]{:S(2)}) collective-permute-start(bf16[48,2048]{1,0:T(8,128)(2,1)S(1)} %get-tuple-element.141), channel_id=1, source_target_pairs={{0,4},{1,5},{2,6},{3,7},{4,0},{5,1},{6,2},{7,3},{8,12},{9,13},{10,... | collective-permute-start | bytes 589832 | tf_op jit(solution)/shard_map/ppermute | solution.py:144
  92.2 6.2 %collective-permute-done.21.refs_2_ = bf16[256,768]{1,0:T(8,128)(2,1)S(1)} collective-permute-done((bf16[256,768]{1,0:T(8,128)(2,1)S(1)}, bf16[256,768]{1,0:T(8,128)(2,1)S(1)}, u32[]{:S(2)}, u32[]{:S(2)}) %collective-permute-start.21) | collective-permute-done | bytes 393248 | tf_op jit(solution)/shard_map/ppermute | solution.py:144
  99.4 3.3 %collective-permute-done.22.refs_2_ = bf16[48,2048]{1,0:T(8,128)(2,1)S(1)} collective-permute-done((bf16[48,2048]{1,0:T(8,128)(2,1)S(1)}, bf16[48,2048]{1,0:T(8,128)(2,1)S(1)}, u32[]{:S(2)}, u32[]{:S(2)}) %collective-permute-start.22) | collective-permute-done | bytes 196640 | tf_op jit(solution)/shard_map/ppermute | solution.py:144
  103.4 2.5 %collective-permute-done.23.refs_2_ = bf16[48,2048]{1,0:T(8,128)(2,1)S(1)} collective-permute-done((bf16[48,2048]{1,0:T(8,128)(2,1)S(1)}, bf16[48,2048]{1,0:T(8,128)(2,1)S(1)}, u32[]{:S(2)}, u32[]{:S(2)}) %collective-permute-start.23) | collective-permute-done | bytes 196640 | tf_op jit(solution)/shard_map/ppermute | solution.py:144
  106.7 1.5 %shard_map.135 = (f32[512,768]{1,0:T(8,128)}, f32[8,128]{1,0:T(8,128)}) custom-call(f32[8,128]{1,0:T(8,128)S(1)} %get-tuple-element.148.refs_0_, f32[512,768]{1,0:T(8,128)S(1)} %get-tuple-element.137.refs_1_, bf16[256,768]{1,0:T(8,128)(2,1)S(1)} %collective-permute-done.24.refs_2_, ...), custom_call_target="tpu_custom_call", output_to_operand_aliasing={{0}: (3, {})} | custom-call | tf_op jit(solution)/shard_map/pallas_call | solution.py:126
  (52 shorter events, 19.5 us)
Async XLA Ops:
  1.8 15.3 %collective-permute-start.2 = (bf16[96,2176]{1,0:T(8,128)(2,1)S(1)}, bf16[96,2176]{1,0:T(8,128)(2,1)S(1)}, u32[]{:S(2)}, u32[]{:S(2)}) collective-permute-start(bf16[96,2176]{1,0:T(8,128)(2,1)S(1)} %get-tuple-element.81.refs_1_), channel_id=1, source_target_pairs={{0,1},{1,0},{2,3},{3,2},{4,5},{5,4},{6,7},{7,6},{8,9},{9,8},{10,11... | collective-permute-start | bytes 1253384 | tf_op jit(solution)/shard_map/ppermute | solution.py:144
  4.9 12.1 %collective-permute-start.1 = (bf16[48,2176]{1,0:T(8,128)(2,1)S(1)}, bf16[48,2176]{1,0:T(8,128)(2,1)S(1)}, u32[]{:S(2)}, u32[]{:S(2)}) collective-permute-start(bf16[48,2176]{1,0:T(8,128)(2,1)S(1)} %get-tuple-element.80.refs_3_), channel_id=1, source_target_pairs={{0,4},{1,5},{2,6},{3,7},{4,0},{5,1},{6,2},{7,3},{8,12},{9,13},{10,... | collective-permute-start | bytes 626696 | tf_op jit(solution)/shard_map/ppermute | solution.py:144
  7.5 9.7 %collective-permute-start = (bf16[48,2176]{1,0:T(8,128)(2,1)S(1)}, bf16[48,2176]{1,0:T(8,128)(2,1)S(1)}, u32[]{:S(2)}, u32[]{:S(2)}) collective-permute-start(bf16[48,2176]{1,0:T(8,128)(2,1)S(1)} %get-tuple-element.80.refs_3_), channel_id=1, source_target_pairs={{0,2},{1,3},{2,0},{3,1},{4,6},{5,7},{6,4},{7,5},{8,10},{9,11},{10,... | collective-permute-start | bytes 626696 | tf_op jit(solution)/shard_map/ppermute | solution.py:144
  17.2 14.9 %collective-permute-start.6 = (bf16[96,2176]{1,0:T(8,128)(2,1)S(1)}, bf16[96,2176]{1,0:T(8,128)(2,1)S(1)}, u32[]{:S(2)}, u32[]{:S(2)}) collective-permute-start(bf16[96,2176]{1,0:T(8,128)(2,1)S(1)} %get-tuple-element.88.refs_4_), channel_id=1, source_target_pairs={{0,1},{1,0},{2,3},{3,2},{4,5},{5,4},{6,7},{7,6},{8,9},{9,8},{10,11... | collective-permute-start | bytes 1253384 | tf_op jit(solution)/shard_map/ppermute | solution.py:144
  17.8 11.6 %collective-permute-start.3 = (bf16[48,2176]{1,0:T(8,128)(2,1)S(1)}, bf16[48,2176]{1,0:T(8,128)(2,1)S(1)}, u32[]{:S(2)}, u32[]{:S(2)}) collective-permute-start(bf16[48,2176]{1,0:T(8,128)(2,1)S(1)} %get-tuple-element.85), channel_id=1, source_target_pairs={{0,2},{1,3},{2,0},{3,1},{4,6},{5,7},{6,4},{7,5},{8,10},{9,11},{10,... | collective-permute-start | bytes 626696 | tf_op jit(solution)/shard_map/ppermute | solution.py:144
  19.3 11.8 %collective-permute-start.5 = (bf16[48,2048]{1,0:T(8,128)(2,1)S(1)}, bf16[48,2048]{1,0:T(8,128)(2,1)S(1)}, u32[]{:S(2)}, u32[]{:S(2)}) collective-permute-start(bf16[48,2048]{1,0:T(8,128)(2,1)S(1)} %get-tuple-element.87.refs_2_), channel_id=1, source_target_pairs={{0,4},{1,5},{2,6},{3,7},{4,0},{5,1},{6,2},{7,3},{8,12},{9,13},{10,... | collective-permute-start | bytes 589832 | tf_op jit(solution)/shard_map/ppermute | solution.py:144
  21.6 10.4 %collective-permute-start.4 = (bf16[48,2048]{1,0:T(8,128)(2,1)S(1)}, bf16[48,2048]{1,0:T(8,128)(2,1)S(1)}, u32[]{:S(2)}, u32[]{:S(2)}) collective-permute-start(bf16[48,2048]{1,0:T(8,128)(2,1)S(1)} %get-tuple-element.87.refs_2_), channel_id=1, source_target_pairs={{0,2},{1,3},{2,0},{3,1},{4,6},{5,7},{6,4},{7,5},{8,10},{9,11},{10,... | collective-permute-start | bytes 589832 | tf_op jit(solution)/shard_map/ppermute | solution.py:144
  29.4 6.4 %collective-permute-start.8 = (bf16[48,2176]{1,0:T(8,128)(2,1)S(1)}, bf16[48,2176]{1,0:T(8,128)(2,1)S(1)}, u32[]{:S(2)}, u32[]{:S(2)}) collective-permute-start(bf16[48,2176]{1,0:T(8,128)(2,1)S(1)} %get-tuple-element.92.refs_5_), channel_id=1, source_target_pairs={{0,1},{1,0},{2,3},{3,2},{4,5},{5,4},{6,7},{7,6},{8,9},{9,8},{10,11... | collective-permute-start | bytes 626696 | tf_op jit(solution)/shard_map/ppermute | solution.py:144
  32.1 5.7 %collective-permute-start.7 = (bf16[48,2048]{1,0:T(8,128)(2,1)S(1)}, bf16[48,2048]{1,0:T(8,128)(2,1)S(1)}, u32[]{:S(2)}, u32[]{:S(2)}) collective-permute-start(bf16[48,2048]{1,0:T(8,128)(2,1)S(1)} %get-tuple-element.91), channel_id=1, source_target_pairs={{0,2},{1,3},{2,0},{3,1},{4,6},{5,7},{6,4},{7,5},{8,10},{9,11},{10,... | collective-permute-start | bytes 589832 | tf_op jit(solution)/shard_map/ppermute | solution.py:144
  33.7 14.2 %collective-permute-start.9 = (bf16[96,2048]{1,0:T(8,128)(2,1)S(1)}, bf16[96,2048]{1,0:T(8,128)(2,1)S(1)}, u32[]{:S(2)}, u32[]{:S(2)}) collective-permute-start(bf16[96,2048]{1,0:T(8,128)(2,1)S(1)} %get-tuple-element.95.refs_3_), channel_id=1, source_target_pairs={{0,1},{1,0},{2,3},{3,2},{4,5},{5,4},{6,7},{7,6},{8,9},{9,8},{10,11... | collective-permute-start | bytes 1179656 | tf_op jit(solution)/shard_map/ppermute | solution.py:144
  37.9 10.0 %collective-permute-start.10 = (bf16[48,2048]{1,0:T(8,128)(2,1)S(1)}, bf16[48,2048]{1,0:T(8,128)(2,1)S(1)}, u32[]{:S(2)}, u32[]{:S(2)}) collective-permute-start(bf16[48,2048]{1,0:T(8,128)(2,1)S(1)} %get-tuple-element.96.refs_4_), channel_id=1, source_target_pairs={{0,1},{1,0},{2,3},{3,2},{4,5},{5,4},{6,7},{7,6},{8,9},{9,8},{10,11... | collective-permute-start | bytes 589832 | tf_op jit(solution)/shard_map/ppermute | solution.py:144
  48.5 4.1 %collective-permute-start.11 = (bf16[192,2048]{1,0:T(8,128)(2,1)S(1)}, bf16[192,2048]{1,0:T(8,128)(2,1)S(1)}, u32[]{:S(2)}, u32[]{:S(2)}) collective-permute-start(bf16[192,2048]{1,0:T(8,128)(2,1)S(1)} %get-tuple-element.107), channel_id=1, source_target_pairs={{0,8},{8,0},{16,24},{24,16},{1,9},{9,1},{17,25},{25,17},{2,10},{10... | collective-permute-start | bytes 2359304 | tf_op jit(solution)/shard_map/ppermute | solution.py:144
  52.0 6.7 %collective-permute-start.13 = (bf16[384,1536]{1,0:T(8,128)(2,1)S(1)}, bf16[384,1536]{1,0:T(8,128)(2,1)S(1)}, u32[]{:S(2)}, u32[]{:S(2)}) collective-permute-start(bf16[384,1536]{1,0:T(8,128)(2,1)S(1)} %get-tuple-element.110.refs_1_.refs_3_), channel_id=1, source_target_pairs={{0,8},{8,0},{16,24},{24,16},{1,9},{9,1},{17,25},{25,17},{2,10},{10... | collective-permute-start | bytes 3538952 | tf_op jit(solution)/shard_map/ppermute | solution.py:144
  52.1 6.6 %collective-permute-start.14 = (bf16[192,2048]{1,0:T(8,128)(2,1)S(1)}, bf16[192,2048]{1,0:T(8,128)(2,1)S(1)}, u32[]{:S(2)}, u32[]{:S(2)}) collective-permute-start(bf16[192,2048]{1,0:T(8,128)(2,1)S(1)} %get-tuple-element.115), channel_id=1, source_target_pairs={{0,8},{8,0},{16,24},{24,16},{1,9},{9,1},{17,25},{25,17},{2,10},{10... | collective-permute-start | bytes 2359304 | tf_op jit(solution)/shard_map/ppermute | solution.py:144
  52.8 20.4 %collective-permute-start.15 = (bf16[192,2048]{1,0:T(8,128)(2,1)S(1)}, bf16[192,2048]{1,0:T(8,128)(2,1)S(1)}, u32[]{:S(2)}, u32[]{:S(2)}) collective-permute-start(bf16[192,2048]{1,0:T(8,128)(2,1)S(1)} %get-tuple-element.118), channel_id=1, source_target_pairs={{0,16},{8,24},{16,0},{24,8},{1,17},{9,25},{17,1},{25,9},{2,18},{10... | collective-permute-start | bytes 2359304 | tf_op jit(solution)/shard_map/ppermute | solution.py:144
  54.4 20.0 %collective-permute-start.16 = (bf16[192,2048]{1,0:T(8,128)(2,1)S(1)}, bf16[192,2048]{1,0:T(8,128)(2,1)S(1)}, u32[]{:S(2)}, u32[]{:S(2)}) collective-permute-start(bf16[192,2048]{1,0:T(8,128)(2,1)S(1)} %get-tuple-element.121), channel_id=1, source_target_pairs={{0,1},{1,0},{2,3},{3,2},{4,5},{5,4},{6,7},{7,6},{8,9},{9,8},{10,11... | collective-permute-start | bytes 2359304 | tf_op jit(solution)/shard_map/ppermute | solution.py:144
  58.6 20.5 %collective-permute-start.17 = (bf16[192,2048]{1,0:T(8,128)(2,1)S(1)}, bf16[192,2048]{1,0:T(8,128)(2,1)S(1)}, u32[]{:S(2)}, u32[]{:S(2)}) collective-permute-start(bf16[192,2048]{1,0:T(8,128)(2,1)S(1)} %get-tuple-element.124), channel_id=1, source_target_pairs={{0,2},{1,3},{2,0},{3,1},{4,6},{5,7},{6,4},{7,5},{8,10},{9,11},{10,... | collective-permute-start | bytes 2359304 | tf_op jit(solution)/shard_map/ppermute | solution.py:144
  62.1 28.9 %collective-permute-start.20 = (bf16[512,768]{1,0:T(8,128)(2,1)S(1)}, bf16[512,768]{1,0:T(8,128)(2,1)S(1)}, u32[]{:S(2)}, u32[]{:S(2)}) collective-permute-start(bf16[512,768]{1,0:T(8,128)(2,1)S(1)} %get-tuple-element.135), channel_id=1, source_target_pairs={{0,16},{8,24},{16,0},{24,8},{1,17},{9,25},{17,1},{25,9},{2,18},{10... | collective-permute-start | bytes 2359304 | tf_op jit(solution)/shard_map/ppermute | solution.py:144
  74.7 11.5 %collective-permute-start.18 = (bf16[96,2048]{1,0:T(8,128)(2,1)S(1)}, bf16[96,2048]{1,0:T(8,128)(2,1)S(1)}, u32[]{:S(2)}, u32[]{:S(2)}) collective-permute-start(bf16[96,2048]{1,0:T(8,128)(2,1)S(1)} %get-tuple-element.127), channel_id=1, source_target_pairs={{0,2},{1,3},{2,0},{3,1},{4,6},{5,7},{6,4},{7,5},{8,10},{9,11},{10,... | collective-permute-start | bytes 1179656 | tf_op jit(solution)/shard_map/ppermute | solution.py:144
  79.3 10.6 %collective-permute-start.19 = (bf16[96,2048]{1,0:T(8,128)(2,1)S(1)}, bf16[96,2048]{1,0:T(8,128)(2,1)S(1)}, u32[]{:S(2)}, u32[]{:S(2)}) collective-permute-start(bf16[96,2048]{1,0:T(8,128)(2,1)S(1)} %get-tuple-element.132), channel_id=1, source_target_pairs={{0,1},{1,0},{2,3},{3,2},{4,5},{5,4},{6,7},{7,6},{8,9},{9,8},{10,11... | collective-permute-start | bytes 1179656 | tf_op jit(solution)/shard_map/ppermute | solution.py:144
  79.4 19.1 %collective-permute-start.21 = (bf16[256,768]{1,0:T(8,128)(2,1)S(1)}, bf16[256,768]{1,0:T(8,128)(2,1)S(1)}, u32[]{:S(2)}, u32[]{:S(2)}) collective-permute-start(bf16[256,768]{1,0:T(8,128)(2,1)S(1)} %get-tuple-element.138), channel_id=1, source_target_pairs={{0,16},{8,24},{16,0},{24,8},{1,17},{9,25},{17,1},{25,9},{2,18},{10... | collective-permute-start | bytes 1179656 | tf_op jit(solution)/shard_map/ppermute | solution.py:144
  86.3 20.4 %collective-permute-start.24 = (bf16[256,768]{1,0:T(8,128)(2,1)S(1)}, bf16[256,768]{1,0:T(8,128)(2,1)S(1)}, u32[]{:S(2)}, u32[]{:S(2)}) collective-permute-start(bf16[256,768]{1,0:T(8,128)(2,1)S(1)} %get-tuple-element.149), channel_id=1, source_target_pairs={{0,16},{8,24},{16,0},{24,8},{1,17},{9,25},{17,1},{25,9},{2,18},{10... | collective-permute-start | bytes 1179656 | tf_op jit(solution)/shard_map/ppermute | solution.py:144
  86.9 15.8 %collective-permute-start.22 = (bf16[48,2048]{1,0:T(8,128)(2,1)S(1)}, bf16[48,2048]{1,0:T(8,128)(2,1)S(1)}, u32[]{:S(2)}, u32[]{:S(2)}) collective-permute-start(bf16[48,2048]{1,0:T(8,128)(2,1)S(1)} %get-tuple-element.141), channel_id=1, source_target_pairs={{0,4},{1,5},{2,6},{3,7},{4,0},{5,1},{6,2},{7,3},{8,12},{9,13},{10,... | collective-permute-start | bytes 589832 | tf_op jit(solution)/shard_map/ppermute | solution.py:144
  90.0 16.0 %collective-permute-start.23 = (bf16[48,2048]{1,0:T(8,128)(2,1)S(1)}, bf16[48,2048]{1,0:T(8,128)(2,1)S(1)}, u32[]{:S(2)}, u32[]{:S(2)}) collective-permute-start(bf16[48,2048]{1,0:T(8,128)(2,1)S(1)} %get-tuple-element.145), channel_id=1, source_target_pairs={{0,4},{1,5},{2,6},{3,7},{4,0},{5,1},{6,2},{7,3},{8,12},{9,13},{10,... | collective-permute-start | bytes 589832 | tf_op jit(solution)/shard_map/ppermute | solution.py:144
  (1 other events, 2.6 us)

commit v6 on v5

--- a/solution.py
+++ b/solution.py
@@ -243,14 +243,14 @@
             after=after,
         )
 
-    tok_pair, done = copied([(tok_near, 0), (tok_far, 0)], wide, [done], [next_both])
+    tok_pair, done = copied([(tok_near, 0), (tok_far, 0)], wide, [done])
     cot_own, done = copied([(both, count)], width, [done])
     tok_far_on, done = copied([(tok_far, 0)], wide, [done])
     next_tok_pair = swap(tok_pair, "expert", 1)
     tok_last = swap(tok_far_on, "expert", near_bit)
     cot_far = swap(cot_own, "expert", far_bit)
     cot_near = swap(cot_own, "expert", near_bit)
-    tok_last_on, done = copied([(tok_last, 0)], wide, [done])
+    tok_last_on, done = copied([(tok_last, 0)], wide, [done], [next_both])
     next_tok_last = swap(tok_last_on, "expert", 1)
     cot_pair, done = copied([(cot_near, 0), (cot_far, 0)], width, [done], [next_tok_pair])
     cot_far_on, done = copied([(cot_far, 0)], width, [done])
@@ -375,15 +375,15 @@
     )
     down_came = swap(down_away, "dp", 1)
 
-    def down_rest(own_ref, left, cot, _, away, send, kept, same):
-        products([1, 2, 0], left, cot, [(away, 0), (send, 0), (kept, 0)], own_ref[0])
-
-    last_away, down_send, down_kept, flipped_sent, done = stage(
+    def down_rest(own_ref, left, cot, _, away, send, same):
+        products([2, 1], left, cot, [(send, 0), (away, 0)], own_ref[0])
+
+    last_away, down_send, flipped_sent, done = stage(
         down_rest,
         [(mine, SMEM), (hidden_t, VMEM), (cot_rows, VMEM), (flipped_sent, ANY)],
-        [((slab, width), BF16, VMEM)] * 3 + [(flipped_sent.shape, BF16, ANY)],
-        after=[done],
-        aliases={3: 3},
+        [((slab, width), BF16, VMEM)] * 2 + [(flipped_sent.shape, BF16, ANY)],
+        after=[done],
+        aliases={3: 2},
     )
     flipped_came = swap(flipped_sent, "dp", 1)
     last_came = swap(last_away, "dp", 1)
@@ -415,28 +415,34 @@
     )
     down_got = swap(down_send, "dp", 2)
 
-    def input_rows(grad, gate, up, kept, sent):
+    side = width // 2
+
+    def input_rows(grad, gate, up, _, *outs):
         for start, size in chunks(width, 512):
+            kept, sent = outs[2 * (start // side)], outs[2 * (start // side) + 1]
             place = slice(start, start + size)
             rows = lax.dot_general(grad[:, :ff], gate[place, :], TURNED, preferred_element_type=F32)
             rows = rows + lax.dot_general(
                 grad[:, ff:], up[place, :], TURNED, preferred_element_type=F32
             )
             rows = rows.astype(BF16)
+            there = slice(start % side, start % side + size)
             for i in range(2):
                 low, high = slice(i * pair, (i + 1) * pair), i * half
-                kept[low, place] = rows[high : high + pair]
-                sent[low, place] = rows[high + pair : high + half]
-
-    in_kept, in_sent, done = stage(
+                kept[low, there] = rows[high : high + pair]
+                sent[low, there] = rows[high + pair : high + half]
+
+    left_kept, left_sent, right_kept, right_sent, done = stage(
         input_rows,
-        [(grads, VMEM), (gate_near, VMEM), (up_near, VMEM)],
-        [((half, width), BF16, VMEM)] * 2,
-        after=[done],
-    )
-    in_came = swap(in_sent, "expert", near_bit)
-
-    def both_parts(left, left_came, grad, grad_came, _, gate_send, up_high, up_low, gate_kept, up_kept):
+        [(grads, VMEM), (gate_near, VMEM), (up_near, VMEM), (last_came, ANY)],
+        [((half, side), BF16, VMEM)] * 4,
+        after=[done],
+    )
+    left_came, right_came = [swap(a, "expert", near_bit) for a in (left_sent, right_sent)]
+
+    cut = 3 * band // 4
+
+    def both_parts(left, left_came, grad, grad_came, gate_send, up_high, up_low, gate_kept, up_kept):
         for j, (gate_out, up_out) in enumerate([(gate_send, None), (gate_kept, up_kept)]):
             row = slice(j * band, (j + 1) * band)
             for start, size in chunks(2 * ff, 256):
@@ -449,19 +455,28 @@
                 elif up_out is not None:
                     up_out[:, place] = value.astype(up_out.dtype)
                 else:
-                    up_high[:, place] = value[: band // 2].astype(BF16)
-                    up_low[:, place] = value[band // 2 :].astype(BF16)
+                    up_high[:, place] = value[:cut].astype(BF16)
+                    up_low[:, place] = value[cut:].astype(BF16)
 
     gate_send, up_high, up_low, gate_kept, up_kept, done = stage(
         both_parts,
-        [(a, VMEM) for a in (flipped, flipped_came, grads, grads_came)] + [(last_came, ANY)],
+        [(a, VMEM) for a in (flipped, flipped_came, grads, grads_came)],
         [((band, ff), BF16, VMEM)]
-        + [((band // 2, ff), BF16, VMEM)] * 2
+        + [((cut, ff), BF16, VMEM), ((band - cut, ff), BF16, VMEM)]
         + [((band, ff), F32, VMEM)] * 2,
         after=[done],
     )
     gate_got = swap(gate_send, "dp", 2)
-    high_got = swap(up_high, "dp", 2)
+
+    def down_own(own_ref, left, cot, kept):
+        products([0], left, cot, [(kept, 0)], own_ref[0])
+
+    down_kept, done = stage(
+        down_own,
+        [(mine, SMEM), (hidden_t, VMEM), (cot_rows, VMEM)],
+        [((slab, width), F32, VMEM)],
+        after=[done],
+    )
 
     def folded(held, came, after, waits=()):
         rows = held.shape[0]
@@ -475,7 +490,7 @@
         return stage(
             body,
             [(held, VMEM), (came, VMEM)] + [(a, ANY) for a in waits],
-            [((rows // parts, width), BF16, VMEM)] * parts,
+            [((rows // parts, held.shape[1]), BF16, VMEM)] * parts,
             after=after,
         )
 
@@ -494,7 +509,8 @@
                 there = slice(first + i * step, first + (i + 1) * step)
                 value = refs[0][there, :].astype(F32)
                 for ref in refs[1:n]:
-                    value = value + ref[at, :].astype(F32)
+                    last = ref.shape[0] - size + i * step
+                    value = value + ref[last : last + step, :].astype(F32)
                 total[at, :] = value
                 copies.append(pltpu.make_async_copy(total.at[at], out.at[there], sems.at[i]))
                 copies[-1].start()
@@ -510,24 +526,45 @@
             aliases=None if into is None else {n: 0},
         )
 
-    def fold_on(held, came, bit, after):
-        held, send, done = folded(held, came, after)
+    def fold_on(held, came, bit, after, waits=()):
+        held, send, done = folded(held, came, after, waits)
         return held, swap(send, "expert", bit), done
 
+    def gated(a, after, waits=()):
+        return stage(
+            lambda *_: None,
+            [(b, ANY) for b in (a, *waits)],
+            [(a.shape, a.dtype, ANY)],
+            after=after,
+            aliases={0: 0},
+        )
+
+    left_held, left_came, done = fold_on(left_kept, left_came, 1, [done])
     down_grad, done = owned([down_kept, last_came, down_got], [done])
     out_held, out_came, done = fold_on(out_kept, out_came, near_bit, [done])
-    in_held, in_came, done = fold_on(in_kept, in_came, 1, [done])
+    right_held, right_came, done = fold_on(right_kept, right_came, 1, [done])
+    left_held, left_came, done = fold_on(left_held, left_came, far_bit, [done])
+    up_high, done = gated(up_high, [done])
+    high_got = swap(up_high, "dp", 2)
+    up_low, done = gated(up_low, [done], [left_came])
+    low_got = swap(up_low, "dp", 2)
+    right_held, right_came, done = fold_on(right_held, right_came, far_bit, [done])
     out_held, out_came, done = fold_on(out_held, out_came, far_bit, [done])
-    up_low, done = stage(
-        lambda *_: None, [(up_low, ANY)], [(up_low.shape, BF16, ANY)], after=[done], aliases={0: 0}
-    )
-    low_got = swap(up_low, "dp", 2)
-    in_held, in_came, done = fold_on(in_held, in_came, far_bit, [done])
+
+    def widened(a, b, c, d, out):
+        out[:, :side] = (a[...].astype(F32) + b[...].astype(F32)).astype(BF16)
+        out[:, side:] = (c[...].astype(F32) + d[...].astype(F32)).astype(BF16)
+
     gate_part, done = owned([gate_kept, gate_got], [done])
+    layer_out, done = folded(out_held, out_came, [done])
     up_part, done = owned([up_kept, high_got], [done])
-    layer_out, done = folded(out_held, out_came, [done])
-    input_grad, done = folded(in_held, in_came, [done])
-    up_part, _ = owned([up_kept, low_got], [done], band // 2, up_part)
+    input_grad, done = stage(
+        widened,
+        [(a, VMEM) for a in (left_held, left_came, right_held, right_came)],
+        [((count, width), BF16, VMEM)],
+        after=[done],
+    )
+    up_part, _ = owned([up_kept, low_got], [done], cut, up_part)
     return (layer_out, input_grad, gate_part[None], up_part[None], down_grad[None])
 
 

time: 108 us -> 107 us (level)
  waiting for transfers between devices: 53.8 us -> 48.6 us
  starting transfers between devices: 28.3 us -> 32.3 us
    ppermute x25 -> x28, waiting for transfers between devices: 53.8 us -> 48.6 us  [swap(): return lax.ppermute(value, axis, [(i, i ^ mask) for i in range(size)])]
    ppermute x25 -> x28, starting transfers between devices: 28.3 us -> 32.3 us  [swap(): return lax.ppermute(value, axis, [(i, i ^ mask) for i in range(size)])]
    pallas_call x26 -> x30, Pallas kernels: 25.2 us -> 25.4 us  [stage(): pl.pallas_call(kernel, in_specs=[pl.BlockSpec(memory_space=VMEM if m == P...]
  transfers between devices with their start and end apart: 25 -> 28, of which waited for: 13 -> 18; matrix products, arithmetic and copies ran while one was open for 0% -> 0% of each run, Pallas kernels for 20% -> 21%
where the time goes in v6:
time: 107 us
  waiting for transfers between devices  48.6 us (45%)
  starting transfers between devices  32.3 us (30%)
  Pallas kernels  25.4 us (24%)
    ppermute x28, waiting for transfers between devices, swap(): return lax.ppermute(value, axis, [(i, i ^ mask) for i in range(size)])  48.6 us
    ppermute x28, starting transfers between devices, swap(): return lax.ppermute(value, axis, [(i, i ^ mask) for i in range(size)])  32.3 us
    pallas_call x30, Pallas kernels, stage(): pl.pallas_call(kernel, in_specs=[pl.BlockSpec(memory_space=VMEM if m == P...  25.4 us
  transfers between devices with their start and end apart: 28, of which 18 were waited for; matrix products, arithmetic and copies ran while one was open for 0% of the time, Pallas kernels for 21%

profile of v6, /device:TPU:0, one launch (start us, length us, event | category | flops | bytes accessed | tf_op | source)
XLA Modules:
  0.0 107.1 jit_solution(1807013319508548658)
XLA Ops:
  1.8 4.1 %collective-permute-start.1 = (bf16[48,2176]{1,0:T(8,128)(2,1)S(1)}, bf16[48,2176]{1,0:T(8,128)(2,1)S(1)}, u32[]{:S(2)}, u32[]{:S(2)}) collective-permute-start(bf16[48,2176]{1,0:T(8,128)(2,1)S(1)} %get-tuple-element.91.refs_3_), channel_id=1, source_target_pairs={{0,4},{1,5},{2,6},{3,7},{4,0},{5,1},{6,2},{7,3},{8,12},{9,13},{10,... | collective-permute-start | bytes 626696 | tf_op jit(solution)/shard_map/ppermute | solution.py:144
  5.9 1.6 %collective-permute-start = (bf16[48,2176]{1,0:T(8,128)(2,1)S(1)}, bf16[48,2176]{1,0:T(8,128)(2,1)S(1)}, u32[]{:S(2)}, u32[]{:S(2)}) collective-permute-start(bf16[48,2176]{1,0:T(8,128)(2,1)S(1)} %get-tuple-element.91.refs_3_), channel_id=1, source_target_pairs={{0,2},{1,3},{2,0},{3,1},{4,6},{5,7},{6,4},{7,5},{8,10},{9,11},{10,... | collective-permute-start | bytes 626696 | tf_op jit(solution)/shard_map/ppermute | solution.py:144
  9.0 6.6 %collective-permute-done.1.refs_2_.refs_1_ = bf16[48,2176]{1,0:T(8,128)(2,1)S(1)} collective-permute-done((bf16[48,2176]{1,0:T(8,128)(2,1)S(1)}, bf16[48,2176]{1,0:T(8,128)(2,1)S(1)}, u32[]{:S(2)}, u32[]{:S(2)}) %collective-permute-start.1) | collective-permute-done | bytes 208928 | tf_op jit(solution)/shard_map/ppermute | solution.py:144
  15.9 1.6 %collective-permute-start.6 = (bf16[96,2176]{1,0:T(8,128)(2,1)S(1)}, bf16[96,2176]{1,0:T(8,128)(2,1)S(1)}, u32[]{:S(2)}, u32[]{:S(2)}) collective-permute-start(bf16[96,2176]{1,0:T(8,128)(2,1)S(1)} %get-tuple-element.99.refs_4_), channel_id=1, source_target_pairs={{0,1},{1,0},{2,3},{3,2},{4,5},{5,4},{6,7},{7,6},{8,9},{9,8},{10,11... | collective-permute-start | bytes 1253384 | tf_op jit(solution)/shard_map/ppermute | solution.py:144
  19.1 2.3 %collective-permute-start.5 = (bf16[48,2048]{1,0:T(8,128)(2,1)S(1)}, bf16[48,2048]{1,0:T(8,128)(2,1)S(1)}, u32[]{:S(2)}, u32[]{:S(2)}) collective-permute-start(bf16[48,2048]{1,0:T(8,128)(2,1)S(1)} %get-tuple-element.98.refs_2_), channel_id=1, source_target_pairs={{0,4},{1,5},{2,6},{3,7},{4,0},{5,1},{6,2},{7,3},{8,12},{9,13},{10,... | collective-permute-start | bytes 589832 | tf_op jit(solution)/shard_map/ppermute | solution.py:144
  21.5 7.7 %collective-permute-done.2.refs_1_ = bf16[48,2176]{1,0:T(8,128)(2,1)S(1)} collective-permute-done((bf16[48,2176]{1,0:T(8,128)(2,1)S(1)}, bf16[48,2176]{1,0:T(8,128)(2,1)S(1)}, u32[]{:S(2)}, u32[]{:S(2)}) %collective-permute-start.2) | collective-permute-done | bytes 208928 | tf_op jit(solution)/shard_map/ppermute | solution.py:144
  29.8 2.1 %collective-permute-done.4.refs_1_ = bf16[48,2048]{1,0:T(8,128)(2,1)S(1)} collective-permute-done((bf16[48,2048]{1,0:T(8,128)(2,1)S(1)}, bf16[48,2048]{1,0:T(8,128)(2,1)S(1)}, u32[]{:S(2)}, u32[]{:S(2)}) %collective-permute-start.4) | collective-permute-done | bytes 196640 | tf_op jit(solution)/shard_map/ppermute | solution.py:144
  33.9 1.8 %collective-permute-done.8.refs_2_.refs_8_ = bf16[48,2176]{1,0:T(8,128)(2,1)S(1)} collective-permute-done((bf16[48,2176]{1,0:T(8,128)(2,1)S(1)}, bf16[48,2176]{1,0:T(8,128)(2,1)S(1)}, u32[]{:S(2)}, u32[]{:S(2)}) %collective-permute-start.8) | collective-permute-done | bytes 208928 | tf_op jit(solution)/shard_map/ppermute | solution.py:144
  35.8 1.9 %collective-permute-done.7.refs_1_ = bf16[48,2048]{1,0:T(8,128)(2,1)S(1)} collective-permute-done((bf16[48,2048]{1,0:T(8,128)(2,1)S(1)}, bf16[48,2048]{1,0:T(8,128)(2,1)S(1)}, u32[]{:S(2)}, u32[]{:S(2)}) %collective-permute-start.7) | collective-permute-done | bytes 196640 | tf_op jit(solution)/shard_map/ppermute | solution.py:144
  38.2 7.3 %shard_map.118 = (bf16[1024,384]{1,0:T(8,128)(2,1)S(1)}, bf16[1024,384]{1,0:T(8,128)(2,1)S(1)}, bf16[768,384]{1,0:T(8,128)(2,1)S(1)}, f32[384,768]{1,0:T(8,128)S...) custom-call(f32[8,128]{1,0:T(8,128)S(1)} %get-tuple-element.104.refs, ...), custom_call_target="tpu_custom_call" | custom-call | tf_op jit(solution)/shard_map/pallas_call | solution.py:126
  45.5 2.3 %collective-permute-done.10.refs_7_ = bf16[48,2048]{1,0:T(8,128)(2,1)S(1)} collective-permute-done((bf16[48,2048]{1,0:T(8,128)(2,1)S(1)}, bf16[48,2048]{1,0:T(8,128)(2,1)S(1)}, u32[]{:S(2)}, u32[]{:S(2)}) %collective-permute-start.10) | collective-permute-done | bytes 196640 | tf_op jit(solution)/shard_map/ppermute | solution.py:144
  52.3 1.5 %collective-permute-start.16 = (bf16[192,2048]{1,0:T(8,128)(2,1)S(1)}, bf16[192,2048]{1,0:T(8,128)(2,1)S(1)}, u32[]{:S(2)}, u32[]{:S(2)}) collective-permute-start(bf16[192,2048]{1,0:T(8,128)(2,1)S(1)} %get-tuple-element.133), channel_id=1, source_target_pairs={{0,16},{8,24},{16,0},{24,8},{1,17},{9,25},{17,1},{25,9},{2,18},{10... | collective-permute-start | bytes 2359304 | tf_op jit(solution)/shard_map/ppermute | solution.py:144
  54.3 2.6 %shard_map.123 = (bf16[192,1024]{1,0:T(8,128)(2,1)S(1)}, bf16[192,1024]{1,0:T(8,128)(2,1)S(1)}, bf16[192,1024]{1,0:T(8,128)(2,1)S(1)}, bf16[192,1024]{1,0:T(8,128)(2,1)S(1)}, f32[8,128]{1,0:T(8,128)S(1)}) custom-call(f32[8,128]{1,0:T(8,128)S(1)} %get-tuple-element.120.refs_0_, bf16[384,1536]{1,0:T(8,128)(2,1)S(1)} %get-tuple-element.121.refs_1_.refs_3_, ...), custom_call_target="tpu_custom_call" | custom-call | tf_op jit(solution)/shard_map/pallas_call | solution.py:126
  57.2 1.8 %collective-permute-start.18 = (bf16[192,1024]{1,0:T(8,128)(2,1)S(1)}, bf16[192,1024]{1,0:T(8,128)(2,1)S(1)}, u32[]{:S(2)}, u32[]{:S(2)}) collective-permute-start(bf16[192,1024]{1,0:T(8,128)(2,1)S(1)} %get-tuple-element.139), channel_id=1, source_target_pairs={{0,2},{1,3},{2,0},{3,1},{4,6},{5,7},{6,4},{7,5},{8,10},{9,11},{10,... | collective-permute-start | bytes 1179656 | tf_op jit(solution)/shard_map/ppermute | solution.py:144
  59.0 3.4 %shard_map.124 = (bf16[512,768]{1,0:T(8,128)(2,1)S(1)}, bf16[384,768]{1,0:T(8,128)(2,1)S(1)}, bf16[128,768]{1,0:T(8,128)(2,1)S(1)}, f32[512,768]{1,0:T(8,128)S(1...) custom-call(f32[8,128]{1,0:T(8,128)S(1)} %get-tuple-element.125.refs_0_, ...), custom_call_target="tpu_custom_call" | custom-call | tf_op jit(solution)/shard_map/pallas_call | solution.py:126
  63.0 6.0 %collective-permute-done.15.refs_2_ = bf16[192,1024]{1,0:T(8,128)(2,1)S(1)} collective-permute-done((bf16[192,1024]{1,0:T(8,128)(2,1)S(1)}, bf16[192,1024]{1,0:T(8,128)(2,1)S(1)}, u32[]{:S(2)}, u32[]{:S(2)}) %collective-permute-start.15) | collective-permute-done | bytes 393248 | tf_op jit(solution)/shard_map/ppermute | solution.py:144
  69.1 1.6 %collective-permute-start.19 = (bf16[96,1024]{1,0:T(8,128)(2,1)S(1)}, bf16[96,1024]{1,0:T(8,128)(2,1)S(1)}, u32[]{:S(2)}, u32[]{:S(2)}) collective-permute-start(bf16[96,1024]{1,0:T(8,128)(2,1)S(1)} %get-tuple-element.142), channel_id=1, source_target_pairs={{0,1},{1,0},{2,3},{3,2},{4,5},{5,4},{6,7},{7,6},{8,9},{9,8},{10,11... | collective-permute-start | bytes 589832 | tf_op jit(solution)/shard_map/ppermute | solution.py:144
  74.5 2.2 %collective-permute-done.18.refs_2_ = bf16[192,1024]{1,0:T(8,128)(2,1)S(1)} collective-permute-done((bf16[192,1024]{1,0:T(8,128)(2,1)S(1)}, bf16[192,1024]{1,0:T(8,128)(2,1)S(1)}, u32[]{:S(2)}, u32[]{:S(2)}) %collective-permute-start.18) | collective-permute-done | bytes 393248 | tf_op jit(solution)/shard_map/ppermute | solution.py:144
  79.3 3.0 %collective-permute-start.20 = (bf16[48,1024]{1,0:T(8,128)(2,1)S(1)}, bf16[48,1024]{1,0:T(8,128)(2,1)S(1)}, u32[]{:S(2)}, u32[]{:S(2)}) collective-permute-start(bf16[48,1024]{1,0:T(8,128)(2,1)S(1)} %get-tuple-element.147), channel_id=1, source_target_pairs={{0,4},{1,5},{2,6},{3,7},{4,0},{5,1},{6,2},{7,3},{8,12},{9,13},{10,... | collective-permute-start | bytes 294920 | tf_op jit(solution)/shard_map/ppermute | solution.py:144
  82.3 2.7 %collective-permute-done.20.refs_2_ = bf16[48,1024]{1,0:T(8,128)(2,1)S(1)} collective-permute-done((bf16[48,1024]{1,0:T(8,128)(2,1)S(1)}, bf16[48,1024]{1,0:T(8,128)(2,1)S(1)}, u32[]{:S(2)}, u32[]{:S(2)}) %collective-permute-start.20) | collective-permute-done | bytes 98336 | tf_op jit(solution)/shard_map/ppermute | solution.py:144
  85.0 1.7 %collective-permute-done.22.refs_2_ = bf16[96,2048]{1,0:T(8,128)(2,1)S(1)} collective-permute-done((bf16[96,2048]{1,0:T(8,128)(2,1)S(1)}, bf16[96,2048]{1,0:T(8,128)(2,1)S(1)}, u32[]{:S(2)}, u32[]{:S(2)}) %collective-permute-start.22) | collective-permute-done | bytes 393248 | tf_op jit(solution)/shard_map/ppermute | solution.py:144
  86.8 2.0 %collective-permute-start.24 = (bf16[48,2048]{1,0:T(8,128)(2,1)S(1)}, bf16[48,2048]{1,0:T(8,128)(2,1)S(1)}, u32[]{:S(2)}, u32[]{:S(2)}) collective-permute-start(bf16[48,2048]{1,0:T(8,128)(2,1)S(1)} %get-tuple-element.159), channel_id=1, source_target_pairs={{0,4},{1,5},{2,6},{3,7},{4,0},{5,1},{6,2},{7,3},{8,12},{9,13},{10,... | collective-permute-start | bytes 589832 | tf_op jit(solution)/shard_map/ppermute | solution.py:144
  92.4 7.7 %collective-permute-done.24.refs_2_ = bf16[48,2048]{1,0:T(8,128)(2,1)S(1)} collective-permute-done((bf16[48,2048]{1,0:T(8,128)(2,1)S(1)}, bf16[48,2048]{1,0:T(8,128)(2,1)S(1)}, u32[]{:S(2)}, u32[]{:S(2)}) %collective-permute-start.24) | collective-permute-done | bytes 196640 | tf_op jit(solution)/shard_map/ppermute | solution.py:144
  100.8 2.8 %collective-permute-done.25.refs_2_ = bf16[384,768]{1,0:T(8,128)(2,1)S(1)} collective-permute-done((bf16[384,768]{1,0:T(8,128)(2,1)S(1)}, bf16[384,768]{1,0:T(8,128)(2,1)S(1)}, u32[]{:S(2)}, u32[]{:S(2)}) %collective-permute-start.25) | collective-permute-done | bytes 589856 | tf_op jit(solution)/shard_map/ppermute | solution.py:144
  (62 shorter events, 28.0 us)
Async XLA Ops:
  1.8 13.8 %collective-permute-start.1 = (bf16[48,2176]{1,0:T(8,128)(2,1)S(1)}, bf16[48,2176]{1,0:T(8,128)(2,1)S(1)}, u32[]{:S(2)}, u32[]{:S(2)}) collective-permute-start(bf16[48,2176]{1,0:T(8,128)(2,1)S(1)} %get-tuple-element.91.refs_3_), channel_id=1, source_target_pairs={{0,4},{1,5},{2,6},{3,7},{4,0},{5,1},{6,2},{7,3},{8,12},{9,13},{10,... | collective-permute-start | bytes 626696 | tf_op jit(solution)/shard_map/ppermute | solution.py:144
  5.9 9.9 %collective-permute-start = (bf16[48,2176]{1,0:T(8,128)(2,1)S(1)}, bf16[48,2176]{1,0:T(8,128)(2,1)S(1)}, u32[]{:S(2)}, u32[]{:S(2)}) collective-permute-start(bf16[48,2176]{1,0:T(8,128)(2,1)S(1)} %get-tuple-element.91.refs_3_), channel_id=1, source_target_pairs={{0,2},{1,3},{2,0},{3,1},{4,6},{5,7},{6,4},{7,5},{8,10},{9,11},{10,... | collective-permute-start | bytes 626696 | tf_op jit(solution)/shard_map/ppermute | solution.py:144
  7.5 21.7 %collective-permute-start.3 = (bf16[96,2176]{1,0:T(8,128)(2,1)S(1)}, bf16[96,2176]{1,0:T(8,128)(2,1)S(1)}, u32[]{:S(2)}, u32[]{:S(2)}) collective-permute-start(bf16[96,2176]{1,0:T(8,128)(2,1)S(1)} %get-tuple-element.93.refs_1_), channel_id=1, source_target_pairs={{0,1},{1,0},{2,3},{3,2},{4,5},{5,4},{6,7},{7,6},{8,9},{9,8},{10,11... | collective-permute-start | bytes 1253384 | tf_op jit(solution)/shard_map/ppermute | solution.py:144
  15.9 16.0 %collective-permute-start.6 = (bf16[96,2176]{1,0:T(8,128)(2,1)S(1)}, bf16[96,2176]{1,0:T(8,128)(2,1)S(1)}, u32[]{:S(2)}, u32[]{:S(2)}) collective-permute-start(bf16[96,2176]{1,0:T(8,128)(2,1)S(1)} %get-tuple-element.99.refs_4_), channel_id=1, source_target_pairs={{0,1},{1,0},{2,3},{3,2},{4,5},{5,4},{6,7},{7,6},{8,9},{9,8},{10,11... | collective-permute-start | bytes 1253384 | tf_op jit(solution)/shard_map/ppermute | solution.py:144
  17.6 11.6 %collective-permute-start.2 = (bf16[48,2176]{1,0:T(8,128)(2,1)S(1)}, bf16[48,2176]{1,0:T(8,128)(2,1)S(1)}, u32[]{:S(2)}, u32[]{:S(2)}) collective-permute-start(bf16[48,2176]{1,0:T(8,128)(2,1)S(1)} %get-tuple-element.96), channel_id=1, source_target_pairs={{0,2},{1,3},{2,0},{3,1},{4,6},{5,7},{6,4},{7,5},{8,10},{9,11},{10,... | collective-permute-start | bytes 626696 | tf_op jit(solution)/shard_map/ppermute | solution.py:144
  19.1 10.7 %collective-permute-start.5 = (bf16[48,2048]{1,0:T(8,128)(2,1)S(1)}, bf16[48,2048]{1,0:T(8,128)(2,1)S(1)}, u32[]{:S(2)}, u32[]{:S(2)}) collective-permute-start(bf16[48,2048]{1,0:T(8,128)(2,1)S(1)} %get-tuple-element.98.refs_2_), channel_id=1, source_target_pairs={{0,4},{1,5},{2,6},{3,7},{4,0},{5,1},{6,2},{7,3},{8,12},{9,13},{10,... | collective-permute-start | bytes 589832 | tf_op jit(solution)/shard_map/ppermute | solution.py:144
  21.4 10.5 %collective-permute-start.4 = (bf16[48,2048]{1,0:T(8,128)(2,1)S(1)}, bf16[48,2048]{1,0:T(8,128)(2,1)S(1)}, u32[]{:S(2)}, u32[]{:S(2)}) collective-permute-start(bf16[48,2048]{1,0:T(8,128)(2,1)S(1)} %get-tuple-element.98.refs_2_), channel_id=1, source_target_pairs={{0,2},{1,3},{2,0},{3,1},{4,6},{5,7},{6,4},{7,5},{8,10},{9,11},{10,... | collective-permute-start | bytes 589832 | tf_op jit(solution)/shard_map/ppermute | solution.py:144
  29.3 6.5 %collective-permute-start.8 = (bf16[48,2176]{1,0:T(8,128)(2,1)S(1)}, bf16[48,2176]{1,0:T(8,128)(2,1)S(1)}, u32[]{:S(2)}, u32[]{:S(2)}) collective-permute-start(bf16[48,2176]{1,0:T(8,128)(2,1)S(1)} %get-tuple-element.103.refs_5_), channel_id=1, source_target_pairs={{0,1},{1,0},{2,3},{3,2},{4,5},{5,4},{6,7},{7,6},{8,9},{9,8},{10,11... | collective-permute-start | bytes 626696 | tf_op jit(solution)/shard_map/ppermute | solution.py:144
  31.9 5.7 %collective-permute-start.7 = (bf16[48,2048]{1,0:T(8,128)(2,1)S(1)}, bf16[48,2048]{1,0:T(8,128)(2,1)S(1)}, u32[]{:S(2)}, u32[]{:S(2)}) collective-permute-start(bf16[48,2048]{1,0:T(8,128)(2,1)S(1)} %get-tuple-element.102), channel_id=1, source_target_pairs={{0,2},{1,3},{2,0},{3,1},{4,6},{5,7},{6,4},{7,5},{8,10},{9,11},{10,... | collective-permute-start | bytes 589832 | tf_op jit(solution)/shard_map/ppermute | solution.py:144
  33.4 14.3 %collective-permute-start.9 = (bf16[96,2048]{1,0:T(8,128)(2,1)S(1)}, bf16[96,2048]{1,0:T(8,128)(2,1)S(1)}, u32[]{:S(2)}, u32[]{:S(2)}) collective-permute-start(bf16[96,2048]{1,0:T(8,128)(2,1)S(1)} %get-tuple-element.106.refs_3_), channel_id=1, source_target_pairs={{0,1},{1,0},{2,3},{3,2},{4,5},{5,4},{6,7},{7,6},{8,9},{9,8},{10,11... | collective-permute-start | bytes 1179656 | tf_op jit(solution)/shard_map/ppermute | solution.py:144
  37.7 10.1 %collective-permute-start.10 = (bf16[48,2048]{1,0:T(8,128)(2,1)S(1)}, bf16[48,2048]{1,0:T(8,128)(2,1)S(1)}, u32[]{:S(2)}, u32[]{:S(2)}) collective-permute-start(bf16[48,2048]{1,0:T(8,128)(2,1)S(1)} %get-tuple-element.107.refs_4_), channel_id=1, source_target_pairs={{0,1},{1,0},{2,3},{3,2},{4,5},{5,4},{6,7},{7,6},{8,9},{9,8},{10,11... | collective-permute-start | bytes 589832 | tf_op jit(solution)/shard_map/ppermute | solution.py:144
  51.6 7.5 %collective-permute-start.14 = (bf16[384,1536]{1,0:T(8,128)(2,1)S(1)}, bf16[384,1536]{1,0:T(8,128)(2,1)S(1)}, u32[]{:S(2)}, u32[]{:S(2)}) collective-permute-start(bf16[384,1536]{1,0:T(8,128)(2,1)S(1)} %get-tuple-element.121.refs_1_.refs_3_), channel_id=1, source_target_pairs={{0,8},{8,0},{16,24},{24,16},{1,9},{9,1},{17,25},{25,17},{2,10},{10... | collective-permute-start | bytes 3538952 | tf_op jit(solution)/shard_map/ppermute | solution.py:144
  52.3 20.4 %collective-permute-start.16 = (bf16[192,2048]{1,0:T(8,128)(2,1)S(1)}, bf16[192,2048]{1,0:T(8,128)(2,1)S(1)}, u32[]{:S(2)}, u32[]{:S(2)}) collective-permute-start(bf16[192,2048]{1,0:T(8,128)(2,1)S(1)} %get-tuple-element.133), channel_id=1, source_target_pairs={{0,16},{8,24},{16,0},{24,8},{1,17},{9,25},{17,1},{25,9},{2,18},{10... | collective-permute-start | bytes 2359304 | tf_op jit(solution)/shard_map/ppermute | solution.py:144
  53.8 20.4 %collective-permute-start.17 = (bf16[192,2048]{1,0:T(8,128)(2,1)S(1)}, bf16[192,2048]{1,0:T(8,128)(2,1)S(1)}, u32[]{:S(2)}, u32[]{:S(2)}) collective-permute-start(bf16[192,2048]{1,0:T(8,128)(2,1)S(1)} %get-tuple-element.136), channel_id=1, source_target_pairs={{0,1},{1,0},{2,3},{3,2},{4,5},{5,4},{6,7},{7,6},{8,9},{9,8},{10,11... | collective-permute-start | bytes 2359304 | tf_op jit(solution)/shard_map/ppermute | solution.py:144
  56.9 12.1 %collective-permute-start.15 = (bf16[192,1024]{1,0:T(8,128)(2,1)S(1)}, bf16[192,1024]{1,0:T(8,128)(2,1)S(1)}, u32[]{:S(2)}, u32[]{:S(2)}) collective-permute-start(bf16[192,1024]{1,0:T(8,128)(2,1)S(1)} %get-tuple-element.130), channel_id=1, source_target_pairs={{0,2},{1,3},{2,0},{3,1},{4,6},{5,7},{6,4},{7,5},{8,10},{9,11},{10,... | collective-permute-start | bytes 1179656 | tf_op jit(solution)/shard_map/ppermute | solution.py:144
  57.2 19.4 %collective-permute-start.18 = (bf16[192,1024]{1,0:T(8,128)(2,1)S(1)}, bf16[192,1024]{1,0:T(8,128)(2,1)S(1)}, u32[]{:S(2)}, u32[]{:S(2)}) collective-permute-start(bf16[192,1024]{1,0:T(8,128)(2,1)S(1)} %get-tuple-element.139), channel_id=1, source_target_pairs={{0,2},{1,3},{2,0},{3,1},{4,6},{5,7},{6,4},{7,5},{8,10},{9,11},{10,... | collective-permute-start | bytes 1179656 | tf_op jit(solution)/shard_map/ppermute | solution.py:144
  69.1 8.3 %collective-permute-start.19 = (bf16[96,1024]{1,0:T(8,128)(2,1)S(1)}, bf16[96,1024]{1,0:T(8,128)(2,1)S(1)}, u32[]{:S(2)}, u32[]{:S(2)}) collective-permute-start(bf16[96,1024]{1,0:T(8,128)(2,1)S(1)} %get-tuple-element.142), channel_id=1, source_target_pairs={{0,1},{1,0},{2,3},{3,2},{4,5},{5,4},{6,7},{7,6},{8,9},{9,8},{10,11... | collective-permute-start | bytes 589832 | tf_op jit(solution)/shard_map/ppermute | solution.py:144
  70.7 20.5 %collective-permute-start.23 = (bf16[512,768]{1,0:T(8,128)(2,1)S(1)}, bf16[512,768]{1,0:T(8,128)(2,1)S(1)}, u32[]{:S(2)}, u32[]{:S(2)}) collective-permute-start(bf16[512,768]{1,0:T(8,128)(2,1)S(1)} %get-tuple-element.156), channel_id=1, source_target_pairs={{0,16},{8,24},{16,0},{24,8},{1,17},{9,25},{17,1},{25,9},{2,18},{10... | collective-permute-start | bytes 2359304 | tf_op jit(solution)/shard_map/ppermute | solution.py:144
  74.4 12.3 %collective-permute-start.22 = (bf16[96,2048]{1,0:T(8,128)(2,1)S(1)}, bf16[96,2048]{1,0:T(8,128)(2,1)S(1)}, u32[]{:S(2)}, u32[]{:S(2)}) collective-permute-start(bf16[96,2048]{1,0:T(8,128)(2,1)S(1)} %get-tuple-element.153), channel_id=1, source_target_pairs={{0,2},{1,3},{2,0},{3,1},{4,6},{5,7},{6,4},{7,5},{8,10},{9,11},{10,... | collective-permute-start | bytes 1179656 | tf_op jit(solution)/shard_map/ppermute | solution.py:144
  77.5 26.1 %collective-permute-start.25 = (bf16[384,768]{1,0:T(8,128)(2,1)S(1)}, bf16[384,768]{1,0:T(8,128)(2,1)S(1)}, u32[]{:S(2)}, u32[]{:S(2)}) collective-permute-start(bf16[384,768]{1,0:T(8,128)(2,1)S(1)} %get-tuple-element.163), channel_id=1, source_target_pairs={{0,16},{8,24},{16,0},{24,8},{1,17},{9,25},{17,1},{25,9},{2,18},{10... | collective-permute-start | bytes 1769480 | tf_op jit(solution)/shard_map/ppermute | solution.py:144
  78.1 6.9 %collective-permute-start.21 = (bf16[96,1024]{1,0:T(8,128)(2,1)S(1)}, bf16[96,1024]{1,0:T(8,128)(2,1)S(1)}, u32[]{:S(2)}, u32[]{:S(2)}) collective-permute-start(bf16[96,1024]{1,0:T(8,128)(2,1)S(1)} %get-tuple-element.150), channel_id=1, source_target_pairs={{0,1},{1,0},{2,3},{3,2},{4,5},{5,4},{6,7},{7,6},{8,9},{9,8},{10,11... | collective-permute-start | bytes 589832 | tf_op jit(solution)/shard_map/ppermute | solution.py:144
  86.8 13.3 %collective-permute-start.24 = (bf16[48,2048]{1,0:T(8,128)(2,1)S(1)}, bf16[48,2048]{1,0:T(8,128)(2,1)S(1)}, u32[]{:S(2)}, u32[]{:S(2)}) collective-permute-start(bf16[48,2048]{1,0:T(8,128)(2,1)S(1)} %get-tuple-element.159), channel_id=1, source_target_pairs={{0,4},{1,5},{2,6},{3,7},{4,0},{5,1},{6,2},{7,3},{8,12},{9,13},{10,... | collective-permute-start | bytes 589832 | tf_op jit(solution)/shard_map/ppermute | solution.py:144
  88.7 17.0 %collective-permute-start.27 = (bf16[128,768]{1,0:T(8,128)(2,1)S(1)}, bf16[128,768]{1,0:T(8,128)(2,1)S(1)}, u32[]{:S(2)}, u32[]{:S(2)}) collective-permute-start(bf16[128,768]{1,0:T(8,128)(2,1)S(1)} %get-tuple-element.171), channel_id=1, source_target_pairs={{0,16},{8,24},{16,0},{24,8},{1,17},{9,25},{17,1},{25,9},{2,18},{10... | collective-permute-start | bytes 589832 | tf_op jit(solution)/shard_map/ppermute | solution.py:144
  90.0 14.6 %collective-permute-start.26 = (bf16[48,1024]{1,0:T(8,128)(2,1)S(1)}, bf16[48,1024]{1,0:T(8,128)(2,1)S(1)}, u32[]{:S(2)}, u32[]{:S(2)}) collective-permute-start(bf16[48,1024]{1,0:T(8,128)(2,1)S(1)} %get-tuple-element.167), channel_id=1, source_target_pairs={{0,4},{1,5},{2,6},{3,7},{4,0},{5,1},{6,2},{7,3},{8,12},{9,13},{10,... | collective-permute-start | bytes 294920 | tf_op jit(solution)/shard_map/ppermute | solution.py:144
  (4 other events, 16.2 us)

commit v7 on v6

--- a/solution.py
+++ b/solution.py
@@ -104,7 +104,6 @@
 
 BF16, F32 = jnp.bfloat16, jnp.float32
 VMEM, SMEM, HBM, ANY = pltpu.VMEM, pltpu.SMEM, pltpu.HBM, pl.ANY
-PINNED = "pinned"
 ORDER = ((8, 128), jnp.float32, pltpu.VMEM)
 
 
@@ -117,25 +116,17 @@
         body(*refs[skipped : given + len(outs)], *refs[given + len(outs) + 1 :])
         token[...] = jnp.zeros(token.shape, token.dtype)
 
-    outs_all = [(shape, dtype, VMEM if m == PINNED else m) for shape, dtype, m in outs] + [ORDER]
-    shapes = [
-        pltpu.VMEM(shape, dtype) if m == PINNED else jax.ShapeDtypeStruct(shape, dtype)
-        for shape, dtype, m in [*outs, ORDER]
-    ]
-    fixed = {HBM: HBM, PINNED: VMEM}
+    outs_all = [*outs, ORDER]
     outputs = pl.pallas_call(
         kernel,
-        in_specs=[
-            pl.BlockSpec(memory_space=VMEM if m == PINNED else m)
-            for m in [ANY] * skipped + [m for _, m in ins]
-        ],
+        in_specs=[pl.BlockSpec(memory_space=m) for m in [ANY] * skipped + [m for _, m in ins]],
         out_specs=[pl.BlockSpec(memory_space=m) for _, _, m in outs_all],
-        out_shape=shapes,
+        out_shape=[jax.ShapeDtypeStruct(shape, dtype) for shape, dtype, _ in outs_all],
         scratch_shapes=list(scratch),
         input_output_aliases={skipped + i: o for i, o in (aliases or {}).items()},
         cost_estimate=pl.CostEstimate(flops=0, bytes_accessed=0, transcendentals=0),
         compiler_params=pltpu.CompilerParams(vmem_limit_bytes=vmem * 2**20),
-    )(*after, *[pltpu.with_memory_space_constraint(a, fixed[m]) if m in fixed else a for a, m in ins])
+    )(*after, *[pltpu.with_memory_space_constraint(a, HBM) if m is HBM else a for a, m in ins])
     return list(outputs)
 
 
@@ -190,19 +181,19 @@
             VMEM((top, count), F32),
             pltpu.SemaphoreType.DMA((5,)),
         ],
-            )
+    )
 
 
 def products(places, left, right, outs, own, tile=512):
     size = left.shape[0] // 4
     width = right.shape[1]
+    blocks = [left[pl.ds(pl.multiple_of((own ^ m) * size, size), size), :] for m in places]
+    rows = jnp.concatenate(blocks, axis=0)
     for start, some in chunks(width, tile):
-        piece = right[:, start : start + some]
-        for m, (out, row) in zip(places, outs):
-            part = left[pl.ds(pl.multiple_of((own ^ m) * size, size), size), :]
-            out[row : row + size, start : start + some] = jnp.dot(
-                part, piece, preferred_element_type=F32
-            ).astype(out.dtype)
+        place = slice(start, start + some)
+        part = jnp.dot(rows, right[:, place], preferred_element_type=F32)
+        for i, out in enumerate(outs):
+            out[:, place] = part[i * size : (i + 1) * size].astype(out.dtype)
 
 
 TURNED = (((1,), (1,)), ((), ()))
@@ -228,6 +219,7 @@
     tok_far = swap(tok_own, "expert", far_bit)
     tok_near = swap(tok_own, "expert", near_bit)
     next_both = swap(both, "expert", 1)
+
     def copied(sources, width, after, waits=()):
         rows = count * len(sources)
 
@@ -273,6 +265,7 @@
     next_cot_last = swap(cot_last_on, "expert", 1)
     cot_pieces = [(cot_own, 0), (cot_pair, count), (cot_pair, 0), (cot_last_on, 0)]
     cot_pieces += [(next_both, count), (next_cot_pair, count), (next_cot_pair, 0), (next_cot_last, 0)]
+
     def forward(me_ref, mine_ref, *refs):
         blocks = refs[: len(tok_arrays)]
         weights = refs[len(tok_arrays) : len(tok_arrays) + 3]
@@ -334,7 +327,9 @@
         gate_near, up_near, down_near, done,
     ) = stage(
         forward,
-        [(me, SMEM), (mine, SMEM)] + [(a, VMEM) for a in tok_arrays] + [(w[0], HBM) for w in (w_gate, w_up, w_down)],
+        [(me, SMEM), (mine, SMEM)]
+        + [(a, VMEM) for a in tok_arrays]
+        + [(w[0], HBM) for w in (w_gate, w_up, w_down)],
         [
             ((width // 2, total), BF16, VMEM),
             ((width // 2, total), BF16, VMEM),
@@ -355,7 +350,6 @@
             pltpu.SemaphoreType.DMA((12,)),
         ],
         after=[done],
-        vmem=8,
     )
 
     cot_arrays, cot_where = refs_of(cot_pieces)
@@ -365,7 +359,7 @@
         left, rows, away = refs[len(cot_arrays) :]
         for b, (i, row) in enumerate(cot_where):
             rows[b * count : (b + 1) * count, :] = blocks[i][row : row + count, :width]
-        products([3], left, rows, [(away, 0)], own_ref[0])
+        products([3], left, rows, [away], own_ref[0])
 
     cot_rows, down_away, done = stage(
         down_first,
@@ -376,7 +370,7 @@
     down_came = swap(down_away, "dp", 1)
 
     def down_rest(own_ref, left, cot, _, away, send, same):
-        products([2, 1], left, cot, [(send, 0), (away, 0)], own_ref[0])
+        products([2, 1], left, cot, [send, away], own_ref[0])
 
     last_away, down_send, flipped_sent, done = stage(
         down_rest,
@@ -469,7 +463,7 @@
     gate_got = swap(gate_send, "dp", 2)
 
     def down_own(own_ref, left, cot, kept):
-        products([0], left, cot, [(kept, 0)], own_ref[0])
+        products([0], left, cot, [kept], own_ref[0])
 
     down_kept, done = stage(
         down_own,

time: 107 us -> 107 us (level)
  no operation moved by 1% of the time
where the time goes in v7:
time: 107 us
  waiting for transfers between devices  48.6 us (45%)
  starting transfers between devices  32.3 us (30%)
  Pallas kernels  25.3 us (24%)
    ppermute x28, waiting for transfers between devices, swap(): return lax.ppermute(value, axis, [(i, i ^ mask) for i in range(size)])  48.6 us
    ppermute x28, starting transfers between devices, swap(): return lax.ppermute(value, axis, [(i, i ^ mask) for i in range(size)])  32.3 us
    pallas_call x30, Pallas kernels, stage(): pl.pallas_call(kernel, in_specs=[pl.BlockSpec(memory_space=m) for m in [A...  25.3 us
  transfers between devices with their start and end apart: 28, of which 18 were waited for; matrix products, arithmetic and copies ran while one was open for 0% of the time, Pallas kernels for 21%

profile of v7, /device:TPU:0, one launch (start us, length us, event | category | flops | bytes accessed | tf_op | source)
XLA Modules:
  0.0 107.1 jit_solution(1052234275754480544)
XLA Ops:
  1.8 4.1 %collective-permute-start.1 = (bf16[48,2176]{1,0:T(8,128)(2,1)S(1)}, bf16[48,2176]{1,0:T(8,128)(2,1)S(1)}, u32[]{:S(2)}, u32[]{:S(2)}) collective-permute-start(bf16[48,2176]{1,0:T(8,128)(2,1)S(1)} %get-tuple-element.91.refs_3_), channel_id=1, source_target_pairs={{0,4},{1,5},{2,6},{3,7},{4,0},{5,1},{6,2},{7,3},{8,12},{9,13},{10,... | collective-permute-start | bytes 626696 | tf_op jit(solution)/shard_map/ppermute | solution.py:135
  5.9 1.6 %collective-permute-start = (bf16[48,2176]{1,0:T(8,128)(2,1)S(1)}, bf16[48,2176]{1,0:T(8,128)(2,1)S(1)}, u32[]{:S(2)}, u32[]{:S(2)}) collective-permute-start(bf16[48,2176]{1,0:T(8,128)(2,1)S(1)} %get-tuple-element.91.refs_3_), channel_id=1, source_target_pairs={{0,2},{1,3},{2,0},{3,1},{4,6},{5,7},{6,4},{7,5},{8,10},{9,11},{10,... | collective-permute-start | bytes 626696 | tf_op jit(solution)/shard_map/ppermute | solution.py:135
  9.0 6.6 %collective-permute-done.1.refs_2_.refs_1_ = bf16[48,2176]{1,0:T(8,128)(2,1)S(1)} collective-permute-done((bf16[48,2176]{1,0:T(8,128)(2,1)S(1)}, bf16[48,2176]{1,0:T(8,128)(2,1)S(1)}, u32[]{:S(2)}, u32[]{:S(2)}) %collective-permute-start.1) | collective-permute-done | bytes 208928 | tf_op jit(solution)/shard_map/ppermute | solution.py:135
  15.9 1.6 %collective-permute-start.6 = (bf16[96,2176]{1,0:T(8,128)(2,1)S(1)}, bf16[96,2176]{1,0:T(8,128)(2,1)S(1)}, u32[]{:S(2)}, u32[]{:S(2)}) collective-permute-start(bf16[96,2176]{1,0:T(8,128)(2,1)S(1)} %get-tuple-element.99.refs_4_), channel_id=1, source_target_pairs={{0,1},{1,0},{2,3},{3,2},{4,5},{5,4},{6,7},{7,6},{8,9},{9,8},{10,11... | collective-permute-start | bytes 1253384 | tf_op jit(solution)/shard_map/ppermute | solution.py:135
  19.1 2.3 %collective-permute-start.5 = (bf16[48,2048]{1,0:T(8,128)(2,1)S(1)}, bf16[48,2048]{1,0:T(8,128)(2,1)S(1)}, u32[]{:S(2)}, u32[]{:S(2)}) collective-permute-start(bf16[48,2048]{1,0:T(8,128)(2,1)S(1)} %get-tuple-element.98.refs_2_), channel_id=1, source_target_pairs={{0,4},{1,5},{2,6},{3,7},{4,0},{5,1},{6,2},{7,3},{8,12},{9,13},{10,... | collective-permute-start | bytes 589832 | tf_op jit(solution)/shard_map/ppermute | solution.py:135
  21.5 7.7 %collective-permute-done.2.refs_1_ = bf16[48,2176]{1,0:T(8,128)(2,1)S(1)} collective-permute-done((bf16[48,2176]{1,0:T(8,128)(2,1)S(1)}, bf16[48,2176]{1,0:T(8,128)(2,1)S(1)}, u32[]{:S(2)}, u32[]{:S(2)}) %collective-permute-start.2) | collective-permute-done | bytes 208928 | tf_op jit(solution)/shard_map/ppermute | solution.py:135
  29.8 2.1 %collective-permute-done.4.refs_1_ = bf16[48,2048]{1,0:T(8,128)(2,1)S(1)} collective-permute-done((bf16[48,2048]{1,0:T(8,128)(2,1)S(1)}, bf16[48,2048]{1,0:T(8,128)(2,1)S(1)}, u32[]{:S(2)}, u32[]{:S(2)}) %collective-permute-start.4) | collective-permute-done | bytes 196640 | tf_op jit(solution)/shard_map/ppermute | solution.py:135
  33.9 1.8 %collective-permute-done.8.refs_2_.refs_8_ = bf16[48,2176]{1,0:T(8,128)(2,1)S(1)} collective-permute-done((bf16[48,2176]{1,0:T(8,128)(2,1)S(1)}, bf16[48,2176]{1,0:T(8,128)(2,1)S(1)}, u32[]{:S(2)}, u32[]{:S(2)}) %collective-permute-start.8) | collective-permute-done | bytes 208928 | tf_op jit(solution)/shard_map/ppermute | solution.py:135
  35.8 1.9 %collective-permute-done.7.refs_1_ = bf16[48,2048]{1,0:T(8,128)(2,1)S(1)} collective-permute-done((bf16[48,2048]{1,0:T(8,128)(2,1)S(1)}, bf16[48,2048]{1,0:T(8,128)(2,1)S(1)}, u32[]{:S(2)}, u32[]{:S(2)}) %collective-permute-start.7) | collective-permute-done | bytes 196640 | tf_op jit(solution)/shard_map/ppermute | solution.py:135
  38.2 7.3 %shard_map.118 = (bf16[1024,384]{1,0:T(8,128)(2,1)S(1)}, bf16[1024,384]{1,0:T(8,128)(2,1)S(1)}, bf16[768,384]{1,0:T(8,128)(2,1)S(1)}, f32[384,768]{1,0:T(8,128)S...) custom-call(f32[8,128]{1,0:T(8,128)S(1)} %get-tuple-element.104.refs, ...), custom_call_target="tpu_custom_call" | custom-call | tf_op jit(solution)/shard_map/pallas_call | solution.py:120
  45.5 2.3 %collective-permute-done.10.refs_7_ = bf16[48,2048]{1,0:T(8,128)(2,1)S(1)} collective-permute-done((bf16[48,2048]{1,0:T(8,128)(2,1)S(1)}, bf16[48,2048]{1,0:T(8,128)(2,1)S(1)}, u32[]{:S(2)}, u32[]{:S(2)}) %collective-permute-start.10) | collective-permute-done | bytes 196640 | tf_op jit(solution)/shard_map/ppermute | solution.py:135
  52.2 1.6 %collective-permute-start.16 = (bf16[192,2048]{1,0:T(8,128)(2,1)S(1)}, bf16[192,2048]{1,0:T(8,128)(2,1)S(1)}, u32[]{:S(2)}, u32[]{:S(2)}) collective-permute-start(bf16[192,2048]{1,0:T(8,128)(2,1)S(1)} %get-tuple-element.133), channel_id=1, source_target_pairs={{0,16},{8,24},{16,0},{24,8},{1,17},{9,25},{17,1},{25,9},{2,18},{10... | collective-permute-start | bytes 2359304 | tf_op jit(solution)/shard_map/ppermute | solution.py:135
  54.3 2.6 %shard_map.123 = (bf16[192,1024]{1,0:T(8,128)(2,1)S(1)}, bf16[192,1024]{1,0:T(8,128)(2,1)S(1)}, bf16[192,1024]{1,0:T(8,128)(2,1)S(1)}, bf16[192,1024]{1,0:T(8,128)(2,1)S(1)}, f32[8,128]{1,0:T(8,128)S(1)}) custom-call(f32[8,128]{1,0:T(8,128)S(1)} %get-tuple-element.120.refs_0_, bf16[384,1536]{1,0:T(8,128)(2,1)S(1)} %get-tuple-element.121.refs_1_.refs_3_, ...), custom_call_target="tpu_custom_call" | custom-call | tf_op jit(solution)/shard_map/pallas_call | solution.py:120
  57.2 1.8 %collective-permute-start.18 = (bf16[192,1024]{1,0:T(8,128)(2,1)S(1)}, bf16[192,1024]{1,0:T(8,128)(2,1)S(1)}, u32[]{:S(2)}, u32[]{:S(2)}) collective-permute-start(bf16[192,1024]{1,0:T(8,128)(2,1)S(1)} %get-tuple-element.139), channel_id=1, source_target_pairs={{0,2},{1,3},{2,0},{3,1},{4,6},{5,7},{6,4},{7,5},{8,10},{9,11},{10,... | collective-permute-start | bytes 1179656 | tf_op jit(solution)/shard_map/ppermute | solution.py:135
  59.0 3.4 %shard_map.124 = (bf16[512,768]{1,0:T(8,128)(2,1)S(1)}, bf16[384,768]{1,0:T(8,128)(2,1)S(1)}, bf16[128,768]{1,0:T(8,128)(2,1)S(1)}, f32[512,768]{1,0:T(8,128)S(1...) custom-call(f32[8,128]{1,0:T(8,128)S(1)} %get-tuple-element.125.refs_0_, ...), custom_call_target="tpu_custom_call" | custom-call | tf_op jit(solution)/shard_map/pallas_call | solution.py:120
  63.0 6.0 %collective-permute-done.15.refs_2_ = bf16[192,1024]{1,0:T(8,128)(2,1)S(1)} collective-permute-done((bf16[192,1024]{1,0:T(8,128)(2,1)S(1)}, bf16[192,1024]{1,0:T(8,128)(2,1)S(1)}, u32[]{:S(2)}, u32[]{:S(2)}) %collective-permute-start.15) | collective-permute-done | bytes 393248 | tf_op jit(solution)/shard_map/ppermute | solution.py:135
  69.1 1.6 %collective-permute-start.19 = (bf16[96,1024]{1,0:T(8,128)(2,1)S(1)}, bf16[96,1024]{1,0:T(8,128)(2,1)S(1)}, u32[]{:S(2)}, u32[]{:S(2)}) collective-permute-start(bf16[96,1024]{1,0:T(8,128)(2,1)S(1)} %get-tuple-element.142), channel_id=1, source_target_pairs={{0,1},{1,0},{2,3},{3,2},{4,5},{5,4},{6,7},{7,6},{8,9},{9,8},{10,11... | collective-permute-start | bytes 589832 | tf_op jit(solution)/shard_map/ppermute | solution.py:135
  74.5 2.2 %collective-permute-done.18.refs_2_ = bf16[192,1024]{1,0:T(8,128)(2,1)S(1)} collective-permute-done((bf16[192,1024]{1,0:T(8,128)(2,1)S(1)}, bf16[192,1024]{1,0:T(8,128)(2,1)S(1)}, u32[]{:S(2)}, u32[]{:S(2)}) %collective-permute-start.18) | collective-permute-done | bytes 393248 | tf_op jit(solution)/shard_map/ppermute | solution.py:135
  79.3 3.0 %collective-permute-start.20 = (bf16[48,1024]{1,0:T(8,128)(2,1)S(1)}, bf16[48,1024]{1,0:T(8,128)(2,1)S(1)}, u32[]{:S(2)}, u32[]{:S(2)}) collective-permute-start(bf16[48,1024]{1,0:T(8,128)(2,1)S(1)} %get-tuple-element.147), channel_id=1, source_target_pairs={{0,4},{1,5},{2,6},{3,7},{4,0},{5,1},{6,2},{7,3},{8,12},{9,13},{10,... | collective-permute-start | bytes 294920 | tf_op jit(solution)/shard_map/ppermute | solution.py:135
  82.3 2.7 %collective-permute-done.20.refs_2_ = bf16[48,1024]{1,0:T(8,128)(2,1)S(1)} collective-permute-done((bf16[48,1024]{1,0:T(8,128)(2,1)S(1)}, bf16[48,1024]{1,0:T(8,128)(2,1)S(1)}, u32[]{:S(2)}, u32[]{:S(2)}) %collective-permute-start.20) | collective-permute-done | bytes 98336 | tf_op jit(solution)/shard_map/ppermute | solution.py:135
  85.0 1.6 %collective-permute-done.22.refs_2_ = bf16[96,2048]{1,0:T(8,128)(2,1)S(1)} collective-permute-done((bf16[96,2048]{1,0:T(8,128)(2,1)S(1)}, bf16[96,2048]{1,0:T(8,128)(2,1)S(1)}, u32[]{:S(2)}, u32[]{:S(2)}) %collective-permute-start.22) | collective-permute-done | bytes 393248 | tf_op jit(solution)/shard_map/ppermute | solution.py:135
  86.7 2.0 %collective-permute-start.24 = (bf16[48,2048]{1,0:T(8,128)(2,1)S(1)}, bf16[48,2048]{1,0:T(8,128)(2,1)S(1)}, u32[]{:S(2)}, u32[]{:S(2)}) collective-permute-start(bf16[48,2048]{1,0:T(8,128)(2,1)S(1)} %get-tuple-element.159), channel_id=1, source_target_pairs={{0,4},{1,5},{2,6},{3,7},{4,0},{5,1},{6,2},{7,3},{8,12},{9,13},{10,... | collective-permute-start | bytes 589832 | tf_op jit(solution)/shard_map/ppermute | solution.py:135
  92.4 7.7 %collective-permute-done.24.refs_2_ = bf16[48,2048]{1,0:T(8,128)(2,1)S(1)} collective-permute-done((bf16[48,2048]{1,0:T(8,128)(2,1)S(1)}, bf16[48,2048]{1,0:T(8,128)(2,1)S(1)}, u32[]{:S(2)}, u32[]{:S(2)}) %collective-permute-start.24) | collective-permute-done | bytes 196640 | tf_op jit(solution)/shard_map/ppermute | solution.py:135
  100.8 2.8 %collective-permute-done.25.refs_2_ = bf16[384,768]{1,0:T(8,128)(2,1)S(1)} collective-permute-done((bf16[384,768]{1,0:T(8,128)(2,1)S(1)}, bf16[384,768]{1,0:T(8,128)(2,1)S(1)}, u32[]{:S(2)}, u32[]{:S(2)}) %collective-permute-start.25) | collective-permute-done | bytes 589856 | tf_op jit(solution)/shard_map/ppermute | solution.py:135
  (62 shorter events, 28.0 us)
Async XLA Ops:
  1.8 13.8 %collective-permute-start.1 = (bf16[48,2176]{1,0:T(8,128)(2,1)S(1)}, bf16[48,2176]{1,0:T(8,128)(2,1)S(1)}, u32[]{:S(2)}, u32[]{:S(2)}) collective-permute-start(bf16[48,2176]{1,0:T(8,128)(2,1)S(1)} %get-tuple-element.91.refs_3_), channel_id=1, source_target_pairs={{0,4},{1,5},{2,6},{3,7},{4,0},{5,1},{6,2},{7,3},{8,12},{9,13},{10,... | collective-permute-start | bytes 626696 | tf_op jit(solution)/shard_map/ppermute | solution.py:135
  5.9 9.9 %collective-permute-start = (bf16[48,2176]{1,0:T(8,128)(2,1)S(1)}, bf16[48,2176]{1,0:T(8,128)(2,1)S(1)}, u32[]{:S(2)}, u32[]{:S(2)}) collective-permute-start(bf16[48,2176]{1,0:T(8,128)(2,1)S(1)} %get-tuple-element.91.refs_3_), channel_id=1, source_target_pairs={{0,2},{1,3},{2,0},{3,1},{4,6},{5,7},{6,4},{7,5},{8,10},{9,11},{10,... | collective-permute-start | bytes 626696 | tf_op jit(solution)/shard_map/ppermute | solution.py:135
  7.5 21.7 %collective-permute-start.3 = (bf16[96,2176]{1,0:T(8,128)(2,1)S(1)}, bf16[96,2176]{1,0:T(8,128)(2,1)S(1)}, u32[]{:S(2)}, u32[]{:S(2)}) collective-permute-start(bf16[96,2176]{1,0:T(8,128)(2,1)S(1)} %get-tuple-element.93.refs_1_), channel_id=1, source_target_pairs={{0,1},{1,0},{2,3},{3,2},{4,5},{5,4},{6,7},{7,6},{8,9},{9,8},{10,11... | collective-permute-start | bytes 1253384 | tf_op jit(solution)/shard_map/ppermute | solution.py:135
  15.9 16.0 %collective-permute-start.6 = (bf16[96,2176]{1,0:T(8,128)(2,1)S(1)}, bf16[96,2176]{1,0:T(8,128)(2,1)S(1)}, u32[]{:S(2)}, u32[]{:S(2)}) collective-permute-start(bf16[96,2176]{1,0:T(8,128)(2,1)S(1)} %get-tuple-element.99.refs_4_), channel_id=1, source_target_pairs={{0,1},{1,0},{2,3},{3,2},{4,5},{5,4},{6,7},{7,6},{8,9},{9,8},{10,11... | collective-permute-start | bytes 1253384 | tf_op jit(solution)/shard_map/ppermute | solution.py:135
  17.6 11.6 %collective-permute-start.2 = (bf16[48,2176]{1,0:T(8,128)(2,1)S(1)}, bf16[48,2176]{1,0:T(8,128)(2,1)S(1)}, u32[]{:S(2)}, u32[]{:S(2)}) collective-permute-start(bf16[48,2176]{1,0:T(8,128)(2,1)S(1)} %get-tuple-element.96), channel_id=1, source_target_pairs={{0,2},{1,3},{2,0},{3,1},{4,6},{5,7},{6,4},{7,5},{8,10},{9,11},{10,... | collective-permute-start | bytes 626696 | tf_op jit(solution)/shard_map/ppermute | solution.py:135
  19.1 10.7 %collective-permute-start.5 = (bf16[48,2048]{1,0:T(8,128)(2,1)S(1)}, bf16[48,2048]{1,0:T(8,128)(2,1)S(1)}, u32[]{:S(2)}, u32[]{:S(2)}) collective-permute-start(bf16[48,2048]{1,0:T(8,128)(2,1)S(1)} %get-tuple-element.98.refs_2_), channel_id=1, source_target_pairs={{0,4},{1,5},{2,6},{3,7},{4,0},{5,1},{6,2},{7,3},{8,12},{9,13},{10,... | collective-permute-start | bytes 589832 | tf_op jit(solution)/shard_map/ppermute | solution.py:135
  21.4 10.5 %collective-permute-start.4 = (bf16[48,2048]{1,0:T(8,128)(2,1)S(1)}, bf16[48,2048]{1,0:T(8,128)(2,1)S(1)}, u32[]{:S(2)}, u32[]{:S(2)}) collective-permute-start(bf16[48,2048]{1,0:T(8,128)(2,1)S(1)} %get-tuple-element.98.refs_2_), channel_id=1, source_target_pairs={{0,2},{1,3},{2,0},{3,1},{4,6},{5,7},{6,4},{7,5},{8,10},{9,11},{10,... | collective-permute-start | bytes 589832 | tf_op jit(solution)/shard_map/ppermute | solution.py:135
  29.3 6.5 %collective-permute-start.8 = (bf16[48,2176]{1,0:T(8,128)(2,1)S(1)}, bf16[48,2176]{1,0:T(8,128)(2,1)S(1)}, u32[]{:S(2)}, u32[]{:S(2)}) collective-permute-start(bf16[48,2176]{1,0:T(8,128)(2,1)S(1)} %get-tuple-element.103.refs_5_), channel_id=1, source_target_pairs={{0,1},{1,0},{2,3},{3,2},{4,5},{5,4},{6,7},{7,6},{8,9},{9,8},{10,11... | collective-permute-start | bytes 626696 | tf_op jit(solution)/shard_map/ppermute | solution.py:135
  31.9 5.7 %collective-permute-start.7 = (bf16[48,2048]{1,0:T(8,128)(2,1)S(1)}, bf16[48,2048]{1,0:T(8,128)(2,1)S(1)}, u32[]{:S(2)}, u32[]{:S(2)}) collective-permute-start(bf16[48,2048]{1,0:T(8,128)(2,1)S(1)} %get-tuple-element.102), channel_id=1, source_target_pairs={{0,2},{1,3},{2,0},{3,1},{4,6},{5,7},{6,4},{7,5},{8,10},{9,11},{10,... | collective-permute-start | bytes 589832 | tf_op jit(solution)/shard_map/ppermute | solution.py:135
  33.4 14.3 %collective-permute-start.9 = (bf16[96,2048]{1,0:T(8,128)(2,1)S(1)}, bf16[96,2048]{1,0:T(8,128)(2,1)S(1)}, u32[]{:S(2)}, u32[]{:S(2)}) collective-permute-start(bf16[96,2048]{1,0:T(8,128)(2,1)S(1)} %get-tuple-element.106.refs_3_), channel_id=1, source_target_pairs={{0,1},{1,0},{2,3},{3,2},{4,5},{5,4},{6,7},{7,6},{8,9},{9,8},{10,11... | collective-permute-start | bytes 1179656 | tf_op jit(solution)/shard_map/ppermute | solution.py:135
  37.7 10.1 %collective-permute-start.10 = (bf16[48,2048]{1,0:T(8,128)(2,1)S(1)}, bf16[48,2048]{1,0:T(8,128)(2,1)S(1)}, u32[]{:S(2)}, u32[]{:S(2)}) collective-permute-start(bf16[48,2048]{1,0:T(8,128)(2,1)S(1)} %get-tuple-element.107.refs_4_), channel_id=1, source_target_pairs={{0,1},{1,0},{2,3},{3,2},{4,5},{5,4},{6,7},{7,6},{8,9},{9,8},{10,11... | collective-permute-start | bytes 589832 | tf_op jit(solution)/shard_map/ppermute | solution.py:135
  51.5 7.5 %collective-permute-start.14 = (bf16[384,1536]{1,0:T(8,128)(2,1)S(1)}, bf16[384,1536]{1,0:T(8,128)(2,1)S(1)}, u32[]{:S(2)}, u32[]{:S(2)}) collective-permute-start(bf16[384,1536]{1,0:T(8,128)(2,1)S(1)} %get-tuple-element.121.refs_1_.refs_3_), channel_id=1, source_target_pairs={{0,8},{8,0},{16,24},{24,16},{1,9},{9,1},{17,25},{25,17},{2,10},{10... | collective-permute-start | bytes 3538952 | tf_op jit(solution)/shard_map/ppermute | solution.py:135
  52.2 20.4 %collective-permute-start.16 = (bf16[192,2048]{1,0:T(8,128)(2,1)S(1)}, bf16[192,2048]{1,0:T(8,128)(2,1)S(1)}, u32[]{:S(2)}, u32[]{:S(2)}) collective-permute-start(bf16[192,2048]{1,0:T(8,128)(2,1)S(1)} %get-tuple-element.133), channel_id=1, source_target_pairs={{0,16},{8,24},{16,0},{24,8},{1,17},{9,25},{17,1},{25,9},{2,18},{10... | collective-permute-start | bytes 2359304 | tf_op jit(solution)/shard_map/ppermute | solution.py:135
  53.8 20.4 %collective-permute-start.17 = (bf16[192,2048]{1,0:T(8,128)(2,1)S(1)}, bf16[192,2048]{1,0:T(8,128)(2,1)S(1)}, u32[]{:S(2)}, u32[]{:S(2)}) collective-permute-start(bf16[192,2048]{1,0:T(8,128)(2,1)S(1)} %get-tuple-element.136), channel_id=1, source_target_pairs={{0,1},{1,0},{2,3},{3,2},{4,5},{5,4},{6,7},{7,6},{8,9},{9,8},{10,11... | collective-permute-start | bytes 2359304 | tf_op jit(solution)/shard_map/ppermute | solution.py:135
  56.9 12.1 %collective-permute-start.15 = (bf16[192,1024]{1,0:T(8,128)(2,1)S(1)}, bf16[192,1024]{1,0:T(8,128)(2,1)S(1)}, u32[]{:S(2)}, u32[]{:S(2)}) collective-permute-start(bf16[192,1024]{1,0:T(8,128)(2,1)S(1)} %get-tuple-element.130), channel_id=1, source_target_pairs={{0,2},{1,3},{2,0},{3,1},{4,6},{5,7},{6,4},{7,5},{8,10},{9,11},{10,... | collective-permute-start | bytes 1179656 | tf_op jit(solution)/shard_map/ppermute | solution.py:135
  57.2 19.4 %collective-permute-start.18 = (bf16[192,1024]{1,0:T(8,128)(2,1)S(1)}, bf16[192,1024]{1,0:T(8,128)(2,1)S(1)}, u32[]{:S(2)}, u32[]{:S(2)}) collective-permute-start(bf16[192,1024]{1,0:T(8,128)(2,1)S(1)} %get-tuple-element.139), channel_id=1, source_target_pairs={{0,2},{1,3},{2,0},{3,1},{4,6},{5,7},{6,4},{7,5},{8,10},{9,11},{10,... | collective-permute-start | bytes 1179656 | tf_op jit(solution)/shard_map/ppermute | solution.py:135
  69.1 8.3 %collective-permute-start.19 = (bf16[96,1024]{1,0:T(8,128)(2,1)S(1)}, bf16[96,1024]{1,0:T(8,128)(2,1)S(1)}, u32[]{:S(2)}, u32[]{:S(2)}) collective-permute-start(bf16[96,1024]{1,0:T(8,128)(2,1)S(1)} %get-tuple-element.142), channel_id=1, source_target_pairs={{0,1},{1,0},{2,3},{3,2},{4,5},{5,4},{6,7},{7,6},{8,9},{9,8},{10,11... | collective-permute-start | bytes 589832 | tf_op jit(solution)/shard_map/ppermute | solution.py:135
  70.7 20.5 %collective-permute-start.23 = (bf16[512,768]{1,0:T(8,128)(2,1)S(1)}, bf16[512,768]{1,0:T(8,128)(2,1)S(1)}, u32[]{:S(2)}, u32[]{:S(2)}) collective-permute-start(bf16[512,768]{1,0:T(8,128)(2,1)S(1)} %get-tuple-element.156), channel_id=1, source_target_pairs={{0,16},{8,24},{16,0},{24,8},{1,17},{9,25},{17,1},{25,9},{2,18},{10... | collective-permute-start | bytes 2359304 | tf_op jit(solution)/shard_map/ppermute | solution.py:135
  74.4 12.3 %collective-permute-start.22 = (bf16[96,2048]{1,0:T(8,128)(2,1)S(1)}, bf16[96,2048]{1,0:T(8,128)(2,1)S(1)}, u32[]{:S(2)}, u32[]{:S(2)}) collective-permute-start(bf16[96,2048]{1,0:T(8,128)(2,1)S(1)} %get-tuple-element.153), channel_id=1, source_target_pairs={{0,2},{1,3},{2,0},{3,1},{4,6},{5,7},{6,4},{7,5},{8,10},{9,11},{10,... | collective-permute-start | bytes 1179656 | tf_op jit(solution)/shard_map/ppermute | solution.py:135
  77.5 26.1 %collective-permute-start.25 = (bf16[384,768]{1,0:T(8,128)(2,1)S(1)}, bf16[384,768]{1,0:T(8,128)(2,1)S(1)}, u32[]{:S(2)}, u32[]{:S(2)}) collective-permute-start(bf16[384,768]{1,0:T(8,128)(2,1)S(1)} %get-tuple-element.163), channel_id=1, source_target_pairs={{0,16},{8,24},{16,0},{24,8},{1,17},{9,25},{17,1},{25,9},{2,18},{10... | collective-permute-start | bytes 1769480 | tf_op jit(solution)/shard_map/ppermute | solution.py:135
  78.1 6.9 %collective-permute-start.21 = (bf16[96,1024]{1,0:T(8,128)(2,1)S(1)}, bf16[96,1024]{1,0:T(8,128)(2,1)S(1)}, u32[]{:S(2)}, u32[]{:S(2)}) collective-permute-start(bf16[96,1024]{1,0:T(8,128)(2,1)S(1)} %get-tuple-element.150), channel_id=1, source_target_pairs={{0,1},{1,0},{2,3},{3,2},{4,5},{5,4},{6,7},{7,6},{8,9},{9,8},{10,11... | collective-permute-start | bytes 589832 | tf_op jit(solution)/shard_map/ppermute | solution.py:135
  86.7 13.3 %collective-permute-start.24 = (bf16[48,2048]{1,0:T(8,128)(2,1)S(1)}, bf16[48,2048]{1,0:T(8,128)(2,1)S(1)}, u32[]{:S(2)}, u32[]{:S(2)}) collective-permute-start(bf16[48,2048]{1,0:T(8,128)(2,1)S(1)} %get-tuple-element.159), channel_id=1, source_target_pairs={{0,4},{1,5},{2,6},{3,7},{4,0},{5,1},{6,2},{7,3},{8,12},{9,13},{10,... | collective-permute-start | bytes 589832 | tf_op jit(solution)/shard_map/ppermute | solution.py:135
  88.7 17.0 %collective-permute-start.27 = (bf16[128,768]{1,0:T(8,128)(2,1)S(1)}, bf16[128,768]{1,0:T(8,128)(2,1)S(1)}, u32[]{:S(2)}, u32[]{:S(2)}) collective-permute-start(bf16[128,768]{1,0:T(8,128)(2,1)S(1)} %get-tuple-element.171), channel_id=1, source_target_pairs={{0,16},{8,24},{16,0},{24,8},{1,17},{9,25},{17,1},{25,9},{2,18},{10... | collective-permute-start | bytes 589832 | tf_op jit(solution)/shard_map/ppermute | solution.py:135
  90.1 14.6 %collective-permute-start.26 = (bf16[48,1024]{1,0:T(8,128)(2,1)S(1)}, bf16[48,1024]{1,0:T(8,128)(2,1)S(1)}, u32[]{:S(2)}, u32[]{:S(2)}) collective-permute-start(bf16[48,1024]{1,0:T(8,128)(2,1)S(1)} %get-tuple-element.167), channel_id=1, source_target_pairs={{0,4},{1,5},{2,6},{3,7},{4,0},{5,1},{6,2},{7,3},{8,12},{9,13},{10,... | collective-permute-start | bytes 294920 | tf_op jit(solution)/shard_map/ppermute | solution.py:135
  (4 other events, 16.2 us)

commit v8 on v7

--- a/solution.py
+++ b/solution.py
@@ -143,11 +143,12 @@
     count, width = tokens.shape
     top = expert_ids.shape[1]
 
-    def body(tok, ids_far, given_far, cot, alone, both, ids, given, sems):
+    def body(tok, ids_far, given_far, cot, alone, both, cot_out, ids, given, sems):
         copies = [
             pltpu.make_async_copy(tok, alone.at[:, :width], sems.at[0]),
             pltpu.make_async_copy(tok, both.at[:count, :width], sems.at[1]),
             pltpu.make_async_copy(cot, both.at[count:, :width], sems.at[2]),
+            pltpu.make_async_copy(cot, cot_out.at[:, :width], sems.at[5]),
         ]
         small = [
             pltpu.make_async_copy(ids_far, ids, sems.at[3]),
@@ -169,17 +170,22 @@
         alone[:, width:] = side
         both[:count, width:] = side
         both[count:, width:] = jnp.zeros((count, lanes), BF16)
+        cot_out[:, width:] = jnp.zeros((count, 2 * lanes), BF16)
         for copy in copies:
             copy.wait()
 
     return stage(
         body,
         [(a, HBM) for a in (tokens, expert_ids.T, gate_probs.T, out_cot)],
-        [((count, width + lanes), BF16, VMEM), ((2 * count, width + lanes), BF16, VMEM)],
+        [
+            ((count, width + lanes), BF16, VMEM),
+            ((2 * count, width + lanes), BF16, VMEM),
+            ((count, width + 2 * lanes), BF16, VMEM),
+        ],
         scratch=[
             VMEM((top, count), jnp.int32),
             VMEM((top, count), F32),
-            pltpu.SemaphoreType.DMA((5,)),
+            pltpu.SemaphoreType.DMA((6,)),
         ],
     )
 
@@ -215,10 +221,11 @@
 
     near_bit, far_bit = 2, 4
     wide = width + lanes
-    tok_own, both, done = packed(tokens, expert_ids, gate_probs, out_cot, experts, lanes)
+    tok_own, both, cot_own, done = packed(tokens, expert_ids, gate_probs, out_cot, experts, lanes)
     tok_far = swap(tok_own, "expert", far_bit)
     tok_near = swap(tok_own, "expert", near_bit)
     next_both = swap(both, "expert", 1)
+    cot_far = swap(cot_own, "expert", far_bit)
 
     def copied(sources, width, after, waits=()):
         rows = count * len(sources)
@@ -236,15 +243,14 @@
         )
 
     tok_pair, done = copied([(tok_near, 0), (tok_far, 0)], wide, [done])
-    cot_own, done = copied([(both, count)], width, [done])
+    cot_here, done = copied([(both, count)], width, [done])
+    cot_near = swap(cot_here, "expert", near_bit)
     tok_far_on, done = copied([(tok_far, 0)], wide, [done])
     next_tok_pair = swap(tok_pair, "expert", 1)
     tok_last = swap(tok_far_on, "expert", near_bit)
-    cot_far = swap(cot_own, "expert", far_bit)
-    cot_near = swap(cot_own, "expert", near_bit)
-    tok_last_on, done = copied([(tok_last, 0)], wide, [done], [next_both])
+    tok_last_on, done = copied([(tok_last, 0)], wide, [done], [next_both, cot_far])
     next_tok_last = swap(tok_last_on, "expert", 1)
-    cot_pair, done = copied([(cot_near, 0), (cot_far, 0)], width, [done], [next_tok_pair])
+    cot_pair, done = copied([(cot_near, 0), (cot_far, 0)], width, [done])
     cot_far_on, done = copied([(cot_far, 0)], width, [done])
     next_cot_pair = swap(cot_pair, "expert", 1)
     cot_last = swap(cot_far_on, "expert", near_bit)
@@ -261,9 +267,9 @@
 
     tok_arrays, tok_where = refs_of(tok_pieces)
 
-    cot_last_on, done = copied([(cot_last, 0)], width, [done], [next_tok_last])
+    cot_last_on, done = copied([(cot_last, 0)], width, [done], [next_tok_last, next_tok_pair])
     next_cot_last = swap(cot_last_on, "expert", 1)
-    cot_pieces = [(cot_own, 0), (cot_pair, count), (cot_pair, 0), (cot_last_on, 0)]
+    cot_pieces = [(cot_here, 0), (cot_pair, count), (cot_pair, 0), (cot_last_on, 0)]
     cot_pieces += [(next_both, count), (next_cot_pair, count), (next_cot_pair, 0), (next_cot_last, 0)]
 
     def forward(me_ref, mine_ref, *refs):

time: 107 us -> 107 us (level); the launches traced: 107 us -> 106 us
  waiting for transfers between devices: 48.6 us -> 40 us
  starting transfers between devices: 32.3 us -> 39.6 us
    ppermute x28, waiting for transfers between devices: 48.6 us -> 40 us  [swap(): return lax.ppermute(value, axis, [(i, i ^ mask) for i in range(size)])]
    ppermute x28, starting transfers between devices: 32.3 us -> 39.6 us  [swap(): return lax.ppermute(value, axis, [(i, i ^ mask) for i in range(size)])]
  transfers between devices with their start and end apart: 28 -> 28, of which waited for: 18 -> 14; matrix products, arithmetic and copies ran while one was open for 0% -> 0% of each run, Pallas kernels for 21% -> 21%
where the time goes in v8:
time: 107 us; the launch traced here: 106 us
  waiting for transfers between devices  40 us (37%)
  starting transfers between devices  39.6 us (37%)
  Pallas kernels  25.4 us (24%)
    ppermute x28, waiting for transfers between devices, swap(): return lax.ppermute(value, axis, [(i, i ^ mask) for i in range(size)])  40 us
    ppermute x28, starting transfers between devices, swap(): return lax.ppermute(value, axis, [(i, i ^ mask) for i in range(size)])  39.6 us
    pallas_call x30, Pallas kernels, stage(): pl.pallas_call(kernel, in_specs=[pl.BlockSpec(memory_space=m) for m in [A...  25.4 us
  transfers between devices with their start and end apart: 28, of which 14 were waited for; matrix products, arithmetic and copies ran while one was open for 0% of the time, Pallas kernels for 21%

profile of v8, /device:TPU:0, one launch (start us, length us, event | category | flops | bytes accessed | tf_op | source)
XLA Modules:
  0.0 105.9 jit_solution(13851424600351387927)
XLA Ops:
  1.9 4.1 %collective-permute-start.1 = (bf16[48,2176]{1,0:T(8,128)(2,1)S(1)}, bf16[48,2176]{1,0:T(8,128)(2,1)S(1)}, u32[]{:S(2)}, u32[]{:S(2)}) collective-permute-start(bf16[48,2176]{1,0:T(8,128)(2,1)S(1)} %get-tuple-element.92.refs_3_), channel_id=1, source_target_pairs={{0,4},{1,5},{2,6},{3,7},{4,0},{5,1},{6,2},{7,3},{8,12},{9,13},{10,... | collective-permute-start | bytes 626696 | tf_op jit(solution)/shard_map/ppermute | solution.py:135
  6.0 1.6 %collective-permute-start = (bf16[48,2176]{1,0:T(8,128)(2,1)S(1)}, bf16[48,2176]{1,0:T(8,128)(2,1)S(1)}, u32[]{:S(2)}, u32[]{:S(2)}) collective-permute-start(bf16[48,2176]{1,0:T(8,128)(2,1)S(1)} %get-tuple-element.92.refs_3_), channel_id=1, source_target_pairs={{0,2},{1,3},{2,0},{3,1},{4,6},{5,7},{6,4},{7,5},{8,10},{9,11},{10,... | collective-permute-start | bytes 626696 | tf_op jit(solution)/shard_map/ppermute | solution.py:135
  7.6 1.5 %collective-permute-start.3 = (bf16[96,2176]{1,0:T(8,128)(2,1)S(1)}, bf16[96,2176]{1,0:T(8,128)(2,1)S(1)}, u32[]{:S(2)}, u32[]{:S(2)}) collective-permute-start(bf16[96,2176]{1,0:T(8,128)(2,1)S(1)} %get-tuple-element.94.refs_1_), channel_id=1, source_target_pairs={{0,1},{1,0},{2,3},{3,2},{4,5},{5,4},{6,7},{7,6},{8,9},{9,8},{10,11... | collective-permute-start | bytes 1253384 | tf_op jit(solution)/shard_map/ppermute | solution.py:135
  9.5 7.9 %collective-permute-done.1.refs_2_.refs_1_ = bf16[48,2176]{1,0:T(8,128)(2,1)S(1)} collective-permute-done((bf16[48,2176]{1,0:T(8,128)(2,1)S(1)}, bf16[48,2176]{1,0:T(8,128)(2,1)S(1)}, u32[]{:S(2)}, u32[]{:S(2)}) %collective-permute-start.1) | collective-permute-done | bytes 208928 | tf_op jit(solution)/shard_map/ppermute | solution.py:135
  18.8 4.4 %collective-permute-start.8 = (bf16[96,2176]{1,0:T(8,128)(2,1)S(1)}, bf16[96,2176]{1,0:T(8,128)(2,1)S(1)}, u32[]{:S(2)}, u32[]{:S(2)}) collective-permute-start(bf16[96,2176]{1,0:T(8,128)(2,1)S(1)} %get-tuple-element.105.refs_4_), channel_id=1, source_target_pairs={{0,1},{1,0},{2,3},{3,2},{4,5},{5,4},{6,7},{7,6},{8,9},{9,8},{10,11... | collective-permute-start | bytes 1253384 | tf_op jit(solution)/shard_map/ppermute | solution.py:135
  23.2 1.9 %collective-permute-start.5 = (bf16[48,2048]{1,0:T(8,128)(2,1)S(1)}, bf16[48,2048]{1,0:T(8,128)(2,1)S(1)}, u32[]{:S(2)}, u32[]{:S(2)}) collective-permute-start(bf16[48,2048]{1,0:T(8,128)(2,1)S(1)} %get-tuple-element.100.refs_2_), channel_id=1, source_target_pairs={{0,2},{1,3},{2,0},{3,1},{4,6},{5,7},{6,4},{7,5},{8,10},{9,11},{10,... | collective-permute-start | bytes 589832 | tf_op jit(solution)/shard_map/ppermute | solution.py:135
  25.3 3.2 %collective-permute-done.2.refs_1_ = bf16[48,2176]{1,0:T(8,128)(2,1)S(1)} collective-permute-done((bf16[48,2176]{1,0:T(8,128)(2,1)S(1)}, bf16[48,2176]{1,0:T(8,128)(2,1)S(1)}, u32[]{:S(2)}, u32[]{:S(2)}) %collective-permute-start.2) | collective-permute-done | bytes 208928 | tf_op jit(solution)/shard_map/ppermute | solution.py:135
  31.1 1.9 %collective-permute-start.9 = (bf16[96,2048]{1,0:T(8,128)(2,1)S(1)}, bf16[96,2048]{1,0:T(8,128)(2,1)S(1)}, u32[]{:S(2)}, u32[]{:S(2)}) collective-permute-start(bf16[96,2048]{1,0:T(8,128)(2,1)S(1)} %get-tuple-element.108.refs_3_), channel_id=1, source_target_pairs={{0,1},{1,0},{2,3},{3,2},{4,5},{5,4},{6,7},{7,6},{8,9},{9,8},{10,11... | collective-permute-start | bytes 1179656 | tf_op jit(solution)/shard_map/ppermute | solution.py:135
  32.9 3.5 %collective-permute-done.6.refs_1_ = bf16[48,2048]{1,0:T(8,128)(2,1)S(1)} collective-permute-done((bf16[48,2048]{1,0:T(8,128)(2,1)S(1)}, bf16[48,2048]{1,0:T(8,128)(2,1)S(1)}, u32[]{:S(2)}, u32[]{:S(2)}) %collective-permute-start.6) | collective-permute-done | bytes 196640 | tf_op jit(solution)/shard_map/ppermute | solution.py:135
  36.8 1.8 %collective-permute-start.10 = (bf16[48,2048]{1,0:T(8,128)(2,1)S(1)}, bf16[48,2048]{1,0:T(8,128)(2,1)S(1)}, u32[]{:S(2)}, u32[]{:S(2)}) collective-permute-start(bf16[48,2048]{1,0:T(8,128)(2,1)S(1)} %get-tuple-element.109.refs_4_), channel_id=1, source_target_pairs={{0,1},{1,0},{2,3},{3,2},{4,5},{5,4},{6,7},{7,6},{8,9},{9,8},{10,11... | collective-permute-start | bytes 589832 | tf_op jit(solution)/shard_map/ppermute | solution.py:135
  38.6 7.3 %shard_map.118 = (bf16[1024,384]{1,0:T(8,128)(2,1)S(1)}, bf16[1024,384]{1,0:T(8,128)(2,1)S(1)}, bf16[768,384]{1,0:T(8,128)(2,1)S(1)}, f32[384,768]{1,0:T(8,128)S...) custom-call(f32[8,128]{1,0:T(8,128)S(1)} %get-tuple-element.106.refs, ...), custom_call_target="tpu_custom_call" | custom-call | tf_op jit(solution)/shard_map/pallas_call | solution.py:120
  48.6 1.4 %shard_map.121 = (bf16[384,1536]{1,0:T(8,128)(2,1)S(1)}, f32[8,128]{1,0:T(8,128)S(1)}) custom-call(f32[8,128]{1,0:T(8,128)S(1)} %get-tuple-element.114.refs_0_, bf16[384,2048]{1,0:T(8,128)(2,1)S(1)} %get-tuple-element.112.refs_3_.refs_1_, bf16[768,2048]{1,0:T(8,128)(2,1)S(1)} %get-tuple-element.115.refs_2_, f32[384,768]{1,0:T(8,128)S(1)} %get-tuple-element.116.refs_3_, ...), custom_call_target="tpu_custom_call" | custom-call | tf_op jit(solution)/shard_map/pallas_call | solution.py:120
  50.8 2.1 %collective-permute-start.16 = (bf16[192,2048]{1,0:T(8,128)(2,1)S(1)}, bf16[192,2048]{1,0:T(8,128)(2,1)S(1)}, u32[]{:S(2)}, u32[]{:S(2)}) collective-permute-start(bf16[192,2048]{1,0:T(8,128)(2,1)S(1)} %get-tuple-element.135), channel_id=1, source_target_pairs={{0,16},{8,24},{16,0},{24,8},{1,17},{9,25},{17,1},{25,9},{2,18},{10... | collective-permute-start | bytes 2359304 | tf_op jit(solution)/shard_map/ppermute | solution.py:135
  52.8 1.5 %collective-permute-start.17 = (bf16[192,2048]{1,0:T(8,128)(2,1)S(1)}, bf16[192,2048]{1,0:T(8,128)(2,1)S(1)}, u32[]{:S(2)}, u32[]{:S(2)}) collective-permute-start(bf16[192,2048]{1,0:T(8,128)(2,1)S(1)} %get-tuple-element.138), channel_id=1, source_target_pairs={{0,1},{1,0},{2,3},{3,2},{4,5},{5,4},{6,7},{7,6},{8,9},{9,8},{10,11... | collective-permute-start | bytes 2359304 | tf_op jit(solution)/shard_map/ppermute | solution.py:135
  54.4 2.6 %shard_map.123 = (bf16[192,1024]{1,0:T(8,128)(2,1)S(1)}, bf16[192,1024]{1,0:T(8,128)(2,1)S(1)}, bf16[192,1024]{1,0:T(8,128)(2,1)S(1)}, bf16[192,1024]{1,0:T(8,128)(2,1)S(1)}, f32[8,128]{1,0:T(8,128)S(1)}) custom-call(f32[8,128]{1,0:T(8,128)S(1)} %get-tuple-element.122.refs_0_, bf16[384,1536]{1,0:T(8,128)(2,1)S(1)} %get-tuple-element.123.refs_1_.refs_3_, ...), custom_call_target="tpu_custom_call" | custom-call | tf_op jit(solution)/shard_map/pallas_call | solution.py:120
  57.0 2.0 %collective-permute-start.15 = (bf16[192,1024]{1,0:T(8,128)(2,1)S(1)}, bf16[192,1024]{1,0:T(8,128)(2,1)S(1)}, u32[]{:S(2)}, u32[]{:S(2)}) collective-permute-start(bf16[192,1024]{1,0:T(8,128)(2,1)S(1)} %get-tuple-element.132), channel_id=1, source_target_pairs={{0,2},{1,3},{2,0},{3,1},{4,6},{5,7},{6,4},{7,5},{8,10},{9,11},{10,... | collective-permute-start | bytes 1179656 | tf_op jit(solution)/shard_map/ppermute | solution.py:135
  59.1 3.4 %shard_map.124 = (bf16[512,768]{1,0:T(8,128)(2,1)S(1)}, bf16[384,768]{1,0:T(8,128)(2,1)S(1)}, bf16[128,768]{1,0:T(8,128)(2,1)S(1)}, f32[512,768]{1,0:T(8,128)S(1...) custom-call(f32[8,128]{1,0:T(8,128)S(1)} %get-tuple-element.127.refs_0_, ...), custom_call_target="tpu_custom_call" | custom-call | tf_op jit(solution)/shard_map/pallas_call | solution.py:120
  63.1 6.0 %collective-permute-done.15.refs_2_ = bf16[192,1024]{1,0:T(8,128)(2,1)S(1)} collective-permute-done((bf16[192,1024]{1,0:T(8,128)(2,1)S(1)}, bf16[192,1024]{1,0:T(8,128)(2,1)S(1)}, u32[]{:S(2)}, u32[]{:S(2)}) %collective-permute-start.15) | collective-permute-done | bytes 393248 | tf_op jit(solution)/shard_map/ppermute | solution.py:135
  73.4 2.0 %collective-permute-start.22 = (bf16[96,2048]{1,0:T(8,128)(2,1)S(1)}, bf16[96,2048]{1,0:T(8,128)(2,1)S(1)}, u32[]{:S(2)}, u32[]{:S(2)}) collective-permute-start(bf16[96,2048]{1,0:T(8,128)(2,1)S(1)} %get-tuple-element.155), channel_id=1, source_target_pairs={{0,2},{1,3},{2,0},{3,1},{4,6},{5,7},{6,4},{7,5},{8,10},{9,11},{10,... | collective-permute-start | bytes 1179656 | tf_op jit(solution)/shard_map/ppermute | solution.py:135
  75.5 2.0 %collective-permute-done.18.refs_2_ = bf16[192,1024]{1,0:T(8,128)(2,1)S(1)} collective-permute-done((bf16[192,1024]{1,0:T(8,128)(2,1)S(1)}, bf16[192,1024]{1,0:T(8,128)(2,1)S(1)}, u32[]{:S(2)}, u32[]{:S(2)}) %collective-permute-start.18) | collective-permute-done | bytes 393248 | tf_op jit(solution)/shard_map/ppermute | solution.py:135
  78.6 4.6 %collective-permute-start.20 = (bf16[48,1024]{1,0:T(8,128)(2,1)S(1)}, bf16[48,1024]{1,0:T(8,128)(2,1)S(1)}, u32[]{:S(2)}, u32[]{:S(2)}) collective-permute-start(bf16[48,1024]{1,0:T(8,128)(2,1)S(1)} %get-tuple-element.149), channel_id=1, source_target_pairs={{0,4},{1,5},{2,6},{3,7},{4,0},{5,1},{6,2},{7,3},{8,12},{9,13},{10,... | collective-permute-start | bytes 294920 | tf_op jit(solution)/shard_map/ppermute | solution.py:135
  83.2 3.0 %collective-permute-done.20.refs_2_ = bf16[48,1024]{1,0:T(8,128)(2,1)S(1)} collective-permute-done((bf16[48,1024]{1,0:T(8,128)(2,1)S(1)}, bf16[48,1024]{1,0:T(8,128)(2,1)S(1)}, u32[]{:S(2)}, u32[]{:S(2)}) %collective-permute-start.20) | collective-permute-done | bytes 98336 | tf_op jit(solution)/shard_map/ppermute | solution.py:135
  87.0 3.4 %collective-permute-start.24 = (bf16[48,2048]{1,0:T(8,128)(2,1)S(1)}, bf16[48,2048]{1,0:T(8,128)(2,1)S(1)}, u32[]{:S(2)}, u32[]{:S(2)}) collective-permute-start(bf16[48,2048]{1,0:T(8,128)(2,1)S(1)} %get-tuple-element.161), channel_id=1, source_target_pairs={{0,4},{1,5},{2,6},{3,7},{4,0},{5,1},{6,2},{7,3},{8,12},{9,13},{10,... | collective-permute-start | bytes 589832 | tf_op jit(solution)/shard_map/ppermute | solution.py:135
  92.2 9.7 %collective-permute-done.24.refs_2_ = bf16[48,2048]{1,0:T(8,128)(2,1)S(1)} collective-permute-done((bf16[48,2048]{1,0:T(8,128)(2,1)S(1)}, bf16[48,2048]{1,0:T(8,128)(2,1)S(1)}, u32[]{:S(2)}, u32[]{:S(2)}) %collective-permute-start.24) | collective-permute-done | bytes 196640 | tf_op jit(solution)/shard_map/ppermute | solution.py:135
  (62 shorter events, 22.1 us)
Async XLA Ops:
  1.9 15.5 %collective-permute-start.1 = (bf16[48,2176]{1,0:T(8,128)(2,1)S(1)}, bf16[48,2176]{1,0:T(8,128)(2,1)S(1)}, u32[]{:S(2)}, u32[]{:S(2)}) collective-permute-start(bf16[48,2176]{1,0:T(8,128)(2,1)S(1)} %get-tuple-element.92.refs_3_), channel_id=1, source_target_pairs={{0,4},{1,5},{2,6},{3,7},{4,0},{5,1},{6,2},{7,3},{8,12},{9,13},{10,... | collective-permute-start | bytes 626696 | tf_op jit(solution)/shard_map/ppermute | solution.py:135
  6.0 11.4 %collective-permute-start = (bf16[48,2176]{1,0:T(8,128)(2,1)S(1)}, bf16[48,2176]{1,0:T(8,128)(2,1)S(1)}, u32[]{:S(2)}, u32[]{:S(2)}) collective-permute-start(bf16[48,2176]{1,0:T(8,128)(2,1)S(1)} %get-tuple-element.92.refs_3_), channel_id=1, source_target_pairs={{0,2},{1,3},{2,0},{3,1},{4,6},{5,7},{6,4},{7,5},{8,10},{9,11},{10,... | collective-permute-start | bytes 626696 | tf_op jit(solution)/shard_map/ppermute | solution.py:135
  7.6 20.9 %collective-permute-start.3 = (bf16[96,2176]{1,0:T(8,128)(2,1)S(1)}, bf16[96,2176]{1,0:T(8,128)(2,1)S(1)}, u32[]{:S(2)}, u32[]{:S(2)}) collective-permute-start(bf16[96,2176]{1,0:T(8,128)(2,1)S(1)} %get-tuple-element.94.refs_1_), channel_id=1, source_target_pairs={{0,1},{1,0},{2,3},{3,2},{4,5},{5,4},{6,7},{7,6},{8,9},{9,8},{10,11... | collective-permute-start | bytes 1253384 | tf_op jit(solution)/shard_map/ppermute | solution.py:135
  9.1 16.2 %collective-permute-start.4 = (bf16[48,2304]{1,0:T(8,128)(2,1)S(1)}, bf16[48,2304]{1,0:T(8,128)(2,1)S(1)}, u32[]{:S(2)}, u32[]{:S(2)}) collective-permute-start(bf16[48,2304]{1,0:T(8,128)(2,1)S(1)} %get-tuple-element.98), channel_id=1, source_target_pairs={{0,4},{1,5},{2,6},{3,7},{4,0},{5,1},{6,2},{7,3},{8,12},{9,13},{10,... | collective-permute-start | bytes 663560 | tf_op jit(solution)/shard_map/ppermute | solution.py:135
  17.5 11.1 %collective-permute-start.2 = (bf16[48,2176]{1,0:T(8,128)(2,1)S(1)}, bf16[48,2176]{1,0:T(8,128)(2,1)S(1)}, u32[]{:S(2)}, u32[]{:S(2)}) collective-permute-start(bf16[48,2176]{1,0:T(8,128)(2,1)S(1)} %get-tuple-element.97), channel_id=1, source_target_pairs={{0,2},{1,3},{2,0},{3,1},{4,6},{5,7},{6,4},{7,5},{8,10},{9,11},{10,... | collective-permute-start | bytes 626696 | tf_op jit(solution)/shard_map/ppermute | solution.py:135
  18.8 17.7 %collective-permute-start.8 = (bf16[96,2176]{1,0:T(8,128)(2,1)S(1)}, bf16[96,2176]{1,0:T(8,128)(2,1)S(1)}, u32[]{:S(2)}, u32[]{:S(2)}) collective-permute-start(bf16[96,2176]{1,0:T(8,128)(2,1)S(1)} %get-tuple-element.105.refs_4_), channel_id=1, source_target_pairs={{0,1},{1,0},{2,3},{3,2},{4,5},{5,4},{6,7},{7,6},{8,9},{9,8},{10,11... | collective-permute-start | bytes 1253384 | tf_op jit(solution)/shard_map/ppermute | solution.py:135
  23.2 7.5 %collective-permute-start.5 = (bf16[48,2048]{1,0:T(8,128)(2,1)S(1)}, bf16[48,2048]{1,0:T(8,128)(2,1)S(1)}, u32[]{:S(2)}, u32[]{:S(2)}) collective-permute-start(bf16[48,2048]{1,0:T(8,128)(2,1)S(1)} %get-tuple-element.100.refs_2_), channel_id=1, source_target_pairs={{0,2},{1,3},{2,0},{3,1},{4,6},{5,7},{6,4},{7,5},{8,10},{9,11},{10,... | collective-permute-start | bytes 589832 | tf_op jit(solution)/shard_map/ppermute | solution.py:135
  28.6 8.2 %collective-permute-start.7 = (bf16[48,2176]{1,0:T(8,128)(2,1)S(1)}, bf16[48,2176]{1,0:T(8,128)(2,1)S(1)}, u32[]{:S(2)}, u32[]{:S(2)}) collective-permute-start(bf16[48,2176]{1,0:T(8,128)(2,1)S(1)} %get-tuple-element.104.refs_5_), channel_id=1, source_target_pairs={{0,1},{1,0},{2,3},{3,2},{4,5},{5,4},{6,7},{7,6},{8,9},{9,8},{10,11... | collective-permute-start | bytes 626696 | tf_op jit(solution)/shard_map/ppermute | solution.py:135
  31.1 14.8 %collective-permute-start.9 = (bf16[96,2048]{1,0:T(8,128)(2,1)S(1)}, bf16[96,2048]{1,0:T(8,128)(2,1)S(1)}, u32[]{:S(2)}, u32[]{:S(2)}) collective-permute-start(bf16[96,2048]{1,0:T(8,128)(2,1)S(1)} %get-tuple-element.108.refs_3_), channel_id=1, source_target_pairs={{0,1},{1,0},{2,3},{3,2},{4,5},{5,4},{6,7},{7,6},{8,9},{9,8},{10,11... | collective-permute-start | bytes 1179656 | tf_op jit(solution)/shard_map/ppermute | solution.py:135
  36.8 9.6 %collective-permute-start.10 = (bf16[48,2048]{1,0:T(8,128)(2,1)S(1)}, bf16[48,2048]{1,0:T(8,128)(2,1)S(1)}, u32[]{:S(2)}, u32[]{:S(2)}) collective-permute-start(bf16[48,2048]{1,0:T(8,128)(2,1)S(1)} %get-tuple-element.109.refs_4_), channel_id=1, source_target_pairs={{0,1},{1,0},{2,3},{3,2},{4,5},{5,4},{6,7},{7,6},{8,9},{9,8},{10,11... | collective-permute-start | bytes 589832 | tf_op jit(solution)/shard_map/ppermute | solution.py:135
  50.1 9.0 %collective-permute-start.14 = (bf16[384,1536]{1,0:T(8,128)(2,1)S(1)}, bf16[384,1536]{1,0:T(8,128)(2,1)S(1)}, u32[]{:S(2)}, u32[]{:S(2)}) collective-permute-start(bf16[384,1536]{1,0:T(8,128)(2,1)S(1)} %get-tuple-element.123.refs_1_.refs_3_), channel_id=1, source_target_pairs={{0,8},{8,0},{16,24},{24,16},{1,9},{9,1},{17,25},{25,17},{2,10},{10... | collective-permute-start | bytes 3538952 | tf_op jit(solution)/shard_map/ppermute | solution.py:135
  50.8 20.4 %collective-permute-start.16 = (bf16[192,2048]{1,0:T(8,128)(2,1)S(1)}, bf16[192,2048]{1,0:T(8,128)(2,1)S(1)}, u32[]{:S(2)}, u32[]{:S(2)}) collective-permute-start(bf16[192,2048]{1,0:T(8,128)(2,1)S(1)} %get-tuple-element.135), channel_id=1, source_target_pairs={{0,16},{8,24},{16,0},{24,8},{1,17},{9,25},{17,1},{25,9},{2,18},{10... | collective-permute-start | bytes 2359304 | tf_op jit(solution)/shard_map/ppermute | solution.py:135
  52.8 20.4 %collective-permute-start.17 = (bf16[192,2048]{1,0:T(8,128)(2,1)S(1)}, bf16[192,2048]{1,0:T(8,128)(2,1)S(1)}, u32[]{:S(2)}, u32[]{:S(2)}) collective-permute-start(bf16[192,2048]{1,0:T(8,128)(2,1)S(1)} %get-tuple-element.138), channel_id=1, source_target_pairs={{0,1},{1,0},{2,3},{3,2},{4,5},{5,4},{6,7},{7,6},{8,9},{9,8},{10,11... | collective-permute-start | bytes 2359304 | tf_op jit(solution)/shard_map/ppermute | solution.py:135
  57.0 12.1 %collective-permute-start.15 = (bf16[192,1024]{1,0:T(8,128)(2,1)S(1)}, bf16[192,1024]{1,0:T(8,128)(2,1)S(1)}, u32[]{:S(2)}, u32[]{:S(2)}) collective-permute-start(bf16[192,1024]{1,0:T(8,128)(2,1)S(1)} %get-tuple-element.132), channel_id=1, source_target_pairs={{0,2},{1,3},{2,0},{3,1},{4,6},{5,7},{6,4},{7,5},{8,10},{9,11},{10,... | collective-permute-start | bytes 1179656 | tf_op jit(solution)/shard_map/ppermute | solution.py:135
  59.0 18.5 %collective-permute-start.18 = (bf16[192,1024]{1,0:T(8,128)(2,1)S(1)}, bf16[192,1024]{1,0:T(8,128)(2,1)S(1)}, u32[]{:S(2)}, u32[]{:S(2)}) collective-permute-start(bf16[192,1024]{1,0:T(8,128)(2,1)S(1)} %get-tuple-element.141), channel_id=1, source_target_pairs={{0,2},{1,3},{2,0},{3,1},{4,6},{5,7},{6,4},{7,5},{8,10},{9,11},{10,... | collective-permute-start | bytes 1179656 | tf_op jit(solution)/shard_map/ppermute | solution.py:135
  69.2 8.4 %collective-permute-start.19 = (bf16[96,1024]{1,0:T(8,128)(2,1)S(1)}, bf16[96,1024]{1,0:T(8,128)(2,1)S(1)}, u32[]{:S(2)}, u32[]{:S(2)}) collective-permute-start(bf16[96,1024]{1,0:T(8,128)(2,1)S(1)} %get-tuple-element.144), channel_id=1, source_target_pairs={{0,1},{1,0},{2,3},{3,2},{4,5},{5,4},{6,7},{7,6},{8,9},{9,8},{10,11... | collective-permute-start | bytes 589832 | tf_op jit(solution)/shard_map/ppermute | solution.py:135
  69.7 21.3 %collective-permute-start.23 = (bf16[512,768]{1,0:T(8,128)(2,1)S(1)}, bf16[512,768]{1,0:T(8,128)(2,1)S(1)}, u32[]{:S(2)}, u32[]{:S(2)}) collective-permute-start(bf16[512,768]{1,0:T(8,128)(2,1)S(1)} %get-tuple-element.158), channel_id=1, source_target_pairs={{0,16},{8,24},{16,0},{24,8},{1,17},{9,25},{17,1},{25,9},{2,18},{10... | collective-permute-start | bytes 2359304 | tf_op jit(solution)/shard_map/ppermute | solution.py:135
  73.4 13.5 %collective-permute-start.22 = (bf16[96,2048]{1,0:T(8,128)(2,1)S(1)}, bf16[96,2048]{1,0:T(8,128)(2,1)S(1)}, u32[]{:S(2)}, u32[]{:S(2)}) collective-permute-start(bf16[96,2048]{1,0:T(8,128)(2,1)S(1)} %get-tuple-element.155), channel_id=1, source_target_pairs={{0,2},{1,3},{2,0},{3,1},{4,6},{5,7},{6,4},{7,5},{8,10},{9,11},{10,... | collective-permute-start | bytes 1179656 | tf_op jit(solution)/shard_map/ppermute | solution.py:135
  77.7 25.0 %collective-permute-start.25 = (bf16[384,768]{1,0:T(8,128)(2,1)S(1)}, bf16[384,768]{1,0:T(8,128)(2,1)S(1)}, u32[]{:S(2)}, u32[]{:S(2)}) collective-permute-start(bf16[384,768]{1,0:T(8,128)(2,1)S(1)} %get-tuple-element.165), channel_id=1, source_target_pairs={{0,16},{8,24},{16,0},{24,8},{1,17},{9,25},{17,1},{25,9},{2,18},{10... | collective-permute-start | bytes 1769480 | tf_op jit(solution)/shard_map/ppermute | solution.py:135
  77.8 8.4 %collective-permute-start.21 = (bf16[96,1024]{1,0:T(8,128)(2,1)S(1)}, bf16[96,1024]{1,0:T(8,128)(2,1)S(1)}, u32[]{:S(2)}, u32[]{:S(2)}) collective-permute-start(bf16[96,1024]{1,0:T(8,128)(2,1)S(1)} %get-tuple-element.152), channel_id=1, source_target_pairs={{0,1},{1,0},{2,3},{3,2},{4,5},{5,4},{6,7},{7,6},{8,9},{9,8},{10,11... | collective-permute-start | bytes 589832 | tf_op jit(solution)/shard_map/ppermute | solution.py:135
  78.6 7.5 %collective-permute-start.20 = (bf16[48,1024]{1,0:T(8,128)(2,1)S(1)}, bf16[48,1024]{1,0:T(8,128)(2,1)S(1)}, u32[]{:S(2)}, u32[]{:S(2)}) collective-permute-start(bf16[48,1024]{1,0:T(8,128)(2,1)S(1)} %get-tuple-element.149), channel_id=1, source_target_pairs={{0,4},{1,5},{2,6},{3,7},{4,0},{5,1},{6,2},{7,3},{8,12},{9,13},{10,... | collective-permute-start | bytes 294920 | tf_op jit(solution)/shard_map/ppermute | solution.py:135
  87.0 14.9 %collective-permute-start.24 = (bf16[48,2048]{1,0:T(8,128)(2,1)S(1)}, bf16[48,2048]{1,0:T(8,128)(2,1)S(1)}, u32[]{:S(2)}, u32[]{:S(2)}) collective-permute-start(bf16[48,2048]{1,0:T(8,128)(2,1)S(1)} %get-tuple-element.161), channel_id=1, source_target_pairs={{0,4},{1,5},{2,6},{3,7},{4,0},{5,1},{6,2},{7,3},{8,12},{9,13},{10,... | collective-permute-start | bytes 589832 | tf_op jit(solution)/shard_map/ppermute | solution.py:135
  90.4 14.1 %collective-permute-start.27 = (bf16[128,768]{1,0:T(8,128)(2,1)S(1)}, bf16[128,768]{1,0:T(8,128)(2,1)S(1)}, u32[]{:S(2)}, u32[]{:S(2)}) collective-permute-start(bf16[128,768]{1,0:T(8,128)(2,1)S(1)} %get-tuple-element.173), channel_id=1, source_target_pairs={{0,16},{8,24},{16,0},{24,8},{1,17},{9,25},{17,1},{25,9},{2,18},{10... | collective-permute-start | bytes 589832 | tf_op jit(solution)/shard_map/ppermute | solution.py:135
  90.9 12.8 %collective-permute-start.26 = (bf16[48,1024]{1,0:T(8,128)(2,1)S(1)}, bf16[48,1024]{1,0:T(8,128)(2,1)S(1)}, u32[]{:S(2)}, u32[]{:S(2)}) collective-permute-start(bf16[48,1024]{1,0:T(8,128)(2,1)S(1)} %get-tuple-element.169), channel_id=1, source_target_pairs={{0,4},{1,5},{2,6},{3,7},{4,0},{5,1},{6,2},{7,3},{8,12},{9,13},{10,... | collective-permute-start | bytes 294920 | tf_op jit(solution)/shard_map/ppermute | solution.py:135
  (4 other events, 17.8 us)

commit v9 on v8

--- a/solution.py
+++ b/solution.py
@@ -225,7 +225,15 @@
     tok_far = swap(tok_own, "expert", far_bit)
     tok_near = swap(tok_own, "expert", near_bit)
     next_both = swap(both, "expert", 1)
-    cot_far = swap(cot_own, "expert", far_bit)
+
+    def gated(a, after, waits=()):
+        return stage(
+            lambda *_: None,
+            [(b, ANY) for b in (a, *waits)],
+            [(a.shape, a.dtype, ANY)],
+            after=after,
+            aliases={0: 0},
+        )
 
     def copied(sources, width, after, waits=()):
         rows = count * len(sources)
@@ -242,6 +250,8 @@
             after=after,
         )
 
+    cot_own, done = gated(cot_own, [done], [tok_near])
+    cot_far = swap(cot_own, "expert", far_bit)
     tok_pair, done = copied([(tok_near, 0), (tok_far, 0)], wide, [done])
     cot_here, done = copied([(both, count)], width, [done])
     cot_near = swap(cot_here, "expert", near_bit)
@@ -530,15 +540,6 @@
         held, send, done = folded(held, came, after, waits)
         return held, swap(send, "expert", bit), done
 
-    def gated(a, after, waits=()):
-        return stage(
-            lambda *_: None,
-            [(b, ANY) for b in (a, *waits)],
-            [(a.shape, a.dtype, ANY)],
-            after=after,
-            aliases={0: 0},
-        )
-
     left_held, left_came, done = fold_on(left_kept, left_came, 1, [done])
     down_grad, done = owned([down_kept, last_came, down_got], [done])
     out_held, out_came, done = fold_on(out_kept, out_came, near_bit, [done])

time: 107 us -> 107 us (level)
  waiting for transfers between devices: 40 us -> 45.1 us
  starting transfers between devices: 39.6 us -> 34.7 us
    ppermute x28, waiting for transfers between devices: 40 us -> 45.1 us  [swap(): return lax.ppermute(value, axis, [(i, i ^ mask) for i in range(size)])]
    ppermute x28, starting transfers between devices: 39.6 us -> 34.7 us  [swap(): return lax.ppermute(value, axis, [(i, i ^ mask) for i in range(size)])]
    pallas_call x30 -> x31, Pallas kernels: 25.4 us -> 25.4 us  [stage(): pl.pallas_call(kernel, in_specs=[pl.BlockSpec(memory_space=m) for m in [A...]
where the time goes in v9:
time: 107 us; the launch traced here: 106 us
  waiting for transfers between devices  45.1 us (42%)
  starting transfers between devices  34.7 us (32%)
  Pallas kernels  25.4 us (24%)
    ppermute x28, waiting for transfers between devices, swap(): return lax.ppermute(value, axis, [(i, i ^ mask) for i in range(size)])  45.1 us
    ppermute x28, starting transfers between devices, swap(): return lax.ppermute(value, axis, [(i, i ^ mask) for i in range(size)])  34.7 us
    pallas_call x31, Pallas kernels, stage(): pl.pallas_call(kernel, in_specs=[pl.BlockSpec(memory_space=m) for m in [A...  25.4 us
  transfers between devices with their start and end apart: 28, of which 14 were waited for; matrix products, arithmetic and copies ran while one was open for 0% of the time, Pallas kernels for 21%

profile of v9, /device:TPU:0, one launch (start us, length us, event | category | flops | bytes accessed | tf_op | source)
XLA Modules:
  0.0 106.1 jit_solution(7179460976913611773)
XLA Ops:
  1.9 3.1 %collective-permute-start = (bf16[48,2176]{1,0:T(8,128)(2,1)S(1)}, bf16[48,2176]{1,0:T(8,128)(2,1)S(1)}, u32[]{:S(2)}, u32[]{:S(2)}) collective-permute-start(bf16[48,2176]{1,0:T(8,128)(2,1)S(1)} %get-tuple-element.95.refs_3_), channel_id=1, source_target_pairs={{0,2},{1,3},{2,0},{3,1},{4,6},{5,7},{6,4},{7,5},{8,10},{9,11},{10,... | collective-permute-start | bytes 626696 | tf_op jit(solution)/shard_map/ppermute | solution.py:135
  5.0 2.6 %collective-permute-start.1 = (bf16[48,2176]{1,0:T(8,128)(2,1)S(1)}, bf16[48,2176]{1,0:T(8,128)(2,1)S(1)}, u32[]{:S(2)}, u32[]{:S(2)}) collective-permute-start(bf16[48,2176]{1,0:T(8,128)(2,1)S(1)} %get-tuple-element.95.refs_3_), channel_id=1, source_target_pairs={{0,4},{1,5},{2,6},{3,7},{4,0},{5,1},{6,2},{7,3},{8,12},{9,13},{10,... | collective-permute-start | bytes 626696 | tf_op jit(solution)/shard_map/ppermute | solution.py:135
  7.6 1.5 %collective-permute-start.3 = (bf16[96,2176]{1,0:T(8,128)(2,1)S(1)}, bf16[96,2176]{1,0:T(8,128)(2,1)S(1)}, u32[]{:S(2)}, u32[]{:S(2)}) collective-permute-start(bf16[96,2176]{1,0:T(8,128)(2,1)S(1)} %get-tuple-element.98.refs_1_), channel_id=1, source_target_pairs={{0,1},{1,0},{2,3},{3,2},{4,5},{5,4},{6,7},{7,6},{8,9},{9,8},{10,11... | collective-permute-start | bytes 1253384 | tf_op jit(solution)/shard_map/ppermute | solution.py:135
  9.1 5.4 %collective-permute-done.refs_2_.refs_1_ = bf16[48,2176]{1,0:T(8,128)(2,1)S(1)} collective-permute-done((bf16[48,2176]{1,0:T(8,128)(2,1)S(1)}, bf16[48,2176]{1,0:T(8,128)(2,1)S(1)}, u32[]{:S(2)}, u32[]{:S(2)}) %collective-permute-start) | collective-permute-done | bytes 208928 | tf_op jit(solution)/shard_map/ppermute | solution.py:135
  15.3 4.8 %collective-permute-done.1.refs_2_.refs_1_ = bf16[48,2176]{1,0:T(8,128)(2,1)S(1)} collective-permute-done((bf16[48,2176]{1,0:T(8,128)(2,1)S(1)}, bf16[48,2176]{1,0:T(8,128)(2,1)S(1)}, u32[]{:S(2)}, u32[]{:S(2)}) %collective-permute-start.1) | collective-permute-done | bytes 208928 | tf_op jit(solution)/shard_map/ppermute | solution.py:135
  20.2 1.5 %collective-permute-start.2 = (bf16[48,2176]{1,0:T(8,128)(2,1)S(1)}, bf16[48,2176]{1,0:T(8,128)(2,1)S(1)}, u32[]{:S(2)}, u32[]{:S(2)}) collective-permute-start(bf16[48,2176]{1,0:T(8,128)(2,1)S(1)} %get-tuple-element.101), channel_id=1, source_target_pairs={{0,2},{1,3},{2,0},{3,1},{4,6},{5,7},{6,4},{7,5},{8,10},{9,11},{10,... | collective-permute-start | bytes 626696 | tf_op jit(solution)/shard_map/ppermute | solution.py:135
  21.6 1.5 %collective-permute-start.8 = (bf16[96,2176]{1,0:T(8,128)(2,1)S(1)}, bf16[96,2176]{1,0:T(8,128)(2,1)S(1)}, u32[]{:S(2)}, u32[]{:S(2)}) collective-permute-start(bf16[96,2176]{1,0:T(8,128)(2,1)S(1)} %get-tuple-element.109.refs_4_), channel_id=1, source_target_pairs={{0,1},{1,0},{2,3},{3,2},{4,5},{5,4},{6,7},{7,6},{8,9},{9,8},{10,11... | collective-permute-start | bytes 1253384 | tf_op jit(solution)/shard_map/ppermute | solution.py:135
  23.8 5.4 %collective-permute-done.2.refs_1_ = bf16[48,2176]{1,0:T(8,128)(2,1)S(1)} collective-permute-done((bf16[48,2176]{1,0:T(8,128)(2,1)S(1)}, bf16[48,2176]{1,0:T(8,128)(2,1)S(1)}, u32[]{:S(2)}, u32[]{:S(2)}) %collective-permute-start.2) | collective-permute-done | bytes 208928 | tf_op jit(solution)/shard_map/ppermute | solution.py:135
  31.9 1.9 %collective-permute-start.9 = (bf16[96,2048]{1,0:T(8,128)(2,1)S(1)}, bf16[96,2048]{1,0:T(8,128)(2,1)S(1)}, u32[]{:S(2)}, u32[]{:S(2)}) collective-permute-start(bf16[96,2048]{1,0:T(8,128)(2,1)S(1)} %get-tuple-element.112.refs_3_), channel_id=1, source_target_pairs={{0,1},{1,0},{2,3},{3,2},{4,5},{5,4},{6,7},{7,6},{8,9},{9,8},{10,11... | collective-permute-start | bytes 1179656 | tf_op jit(solution)/shard_map/ppermute | solution.py:135
  33.8 3.8 %collective-permute-done.6.refs_1_ = bf16[48,2048]{1,0:T(8,128)(2,1)S(1)} collective-permute-done((bf16[48,2048]{1,0:T(8,128)(2,1)S(1)}, bf16[48,2048]{1,0:T(8,128)(2,1)S(1)}, u32[]{:S(2)}, u32[]{:S(2)}) %collective-permute-start.6) | collective-permute-done | bytes 196640 | tf_op jit(solution)/shard_map/ppermute | solution.py:135
  37.6 1.9 %collective-permute-start.10 = (bf16[48,2048]{1,0:T(8,128)(2,1)S(1)}, bf16[48,2048]{1,0:T(8,128)(2,1)S(1)}, u32[]{:S(2)}, u32[]{:S(2)}) collective-permute-start(bf16[48,2048]{1,0:T(8,128)(2,1)S(1)} %get-tuple-element.113.refs_4_), channel_id=1, source_target_pairs={{0,1},{1,0},{2,3},{3,2},{4,5},{5,4},{6,7},{7,6},{8,9},{9,8},{10,11... | collective-permute-start | bytes 589832 | tf_op jit(solution)/shard_map/ppermute | solution.py:135
  39.5 7.3 %shard_map.119 = (bf16[1024,384]{1,0:T(8,128)(2,1)S(1)}, bf16[1024,384]{1,0:T(8,128)(2,1)S(1)}, bf16[768,384]{1,0:T(8,128)(2,1)S(1)}, f32[384,768]{1,0:T(8,128)S...) custom-call(f32[8,128]{1,0:T(8,128)S(1)} %get-tuple-element.110.refs, ...), custom_call_target="tpu_custom_call" | custom-call | tf_op jit(solution)/shard_map/pallas_call | solution.py:120
  49.1 1.5 %shard_map.122 = (bf16[384,1536]{1,0:T(8,128)(2,1)S(1)}, f32[8,128]{1,0:T(8,128)S(1)}) custom-call(f32[8,128]{1,0:T(8,128)S(1)} %get-tuple-element.118.refs_0_, bf16[384,2048]{1,0:T(8,128)(2,1)S(1)} %get-tuple-element.116.refs_3_.refs_1_, bf16[768,2048]{1,0:T(8,128)(2,1)S(1)} %get-tuple-element.119.refs_2_, f32[384,768]{1,0:T(8,128)S(1)} %get-tuple-element.120.refs_3_, ...), custom_call_target="tpu_custom_call" | custom-call | tf_op jit(solution)/shard_map/pallas_call | solution.py:120
  51.2 1.6 %collective-permute-start.16 = (bf16[192,2048]{1,0:T(8,128)(2,1)S(1)}, bf16[192,2048]{1,0:T(8,128)(2,1)S(1)}, u32[]{:S(2)}, u32[]{:S(2)}) collective-permute-start(bf16[192,2048]{1,0:T(8,128)(2,1)S(1)} %get-tuple-element.139), channel_id=1, source_target_pairs={{0,16},{8,24},{16,0},{24,8},{1,17},{9,25},{17,1},{25,9},{2,18},{10... | collective-permute-start | bytes 2359304 | tf_op jit(solution)/shard_map/ppermute | solution.py:135
  52.8 1.5 %collective-permute-start.17 = (bf16[192,2048]{1,0:T(8,128)(2,1)S(1)}, bf16[192,2048]{1,0:T(8,128)(2,1)S(1)}, u32[]{:S(2)}, u32[]{:S(2)}) collective-permute-start(bf16[192,2048]{1,0:T(8,128)(2,1)S(1)} %get-tuple-element.142), channel_id=1, source_target_pairs={{0,1},{1,0},{2,3},{3,2},{4,5},{5,4},{6,7},{7,6},{8,9},{9,8},{10,11... | collective-permute-start | bytes 2359304 | tf_op jit(solution)/shard_map/ppermute | solution.py:135
  54.3 2.6 %shard_map.124 = (bf16[192,1024]{1,0:T(8,128)(2,1)S(1)}, bf16[192,1024]{1,0:T(8,128)(2,1)S(1)}, bf16[192,1024]{1,0:T(8,128)(2,1)S(1)}, bf16[192,1024]{1,0:T(8,128)(2,1)S(1)}, f32[8,128]{1,0:T(8,128)S(1)}) custom-call(f32[8,128]{1,0:T(8,128)S(1)} %get-tuple-element.126.refs_0_, bf16[384,1536]{1,0:T(8,128)(2,1)S(1)} %get-tuple-element.127.refs_1_.refs_3_, ...), custom_call_target="tpu_custom_call" | custom-call | tf_op jit(solution)/shard_map/pallas_call | solution.py:120
  59.1 3.4 %shard_map.125 = (bf16[512,768]{1,0:T(8,128)(2,1)S(1)}, bf16[384,768]{1,0:T(8,128)(2,1)S(1)}, bf16[128,768]{1,0:T(8,128)(2,1)S(1)}, f32[512,768]{1,0:T(8,128)S(1...) custom-call(f32[8,128]{1,0:T(8,128)S(1)} %get-tuple-element.131.refs_0_, ...), custom_call_target="tpu_custom_call" | custom-call | tf_op jit(solution)/shard_map/pallas_call | solution.py:120
  63.1 6.0 %collective-permute-done.15.refs_2_ = bf16[192,1024]{1,0:T(8,128)(2,1)S(1)} collective-permute-done((bf16[192,1024]{1,0:T(8,128)(2,1)S(1)}, bf16[192,1024]{1,0:T(8,128)(2,1)S(1)}, u32[]{:S(2)}, u32[]{:S(2)}) %collective-permute-start.15) | collective-permute-done | bytes 393248 | tf_op jit(solution)/shard_map/ppermute | solution.py:135
  70.2 1.5 %collective-permute-done.16.refs_3_ = bf16[192,2048]{1,0:T(8,128)(2,1)S(1)} collective-permute-done((bf16[192,2048]{1,0:T(8,128)(2,1)S(1)}, bf16[192,2048]{1,0:T(8,128)(2,1)S(1)}, u32[]{:S(2)}, u32[]{:S(2)}) %collective-permute-start.16) | collective-permute-done | bytes 786464 | tf_op jit(solution)/shard_map/ppermute | solution.py:135
  74.1 3.4 %collective-permute-done.18.refs_2_ = bf16[192,1024]{1,0:T(8,128)(2,1)S(1)} collective-permute-done((bf16[192,1024]{1,0:T(8,128)(2,1)S(1)}, bf16[192,1024]{1,0:T(8,128)(2,1)S(1)}, u32[]{:S(2)}, u32[]{:S(2)}) %collective-permute-start.18) | collective-permute-done | bytes 393248 | tf_op jit(solution)/shard_map/ppermute | solution.py:135
  78.6 4.3 %collective-permute-start.20 = (bf16[48,1024]{1,0:T(8,128)(2,1)S(1)}, bf16[48,1024]{1,0:T(8,128)(2,1)S(1)}, u32[]{:S(2)}, u32[]{:S(2)}) collective-permute-start(bf16[48,1024]{1,0:T(8,128)(2,1)S(1)} %get-tuple-element.153), channel_id=1, source_target_pairs={{0,4},{1,5},{2,6},{3,7},{4,0},{5,1},{6,2},{7,3},{8,12},{9,13},{10,... | collective-permute-start | bytes 294920 | tf_op jit(solution)/shard_map/ppermute | solution.py:135
  82.9 2.7 %collective-permute-done.20.refs_2_ = bf16[48,1024]{1,0:T(8,128)(2,1)S(1)} collective-permute-done((bf16[48,1024]{1,0:T(8,128)(2,1)S(1)}, bf16[48,1024]{1,0:T(8,128)(2,1)S(1)}, u32[]{:S(2)}, u32[]{:S(2)}) %collective-permute-start.20) | collective-permute-done | bytes 98336 | tf_op jit(solution)/shard_map/ppermute | solution.py:135
  86.8 2.8 %collective-permute-start.24 = (bf16[48,2048]{1,0:T(8,128)(2,1)S(1)}, bf16[48,2048]{1,0:T(8,128)(2,1)S(1)}, u32[]{:S(2)}, u32[]{:S(2)}) collective-permute-start(bf16[48,2048]{1,0:T(8,128)(2,1)S(1)} %get-tuple-element.165), channel_id=1, source_target_pairs={{0,4},{1,5},{2,6},{3,7},{4,0},{5,1},{6,2},{7,3},{8,12},{9,13},{10,... | collective-permute-start | bytes 589832 | tf_op jit(solution)/shard_map/ppermute | solution.py:135
  92.8 7.9 %collective-permute-done.24.refs_2_ = bf16[48,2048]{1,0:T(8,128)(2,1)S(1)} collective-permute-done((bf16[48,2048]{1,0:T(8,128)(2,1)S(1)}, bf16[48,2048]{1,0:T(8,128)(2,1)S(1)}, u32[]{:S(2)}, u32[]{:S(2)}) %collective-permute-start.24) | collective-permute-done | bytes 196640 | tf_op jit(solution)/shard_map/ppermute | solution.py:135
  (63 shorter events, 25.5 us)
Async XLA Ops:
  1.9 12.6 %collective-permute-start = (bf16[48,2176]{1,0:T(8,128)(2,1)S(1)}, bf16[48,2176]{1,0:T(8,128)(2,1)S(1)}, u32[]{:S(2)}, u32[]{:S(2)}) collective-permute-start(bf16[48,2176]{1,0:T(8,128)(2,1)S(1)} %get-tuple-element.95.refs_3_), channel_id=1, source_target_pairs={{0,2},{1,3},{2,0},{3,1},{4,6},{5,7},{6,4},{7,5},{8,10},{9,11},{10,... | collective-permute-start | bytes 626696 | tf_op jit(solution)/shard_map/ppermute | solution.py:135
  5.0 15.1 %collective-permute-start.1 = (bf16[48,2176]{1,0:T(8,128)(2,1)S(1)}, bf16[48,2176]{1,0:T(8,128)(2,1)S(1)}, u32[]{:S(2)}, u32[]{:S(2)}) collective-permute-start(bf16[48,2176]{1,0:T(8,128)(2,1)S(1)} %get-tuple-element.95.refs_3_), channel_id=1, source_target_pairs={{0,4},{1,5},{2,6},{3,7},{4,0},{5,1},{6,2},{7,3},{8,12},{9,13},{10,... | collective-permute-start | bytes 626696 | tf_op jit(solution)/shard_map/ppermute | solution.py:135
  7.6 21.6 %collective-permute-start.3 = (bf16[96,2176]{1,0:T(8,128)(2,1)S(1)}, bf16[96,2176]{1,0:T(8,128)(2,1)S(1)}, u32[]{:S(2)}, u32[]{:S(2)}) collective-permute-start(bf16[96,2176]{1,0:T(8,128)(2,1)S(1)} %get-tuple-element.98.refs_1_), channel_id=1, source_target_pairs={{0,1},{1,0},{2,3},{3,2},{4,5},{5,4},{6,7},{7,6},{8,9},{9,8},{10,11... | collective-permute-start | bytes 1253384 | tf_op jit(solution)/shard_map/ppermute | solution.py:135
  14.6 14.7 %collective-permute-start.4 = (bf16[48,2304]{1,0:T(8,128)(2,1)S(1)}, bf16[48,2304]{1,0:T(8,128)(2,1)S(1)}, u32[]{:S(2)}, u32[]{:S(2)}) collective-permute-start(bf16[48,2304]{1,0:T(8,128)(2,1)S(1)} %get-tuple-element.102), channel_id=1, source_target_pairs={{0,4},{1,5},{2,6},{3,7},{4,0},{5,1},{6,2},{7,3},{8,12},{9,13},{10,... | collective-permute-start | bytes 663560 | tf_op jit(solution)/shard_map/ppermute | solution.py:135
  20.2 9.0 %collective-permute-start.2 = (bf16[48,2176]{1,0:T(8,128)(2,1)S(1)}, bf16[48,2176]{1,0:T(8,128)(2,1)S(1)}, u32[]{:S(2)}, u32[]{:S(2)}) collective-permute-start(bf16[48,2176]{1,0:T(8,128)(2,1)S(1)} %get-tuple-element.101), channel_id=1, source_target_pairs={{0,2},{1,3},{2,0},{3,1},{4,6},{5,7},{6,4},{7,5},{8,10},{9,11},{10,... | collective-permute-start | bytes 626696 | tf_op jit(solution)/shard_map/ppermute | solution.py:135
  21.6 12.2 %collective-permute-start.8 = (bf16[96,2176]{1,0:T(8,128)(2,1)S(1)}, bf16[96,2176]{1,0:T(8,128)(2,1)S(1)}, u32[]{:S(2)}, u32[]{:S(2)}) collective-permute-start(bf16[96,2176]{1,0:T(8,128)(2,1)S(1)} %get-tuple-element.109.refs_4_), channel_id=1, source_target_pairs={{0,1},{1,0},{2,3},{3,2},{4,5},{5,4},{6,7},{7,6},{8,9},{9,8},{10,11... | collective-permute-start | bytes 1253384 | tf_op jit(solution)/shard_map/ppermute | solution.py:135
  23.1 8.7 %collective-permute-start.5 = (bf16[48,2048]{1,0:T(8,128)(2,1)S(1)}, bf16[48,2048]{1,0:T(8,128)(2,1)S(1)}, u32[]{:S(2)}, u32[]{:S(2)}) collective-permute-start(bf16[48,2048]{1,0:T(8,128)(2,1)S(1)} %get-tuple-element.104.refs_2_), channel_id=1, source_target_pairs={{0,2},{1,3},{2,0},{3,1},{4,6},{5,7},{6,4},{7,5},{8,10},{9,11},{10,... | collective-permute-start | bytes 589832 | tf_op jit(solution)/shard_map/ppermute | solution.py:135
  29.2 8.4 %collective-permute-start.7 = (bf16[48,2176]{1,0:T(8,128)(2,1)S(1)}, bf16[48,2176]{1,0:T(8,128)(2,1)S(1)}, u32[]{:S(2)}, u32[]{:S(2)}) collective-permute-start(bf16[48,2176]{1,0:T(8,128)(2,1)S(1)} %get-tuple-element.108.refs_5_), channel_id=1, source_target_pairs={{0,1},{1,0},{2,3},{3,2},{4,5},{5,4},{6,7},{7,6},{8,9},{9,8},{10,11... | collective-permute-start | bytes 626696 | tf_op jit(solution)/shard_map/ppermute | solution.py:135
  31.9 14.8 %collective-permute-start.9 = (bf16[96,2048]{1,0:T(8,128)(2,1)S(1)}, bf16[96,2048]{1,0:T(8,128)(2,1)S(1)}, u32[]{:S(2)}, u32[]{:S(2)}) collective-permute-start(bf16[96,2048]{1,0:T(8,128)(2,1)S(1)} %get-tuple-element.112.refs_3_), channel_id=1, source_target_pairs={{0,1},{1,0},{2,3},{3,2},{4,5},{5,4},{6,7},{7,6},{8,9},{9,8},{10,11... | collective-permute-start | bytes 1179656 | tf_op jit(solution)/shard_map/ppermute | solution.py:135
  37.6 9.2 %collective-permute-start.10 = (bf16[48,2048]{1,0:T(8,128)(2,1)S(1)}, bf16[48,2048]{1,0:T(8,128)(2,1)S(1)}, u32[]{:S(2)}, u32[]{:S(2)}) collective-permute-start(bf16[48,2048]{1,0:T(8,128)(2,1)S(1)} %get-tuple-element.113.refs_4_), channel_id=1, source_target_pairs={{0,1},{1,0},{2,3},{3,2},{4,5},{5,4},{6,7},{7,6},{8,9},{9,8},{10,11... | collective-permute-start | bytes 589832 | tf_op jit(solution)/shard_map/ppermute | solution.py:135
  50.6 8.5 %collective-permute-start.14 = (bf16[384,1536]{1,0:T(8,128)(2,1)S(1)}, bf16[384,1536]{1,0:T(8,128)(2,1)S(1)}, u32[]{:S(2)}, u32[]{:S(2)}) collective-permute-start(bf16[384,1536]{1,0:T(8,128)(2,1)S(1)} %get-tuple-element.127.refs_1_.refs_3_), channel_id=1, source_target_pairs={{0,8},{8,0},{16,24},{24,16},{1,9},{9,1},{17,25},{25,17},{2,10},{10... | collective-permute-start | bytes 3538952 | tf_op jit(solution)/shard_map/ppermute | solution.py:135
  51.2 20.4 %collective-permute-start.16 = (bf16[192,2048]{1,0:T(8,128)(2,1)S(1)}, bf16[192,2048]{1,0:T(8,128)(2,1)S(1)}, u32[]{:S(2)}, u32[]{:S(2)}) collective-permute-start(bf16[192,2048]{1,0:T(8,128)(2,1)S(1)} %get-tuple-element.139), channel_id=1, source_target_pairs={{0,16},{8,24},{16,0},{24,8},{1,17},{9,25},{17,1},{25,9},{2,18},{10... | collective-permute-start | bytes 2359304 | tf_op jit(solution)/shard_map/ppermute | solution.py:135
  52.8 20.4 %collective-permute-start.17 = (bf16[192,2048]{1,0:T(8,128)(2,1)S(1)}, bf16[192,2048]{1,0:T(8,128)(2,1)S(1)}, u32[]{:S(2)}, u32[]{:S(2)}) collective-permute-start(bf16[192,2048]{1,0:T(8,128)(2,1)S(1)} %get-tuple-element.142), channel_id=1, source_target_pairs={{0,1},{1,0},{2,3},{3,2},{4,5},{5,4},{6,7},{7,6},{8,9},{9,8},{10,11... | collective-permute-start | bytes 2359304 | tf_op jit(solution)/shard_map/ppermute | solution.py:135
  57.0 12.1 %collective-permute-start.15 = (bf16[192,1024]{1,0:T(8,128)(2,1)S(1)}, bf16[192,1024]{1,0:T(8,128)(2,1)S(1)}, u32[]{:S(2)}, u32[]{:S(2)}) collective-permute-start(bf16[192,1024]{1,0:T(8,128)(2,1)S(1)} %get-tuple-element.136), channel_id=1, source_target_pairs={{0,2},{1,3},{2,0},{3,1},{4,6},{5,7},{6,4},{7,5},{8,10},{9,11},{10,... | collective-permute-start | bytes 1179656 | tf_op jit(solution)/shard_map/ppermute | solution.py:135
  57.7 19.8 %collective-permute-start.18 = (bf16[192,1024]{1,0:T(8,128)(2,1)S(1)}, bf16[192,1024]{1,0:T(8,128)(2,1)S(1)}, u32[]{:S(2)}, u32[]{:S(2)}) collective-permute-start(bf16[192,1024]{1,0:T(8,128)(2,1)S(1)} %get-tuple-element.145), channel_id=1, source_target_pairs={{0,2},{1,3},{2,0},{3,1},{4,6},{5,7},{6,4},{7,5},{8,10},{9,11},{10,... | collective-permute-start | bytes 1179656 | tf_op jit(solution)/shard_map/ppermute | solution.py:135
  69.1 8.4 %collective-permute-start.19 = (bf16[96,1024]{1,0:T(8,128)(2,1)S(1)}, bf16[96,1024]{1,0:T(8,128)(2,1)S(1)}, u32[]{:S(2)}, u32[]{:S(2)}) collective-permute-start(bf16[96,1024]{1,0:T(8,128)(2,1)S(1)} %get-tuple-element.148), channel_id=1, source_target_pairs={{0,1},{1,0},{2,3},{3,2},{4,5},{5,4},{6,7},{7,6},{8,9},{9,8},{10,11... | collective-permute-start | bytes 589832 | tf_op jit(solution)/shard_map/ppermute | solution.py:135
  69.7 21.9 %collective-permute-start.23 = (bf16[512,768]{1,0:T(8,128)(2,1)S(1)}, bf16[512,768]{1,0:T(8,128)(2,1)S(1)}, u32[]{:S(2)}, u32[]{:S(2)}) collective-permute-start(bf16[512,768]{1,0:T(8,128)(2,1)S(1)} %get-tuple-element.162), channel_id=1, source_target_pairs={{0,16},{8,24},{16,0},{24,8},{1,17},{9,25},{17,1},{25,9},{2,18},{10... | collective-permute-start | bytes 2359304 | tf_op jit(solution)/shard_map/ppermute | solution.py:135
  73.4 13.3 %collective-permute-start.22 = (bf16[96,2048]{1,0:T(8,128)(2,1)S(1)}, bf16[96,2048]{1,0:T(8,128)(2,1)S(1)}, u32[]{:S(2)}, u32[]{:S(2)}) collective-permute-start(bf16[96,2048]{1,0:T(8,128)(2,1)S(1)} %get-tuple-element.159), channel_id=1, source_target_pairs={{0,2},{1,3},{2,0},{3,1},{4,6},{5,7},{6,4},{7,5},{8,10},{9,11},{10,... | collective-permute-start | bytes 1179656 | tf_op jit(solution)/shard_map/ppermute | solution.py:135
  77.7 24.9 %collective-permute-start.25 = (bf16[384,768]{1,0:T(8,128)(2,1)S(1)}, bf16[384,768]{1,0:T(8,128)(2,1)S(1)}, u32[]{:S(2)}, u32[]{:S(2)}) collective-permute-start(bf16[384,768]{1,0:T(8,128)(2,1)S(1)} %get-tuple-element.169), channel_id=1, source_target_pairs={{0,16},{8,24},{16,0},{24,8},{1,17},{9,25},{17,1},{25,9},{2,18},{10... | collective-permute-start | bytes 1769480 | tf_op jit(solution)/shard_map/ppermute | solution.py:135
  77.7 7.9 %collective-permute-start.21 = (bf16[96,1024]{1,0:T(8,128)(2,1)S(1)}, bf16[96,1024]{1,0:T(8,128)(2,1)S(1)}, u32[]{:S(2)}, u32[]{:S(2)}) collective-permute-start(bf16[96,1024]{1,0:T(8,128)(2,1)S(1)} %get-tuple-element.156), channel_id=1, source_target_pairs={{0,1},{1,0},{2,3},{3,2},{4,5},{5,4},{6,7},{7,6},{8,9},{9,8},{10,11... | collective-permute-start | bytes 589832 | tf_op jit(solution)/shard_map/ppermute | solution.py:135
  78.6 7.0 %collective-permute-start.20 = (bf16[48,1024]{1,0:T(8,128)(2,1)S(1)}, bf16[48,1024]{1,0:T(8,128)(2,1)S(1)}, u32[]{:S(2)}, u32[]{:S(2)}) collective-permute-start(bf16[48,1024]{1,0:T(8,128)(2,1)S(1)} %get-tuple-element.153), channel_id=1, source_target_pairs={{0,4},{1,5},{2,6},{3,7},{4,0},{5,1},{6,2},{7,3},{8,12},{9,13},{10,... | collective-permute-start | bytes 294920 | tf_op jit(solution)/shard_map/ppermute | solution.py:135
  86.8 13.9 %collective-permute-start.24 = (bf16[48,2048]{1,0:T(8,128)(2,1)S(1)}, bf16[48,2048]{1,0:T(8,128)(2,1)S(1)}, u32[]{:S(2)}, u32[]{:S(2)}) collective-permute-start(bf16[48,2048]{1,0:T(8,128)(2,1)S(1)} %get-tuple-element.165), channel_id=1, source_target_pairs={{0,4},{1,5},{2,6},{3,7},{4,0},{5,1},{6,2},{7,3},{8,12},{9,13},{10,... | collective-permute-start | bytes 589832 | tf_op jit(solution)/shard_map/ppermute | solution.py:135
  89.5 15.2 %collective-permute-start.27 = (bf16[128,768]{1,0:T(8,128)(2,1)S(1)}, bf16[128,768]{1,0:T(8,128)(2,1)S(1)}, u32[]{:S(2)}, u32[]{:S(2)}) collective-permute-start(bf16[128,768]{1,0:T(8,128)(2,1)S(1)} %get-tuple-element.177), channel_id=1, source_target_pairs={{0,16},{8,24},{16,0},{24,8},{1,17},{9,25},{17,1},{25,9},{2,18},{10... | collective-permute-start | bytes 589832 | tf_op jit(solution)/shard_map/ppermute | solution.py:135
  90.6 13.1 %collective-permute-start.26 = (bf16[48,1024]{1,0:T(8,128)(2,1)S(1)}, bf16[48,1024]{1,0:T(8,128)(2,1)S(1)}, u32[]{:S(2)}, u32[]{:S(2)}) collective-permute-start(bf16[48,1024]{1,0:T(8,128)(2,1)S(1)} %get-tuple-element.173), channel_id=1, source_target_pairs={{0,4},{1,5},{2,6},{3,7},{4,0},{5,1},{6,2},{7,3},{8,12},{9,13},{10,... | collective-permute-start | bytes 294920 | tf_op jit(solution)/shard_map/ppermute | solution.py:135
  (4 other events, 17.3 us)

commit v10 on v9

--- a/solution.py
+++ b/solution.py
@@ -285,10 +285,10 @@
     def forward(me_ref, mine_ref, *refs):
         blocks = refs[: len(tok_arrays)]
         weights = refs[len(tok_arrays) : len(tok_arrays) + 3]
-        flipped, flipped_sent, hidden_t, gate_by, up_by, kept, sent, gate, up, down = refs[
-            len(tok_arrays) + 3 : len(tok_arrays) + 13
+        flipped, flipped_sent, hidden_t, hidden, gate_by, up_by, gate, up, down = refs[
+            len(tok_arrays) + 3 : len(tok_arrays) + 12
         ]
-        rows, probs, hidden, gates, sems = refs[len(tok_arrays) + 13 :]
+        rows, probs, gates, sems = refs[len(tok_arrays) + 12 :]
         copies = []
         for j, (far_ref, near_ref) in enumerate(zip(weights, (gate, up, down))):
             size = far_ref.shape[0] // 4
@@ -332,15 +332,9 @@
             hidden_t[place, :] = hidden[:, place].T
         for copy in copies[8:]:
             copy.wait()
-        for start, size in chunks(width, 512):
-            place = slice(start, start + size)
-            part = jnp.dot(hidden[...], down[:, place], preferred_element_type=F32).astype(BF16)
-            kept[:, place] = part[:half]
-            sent[:, place] = part[half:]
 
     (
-        flipped, flipped_sent, hidden_t, gate_by, up_by, out_kept, out_sent,
-        gate_near, up_near, down_near, done,
+        flipped, flipped_sent, hidden_t, hidden, gate_by, up_by, gate_near, up_near, down_near, done
     ) = stage(
         forward,
         [(me, SMEM), (mine, SMEM)]
@@ -350,10 +344,9 @@
             ((width // 2, total), BF16, VMEM),
             ((width // 2, total), BF16, VMEM),
             ((ff, total), BF16, VMEM),
+            ((total, ff), BF16, VMEM),
             ((total, ff), F32, VMEM),
             ((total, ff), F32, VMEM),
-            ((half, width), BF16, VMEM),
-            ((half, width), BF16, VMEM),
             ((width, ff), BF16, VMEM),
             ((width, ff), BF16, VMEM),
             ((ff, width), BF16, VMEM),
@@ -361,7 +354,6 @@
         scratch=[
             VMEM((total, width), BF16),
             VMEM((total, 1), F32),
-            VMEM((total, ff), BF16),
             VMEM((total, ff), F32),
             pltpu.SemaphoreType.DMA((12,)),
         ],
@@ -397,7 +389,6 @@
     )
     flipped_came = swap(flipped_sent, "dp", 1)
     last_came = swap(last_away, "dp", 1)
-    out_came = swap(out_sent, "expert", 1)
 
     def backward(cot, down, gate_ref, up_ref, grads):
         for start, size in chunks(ff, 256):
@@ -424,6 +415,21 @@
         after=[done],
     )
     down_got = swap(down_send, "dp", 2)
+
+    def output_rows(left, down, kept, sent):
+        for start, size in chunks(width, 512):
+            place = slice(start, start + size)
+            part = jnp.dot(left[...], down[:, place], preferred_element_type=F32).astype(BF16)
+            kept[:, place] = part[:half]
+            sent[:, place] = part[half:]
+
+    out_kept, out_sent, done = stage(
+        output_rows,
+        [(hidden, VMEM), (down_near, VMEM)],
+        [((half, width), BF16, VMEM)] * 2,
+        after=[done],
+    )
+    out_came = swap(out_sent, "expert", 1)
 
     side = width // 2
 
@@ -552,17 +558,18 @@
     right_held, right_came, done = fold_on(right_held, right_came, far_bit, [done])
     out_held, out_came, done = fold_on(out_held, out_came, far_bit, [done])
 
-    def widened(a, b, c, d, out):
-        out[:, :side] = (a[...].astype(F32) + b[...].astype(F32)).astype(BF16)
-        out[:, side:] = (c[...].astype(F32) + d[...].astype(F32)).astype(BF16)
-
     gate_part, done = owned([gate_kept, gate_got], [done])
-    layer_out, done = folded(out_held, out_came, [done])
     up_part, done = owned([up_kept, high_got], [done])
-    input_grad, done = stage(
-        widened,
-        [(a, VMEM) for a in (left_held, left_came, right_held, right_came)],
-        [((count, width), BF16, VMEM)],
+
+    def finished(kept, came, a, b, c, d, out, grad):
+        out[...] = (kept[...].astype(F32) + came[...].astype(F32)).astype(BF16)
+        grad[:, :side] = (a[...].astype(F32) + b[...].astype(F32)).astype(BF16)
+        grad[:, side:] = (c[...].astype(F32) + d[...].astype(F32)).astype(BF16)
+
+    layer_out, input_grad, done = stage(
+        finished,
+        [(a, VMEM) for a in (out_held, out_came, left_held, left_came, right_held, right_came)],
+        [((count, width), BF16, VMEM)] * 2,
         after=[done],
     )
     up_part, _ = owned([up_kept, low_got], [done], cut, up_part)

time: 107 us -> 106 us (level)
  waiting for transfers between devices: 45.1 us -> 47.6 us
  starting transfers between devices: 34.7 us -> 33 us
    ppermute x28, waiting for transfers between devices: 45.1 us -> 47.6 us  [swap(): return lax.ppermute(value, axis, [(i, i ^ mask) for i in range(size)])]
    ppermute x28, starting transfers between devices: 34.7 us -> 33 us  [swap(): return lax.ppermute(value, axis, [(i, i ^ mask) for i in range(size)])]
  transfers between devices with their start and end apart: 28 -> 28, of which waited for: 14 -> 13; matrix products, arithmetic and copies ran while one was open for 0% -> 0% of each run, Pallas kernels for 21% -> 20%
where the time goes in v10:
time: 106 us
  waiting for transfers between devices  47.6 us (45%)
  starting transfers between devices  33 us (31%)
  Pallas kernels  24.8 us (23%)
    ppermute x28, waiting for transfers between devices, swap(): return lax.ppermute(value, axis, [(i, i ^ mask) for i in range(size)])  47.6 us
    ppermute x28, starting transfers between devices, swap(): return lax.ppermute(value, axis, [(i, i ^ mask) for i in range(size)])  33 us
    pallas_call x31, Pallas kernels, stage(): pl.pallas_call(kernel, in_specs=[pl.BlockSpec(memory_space=m) for m in [A...  24.8 us
  transfers between devices with their start and end apart: 28, of which 13 were waited for; matrix products, arithmetic and copies ran while one was open for 0% of the time, Pallas kernels for 20%

profile of v10, /device:TPU:0, one launch (start us, length us, event | category | flops | bytes accessed | tf_op | source)
XLA Modules:
  0.0 106.1 jit_solution(2661531394785455407)
XLA Ops:
  1.9 3.1 %collective-permute-start = (bf16[48,2176]{1,0:T(8,128)(2,1)S(1)}, bf16[48,2176]{1,0:T(8,128)(2,1)S(1)}, u32[]{:S(2)}, u32[]{:S(2)}) collective-permute-start(bf16[48,2176]{1,0:T(8,128)(2,1)S(1)} %get-tuple-element.96.refs_3_), channel_id=1, source_target_pairs={{0,2},{1,3},{2,0},{3,1},{4,6},{5,7},{6,4},{7,5},{8,10},{9,11},{10,... | collective-permute-start | bytes 626696 | tf_op jit(solution)/shard_map/ppermute | solution.py:135
  5.0 2.6 %collective-permute-start.1 = (bf16[48,2176]{1,0:T(8,128)(2,1)S(1)}, bf16[48,2176]{1,0:T(8,128)(2,1)S(1)}, u32[]{:S(2)}, u32[]{:S(2)}) collective-permute-start(bf16[48,2176]{1,0:T(8,128)(2,1)S(1)} %get-tuple-element.96.refs_3_), channel_id=1, source_target_pairs={{0,4},{1,5},{2,6},{3,7},{4,0},{5,1},{6,2},{7,3},{8,12},{9,13},{10,... | collective-permute-start | bytes 626696 | tf_op jit(solution)/shard_map/ppermute | solution.py:135
  7.6 1.5 %collective-permute-start.3 = (bf16[96,2176]{1,0:T(8,128)(2,1)S(1)}, bf16[96,2176]{1,0:T(8,128)(2,1)S(1)}, u32[]{:S(2)}, u32[]{:S(2)}) collective-permute-start(bf16[96,2176]{1,0:T(8,128)(2,1)S(1)} %get-tuple-element.99.refs_1_), channel_id=1, source_target_pairs={{0,1},{1,0},{2,3},{3,2},{4,5},{5,4},{6,7},{7,6},{8,9},{9,8},{10,11... | collective-permute-start | bytes 1253384 | tf_op jit(solution)/shard_map/ppermute | solution.py:135
  9.1 5.4 %collective-permute-done.refs_2_.refs_1_ = bf16[48,2176]{1,0:T(8,128)(2,1)S(1)} collective-permute-done((bf16[48,2176]{1,0:T(8,128)(2,1)S(1)}, bf16[48,2176]{1,0:T(8,128)(2,1)S(1)}, u32[]{:S(2)}, u32[]{:S(2)}) %collective-permute-start) | collective-permute-done | bytes 208928 | tf_op jit(solution)/shard_map/ppermute | solution.py:135
  15.3 4.8 %collective-permute-done.1.refs_2_.refs_1_ = bf16[48,2176]{1,0:T(8,128)(2,1)S(1)} collective-permute-done((bf16[48,2176]{1,0:T(8,128)(2,1)S(1)}, bf16[48,2176]{1,0:T(8,128)(2,1)S(1)}, u32[]{:S(2)}, u32[]{:S(2)}) %collective-permute-start.1) | collective-permute-done | bytes 208928 | tf_op jit(solution)/shard_map/ppermute | solution.py:135
  21.6 1.5 %collective-permute-start.8 = (bf16[96,2176]{1,0:T(8,128)(2,1)S(1)}, bf16[96,2176]{1,0:T(8,128)(2,1)S(1)}, u32[]{:S(2)}, u32[]{:S(2)}) collective-permute-start(bf16[96,2176]{1,0:T(8,128)(2,1)S(1)} %get-tuple-element.110.refs_4_), channel_id=1, source_target_pairs={{0,1},{1,0},{2,3},{3,2},{4,5},{5,4},{6,7},{7,6},{8,9},{9,8},{10,11... | collective-permute-start | bytes 1253384 | tf_op jit(solution)/shard_map/ppermute | solution.py:135
  23.8 5.4 %collective-permute-done.2.refs_1_ = bf16[48,2176]{1,0:T(8,128)(2,1)S(1)} collective-permute-done((bf16[48,2176]{1,0:T(8,128)(2,1)S(1)}, bf16[48,2176]{1,0:T(8,128)(2,1)S(1)}, u32[]{:S(2)}, u32[]{:S(2)}) %collective-permute-start.2) | collective-permute-done | bytes 208928 | tf_op jit(solution)/shard_map/ppermute | solution.py:135
  31.9 1.9 %collective-permute-start.9 = (bf16[96,2048]{1,0:T(8,128)(2,1)S(1)}, bf16[96,2048]{1,0:T(8,128)(2,1)S(1)}, u32[]{:S(2)}, u32[]{:S(2)}) collective-permute-start(bf16[96,2048]{1,0:T(8,128)(2,1)S(1)} %get-tuple-element.113.refs_3_), channel_id=1, source_target_pairs={{0,1},{1,0},{2,3},{3,2},{4,5},{5,4},{6,7},{7,6},{8,9},{9,8},{10,11... | collective-permute-start | bytes 1179656 | tf_op jit(solution)/shard_map/ppermute | solution.py:135
  33.8 3.8 %collective-permute-done.6.refs_1_ = bf16[48,2048]{1,0:T(8,128)(2,1)S(1)} collective-permute-done((bf16[48,2048]{1,0:T(8,128)(2,1)S(1)}, bf16[48,2048]{1,0:T(8,128)(2,1)S(1)}, u32[]{:S(2)}, u32[]{:S(2)}) %collective-permute-start.6) | collective-permute-done | bytes 196640 | tf_op jit(solution)/shard_map/ppermute | solution.py:135
  37.6 1.9 %collective-permute-start.10 = (bf16[48,2048]{1,0:T(8,128)(2,1)S(1)}, bf16[48,2048]{1,0:T(8,128)(2,1)S(1)}, u32[]{:S(2)}, u32[]{:S(2)}) collective-permute-start(bf16[48,2048]{1,0:T(8,128)(2,1)S(1)} %get-tuple-element.114.refs_4_), channel_id=1, source_target_pairs={{0,1},{1,0},{2,3},{3,2},{4,5},{5,4},{6,7},{7,6},{8,9},{9,8},{10,11... | collective-permute-start | bytes 589832 | tf_op jit(solution)/shard_map/ppermute | solution.py:135
  39.5 5.8 %shard_map.119 = (bf16[1024,384]{1,0:T(8,128)(2,1)S(1)}, bf16[1024,384]{1,0:T(8,128)(2,1)S(1)}, bf16[768,384]{1,0:T(8,128)(2,1)S(1)}, bf16[384,768]{1,0:T(8,128)...) custom-call(f32[8,128]{1,0:T(8,128)S(1)} %get-tuple-element.111.refs, ...), custom_call_target="tpu_custom_call" | custom-call | tf_op jit(solution)/shard_map/pallas_call | solution.py:120
  45.3 1.5 %collective-permute-done.10.refs_7_ = bf16[48,2048]{1,0:T(8,128)(2,1)S(1)} collective-permute-done((bf16[48,2048]{1,0:T(8,128)(2,1)S(1)}, bf16[48,2048]{1,0:T(8,128)(2,1)S(1)}, u32[]{:S(2)}, u32[]{:S(2)}) %collective-permute-start.10) | collective-permute-done | bytes 196640 | tf_op jit(solution)/shard_map/ppermute | solution.py:135
  51.3 1.6 %collective-permute-start.16 = (bf16[192,2048]{1,0:T(8,128)(2,1)S(1)}, bf16[192,2048]{1,0:T(8,128)(2,1)S(1)}, u32[]{:S(2)}, u32[]{:S(2)}) collective-permute-start(bf16[192,2048]{1,0:T(8,128)(2,1)S(1)} %get-tuple-element.142), channel_id=1, source_target_pairs={{0,16},{8,24},{16,0},{24,8},{1,17},{9,25},{17,1},{25,9},{2,18},{10... | collective-permute-start | bytes 2359304 | tf_op jit(solution)/shard_map/ppermute | solution.py:135
  54.2 1.6 %collective-permute-start.17 = (bf16[192,2048]{1,0:T(8,128)(2,1)S(1)}, bf16[192,2048]{1,0:T(8,128)(2,1)S(1)}, u32[]{:S(2)}, u32[]{:S(2)}) collective-permute-start(bf16[192,2048]{1,0:T(8,128)(2,1)S(1)} %get-tuple-element.145), channel_id=1, source_target_pairs={{0,1},{1,0},{2,3},{3,2},{4,5},{5,4},{6,7},{7,6},{8,9},{9,8},{10,11... | collective-permute-start | bytes 2359304 | tf_op jit(solution)/shard_map/ppermute | solution.py:135
  55.8 2.6 %shard_map.125 = (bf16[192,1024]{1,0:T(8,128)(2,1)S(1)}, bf16[192,1024]{1,0:T(8,128)(2,1)S(1)}, bf16[192,1024]{1,0:T(8,128)(2,1)S(1)}, bf16[192,1024]{1,0:T(8,128)(2,1)S(1)}, f32[8,128]{1,0:T(8,128)S(1)}) custom-call(f32[8,128]{1,0:T(8,128)S(1)} %get-tuple-element.129.refs_0_, bf16[384,1536]{1,0:T(8,128)(2,1)S(1)} %get-tuple-element.130.refs_1_.refs_3_, ...), custom_call_target="tpu_custom_call" | custom-call | tf_op jit(solution)/shard_map/pallas_call | solution.py:120
  60.5 3.4 %shard_map.126 = (bf16[512,768]{1,0:T(8,128)(2,1)S(1)}, bf16[384,768]{1,0:T(8,128)(2,1)S(1)}, bf16[128,768]{1,0:T(8,128)(2,1)S(1)}, f32[512,768]{1,0:T(8,128)S(1...) custom-call(f32[8,128]{1,0:T(8,128)S(1)} %get-tuple-element.134.refs_0_, ...), custom_call_target="tpu_custom_call" | custom-call | tf_op jit(solution)/shard_map/pallas_call | solution.py:120
  64.5 6.0 %collective-permute-done.15.refs_2_ = bf16[192,1024]{1,0:T(8,128)(2,1)S(1)} collective-permute-done((bf16[192,1024]{1,0:T(8,128)(2,1)S(1)}, bf16[192,1024]{1,0:T(8,128)(2,1)S(1)}, u32[]{:S(2)}, u32[]{:S(2)}) %collective-permute-start.15) | collective-permute-done | bytes 393248 | tf_op jit(solution)/shard_map/ppermute | solution.py:135
  73.0 1.7 %collective-permute-done.17.refs_2_ = bf16[192,2048]{1,0:T(8,128)(2,1)S(1)} collective-permute-done((bf16[192,2048]{1,0:T(8,128)(2,1)S(1)}, bf16[192,2048]{1,0:T(8,128)(2,1)S(1)}, u32[]{:S(2)}, u32[]{:S(2)}) %collective-permute-start.17) | collective-permute-done | bytes 786464 | tf_op jit(solution)/shard_map/ppermute | solution.py:135
  75.6 3.4 %collective-permute-done.18.refs_2_ = bf16[192,1024]{1,0:T(8,128)(2,1)S(1)} collective-permute-done((bf16[192,1024]{1,0:T(8,128)(2,1)S(1)}, bf16[192,1024]{1,0:T(8,128)(2,1)S(1)}, u32[]{:S(2)}, u32[]{:S(2)}) %collective-permute-start.18) | collective-permute-done | bytes 393248 | tf_op jit(solution)/shard_map/ppermute | solution.py:135
  80.1 3.7 %collective-permute-start.20 = (bf16[48,1024]{1,0:T(8,128)(2,1)S(1)}, bf16[48,1024]{1,0:T(8,128)(2,1)S(1)}, u32[]{:S(2)}, u32[]{:S(2)}) collective-permute-start(bf16[48,1024]{1,0:T(8,128)(2,1)S(1)} %get-tuple-element.156), channel_id=1, source_target_pairs={{0,4},{1,5},{2,6},{3,7},{4,0},{5,1},{6,2},{7,3},{8,12},{9,13},{10,... | collective-permute-start | bytes 294920 | tf_op jit(solution)/shard_map/ppermute | solution.py:135
  83.8 2.7 %collective-permute-done.20.refs_2_.refs_4_ = bf16[48,1024]{1,0:T(8,128)(2,1)S(1)} collective-permute-done((bf16[48,1024]{1,0:T(8,128)(2,1)S(1)}, bf16[48,1024]{1,0:T(8,128)(2,1)S(1)}, u32[]{:S(2)}, u32[]{:S(2)}) %collective-permute-start.20) | collective-permute-done | bytes 98336 | tf_op jit(solution)/shard_map/ppermute | solution.py:135
  86.6 1.6 %collective-permute-done.22.refs_2_ = bf16[96,2048]{1,0:T(8,128)(2,1)S(1)} collective-permute-done((bf16[96,2048]{1,0:T(8,128)(2,1)S(1)}, bf16[96,2048]{1,0:T(8,128)(2,1)S(1)}, u32[]{:S(2)}, u32[]{:S(2)}) %collective-permute-start.22) | collective-permute-done | bytes 393248 | tf_op jit(solution)/shard_map/ppermute | solution.py:135
  88.2 2.8 %collective-permute-start.25 = (bf16[48,2048]{1,0:T(8,128)(2,1)S(1)}, bf16[48,2048]{1,0:T(8,128)(2,1)S(1)}, u32[]{:S(2)}, u32[]{:S(2)}) collective-permute-start(bf16[48,2048]{1,0:T(8,128)(2,1)S(1)} %get-tuple-element.171), channel_id=1, source_target_pairs={{0,4},{1,5},{2,6},{3,7},{4,0},{5,1},{6,2},{7,3},{8,12},{9,13},{10,... | collective-permute-start | bytes 589832 | tf_op jit(solution)/shard_map/ppermute | solution.py:135
  93.0 9.6 %collective-permute-done.24.refs_2_ = bf16[384,768]{1,0:T(8,128)(2,1)S(1)} collective-permute-done((bf16[384,768]{1,0:T(8,128)(2,1)S(1)}, bf16[384,768]{1,0:T(8,128)(2,1)S(1)}, u32[]{:S(2)}, u32[]{:S(2)}) %collective-permute-start.24) | collective-permute-done | bytes 589856 | tf_op jit(solution)/shard_map/ppermute | solution.py:135
  (63 shorter events, 25.4 us)
Async XLA Ops:
  1.9 12.6 %collective-permute-start = (bf16[48,2176]{1,0:T(8,128)(2,1)S(1)}, bf16[48,2176]{1,0:T(8,128)(2,1)S(1)}, u32[]{:S(2)}, u32[]{:S(2)}) collective-permute-start(bf16[48,2176]{1,0:T(8,128)(2,1)S(1)} %get-tuple-element.96.refs_3_), channel_id=1, source_target_pairs={{0,2},{1,3},{2,0},{3,1},{4,6},{5,7},{6,4},{7,5},{8,10},{9,11},{10,... | collective-permute-start | bytes 626696 | tf_op jit(solution)/shard_map/ppermute | solution.py:135
  5.0 15.1 %collective-permute-start.1 = (bf16[48,2176]{1,0:T(8,128)(2,1)S(1)}, bf16[48,2176]{1,0:T(8,128)(2,1)S(1)}, u32[]{:S(2)}, u32[]{:S(2)}) collective-permute-start(bf16[48,2176]{1,0:T(8,128)(2,1)S(1)} %get-tuple-element.96.refs_3_), channel_id=1, source_target_pairs={{0,4},{1,5},{2,6},{3,7},{4,0},{5,1},{6,2},{7,3},{8,12},{9,13},{10,... | collective-permute-start | bytes 626696 | tf_op jit(solution)/shard_map/ppermute | solution.py:135
  7.6 21.6 %collective-permute-start.3 = (bf16[96,2176]{1,0:T(8,128)(2,1)S(1)}, bf16[96,2176]{1,0:T(8,128)(2,1)S(1)}, u32[]{:S(2)}, u32[]{:S(2)}) collective-permute-start(bf16[96,2176]{1,0:T(8,128)(2,1)S(1)} %get-tuple-element.99.refs_1_), channel_id=1, source_target_pairs={{0,1},{1,0},{2,3},{3,2},{4,5},{5,4},{6,7},{7,6},{8,9},{9,8},{10,11... | collective-permute-start | bytes 1253384 | tf_op jit(solution)/shard_map/ppermute | solution.py:135
  14.6 14.7 %collective-permute-start.4 = (bf16[48,2304]{1,0:T(8,128)(2,1)S(1)}, bf16[48,2304]{1,0:T(8,128)(2,1)S(1)}, u32[]{:S(2)}, u32[]{:S(2)}) collective-permute-start(bf16[48,2304]{1,0:T(8,128)(2,1)S(1)} %get-tuple-element.103), channel_id=1, source_target_pairs={{0,4},{1,5},{2,6},{3,7},{4,0},{5,1},{6,2},{7,3},{8,12},{9,13},{10,... | collective-permute-start | bytes 663560 | tf_op jit(solution)/shard_map/ppermute | solution.py:135
  20.2 9.0 %collective-permute-start.2 = (bf16[48,2176]{1,0:T(8,128)(2,1)S(1)}, bf16[48,2176]{1,0:T(8,128)(2,1)S(1)}, u32[]{:S(2)}, u32[]{:S(2)}) collective-permute-start(bf16[48,2176]{1,0:T(8,128)(2,1)S(1)} %get-tuple-element.102), channel_id=1, source_target_pairs={{0,2},{1,3},{2,0},{3,1},{4,6},{5,7},{6,4},{7,5},{8,10},{9,11},{10,... | collective-permute-start | bytes 626696 | tf_op jit(solution)/shard_map/ppermute | solution.py:135
  21.6 12.2 %collective-permute-start.8 = (bf16[96,2176]{1,0:T(8,128)(2,1)S(1)}, bf16[96,2176]{1,0:T(8,128)(2,1)S(1)}, u32[]{:S(2)}, u32[]{:S(2)}) collective-permute-start(bf16[96,2176]{1,0:T(8,128)(2,1)S(1)} %get-tuple-element.110.refs_4_), channel_id=1, source_target_pairs={{0,1},{1,0},{2,3},{3,2},{4,5},{5,4},{6,7},{7,6},{8,9},{9,8},{10,11... | collective-permute-start | bytes 1253384 | tf_op jit(solution)/shard_map/ppermute | solution.py:135
  23.1 8.7 %collective-permute-start.5 = (bf16[48,2048]{1,0:T(8,128)(2,1)S(1)}, bf16[48,2048]{1,0:T(8,128)(2,1)S(1)}, u32[]{:S(2)}, u32[]{:S(2)}) collective-permute-start(bf16[48,2048]{1,0:T(8,128)(2,1)S(1)} %get-tuple-element.105.refs_2_), channel_id=1, source_target_pairs={{0,2},{1,3},{2,0},{3,1},{4,6},{5,7},{6,4},{7,5},{8,10},{9,11},{10,... | collective-permute-start | bytes 589832 | tf_op jit(solution)/shard_map/ppermute | solution.py:135
  29.2 8.4 %collective-permute-start.7 = (bf16[48,2176]{1,0:T(8,128)(2,1)S(1)}, bf16[48,2176]{1,0:T(8,128)(2,1)S(1)}, u32[]{:S(2)}, u32[]{:S(2)}) collective-permute-start(bf16[48,2176]{1,0:T(8,128)(2,1)S(1)} %get-tuple-element.109.refs_5_), channel_id=1, source_target_pairs={{0,1},{1,0},{2,3},{3,2},{4,5},{5,4},{6,7},{7,6},{8,9},{9,8},{10,11... | collective-permute-start | bytes 626696 | tf_op jit(solution)/shard_map/ppermute | solution.py:135
  31.9 13.4 %collective-permute-start.9 = (bf16[96,2048]{1,0:T(8,128)(2,1)S(1)}, bf16[96,2048]{1,0:T(8,128)(2,1)S(1)}, u32[]{:S(2)}, u32[]{:S(2)}) collective-permute-start(bf16[96,2048]{1,0:T(8,128)(2,1)S(1)} %get-tuple-element.113.refs_3_), channel_id=1, source_target_pairs={{0,1},{1,0},{2,3},{3,2},{4,5},{5,4},{6,7},{7,6},{8,9},{9,8},{10,11... | collective-permute-start | bytes 1179656 | tf_op jit(solution)/shard_map/ppermute | solution.py:135
  37.6 9.2 %collective-permute-start.10 = (bf16[48,2048]{1,0:T(8,128)(2,1)S(1)}, bf16[48,2048]{1,0:T(8,128)(2,1)S(1)}, u32[]{:S(2)}, u32[]{:S(2)}) collective-permute-start(bf16[48,2048]{1,0:T(8,128)(2,1)S(1)} %get-tuple-element.114.refs_4_), channel_id=1, source_target_pairs={{0,1},{1,0},{2,3},{3,2},{4,5},{5,4},{6,7},{7,6},{8,9},{9,8},{10,11... | collective-permute-start | bytes 589832 | tf_op jit(solution)/shard_map/ppermute | solution.py:135
  49.0 6.8 %collective-permute-start.13 = (bf16[192,2048]{1,0:T(8,128)(2,1)S(1)}, bf16[192,2048]{1,0:T(8,128)(2,1)S(1)}, u32[]{:S(2)}, u32[]{:S(2)}) collective-permute-start(bf16[192,2048]{1,0:T(8,128)(2,1)S(1)} %get-tuple-element.133), channel_id=1, source_target_pairs={{0,8},{8,0},{16,24},{24,16},{1,9},{9,1},{17,25},{25,17},{2,10},{10... | collective-permute-start | bytes 2359304 | tf_op jit(solution)/shard_map/ppermute | solution.py:135
  50.6 9.9 %collective-permute-start.14 = (bf16[384,1536]{1,0:T(8,128)(2,1)S(1)}, bf16[384,1536]{1,0:T(8,128)(2,1)S(1)}, u32[]{:S(2)}, u32[]{:S(2)}) collective-permute-start(bf16[384,1536]{1,0:T(8,128)(2,1)S(1)} %get-tuple-element.130.refs_1_.refs_3_), channel_id=1, source_target_pairs={{0,8},{8,0},{16,24},{24,16},{1,9},{9,1},{17,25},{25,17},{2,10},{10... | collective-permute-start | bytes 3538952 | tf_op jit(solution)/shard_map/ppermute | solution.py:135
  51.3 20.5 %collective-permute-start.16 = (bf16[192,2048]{1,0:T(8,128)(2,1)S(1)}, bf16[192,2048]{1,0:T(8,128)(2,1)S(1)}, u32[]{:S(2)}, u32[]{:S(2)}) collective-permute-start(bf16[192,2048]{1,0:T(8,128)(2,1)S(1)} %get-tuple-element.142), channel_id=1, source_target_pairs={{0,16},{8,24},{16,0},{24,8},{1,17},{9,25},{17,1},{25,9},{2,18},{10... | collective-permute-start | bytes 2359304 | tf_op jit(solution)/shard_map/ppermute | solution.py:135
  54.2 20.5 %collective-permute-start.17 = (bf16[192,2048]{1,0:T(8,128)(2,1)S(1)}, bf16[192,2048]{1,0:T(8,128)(2,1)S(1)}, u32[]{:S(2)}, u32[]{:S(2)}) collective-permute-start(bf16[192,2048]{1,0:T(8,128)(2,1)S(1)} %get-tuple-element.145), channel_id=1, source_target_pairs={{0,1},{1,0},{2,3},{3,2},{4,5},{5,4},{6,7},{7,6},{8,9},{9,8},{10,11... | collective-permute-start | bytes 2359304 | tf_op jit(solution)/shard_map/ppermute | solution.py:135
  58.4 12.1 %collective-permute-start.15 = (bf16[192,1024]{1,0:T(8,128)(2,1)S(1)}, bf16[192,1024]{1,0:T(8,128)(2,1)S(1)}, u32[]{:S(2)}, u32[]{:S(2)}) collective-permute-start(bf16[192,1024]{1,0:T(8,128)(2,1)S(1)} %get-tuple-element.139), channel_id=1, source_target_pairs={{0,2},{1,3},{2,0},{3,1},{4,6},{5,7},{6,4},{7,5},{8,10},{9,11},{10,... | collective-permute-start | bytes 1179656 | tf_op jit(solution)/shard_map/ppermute | solution.py:135
  59.1 19.8 %collective-permute-start.18 = (bf16[192,1024]{1,0:T(8,128)(2,1)S(1)}, bf16[192,1024]{1,0:T(8,128)(2,1)S(1)}, u32[]{:S(2)}, u32[]{:S(2)}) collective-permute-start(bf16[192,1024]{1,0:T(8,128)(2,1)S(1)} %get-tuple-element.148), channel_id=1, source_target_pairs={{0,2},{1,3},{2,0},{3,1},{4,6},{5,7},{6,4},{7,5},{8,10},{9,11},{10,... | collective-permute-start | bytes 1179656 | tf_op jit(solution)/shard_map/ppermute | solution.py:135
  70.6 8.4 %collective-permute-start.19 = (bf16[96,1024]{1,0:T(8,128)(2,1)S(1)}, bf16[96,1024]{1,0:T(8,128)(2,1)S(1)}, u32[]{:S(2)}, u32[]{:S(2)}) collective-permute-start(bf16[96,1024]{1,0:T(8,128)(2,1)S(1)} %get-tuple-element.151), channel_id=1, source_target_pairs={{0,1},{1,0},{2,3},{3,2},{4,5},{5,4},{6,7},{7,6},{8,9},{9,8},{10,11... | collective-permute-start | bytes 589832 | tf_op jit(solution)/shard_map/ppermute | solution.py:135
  71.2 20.6 %collective-permute-start.23 = (bf16[512,768]{1,0:T(8,128)(2,1)S(1)}, bf16[512,768]{1,0:T(8,128)(2,1)S(1)}, u32[]{:S(2)}, u32[]{:S(2)}) collective-permute-start(bf16[512,768]{1,0:T(8,128)(2,1)S(1)} %get-tuple-element.165), channel_id=1, source_target_pairs={{0,16},{8,24},{16,0},{24,8},{1,17},{9,25},{17,1},{25,9},{2,18},{10... | collective-permute-start | bytes 2359304 | tf_op jit(solution)/shard_map/ppermute | solution.py:135
  74.9 13.3 %collective-permute-start.22 = (bf16[96,2048]{1,0:T(8,128)(2,1)S(1)}, bf16[96,2048]{1,0:T(8,128)(2,1)S(1)}, u32[]{:S(2)}, u32[]{:S(2)}) collective-permute-start(bf16[96,2048]{1,0:T(8,128)(2,1)S(1)} %get-tuple-element.162), channel_id=1, source_target_pairs={{0,2},{1,3},{2,0},{3,1},{4,6},{5,7},{6,4},{7,5},{8,10},{9,11},{10,... | collective-permute-start | bytes 1179656 | tf_op jit(solution)/shard_map/ppermute | solution.py:135
  79.1 23.5 %collective-permute-start.24 = (bf16[384,768]{1,0:T(8,128)(2,1)S(1)}, bf16[384,768]{1,0:T(8,128)(2,1)S(1)}, u32[]{:S(2)}, u32[]{:S(2)}) collective-permute-start(bf16[384,768]{1,0:T(8,128)(2,1)S(1)} %get-tuple-element.168), channel_id=1, source_target_pairs={{0,16},{8,24},{16,0},{24,8},{1,17},{9,25},{17,1},{25,9},{2,18},{10... | collective-permute-start | bytes 1769480 | tf_op jit(solution)/shard_map/ppermute | solution.py:135
  79.7 6.8 %collective-permute-start.21 = (bf16[96,1024]{1,0:T(8,128)(2,1)S(1)}, bf16[96,1024]{1,0:T(8,128)(2,1)S(1)}, u32[]{:S(2)}, u32[]{:S(2)}) collective-permute-start(bf16[96,1024]{1,0:T(8,128)(2,1)S(1)} %get-tuple-element.159), channel_id=1, source_target_pairs={{0,1},{1,0},{2,3},{3,2},{4,5},{5,4},{6,7},{7,6},{8,9},{9,8},{10,11... | collective-permute-start | bytes 589832 | tf_op jit(solution)/shard_map/ppermute | solution.py:135
  88.2 15.7 %collective-permute-start.25 = (bf16[48,2048]{1,0:T(8,128)(2,1)S(1)}, bf16[48,2048]{1,0:T(8,128)(2,1)S(1)}, u32[]{:S(2)}, u32[]{:S(2)}) collective-permute-start(bf16[48,2048]{1,0:T(8,128)(2,1)S(1)} %get-tuple-element.171), channel_id=1, source_target_pairs={{0,4},{1,5},{2,6},{3,7},{4,0},{5,1},{6,2},{7,3},{8,12},{9,13},{10,... | collective-permute-start | bytes 589832 | tf_op jit(solution)/shard_map/ppermute | solution.py:135
  91.0 13.8 %collective-permute-start.27 = (bf16[128,768]{1,0:T(8,128)(2,1)S(1)}, bf16[128,768]{1,0:T(8,128)(2,1)S(1)}, u32[]{:S(2)}, u32[]{:S(2)}) collective-permute-start(bf16[128,768]{1,0:T(8,128)(2,1)S(1)} %get-tuple-element.179), channel_id=1, source_target_pairs={{0,16},{8,24},{16,0},{24,8},{1,17},{9,25},{17,1},{25,9},{2,18},{10... | collective-permute-start | bytes 589832 | tf_op jit(solution)/shard_map/ppermute | solution.py:135
  91.5 12.4 %collective-permute-start.26 = (bf16[48,1024]{1,0:T(8,128)(2,1)S(1)}, bf16[48,1024]{1,0:T(8,128)(2,1)S(1)}, u32[]{:S(2)}, u32[]{:S(2)}) collective-permute-start(bf16[48,1024]{1,0:T(8,128)(2,1)S(1)} %get-tuple-element.174), channel_id=1, source_target_pairs={{0,4},{1,5},{2,6},{3,7},{4,0},{5,1},{6,2},{7,3},{8,12},{9,13},{10,... | collective-permute-start | bytes 294920 | tf_op jit(solution)/shard_map/ppermute | solution.py:135
  (4 other events, 18.5 us)

commit v11 on v10

--- a/solution.py
+++ b/solution.py
@@ -456,7 +456,7 @@
     )
     left_came, right_came = [swap(a, "expert", near_bit) for a in (left_sent, right_sent)]
 
-    cut = 3 * band // 4
+    cut = 5 * band // 8
 
     def both_parts(left, left_came, grad, grad_came, gate_send, up_high, up_low, gate_kept, up_kept):
         for j, (gate_out, up_out) in enumerate([(gate_send, None), (gate_kept, up_kept)]):

time: 106 us -> 106 us (level)
  starting transfers between devices: 33 us -> 34.2 us
  waiting for transfers between devices: 47.6 us -> 46.4 us
    ppermute x28, starting transfers between devices: 33 us -> 34.2 us  [swap(): return lax.ppermute(value, axis, [(i, i ^ mask) for i in range(size)])]
    ppermute x28, waiting for transfers between devices: 47.6 us -> 46.4 us  [swap(): return lax.ppermute(value, axis, [(i, i ^ mask) for i in range(size)])]
  transfers between devices with their start and end apart: 28 -> 28, of which waited for: 13 -> 14; matrix products, arithmetic and copies ran while one was open for 0% -> 0% of each run, Pallas kernels for 20% -> 20%
where the time goes in v11:
time: 106 us
  waiting for transfers between devices  46.4 us (44%)
  starting transfers between devices  34.2 us (32%)
  Pallas kernels  24.7 us (23%)
    ppermute x28, waiting for transfers between devices, swap(): return lax.ppermute(value, axis, [(i, i ^ mask) for i in range(size)])  46.4 us
    ppermute x28, starting transfers between devices, swap(): return lax.ppermute(value, axis, [(i, i ^ mask) for i in range(size)])  34.2 us
    pallas_call x31, Pallas kernels, stage(): pl.pallas_call(kernel, in_specs=[pl.BlockSpec(memory_space=m) for m in [A...  24.7 us
  transfers between devices with their start and end apart: 28, of which 14 were waited for; matrix products, arithmetic and copies ran while one was open for 0% of the time, Pallas kernels for 20%

profile of v11, /device:TPU:0, one launch (start us, length us, event | category | flops | bytes accessed | tf_op | source)
XLA Modules:
  0.0 106.1 jit_solution(52126366411148386)
XLA Ops:
  1.9 3.1 %collective-permute-start = (bf16[48,2176]{1,0:T(8,128)(2,1)S(1)}, bf16[48,2176]{1,0:T(8,128)(2,1)S(1)}, u32[]{:S(2)}, u32[]{:S(2)}) collective-permute-start(bf16[48,2176]{1,0:T(8,128)(2,1)S(1)} %get-tuple-element.96.refs_3_), channel_id=1, source_target_pairs={{0,2},{1,3},{2,0},{3,1},{4,6},{5,7},{6,4},{7,5},{8,10},{9,11},{10,... | collective-permute-start | bytes 626696 | tf_op jit(solution)/shard_map/ppermute | solution.py:135
  5.0 2.6 %collective-permute-start.1 = (bf16[48,2176]{1,0:T(8,128)(2,1)S(1)}, bf16[48,2176]{1,0:T(8,128)(2,1)S(1)}, u32[]{:S(2)}, u32[]{:S(2)}) collective-permute-start(bf16[48,2176]{1,0:T(8,128)(2,1)S(1)} %get-tuple-element.96.refs_3_), channel_id=1, source_target_pairs={{0,4},{1,5},{2,6},{3,7},{4,0},{5,1},{6,2},{7,3},{8,12},{9,13},{10,... | collective-permute-start | bytes 626696 | tf_op jit(solution)/shard_map/ppermute | solution.py:135
  7.6 1.5 %collective-permute-start.3 = (bf16[96,2176]{1,0:T(8,128)(2,1)S(1)}, bf16[96,2176]{1,0:T(8,128)(2,1)S(1)}, u32[]{:S(2)}, u32[]{:S(2)}) collective-permute-start(bf16[96,2176]{1,0:T(8,128)(2,1)S(1)} %get-tuple-element.99.refs_1_), channel_id=1, source_target_pairs={{0,1},{1,0},{2,3},{3,2},{4,5},{5,4},{6,7},{7,6},{8,9},{9,8},{10,11... | collective-permute-start | bytes 1253384 | tf_op jit(solution)/shard_map/ppermute | solution.py:135
  9.1 5.4 %collective-permute-done.refs_2_.refs_1_ = bf16[48,2176]{1,0:T(8,128)(2,1)S(1)} collective-permute-done((bf16[48,2176]{1,0:T(8,128)(2,1)S(1)}, bf16[48,2176]{1,0:T(8,128)(2,1)S(1)}, u32[]{:S(2)}, u32[]{:S(2)}) %collective-permute-start) | collective-permute-done | bytes 208928 | tf_op jit(solution)/shard_map/ppermute | solution.py:135
  15.3 4.8 %collective-permute-done.1.refs_2_.refs_1_ = bf16[48,2176]{1,0:T(8,128)(2,1)S(1)} collective-permute-done((bf16[48,2176]{1,0:T(8,128)(2,1)S(1)}, bf16[48,2176]{1,0:T(8,128)(2,1)S(1)}, u32[]{:S(2)}, u32[]{:S(2)}) %collective-permute-start.1) | collective-permute-done | bytes 208928 | tf_op jit(solution)/shard_map/ppermute | solution.py:135
  21.6 1.5 %collective-permute-start.8 = (bf16[96,2176]{1,0:T(8,128)(2,1)S(1)}, bf16[96,2176]{1,0:T(8,128)(2,1)S(1)}, u32[]{:S(2)}, u32[]{:S(2)}) collective-permute-start(bf16[96,2176]{1,0:T(8,128)(2,1)S(1)} %get-tuple-element.110.refs_4_), channel_id=1, source_target_pairs={{0,1},{1,0},{2,3},{3,2},{4,5},{5,4},{6,7},{7,6},{8,9},{9,8},{10,11... | collective-permute-start | bytes 1253384 | tf_op jit(solution)/shard_map/ppermute | solution.py:135
  23.8 5.4 %collective-permute-done.2.refs_1_ = bf16[48,2176]{1,0:T(8,128)(2,1)S(1)} collective-permute-done((bf16[48,2176]{1,0:T(8,128)(2,1)S(1)}, bf16[48,2176]{1,0:T(8,128)(2,1)S(1)}, u32[]{:S(2)}, u32[]{:S(2)}) %collective-permute-start.2) | collective-permute-done | bytes 208928 | tf_op jit(solution)/shard_map/ppermute | solution.py:135
  31.9 1.9 %collective-permute-start.9 = (bf16[96,2048]{1,0:T(8,128)(2,1)S(1)}, bf16[96,2048]{1,0:T(8,128)(2,1)S(1)}, u32[]{:S(2)}, u32[]{:S(2)}) collective-permute-start(bf16[96,2048]{1,0:T(8,128)(2,1)S(1)} %get-tuple-element.113.refs_3_), channel_id=1, source_target_pairs={{0,1},{1,0},{2,3},{3,2},{4,5},{5,4},{6,7},{7,6},{8,9},{9,8},{10,11... | collective-permute-start | bytes 1179656 | tf_op jit(solution)/shard_map/ppermute | solution.py:135
  33.8 3.8 %collective-permute-done.6.refs_1_ = bf16[48,2048]{1,0:T(8,128)(2,1)S(1)} collective-permute-done((bf16[48,2048]{1,0:T(8,128)(2,1)S(1)}, bf16[48,2048]{1,0:T(8,128)(2,1)S(1)}, u32[]{:S(2)}, u32[]{:S(2)}) %collective-permute-start.6) | collective-permute-done | bytes 196640 | tf_op jit(solution)/shard_map/ppermute | solution.py:135
  37.6 1.9 %collective-permute-start.10 = (bf16[48,2048]{1,0:T(8,128)(2,1)S(1)}, bf16[48,2048]{1,0:T(8,128)(2,1)S(1)}, u32[]{:S(2)}, u32[]{:S(2)}) collective-permute-start(bf16[48,2048]{1,0:T(8,128)(2,1)S(1)} %get-tuple-element.114.refs_4_), channel_id=1, source_target_pairs={{0,1},{1,0},{2,3},{3,2},{4,5},{5,4},{6,7},{7,6},{8,9},{9,8},{10,11... | collective-permute-start | bytes 589832 | tf_op jit(solution)/shard_map/ppermute | solution.py:135
  39.5 5.8 %shard_map.119 = (bf16[1024,384]{1,0:T(8,128)(2,1)S(1)}, bf16[1024,384]{1,0:T(8,128)(2,1)S(1)}, bf16[768,384]{1,0:T(8,128)(2,1)S(1)}, bf16[384,768]{1,0:T(8,128)...) custom-call(f32[8,128]{1,0:T(8,128)S(1)} %get-tuple-element.111.refs, ...), custom_call_target="tpu_custom_call" | custom-call | tf_op jit(solution)/shard_map/pallas_call | solution.py:120
  45.3 1.5 %collective-permute-done.10.refs_7_ = bf16[48,2048]{1,0:T(8,128)(2,1)S(1)} collective-permute-done((bf16[48,2048]{1,0:T(8,128)(2,1)S(1)}, bf16[48,2048]{1,0:T(8,128)(2,1)S(1)}, u32[]{:S(2)}, u32[]{:S(2)}) %collective-permute-start.10) | collective-permute-done | bytes 196640 | tf_op jit(solution)/shard_map/ppermute | solution.py:135
  51.3 1.6 %collective-permute-start.16 = (bf16[192,2048]{1,0:T(8,128)(2,1)S(1)}, bf16[192,2048]{1,0:T(8,128)(2,1)S(1)}, u32[]{:S(2)}, u32[]{:S(2)}) collective-permute-start(bf16[192,2048]{1,0:T(8,128)(2,1)S(1)} %get-tuple-element.142), channel_id=1, source_target_pairs={{0,16},{8,24},{16,0},{24,8},{1,17},{9,25},{17,1},{25,9},{2,18},{10... | collective-permute-start | bytes 2359304 | tf_op jit(solution)/shard_map/ppermute | solution.py:135
  54.2 1.6 %collective-permute-start.17 = (bf16[192,2048]{1,0:T(8,128)(2,1)S(1)}, bf16[192,2048]{1,0:T(8,128)(2,1)S(1)}, u32[]{:S(2)}, u32[]{:S(2)}) collective-permute-start(bf16[192,2048]{1,0:T(8,128)(2,1)S(1)} %get-tuple-element.145), channel_id=1, source_target_pairs={{0,1},{1,0},{2,3},{3,2},{4,5},{5,4},{6,7},{7,6},{8,9},{9,8},{10,11... | collective-permute-start | bytes 2359304 | tf_op jit(solution)/shard_map/ppermute | solution.py:135
  55.8 2.6 %shard_map.125 = (bf16[192,1024]{1,0:T(8,128)(2,1)S(1)}, bf16[192,1024]{1,0:T(8,128)(2,1)S(1)}, bf16[192,1024]{1,0:T(8,128)(2,1)S(1)}, bf16[192,1024]{1,0:T(8,128)(2,1)S(1)}, f32[8,128]{1,0:T(8,128)S(1)}) custom-call(f32[8,128]{1,0:T(8,128)S(1)} %get-tuple-element.129.refs_0_, bf16[384,1536]{1,0:T(8,128)(2,1)S(1)} %get-tuple-element.130.refs_1_.refs_3_, ...), custom_call_target="tpu_custom_call" | custom-call | tf_op jit(solution)/shard_map/pallas_call | solution.py:120
  60.5 3.4 %shard_map.126 = (bf16[512,768]{1,0:T(8,128)(2,1)S(1)}, bf16[320,768]{1,0:T(8,128)(2,1)S(1)}, bf16[192,768]{1,0:T(8,128)(2,1)S(1)}, f32[512,768]{1,0:T(8,128)S(1...) custom-call(f32[8,128]{1,0:T(8,128)S(1)} %get-tuple-element.134.refs_0_, ...), custom_call_target="tpu_custom_call" | custom-call | tf_op jit(solution)/shard_map/pallas_call | solution.py:120
  65.1 5.4 %collective-permute-done.15.refs_2_ = bf16[192,1024]{1,0:T(8,128)(2,1)S(1)} collective-permute-done((bf16[192,1024]{1,0:T(8,128)(2,1)S(1)}, bf16[192,1024]{1,0:T(8,128)(2,1)S(1)}, u32[]{:S(2)}, u32[]{:S(2)}) %collective-permute-start.15) | collective-permute-done | bytes 393248 | tf_op jit(solution)/shard_map/ppermute | solution.py:135
  72.9 1.7 %collective-permute-done.17.refs_2_ = bf16[192,2048]{1,0:T(8,128)(2,1)S(1)} collective-permute-done((bf16[192,2048]{1,0:T(8,128)(2,1)S(1)}, bf16[192,2048]{1,0:T(8,128)(2,1)S(1)}, u32[]{:S(2)}, u32[]{:S(2)}) %collective-permute-start.17) | collective-permute-done | bytes 786464 | tf_op jit(solution)/shard_map/ppermute | solution.py:135
  75.6 3.4 %collective-permute-done.18.refs_2_ = bf16[192,1024]{1,0:T(8,128)(2,1)S(1)} collective-permute-done((bf16[192,1024]{1,0:T(8,128)(2,1)S(1)}, bf16[192,1024]{1,0:T(8,128)(2,1)S(1)}, u32[]{:S(2)}, u32[]{:S(2)}) %collective-permute-start.18) | collective-permute-done | bytes 393248 | tf_op jit(solution)/shard_map/ppermute | solution.py:135
  80.9 3.7 %collective-permute-start.20 = (bf16[48,1024]{1,0:T(8,128)(2,1)S(1)}, bf16[48,1024]{1,0:T(8,128)(2,1)S(1)}, u32[]{:S(2)}, u32[]{:S(2)}) collective-permute-start(bf16[48,1024]{1,0:T(8,128)(2,1)S(1)} %get-tuple-element.156), channel_id=1, source_target_pairs={{0,4},{1,5},{2,6},{3,7},{4,0},{5,1},{6,2},{7,3},{8,12},{9,13},{10,... | collective-permute-start | bytes 294920 | tf_op jit(solution)/shard_map/ppermute | solution.py:135
  84.6 2.7 %collective-permute-done.20.refs_2_.refs_4_ = bf16[48,1024]{1,0:T(8,128)(2,1)S(1)} collective-permute-done((bf16[48,1024]{1,0:T(8,128)(2,1)S(1)}, bf16[48,1024]{1,0:T(8,128)(2,1)S(1)}, u32[]{:S(2)}, u32[]{:S(2)}) %collective-permute-start.20) | collective-permute-done | bytes 98336 | tf_op jit(solution)/shard_map/ppermute | solution.py:135
  88.3 3.0 %collective-permute-start.25 = (bf16[48,2048]{1,0:T(8,128)(2,1)S(1)}, bf16[48,2048]{1,0:T(8,128)(2,1)S(1)}, u32[]{:S(2)}, u32[]{:S(2)}) collective-permute-start(bf16[48,2048]{1,0:T(8,128)(2,1)S(1)} %get-tuple-element.171), channel_id=1, source_target_pairs={{0,4},{1,5},{2,6},{3,7},{4,0},{5,1},{6,2},{7,3},{8,12},{9,13},{10,... | collective-permute-start | bytes 589832 | tf_op jit(solution)/shard_map/ppermute | solution.py:135
  92.6 6.5 %collective-permute-done.24.refs_2_ = bf16[320,768]{1,0:T(8,128)(2,1)S(1)} collective-permute-done((bf16[320,768]{1,0:T(8,128)(2,1)S(1)}, bf16[320,768]{1,0:T(8,128)(2,1)S(1)}, u32[]{:S(2)}, u32[]{:S(2)}) %collective-permute-start.24) | collective-permute-done | bytes 491552 | tf_op jit(solution)/shard_map/ppermute | solution.py:135
  100.1 3.6 %collective-permute-done.26.refs_6_ = bf16[48,1024]{1,0:T(8,128)(2,1)S(1)} collective-permute-done((bf16[48,1024]{1,0:T(8,128)(2,1)S(1)}, bf16[48,1024]{1,0:T(8,128)(2,1)S(1)}, u32[]{:S(2)}, u32[]{:S(2)}) %collective-permute-start.26) | collective-permute-done | bytes 98336 | tf_op jit(solution)/shard_map/ppermute | solution.py:135
  (63 shorter events, 26.9 us)
Async XLA Ops:
  1.9 12.6 %collective-permute-start = (bf16[48,2176]{1,0:T(8,128)(2,1)S(1)}, bf16[48,2176]{1,0:T(8,128)(2,1)S(1)}, u32[]{:S(2)}, u32[]{:S(2)}) collective-permute-start(bf16[48,2176]{1,0:T(8,128)(2,1)S(1)} %get-tuple-element.96.refs_3_), channel_id=1, source_target_pairs={{0,2},{1,3},{2,0},{3,1},{4,6},{5,7},{6,4},{7,5},{8,10},{9,11},{10,... | collective-permute-start | bytes 626696 | tf_op jit(solution)/shard_map/ppermute | solution.py:135
  5.0 15.1 %collective-permute-start.1 = (bf16[48,2176]{1,0:T(8,128)(2,1)S(1)}, bf16[48,2176]{1,0:T(8,128)(2,1)S(1)}, u32[]{:S(2)}, u32[]{:S(2)}) collective-permute-start(bf16[48,2176]{1,0:T(8,128)(2,1)S(1)} %get-tuple-element.96.refs_3_), channel_id=1, source_target_pairs={{0,4},{1,5},{2,6},{3,7},{4,0},{5,1},{6,2},{7,3},{8,12},{9,13},{10,... | collective-permute-start | bytes 626696 | tf_op jit(solution)/shard_map/ppermute | solution.py:135
  7.6 21.6 %collective-permute-start.3 = (bf16[96,2176]{1,0:T(8,128)(2,1)S(1)}, bf16[96,2176]{1,0:T(8,128)(2,1)S(1)}, u32[]{:S(2)}, u32[]{:S(2)}) collective-permute-start(bf16[96,2176]{1,0:T(8,128)(2,1)S(1)} %get-tuple-element.99.refs_1_), channel_id=1, source_target_pairs={{0,1},{1,0},{2,3},{3,2},{4,5},{5,4},{6,7},{7,6},{8,9},{9,8},{10,11... | collective-permute-start | bytes 1253384 | tf_op jit(solution)/shard_map/ppermute | solution.py:135
  14.6 14.7 %collective-permute-start.4 = (bf16[48,2304]{1,0:T(8,128)(2,1)S(1)}, bf16[48,2304]{1,0:T(8,128)(2,1)S(1)}, u32[]{:S(2)}, u32[]{:S(2)}) collective-permute-start(bf16[48,2304]{1,0:T(8,128)(2,1)S(1)} %get-tuple-element.103), channel_id=1, source_target_pairs={{0,4},{1,5},{2,6},{3,7},{4,0},{5,1},{6,2},{7,3},{8,12},{9,13},{10,... | collective-permute-start | bytes 663560 | tf_op jit(solution)/shard_map/ppermute | solution.py:135
  20.2 9.0 %collective-permute-start.2 = (bf16[48,2176]{1,0:T(8,128)(2,1)S(1)}, bf16[48,2176]{1,0:T(8,128)(2,1)S(1)}, u32[]{:S(2)}, u32[]{:S(2)}) collective-permute-start(bf16[48,2176]{1,0:T(8,128)(2,1)S(1)} %get-tuple-element.102), channel_id=1, source_target_pairs={{0,2},{1,3},{2,0},{3,1},{4,6},{5,7},{6,4},{7,5},{8,10},{9,11},{10,... | collective-permute-start | bytes 626696 | tf_op jit(solution)/shard_map/ppermute | solution.py:135
  21.6 12.2 %collective-permute-start.8 = (bf16[96,2176]{1,0:T(8,128)(2,1)S(1)}, bf16[96,2176]{1,0:T(8,128)(2,1)S(1)}, u32[]{:S(2)}, u32[]{:S(2)}) collective-permute-start(bf16[96,2176]{1,0:T(8,128)(2,1)S(1)} %get-tuple-element.110.refs_4_), channel_id=1, source_target_pairs={{0,1},{1,0},{2,3},{3,2},{4,5},{5,4},{6,7},{7,6},{8,9},{9,8},{10,11... | collective-permute-start | bytes 1253384 | tf_op jit(solution)/shard_map/ppermute | solution.py:135
  23.1 8.7 %collective-permute-start.5 = (bf16[48,2048]{1,0:T(8,128)(2,1)S(1)}, bf16[48,2048]{1,0:T(8,128)(2,1)S(1)}, u32[]{:S(2)}, u32[]{:S(2)}) collective-permute-start(bf16[48,2048]{1,0:T(8,128)(2,1)S(1)} %get-tuple-element.105.refs_2_), channel_id=1, source_target_pairs={{0,2},{1,3},{2,0},{3,1},{4,6},{5,7},{6,4},{7,5},{8,10},{9,11},{10,... | collective-permute-start | bytes 589832 | tf_op jit(solution)/shard_map/ppermute | solution.py:135
  29.2 8.4 %collective-permute-start.7 = (bf16[48,2176]{1,0:T(8,128)(2,1)S(1)}, bf16[48,2176]{1,0:T(8,128)(2,1)S(1)}, u32[]{:S(2)}, u32[]{:S(2)}) collective-permute-start(bf16[48,2176]{1,0:T(8,128)(2,1)S(1)} %get-tuple-element.109.refs_5_), channel_id=1, source_target_pairs={{0,1},{1,0},{2,3},{3,2},{4,5},{5,4},{6,7},{7,6},{8,9},{9,8},{10,11... | collective-permute-start | bytes 626696 | tf_op jit(solution)/shard_map/ppermute | solution.py:135
  31.9 13.4 %collective-permute-start.9 = (bf16[96,2048]{1,0:T(8,128)(2,1)S(1)}, bf16[96,2048]{1,0:T(8,128)(2,1)S(1)}, u32[]{:S(2)}, u32[]{:S(2)}) collective-permute-start(bf16[96,2048]{1,0:T(8,128)(2,1)S(1)} %get-tuple-element.113.refs_3_), channel_id=1, source_target_pairs={{0,1},{1,0},{2,3},{3,2},{4,5},{5,4},{6,7},{7,6},{8,9},{9,8},{10,11... | collective-permute-start | bytes 1179656 | tf_op jit(solution)/shard_map/ppermute | solution.py:135
  37.6 9.2 %collective-permute-start.10 = (bf16[48,2048]{1,0:T(8,128)(2,1)S(1)}, bf16[48,2048]{1,0:T(8,128)(2,1)S(1)}, u32[]{:S(2)}, u32[]{:S(2)}) collective-permute-start(bf16[48,2048]{1,0:T(8,128)(2,1)S(1)} %get-tuple-element.114.refs_4_), channel_id=1, source_target_pairs={{0,1},{1,0},{2,3},{3,2},{4,5},{5,4},{6,7},{7,6},{8,9},{9,8},{10,11... | collective-permute-start | bytes 589832 | tf_op jit(solution)/shard_map/ppermute | solution.py:135
  50.5 10.0 %collective-permute-start.14 = (bf16[384,1536]{1,0:T(8,128)(2,1)S(1)}, bf16[384,1536]{1,0:T(8,128)(2,1)S(1)}, u32[]{:S(2)}, u32[]{:S(2)}) collective-permute-start(bf16[384,1536]{1,0:T(8,128)(2,1)S(1)} %get-tuple-element.130.refs_1_.refs_3_), channel_id=1, source_target_pairs={{0,8},{8,0},{16,24},{24,16},{1,9},{9,1},{17,25},{25,17},{2,10},{10... | collective-permute-start | bytes 3538952 | tf_op jit(solution)/shard_map/ppermute | solution.py:135
  51.3 20.4 %collective-permute-start.16 = (bf16[192,2048]{1,0:T(8,128)(2,1)S(1)}, bf16[192,2048]{1,0:T(8,128)(2,1)S(1)}, u32[]{:S(2)}, u32[]{:S(2)}) collective-permute-start(bf16[192,2048]{1,0:T(8,128)(2,1)S(1)} %get-tuple-element.142), channel_id=1, source_target_pairs={{0,16},{8,24},{16,0},{24,8},{1,17},{9,25},{17,1},{25,9},{2,18},{10... | collective-permute-start | bytes 2359304 | tf_op jit(solution)/shard_map/ppermute | solution.py:135
  54.2 20.5 %collective-permute-start.17 = (bf16[192,2048]{1,0:T(8,128)(2,1)S(1)}, bf16[192,2048]{1,0:T(8,128)(2,1)S(1)}, u32[]{:S(2)}, u32[]{:S(2)}) collective-permute-start(bf16[192,2048]{1,0:T(8,128)(2,1)S(1)} %get-tuple-element.145), channel_id=1, source_target_pairs={{0,1},{1,0},{2,3},{3,2},{4,5},{5,4},{6,7},{7,6},{8,9},{9,8},{10,11... | collective-permute-start | bytes 2359304 | tf_op jit(solution)/shard_map/ppermute | solution.py:135
  58.4 12.1 %collective-permute-start.15 = (bf16[192,1024]{1,0:T(8,128)(2,1)S(1)}, bf16[192,1024]{1,0:T(8,128)(2,1)S(1)}, u32[]{:S(2)}, u32[]{:S(2)}) collective-permute-start(bf16[192,1024]{1,0:T(8,128)(2,1)S(1)} %get-tuple-element.139), channel_id=1, source_target_pairs={{0,2},{1,3},{2,0},{3,1},{4,6},{5,7},{6,4},{7,5},{8,10},{9,11},{10,... | collective-permute-start | bytes 1179656 | tf_op jit(solution)/shard_map/ppermute | solution.py:135
  59.1 19.8 %collective-permute-start.18 = (bf16[192,1024]{1,0:T(8,128)(2,1)S(1)}, bf16[192,1024]{1,0:T(8,128)(2,1)S(1)}, u32[]{:S(2)}, u32[]{:S(2)}) collective-permute-start(bf16[192,1024]{1,0:T(8,128)(2,1)S(1)} %get-tuple-element.148), channel_id=1, source_target_pairs={{0,2},{1,3},{2,0},{3,1},{4,6},{5,7},{6,4},{7,5},{8,10},{9,11},{10,... | collective-permute-start | bytes 1179656 | tf_op jit(solution)/shard_map/ppermute | solution.py:135
  63.9 27.4 %collective-permute-start.23 = (bf16[512,768]{1,0:T(8,128)(2,1)S(1)}, bf16[512,768]{1,0:T(8,128)(2,1)S(1)}, u32[]{:S(2)}, u32[]{:S(2)}) collective-permute-start(bf16[512,768]{1,0:T(8,128)(2,1)S(1)} %get-tuple-element.165), channel_id=1, source_target_pairs={{0,16},{8,24},{16,0},{24,8},{1,17},{9,25},{17,1},{25,9},{2,18},{10... | collective-permute-start | bytes 2359304 | tf_op jit(solution)/shard_map/ppermute | solution.py:135
  70.6 8.4 %collective-permute-start.19 = (bf16[96,1024]{1,0:T(8,128)(2,1)S(1)}, bf16[96,1024]{1,0:T(8,128)(2,1)S(1)}, u32[]{:S(2)}, u32[]{:S(2)}) collective-permute-start(bf16[96,1024]{1,0:T(8,128)(2,1)S(1)} %get-tuple-element.151), channel_id=1, source_target_pairs={{0,1},{1,0},{2,3},{3,2},{4,5},{5,4},{6,7},{7,6},{8,9},{9,8},{10,11... | collective-permute-start | bytes 589832 | tf_op jit(solution)/shard_map/ppermute | solution.py:135
  74.9 13.3 %collective-permute-start.22 = (bf16[96,2048]{1,0:T(8,128)(2,1)S(1)}, bf16[96,2048]{1,0:T(8,128)(2,1)S(1)}, u32[]{:S(2)}, u32[]{:S(2)}) collective-permute-start(bf16[96,2048]{1,0:T(8,128)(2,1)S(1)} %get-tuple-element.162), channel_id=1, source_target_pairs={{0,2},{1,3},{2,0},{3,1},{4,6},{5,7},{6,4},{7,5},{8,10},{9,11},{10,... | collective-permute-start | bytes 1179656 | tf_op jit(solution)/shard_map/ppermute | solution.py:135
  79.1 20.0 %collective-permute-start.24 = (bf16[320,768]{1,0:T(8,128)(2,1)S(1)}, bf16[320,768]{1,0:T(8,128)(2,1)S(1)}, u32[]{:S(2)}, u32[]{:S(2)}) collective-permute-start(bf16[320,768]{1,0:T(8,128)(2,1)S(1)} %get-tuple-element.168), channel_id=1, source_target_pairs={{0,16},{8,24},{16,0},{24,8},{1,17},{9,25},{17,1},{25,9},{2,18},{10... | collective-permute-start | bytes 1474568 | tf_op jit(solution)/shard_map/ppermute | solution.py:135
  79.7 8.4 %collective-permute-start.21 = (bf16[96,1024]{1,0:T(8,128)(2,1)S(1)}, bf16[96,1024]{1,0:T(8,128)(2,1)S(1)}, u32[]{:S(2)}, u32[]{:S(2)}) collective-permute-start(bf16[96,1024]{1,0:T(8,128)(2,1)S(1)} %get-tuple-element.159), channel_id=1, source_target_pairs={{0,1},{1,0},{2,3},{3,2},{4,5},{5,4},{6,7},{7,6},{8,9},{9,8},{10,11... | collective-permute-start | bytes 589832 | tf_op jit(solution)/shard_map/ppermute | solution.py:135
  80.9 6.4 %collective-permute-start.20 = (bf16[48,1024]{1,0:T(8,128)(2,1)S(1)}, bf16[48,1024]{1,0:T(8,128)(2,1)S(1)}, u32[]{:S(2)}, u32[]{:S(2)}) collective-permute-start(bf16[48,1024]{1,0:T(8,128)(2,1)S(1)} %get-tuple-element.156), channel_id=1, source_target_pairs={{0,4},{1,5},{2,6},{3,7},{4,0},{5,1},{6,2},{7,3},{8,12},{9,13},{10,... | collective-permute-start | bytes 294920 | tf_op jit(solution)/shard_map/ppermute | solution.py:135
  87.3 17.4 %collective-permute-start.27 = (bf16[192,768]{1,0:T(8,128)(2,1)S(1)}, bf16[192,768]{1,0:T(8,128)(2,1)S(1)}, u32[]{:S(2)}, u32[]{:S(2)}) collective-permute-start(bf16[192,768]{1,0:T(8,128)(2,1)S(1)} %get-tuple-element.179), channel_id=1, source_target_pairs={{0,16},{8,24},{16,0},{24,8},{1,17},{9,25},{17,1},{25,9},{2,18},{10... | collective-permute-start | bytes 884744 | tf_op jit(solution)/shard_map/ppermute | solution.py:135
  88.3 15.4 %collective-permute-start.25 = (bf16[48,2048]{1,0:T(8,128)(2,1)S(1)}, bf16[48,2048]{1,0:T(8,128)(2,1)S(1)}, u32[]{:S(2)}, u32[]{:S(2)}) collective-permute-start(bf16[48,2048]{1,0:T(8,128)(2,1)S(1)} %get-tuple-element.171), channel_id=1, source_target_pairs={{0,4},{1,5},{2,6},{3,7},{4,0},{5,1},{6,2},{7,3},{8,12},{9,13},{10,... | collective-permute-start | bytes 589832 | tf_op jit(solution)/shard_map/ppermute | solution.py:135
  91.3 12.4 %collective-permute-start.26 = (bf16[48,1024]{1,0:T(8,128)(2,1)S(1)}, bf16[48,1024]{1,0:T(8,128)(2,1)S(1)}, u32[]{:S(2)}, u32[]{:S(2)}) collective-permute-start(bf16[48,1024]{1,0:T(8,128)(2,1)S(1)} %get-tuple-element.174), channel_id=1, source_target_pairs={{0,4},{1,5},{2,6},{3,7},{4,0},{5,1},{6,2},{7,3},{8,12},{9,13},{10,... | collective-permute-start | bytes 294920 | tf_op jit(solution)/shard_map/ppermute | solution.py:135
  (4 other events, 17.2 us)

commit v12 on v10

--- a/solution.py
+++ b/solution.py
@@ -551,7 +551,6 @@
     out_held, out_came, done = fold_on(out_kept, out_came, near_bit, [done])
     right_held, right_came, done = fold_on(right_kept, right_came, 1, [done])
     left_held, left_came, done = fold_on(left_held, left_came, far_bit, [done])
-    up_high, done = gated(up_high, [done])
     high_got = swap(up_high, "dp", 2)
     up_low, done = gated(up_low, [done], [left_came])
     low_got = swap(up_low, "dp", 2)

time: 106 us -> 106 us (level)
    pallas_call x31 -> x30, Pallas kernels: 24.8 us -> 24.7 us  [stage(): pl.pallas_call(kernel, in_specs=[pl.BlockSpec(memory_space=m) for m in [A...]
  transfers between devices with their start and end apart: 28 -> 28, of which waited for: 13 -> 16; matrix products, arithmetic and copies ran while one was open for 0% -> 0% of each run, Pallas kernels for 20% -> 20%
where the time goes in v12:
time: 106 us
  waiting for transfers between devices  46.9 us (44%)
  starting transfers between devices  33.7 us (32%)
  Pallas kernels  24.7 us (23%)
    ppermute x28, waiting for transfers between devices, swap(): return lax.ppermute(value, axis, [(i, i ^ mask) for i in range(size)])  46.9 us
    ppermute x28, starting transfers between devices, swap(): return lax.ppermute(value, axis, [(i, i ^ mask) for i in range(size)])  33.7 us
    pallas_call x30, Pallas kernels, stage(): pl.pallas_call(kernel, in_specs=[pl.BlockSpec(memory_space=m) for m in [A...  24.7 us
  transfers between devices with their start and end apart: 28, of which 16 were waited for; matrix products, arithmetic and copies ran while one was open for 0% of the time, Pallas kernels for 20%

profile of v12, /device:TPU:0, one launch (start us, length us, event | category | flops | bytes accessed | tf_op | source)
XLA Modules:
  0.0 106.1 jit_solution(3142168012117119309)
XLA Ops:
  1.9 3.1 %collective-permute-start = (bf16[48,2176]{1,0:T(8,128)(2,1)S(1)}, bf16[48,2176]{1,0:T(8,128)(2,1)S(1)}, u32[]{:S(2)}, u32[]{:S(2)}) collective-permute-start(bf16[48,2176]{1,0:T(8,128)(2,1)S(1)} %get-tuple-element.94.refs_3_), channel_id=1, source_target_pairs={{0,2},{1,3},{2,0},{3,1},{4,6},{5,7},{6,4},{7,5},{8,10},{9,11},{10,... | collective-permute-start | bytes 626696 | tf_op jit(solution)/shard_map/ppermute | solution.py:135
  5.0 2.6 %collective-permute-start.1 = (bf16[48,2176]{1,0:T(8,128)(2,1)S(1)}, bf16[48,2176]{1,0:T(8,128)(2,1)S(1)}, u32[]{:S(2)}, u32[]{:S(2)}) collective-permute-start(bf16[48,2176]{1,0:T(8,128)(2,1)S(1)} %get-tuple-element.94.refs_3_), channel_id=1, source_target_pairs={{0,4},{1,5},{2,6},{3,7},{4,0},{5,1},{6,2},{7,3},{8,12},{9,13},{10,... | collective-permute-start | bytes 626696 | tf_op jit(solution)/shard_map/ppermute | solution.py:135
  7.6 1.5 %collective-permute-start.3 = (bf16[96,2176]{1,0:T(8,128)(2,1)S(1)}, bf16[96,2176]{1,0:T(8,128)(2,1)S(1)}, u32[]{:S(2)}, u32[]{:S(2)}) collective-permute-start(bf16[96,2176]{1,0:T(8,128)(2,1)S(1)} %get-tuple-element.97.refs_1_), channel_id=1, source_target_pairs={{0,1},{1,0},{2,3},{3,2},{4,5},{5,4},{6,7},{7,6},{8,9},{9,8},{10,11... | collective-permute-start | bytes 1253384 | tf_op jit(solution)/shard_map/ppermute | solution.py:135
  9.1 5.4 %collective-permute-done.refs_2_.refs_1_ = bf16[48,2176]{1,0:T(8,128)(2,1)S(1)} collective-permute-done((bf16[48,2176]{1,0:T(8,128)(2,1)S(1)}, bf16[48,2176]{1,0:T(8,128)(2,1)S(1)}, u32[]{:S(2)}, u32[]{:S(2)}) %collective-permute-start) | collective-permute-done | bytes 208928 | tf_op jit(solution)/shard_map/ppermute | solution.py:135
  15.3 4.8 %collective-permute-done.1.refs_2_.refs_1_ = bf16[48,2176]{1,0:T(8,128)(2,1)S(1)} collective-permute-done((bf16[48,2176]{1,0:T(8,128)(2,1)S(1)}, bf16[48,2176]{1,0:T(8,128)(2,1)S(1)}, u32[]{:S(2)}, u32[]{:S(2)}) %collective-permute-start.1) | collective-permute-done | bytes 208928 | tf_op jit(solution)/shard_map/ppermute | solution.py:135
  21.6 1.5 %collective-permute-start.8 = (bf16[96,2176]{1,0:T(8,128)(2,1)S(1)}, bf16[96,2176]{1,0:T(8,128)(2,1)S(1)}, u32[]{:S(2)}, u32[]{:S(2)}) collective-permute-start(bf16[96,2176]{1,0:T(8,128)(2,1)S(1)} %get-tuple-element.108.refs_4_), channel_id=1, source_target_pairs={{0,1},{1,0},{2,3},{3,2},{4,5},{5,4},{6,7},{7,6},{8,9},{9,8},{10,11... | collective-permute-start | bytes 1253384 | tf_op jit(solution)/shard_map/ppermute | solution.py:135
  23.8 5.4 %collective-permute-done.2.refs_1_ = bf16[48,2176]{1,0:T(8,128)(2,1)S(1)} collective-permute-done((bf16[48,2176]{1,0:T(8,128)(2,1)S(1)}, bf16[48,2176]{1,0:T(8,128)(2,1)S(1)}, u32[]{:S(2)}, u32[]{:S(2)}) %collective-permute-start.2) | collective-permute-done | bytes 208928 | tf_op jit(solution)/shard_map/ppermute | solution.py:135
  31.9 1.9 %collective-permute-start.9 = (bf16[96,2048]{1,0:T(8,128)(2,1)S(1)}, bf16[96,2048]{1,0:T(8,128)(2,1)S(1)}, u32[]{:S(2)}, u32[]{:S(2)}) collective-permute-start(bf16[96,2048]{1,0:T(8,128)(2,1)S(1)} %get-tuple-element.111.refs_3_), channel_id=1, source_target_pairs={{0,1},{1,0},{2,3},{3,2},{4,5},{5,4},{6,7},{7,6},{8,9},{9,8},{10,11... | collective-permute-start | bytes 1179656 | tf_op jit(solution)/shard_map/ppermute | solution.py:135
  33.8 3.8 %collective-permute-done.6.refs_1_ = bf16[48,2048]{1,0:T(8,128)(2,1)S(1)} collective-permute-done((bf16[48,2048]{1,0:T(8,128)(2,1)S(1)}, bf16[48,2048]{1,0:T(8,128)(2,1)S(1)}, u32[]{:S(2)}, u32[]{:S(2)}) %collective-permute-start.6) | collective-permute-done | bytes 196640 | tf_op jit(solution)/shard_map/ppermute | solution.py:135
  37.6 1.9 %collective-permute-start.10 = (bf16[48,2048]{1,0:T(8,128)(2,1)S(1)}, bf16[48,2048]{1,0:T(8,128)(2,1)S(1)}, u32[]{:S(2)}, u32[]{:S(2)}) collective-permute-start(bf16[48,2048]{1,0:T(8,128)(2,1)S(1)} %get-tuple-element.112.refs_4_), channel_id=1, source_target_pairs={{0,1},{1,0},{2,3},{3,2},{4,5},{5,4},{6,7},{7,6},{8,9},{9,8},{10,11... | collective-permute-start | bytes 589832 | tf_op jit(solution)/shard_map/ppermute | solution.py:135
  39.5 5.8 %shard_map.119 = (bf16[1024,384]{1,0:T(8,128)(2,1)S(1)}, bf16[1024,384]{1,0:T(8,128)(2,1)S(1)}, bf16[768,384]{1,0:T(8,128)(2,1)S(1)}, bf16[384,768]{1,0:T(8,128)...) custom-call(f32[8,128]{1,0:T(8,128)S(1)} %get-tuple-element.109.refs, ...), custom_call_target="tpu_custom_call" | custom-call | tf_op jit(solution)/shard_map/pallas_call | solution.py:120
  45.3 1.5 %collective-permute-done.10.refs_7_ = bf16[48,2048]{1,0:T(8,128)(2,1)S(1)} collective-permute-done((bf16[48,2048]{1,0:T(8,128)(2,1)S(1)}, bf16[48,2048]{1,0:T(8,128)(2,1)S(1)}, u32[]{:S(2)}, u32[]{:S(2)}) %collective-permute-start.10) | collective-permute-done | bytes 196640 | tf_op jit(solution)/shard_map/ppermute | solution.py:135
  51.3 1.6 %collective-permute-start.16 = (bf16[192,2048]{1,0:T(8,128)(2,1)S(1)}, bf16[192,2048]{1,0:T(8,128)(2,1)S(1)}, u32[]{:S(2)}, u32[]{:S(2)}) collective-permute-start(bf16[192,2048]{1,0:T(8,128)(2,1)S(1)} %get-tuple-element.140), channel_id=1, source_target_pairs={{0,16},{8,24},{16,0},{24,8},{1,17},{9,25},{17,1},{25,9},{2,18},{10... | collective-permute-start | bytes 2359304 | tf_op jit(solution)/shard_map/ppermute | solution.py:135
  54.2 1.6 %collective-permute-start.17 = (bf16[192,2048]{1,0:T(8,128)(2,1)S(1)}, bf16[192,2048]{1,0:T(8,128)(2,1)S(1)}, u32[]{:S(2)}, u32[]{:S(2)}) collective-permute-start(bf16[192,2048]{1,0:T(8,128)(2,1)S(1)} %get-tuple-element.143), channel_id=1, source_target_pairs={{0,1},{1,0},{2,3},{3,2},{4,5},{5,4},{6,7},{7,6},{8,9},{9,8},{10,11... | collective-permute-start | bytes 2359304 | tf_op jit(solution)/shard_map/ppermute | solution.py:135
  55.8 2.6 %shard_map.125 = (bf16[192,1024]{1,0:T(8,128)(2,1)S(1)}, bf16[192,1024]{1,0:T(8,128)(2,1)S(1)}, bf16[192,1024]{1,0:T(8,128)(2,1)S(1)}, bf16[192,1024]{1,0:T(8,128)(2,1)S(1)}, f32[8,128]{1,0:T(8,128)S(1)}) custom-call(f32[8,128]{1,0:T(8,128)S(1)} %get-tuple-element.127.refs_0_, bf16[384,1536]{1,0:T(8,128)(2,1)S(1)} %get-tuple-element.128.refs_1_.refs_3_, ...), custom_call_target="tpu_custom_call" | custom-call | tf_op jit(solution)/shard_map/pallas_call | solution.py:120
  60.5 3.4 %shard_map.126 = (bf16[512,768]{1,0:T(8,128)(2,1)S(1)}, bf16[384,768]{1,0:T(8,128)(2,1)S(1)}, bf16[128,768]{1,0:T(8,128)(2,1)S(1)}, f32[512,768]{1,0:T(8,128)S(1...) custom-call(f32[8,128]{1,0:T(8,128)S(1)} %get-tuple-element.132.refs_0_, ...), custom_call_target="tpu_custom_call" | custom-call | tf_op jit(solution)/shard_map/pallas_call | solution.py:120
  65.1 5.4 %collective-permute-done.15.refs_2_ = bf16[192,1024]{1,0:T(8,128)(2,1)S(1)} collective-permute-done((bf16[192,1024]{1,0:T(8,128)(2,1)S(1)}, bf16[192,1024]{1,0:T(8,128)(2,1)S(1)}, u32[]{:S(2)}, u32[]{:S(2)}) %collective-permute-start.15) | collective-permute-done | bytes 393248 | tf_op jit(solution)/shard_map/ppermute | solution.py:135
  74.5 1.5 %collective-permute-start.19 = (bf16[96,1024]{1,0:T(8,128)(2,1)S(1)}, bf16[96,1024]{1,0:T(8,128)(2,1)S(1)}, u32[]{:S(2)}, u32[]{:S(2)}) collective-permute-start(bf16[96,1024]{1,0:T(8,128)(2,1)S(1)} %get-tuple-element.149), channel_id=1, source_target_pairs={{0,1},{1,0},{2,3},{3,2},{4,5},{5,4},{6,7},{7,6},{8,9},{9,8},{10,11... | collective-permute-start | bytes 589832 | tf_op jit(solution)/shard_map/ppermute | solution.py:135
  76.1 2.9 %collective-permute-done.18.refs_2_ = bf16[192,1024]{1,0:T(8,128)(2,1)S(1)} collective-permute-done((bf16[192,1024]{1,0:T(8,128)(2,1)S(1)}, bf16[192,1024]{1,0:T(8,128)(2,1)S(1)}, u32[]{:S(2)}, u32[]{:S(2)}) %collective-permute-start.18) | collective-permute-done | bytes 393248 | tf_op jit(solution)/shard_map/ppermute | solution.py:135
  79.6 1.7 %collective-permute-done.19.refs_2_ = bf16[96,1024]{1,0:T(8,128)(2,1)S(1)} collective-permute-done((bf16[96,1024]{1,0:T(8,128)(2,1)S(1)}, bf16[96,1024]{1,0:T(8,128)(2,1)S(1)}, u32[]{:S(2)}, u32[]{:S(2)}) %collective-permute-start.19) | collective-permute-done | bytes 196640 | tf_op jit(solution)/shard_map/ppermute | solution.py:135
  81.3 3.1 %collective-permute-start.20 = (bf16[48,1024]{1,0:T(8,128)(2,1)S(1)}, bf16[48,1024]{1,0:T(8,128)(2,1)S(1)}, u32[]{:S(2)}, u32[]{:S(2)}) collective-permute-start(bf16[48,1024]{1,0:T(8,128)(2,1)S(1)} %get-tuple-element.152), channel_id=1, source_target_pairs={{0,4},{1,5},{2,6},{3,7},{4,0},{5,1},{6,2},{7,3},{8,12},{9,13},{10,... | collective-permute-start | bytes 294920 | tf_op jit(solution)/shard_map/ppermute | solution.py:135
  84.4 2.7 %collective-permute-done.20.refs_2_.refs_4_ = bf16[48,1024]{1,0:T(8,128)(2,1)S(1)} collective-permute-done((bf16[48,1024]{1,0:T(8,128)(2,1)S(1)}, bf16[48,1024]{1,0:T(8,128)(2,1)S(1)}, u32[]{:S(2)}, u32[]{:S(2)}) %collective-permute-start.20) | collective-permute-done | bytes 98336 | tf_op jit(solution)/shard_map/ppermute | solution.py:135
  88.2 2.8 %collective-permute-start.25 = (bf16[48,2048]{1,0:T(8,128)(2,1)S(1)}, bf16[48,2048]{1,0:T(8,128)(2,1)S(1)}, u32[]{:S(2)}, u32[]{:S(2)}) collective-permute-start(bf16[48,2048]{1,0:T(8,128)(2,1)S(1)} %get-tuple-element.167), channel_id=1, source_target_pairs={{0,4},{1,5},{2,6},{3,7},{4,0},{5,1},{6,2},{7,3},{8,12},{9,13},{10,... | collective-permute-start | bytes 589832 | tf_op jit(solution)/shard_map/ppermute | solution.py:135
  93.1 8.1 %collective-permute-done.24.refs_2_ = bf16[384,768]{1,0:T(8,128)(2,1)S(1)} collective-permute-done((bf16[384,768]{1,0:T(8,128)(2,1)S(1)}, bf16[384,768]{1,0:T(8,128)(2,1)S(1)}, u32[]{:S(2)}, u32[]{:S(2)}) %collective-permute-start.24) | collective-permute-done | bytes 589856 | tf_op jit(solution)/shard_map/ppermute | solution.py:135
  (62 shorter events, 28.8 us)
Async XLA Ops:
  1.9 12.6 %collective-permute-start = (bf16[48,2176]{1,0:T(8,128)(2,1)S(1)}, bf16[48,2176]{1,0:T(8,128)(2,1)S(1)}, u32[]{:S(2)}, u32[]{:S(2)}) collective-permute-start(bf16[48,2176]{1,0:T(8,128)(2,1)S(1)} %get-tuple-element.94.refs_3_), channel_id=1, source_target_pairs={{0,2},{1,3},{2,0},{3,1},{4,6},{5,7},{6,4},{7,5},{8,10},{9,11},{10,... | collective-permute-start | bytes 626696 | tf_op jit(solution)/shard_map/ppermute | solution.py:135
  5.0 15.1 %collective-permute-start.1 = (bf16[48,2176]{1,0:T(8,128)(2,1)S(1)}, bf16[48,2176]{1,0:T(8,128)(2,1)S(1)}, u32[]{:S(2)}, u32[]{:S(2)}) collective-permute-start(bf16[48,2176]{1,0:T(8,128)(2,1)S(1)} %get-tuple-element.94.refs_3_), channel_id=1, source_target_pairs={{0,4},{1,5},{2,6},{3,7},{4,0},{5,1},{6,2},{7,3},{8,12},{9,13},{10,... | collective-permute-start | bytes 626696 | tf_op jit(solution)/shard_map/ppermute | solution.py:135
  7.6 21.6 %collective-permute-start.3 = (bf16[96,2176]{1,0:T(8,128)(2,1)S(1)}, bf16[96,2176]{1,0:T(8,128)(2,1)S(1)}, u32[]{:S(2)}, u32[]{:S(2)}) collective-permute-start(bf16[96,2176]{1,0:T(8,128)(2,1)S(1)} %get-tuple-element.97.refs_1_), channel_id=1, source_target_pairs={{0,1},{1,0},{2,3},{3,2},{4,5},{5,4},{6,7},{7,6},{8,9},{9,8},{10,11... | collective-permute-start | bytes 1253384 | tf_op jit(solution)/shard_map/ppermute | solution.py:135
  14.6 14.7 %collective-permute-start.4 = (bf16[48,2304]{1,0:T(8,128)(2,1)S(1)}, bf16[48,2304]{1,0:T(8,128)(2,1)S(1)}, u32[]{:S(2)}, u32[]{:S(2)}) collective-permute-start(bf16[48,2304]{1,0:T(8,128)(2,1)S(1)} %get-tuple-element.101), channel_id=1, source_target_pairs={{0,4},{1,5},{2,6},{3,7},{4,0},{5,1},{6,2},{7,3},{8,12},{9,13},{10,... | collective-permute-start | bytes 663560 | tf_op jit(solution)/shard_map/ppermute | solution.py:135
  20.2 9.0 %collective-permute-start.2 = (bf16[48,2176]{1,0:T(8,128)(2,1)S(1)}, bf16[48,2176]{1,0:T(8,128)(2,1)S(1)}, u32[]{:S(2)}, u32[]{:S(2)}) collective-permute-start(bf16[48,2176]{1,0:T(8,128)(2,1)S(1)} %get-tuple-element.100), channel_id=1, source_target_pairs={{0,2},{1,3},{2,0},{3,1},{4,6},{5,7},{6,4},{7,5},{8,10},{9,11},{10,... | collective-permute-start | bytes 626696 | tf_op jit(solution)/shard_map/ppermute | solution.py:135
  21.6 12.2 %collective-permute-start.8 = (bf16[96,2176]{1,0:T(8,128)(2,1)S(1)}, bf16[96,2176]{1,0:T(8,128)(2,1)S(1)}, u32[]{:S(2)}, u32[]{:S(2)}) collective-permute-start(bf16[96,2176]{1,0:T(8,128)(2,1)S(1)} %get-tuple-element.108.refs_4_), channel_id=1, source_target_pairs={{0,1},{1,0},{2,3},{3,2},{4,5},{5,4},{6,7},{7,6},{8,9},{9,8},{10,11... | collective-permute-start | bytes 1253384 | tf_op jit(solution)/shard_map/ppermute | solution.py:135
  23.1 8.7 %collective-permute-start.5 = (bf16[48,2048]{1,0:T(8,128)(2,1)S(1)}, bf16[48,2048]{1,0:T(8,128)(2,1)S(1)}, u32[]{:S(2)}, u32[]{:S(2)}) collective-permute-start(bf16[48,2048]{1,0:T(8,128)(2,1)S(1)} %get-tuple-element.103.refs_2_), channel_id=1, source_target_pairs={{0,2},{1,3},{2,0},{3,1},{4,6},{5,7},{6,4},{7,5},{8,10},{9,11},{10,... | collective-permute-start | bytes 589832 | tf_op jit(solution)/shard_map/ppermute | solution.py:135
  29.2 8.4 %collective-permute-start.7 = (bf16[48,2176]{1,0:T(8,128)(2,1)S(1)}, bf16[48,2176]{1,0:T(8,128)(2,1)S(1)}, u32[]{:S(2)}, u32[]{:S(2)}) collective-permute-start(bf16[48,2176]{1,0:T(8,128)(2,1)S(1)} %get-tuple-element.107.refs_5_), channel_id=1, source_target_pairs={{0,1},{1,0},{2,3},{3,2},{4,5},{5,4},{6,7},{7,6},{8,9},{9,8},{10,11... | collective-permute-start | bytes 626696 | tf_op jit(solution)/shard_map/ppermute | solution.py:135
  31.9 13.4 %collective-permute-start.9 = (bf16[96,2048]{1,0:T(8,128)(2,1)S(1)}, bf16[96,2048]{1,0:T(8,128)(2,1)S(1)}, u32[]{:S(2)}, u32[]{:S(2)}) collective-permute-start(bf16[96,2048]{1,0:T(8,128)(2,1)S(1)} %get-tuple-element.111.refs_3_), channel_id=1, source_target_pairs={{0,1},{1,0},{2,3},{3,2},{4,5},{5,4},{6,7},{7,6},{8,9},{9,8},{10,11... | collective-permute-start | bytes 1179656 | tf_op jit(solution)/shard_map/ppermute | solution.py:135
  37.6 9.2 %collective-permute-start.10 = (bf16[48,2048]{1,0:T(8,128)(2,1)S(1)}, bf16[48,2048]{1,0:T(8,128)(2,1)S(1)}, u32[]{:S(2)}, u32[]{:S(2)}) collective-permute-start(bf16[48,2048]{1,0:T(8,128)(2,1)S(1)} %get-tuple-element.112.refs_4_), channel_id=1, source_target_pairs={{0,1},{1,0},{2,3},{3,2},{4,5},{5,4},{6,7},{7,6},{8,9},{9,8},{10,11... | collective-permute-start | bytes 589832 | tf_op jit(solution)/shard_map/ppermute | solution.py:135
  50.5 10.0 %collective-permute-start.14 = (bf16[384,1536]{1,0:T(8,128)(2,1)S(1)}, bf16[384,1536]{1,0:T(8,128)(2,1)S(1)}, u32[]{:S(2)}, u32[]{:S(2)}) collective-permute-start(bf16[384,1536]{1,0:T(8,128)(2,1)S(1)} %get-tuple-element.128.refs_1_.refs_3_), channel_id=1, source_target_pairs={{0,8},{8,0},{16,24},{24,16},{1,9},{9,1},{17,25},{25,17},{2,10},{10... | collective-permute-start | bytes 3538952 | tf_op jit(solution)/shard_map/ppermute | solution.py:135
  51.3 20.4 %collective-permute-start.16 = (bf16[192,2048]{1,0:T(8,128)(2,1)S(1)}, bf16[192,2048]{1,0:T(8,128)(2,1)S(1)}, u32[]{:S(2)}, u32[]{:S(2)}) collective-permute-start(bf16[192,2048]{1,0:T(8,128)(2,1)S(1)} %get-tuple-element.140), channel_id=1, source_target_pairs={{0,16},{8,24},{16,0},{24,8},{1,17},{9,25},{17,1},{25,9},{2,18},{10... | collective-permute-start | bytes 2359304 | tf_op jit(solution)/shard_map/ppermute | solution.py:135
  54.2 19.5 %collective-permute-start.17 = (bf16[192,2048]{1,0:T(8,128)(2,1)S(1)}, bf16[192,2048]{1,0:T(8,128)(2,1)S(1)}, u32[]{:S(2)}, u32[]{:S(2)}) collective-permute-start(bf16[192,2048]{1,0:T(8,128)(2,1)S(1)} %get-tuple-element.143), channel_id=1, source_target_pairs={{0,1},{1,0},{2,3},{3,2},{4,5},{5,4},{6,7},{7,6},{8,9},{9,8},{10,11... | collective-permute-start | bytes 2359304 | tf_op jit(solution)/shard_map/ppermute | solution.py:135
  58.4 12.1 %collective-permute-start.15 = (bf16[192,1024]{1,0:T(8,128)(2,1)S(1)}, bf16[192,1024]{1,0:T(8,128)(2,1)S(1)}, u32[]{:S(2)}, u32[]{:S(2)}) collective-permute-start(bf16[192,1024]{1,0:T(8,128)(2,1)S(1)} %get-tuple-element.137), channel_id=1, source_target_pairs={{0,2},{1,3},{2,0},{3,1},{4,6},{5,7},{6,4},{7,5},{8,10},{9,11},{10,... | collective-permute-start | bytes 1179656 | tf_op jit(solution)/shard_map/ppermute | solution.py:135
  59.1 19.8 %collective-permute-start.18 = (bf16[192,1024]{1,0:T(8,128)(2,1)S(1)}, bf16[192,1024]{1,0:T(8,128)(2,1)S(1)}, u32[]{:S(2)}, u32[]{:S(2)}) collective-permute-start(bf16[192,1024]{1,0:T(8,128)(2,1)S(1)} %get-tuple-element.146), channel_id=1, source_target_pairs={{0,2},{1,3},{2,0},{3,1},{4,6},{5,7},{6,4},{7,5},{8,10},{9,11},{10,... | collective-permute-start | bytes 1179656 | tf_op jit(solution)/shard_map/ppermute | solution.py:135
  63.9 28.0 %collective-permute-start.23 = (bf16[512,768]{1,0:T(8,128)(2,1)S(1)}, bf16[512,768]{1,0:T(8,128)(2,1)S(1)}, u32[]{:S(2)}, u32[]{:S(2)}) collective-permute-start(bf16[512,768]{1,0:T(8,128)(2,1)S(1)} %get-tuple-element.161), channel_id=1, source_target_pairs={{0,16},{8,24},{16,0},{24,8},{1,17},{9,25},{17,1},{25,9},{2,18},{10... | collective-permute-start | bytes 2359304 | tf_op jit(solution)/shard_map/ppermute | solution.py:135
  70.5 30.7 %collective-permute-start.24 = (bf16[384,768]{1,0:T(8,128)(2,1)S(1)}, bf16[384,768]{1,0:T(8,128)(2,1)S(1)}, u32[]{:S(2)}, u32[]{:S(2)}) collective-permute-start(bf16[384,768]{1,0:T(8,128)(2,1)S(1)} %get-tuple-element.164), channel_id=1, source_target_pairs={{0,16},{8,24},{16,0},{24,8},{1,17},{9,25},{17,1},{25,9},{2,18},{10... | collective-permute-start | bytes 1769480 | tf_op jit(solution)/shard_map/ppermute | solution.py:135
  73.8 14.3 %collective-permute-start.22 = (bf16[96,2048]{1,0:T(8,128)(2,1)S(1)}, bf16[96,2048]{1,0:T(8,128)(2,1)S(1)}, u32[]{:S(2)}, u32[]{:S(2)}) collective-permute-start(bf16[96,2048]{1,0:T(8,128)(2,1)S(1)} %get-tuple-element.158), channel_id=1, source_target_pairs={{0,2},{1,3},{2,0},{3,1},{4,6},{5,7},{6,4},{7,5},{8,10},{9,11},{10,... | collective-permute-start | bytes 1179656 | tf_op jit(solution)/shard_map/ppermute | solution.py:135
  74.5 6.7 %collective-permute-start.19 = (bf16[96,1024]{1,0:T(8,128)(2,1)S(1)}, bf16[96,1024]{1,0:T(8,128)(2,1)S(1)}, u32[]{:S(2)}, u32[]{:S(2)}) collective-permute-start(bf16[96,1024]{1,0:T(8,128)(2,1)S(1)} %get-tuple-element.149), channel_id=1, source_target_pairs={{0,1},{1,0},{2,3},{3,2},{4,5},{5,4},{6,7},{7,6},{8,9},{9,8},{10,11... | collective-permute-start | bytes 589832 | tf_op jit(solution)/shard_map/ppermute | solution.py:135
  79.0 8.1 %collective-permute-start.21 = (bf16[96,1024]{1,0:T(8,128)(2,1)S(1)}, bf16[96,1024]{1,0:T(8,128)(2,1)S(1)}, u32[]{:S(2)}, u32[]{:S(2)}) collective-permute-start(bf16[96,1024]{1,0:T(8,128)(2,1)S(1)} %get-tuple-element.155), channel_id=1, source_target_pairs={{0,1},{1,0},{2,3},{3,2},{4,5},{5,4},{6,7},{7,6},{8,9},{9,8},{10,11... | collective-permute-start | bytes 589832 | tf_op jit(solution)/shard_map/ppermute | solution.py:135
  81.3 5.8 %collective-permute-start.20 = (bf16[48,1024]{1,0:T(8,128)(2,1)S(1)}, bf16[48,1024]{1,0:T(8,128)(2,1)S(1)}, u32[]{:S(2)}, u32[]{:S(2)}) collective-permute-start(bf16[48,1024]{1,0:T(8,128)(2,1)S(1)} %get-tuple-element.152), channel_id=1, source_target_pairs={{0,4},{1,5},{2,6},{3,7},{4,0},{5,1},{6,2},{7,3},{8,12},{9,13},{10,... | collective-permute-start | bytes 294920 | tf_op jit(solution)/shard_map/ppermute | solution.py:135
  88.2 15.2 %collective-permute-start.25 = (bf16[48,2048]{1,0:T(8,128)(2,1)S(1)}, bf16[48,2048]{1,0:T(8,128)(2,1)S(1)}, u32[]{:S(2)}, u32[]{:S(2)}) collective-permute-start(bf16[48,2048]{1,0:T(8,128)(2,1)S(1)} %get-tuple-element.167), channel_id=1, source_target_pairs={{0,4},{1,5},{2,6},{3,7},{4,0},{5,1},{6,2},{7,3},{8,12},{9,13},{10,... | collective-permute-start | bytes 589832 | tf_op jit(solution)/shard_map/ppermute | solution.py:135
  91.0 13.7 %collective-permute-start.27 = (bf16[128,768]{1,0:T(8,128)(2,1)S(1)}, bf16[128,768]{1,0:T(8,128)(2,1)S(1)}, u32[]{:S(2)}, u32[]{:S(2)}) collective-permute-start(bf16[128,768]{1,0:T(8,128)(2,1)S(1)} %get-tuple-element.175), channel_id=1, source_target_pairs={{0,16},{8,24},{16,0},{24,8},{1,17},{9,25},{17,1},{25,9},{2,18},{10... | collective-permute-start | bytes 589832 | tf_op jit(solution)/shard_map/ppermute | solution.py:135
  91.7 11.8 %collective-permute-start.26 = (bf16[48,1024]{1,0:T(8,128)(2,1)S(1)}, bf16[48,1024]{1,0:T(8,128)(2,1)S(1)}, u32[]{:S(2)}, u32[]{:S(2)}) collective-permute-start(bf16[48,1024]{1,0:T(8,128)(2,1)S(1)} %get-tuple-element.170), channel_id=1, source_target_pairs={{0,4},{1,5},{2,6},{3,7},{4,0},{5,1},{6,2},{7,3},{8,12},{9,13},{10,... | collective-permute-start | bytes 294920 | tf_op jit(solution)/shard_map/ppermute | solution.py:135
  (4 other events, 17.2 us)
